TPU v7x, 32 devices: a whole 2x2x4 slice. The times are simulated.
32 devices in a mesh: seq: 4 (over y, core), tp: 8 (over z, x).
Axes of the slice: x: 2, y: 2, z: 4, core: 2. Of those that a mesh axis runs over, the one named last changes fastest.
Arguments:
- layer_input: bfloat16 [16384, 2048], P(('seq', 'tp')), may hold values from -6 to 6
- cotangent: bfloat16 [16384, 2048], P(('seq', 'tp')), may hold values from -6 to 6
- counts: int32 [4], P('seq'), may hold values from 100 to 320
- positions: int32 [16384], P('seq'), may hold values from 0 to 4095, as said below
- qkv_master: float32 [2048, 6144], P('seq', 'tp'), may hold values from -0.125 to 0.125
- qkv_moment: float32 [2048, 6144], P('seq', 'tp'), may hold values from -1536 to 1536
- qkv_average: float32 [2048, 6144], P('seq', 'tp'), may hold values from -0.125 to 0.125
- out_master: float32 [2048, 2048], P('tp', 'seq'), may hold values from -2 to 2
- out_moment: float32 [2048, 2048], P('tp', 'seq'), may hold values from -40 to 40
- out_average: float32 [2048, 2048], P('tp', 'seq'), may hold values from -2 to 2
- gate_up_master: float32 [2, 2048, 8192], P(None, 'seq', 'tp'), may hold values from -0.125 to 0.125
- gate_up_moment: float32 [2, 2048, 8192], P(None, 'seq', 'tp'), may hold values from -224 to 224
- gate_up_average: float32 [2, 2048, 8192], P(None, 'seq', 'tp'), may hold values from -0.125 to 0.125
- down_master: float32 [8192, 2048], P('tp', 'seq'), may hold values from -0.0625 to 0.0625
- down_moment: float32 [8192, 2048], P('tp', 'seq'), may hold values from -384 to 384
- down_average: float32 [8192, 2048], P('tp', 'seq'), may hold values from -0.0625 to 0.0625
- gains_master: float32 [2, 2048], P(None, 'seq'), may hold values from 0.5 to 1.5
- gains_moment: float32 [2, 2048], P(None, 'seq'), may hold values from -1536 to 1536
- gains_average: float32 [2, 2048], P(None, 'seq'), may hold values from 0.5 to 1.5
Outputs:
- layer_output: bfloat16 [16384, 2048], P(('seq', 'tp'))
- input_grad: float32 [16384, 2048], P(('seq', 'tp'))
- qkv_moment_new: float32 [2048, 6144], P('seq', 'tp')
- qkv_average_new: float32 [2048, 6144], P('seq', 'tp')
- qkv_master_new: float32 [2048, 6144], P('seq', 'tp')
- qkv_copy_new: bfloat16 [2048, 6144], P('seq', 'tp')
- out_moment_new: float32 [2048, 2048], P('tp', 'seq')
- out_average_new: float32 [2048, 2048], P('tp', 'seq')
- out_master_new: float32 [2048, 2048], P('tp', 'seq')
- out_copy_new: bfloat16 [2048, 2048], P('tp', 'seq')
- gate_up_moment_new: float32 [2, 2048, 8192], P(None, 'seq', 'tp')
- gate_up_average_new: float32 [2, 2048, 8192], P(None, 'seq', 'tp')
- gate_up_master_new: float32 [2, 2048, 8192], P(None, 'seq', 'tp')
- gate_up_copy_new: bfloat16 [2, 2048, 8192], P(None, 'seq', 'tp')
- down_moment_new: float32 [8192, 2048], P('tp', 'seq')
- down_average_new: float32 [8192, 2048], P('tp', 'seq')
- down_master_new: float32 [8192, 2048], P('tp', 'seq')
- down_copy_new: bfloat16 [8192, 2048], P('tp', 'seq')
- gains_moment_new: float32 [2, 2048], P(None, 'seq')
- gains_average_new: float32 [2, 2048], P(None, 'seq')
- gains_master_new: float32 [2, 2048], P(None, 'seq')
- gains_copy_new: bfloat16 [2, 2048], P(None, 'seq')
Inputs may be any that keep to these rules, and one draw needn't show every extreme that they name: `positions`: in each sequence of 4096 tokens the position is 0 at the first token and at up to 3 document starts, and rises by one from token to token elsewhere; the first sequence holds a single document.
All inputs are finite; a program needn't handle non-finite values.
Results may differ from a plain program's by a relative error of at most 0.02.
Values may be sent and summed in bfloat16 or wider, within the bound.
A program may use at most 640 MiB of HBM per device.

v0:
```python
import jax
import jax.numpy as jnp
from jax import lax
from jax.sharding import PartitionSpec as P

HD = 64


norm_epsilon = 1e-05
rope_theta = 130000.0
momentum_coef = 0.9
average_coef = 0.5
masked_score = -1e30
rate_qkv = 0.004
rate_out = 2.0
rate_gate_up = 0.03
rate_down = 0.009
rate_gains = 0.1


def rms_scale(values):
    return lax.rsqrt(jnp.mean(values * values, axis=-1, keepdims=True) + norm_epsilon)


def rope_tables(positions, head_size):
    frequency = rope_theta ** (-(jnp.arange(head_size // 2, dtype=jnp.float32) * 2.0) / head_size)
    angles = positions.astype(jnp.float32)[:, None] * frequency[None, :]
    return (jnp.cos(angles)[:, None, :], jnp.sin(angles)[:, None, :])


def rotate(vectors, cosine_table, sine_table):
    half_width = vectors.shape[-1] // 2
    lower_half = vectors[..., :half_width]
    upper_half = vectors[..., half_width:]
    return jnp.concatenate(
        [
            lower_half * cosine_table - upper_half * sine_table,
            upper_half * cosine_table + lower_half * sine_table,
        ],
        axis=-1,
    )


def unrotate(grads, cosine_table, sine_table):
    half_width = grads.shape[-1] // 2
    lower_half = grads[..., :half_width]
    upper_half = grads[..., half_width:]
    return jnp.concatenate(
        [
            lower_half * cosine_table + upper_half * sine_table,
            upper_half * cosine_table - lower_half * sine_table,
        ],
        axis=-1,
    )


def norm_back(values, gain, grad):
    scale_rows = rms_scale(values)
    scaled = grad * gain
    back = scale_rows * (
        scaled
        - values * scale_rows * scale_rows * jnp.mean(scaled * values, axis=-1, keepdims=True)
    )
    return (back, jnp.sum(grad * values * scale_rows, axis=0))


def apply_update(master, grad, moment, average, rate):
    moment_new = momentum_coef * moment + grad
    master_new = master - rate * (grad + momentum_coef * moment_new)
    average_new = average_coef * average + (1.0 - average_coef) * master_new
    return (moment_new, average_new, master_new, master_new.astype(jnp.bfloat16))


def shards(
    layer_input,
    cotangent,
    counts,
    positions,
    qkv_master,
    qkv_moment,
    qkv_average,
    out_master,
    out_moment,
    out_average,
    gate_up_master,
    gate_up_moment,
    gate_up_average,
    down_master,
    down_moment,
    down_average,
    gains_master,
    gains_moment,
    gains_average,
):
    tp_size = lax.axis_size("tp")
    seq_size = lax.axis_size("seq")
    own_rows = layer_input.shape[0]
    length = own_rows * tp_size
    qkv_weight, out_weight, gate_up_weight, down_weight, gain_weight = (
        lax.all_gather(qkv_master.astype(jnp.bfloat16), "seq", axis=0, tiled=True),
        lax.all_gather(out_master.astype(jnp.bfloat16), "seq", axis=1, tiled=True),
        lax.all_gather(gate_up_master.astype(jnp.bfloat16), "seq", axis=1, tiled=True),
        lax.all_gather(down_master.astype(jnp.bfloat16), "seq", axis=1, tiled=True),
        lax.all_gather(gains_master.astype(jnp.bfloat16), "seq", axis=1, tiled=True),
    )
    heads_local = qkv_weight.shape[1] // (3 * HD)
    count_total = lax.psum(counts.astype(jnp.float32), "seq")
    seq_weight = seq_size * counts.astype(jnp.float32)[0] / count_total[0]
    gain_first = gain_weight[0].astype(jnp.float32)
    gain_second = gain_weight[1].astype(jnp.float32)
    gathered = lax.all_gather(layer_input, "tp", axis=0, tiled=True)
    inputs = gathered.astype(jnp.float32)
    normed = (inputs * rms_scale(inputs) * gain_first).astype(jnp.bfloat16)
    mixture = jnp.dot(normed, qkv_weight, preferred_element_type=jnp.float32).reshape(
        length, heads_local, 3, HD
    )
    cosine_table, sine_table = rope_tables(positions, HD)
    queries = rotate(mixture[:, :, 0], cosine_table, sine_table).astype(jnp.bfloat16)
    key_rows = rotate(mixture[:, :, 1], cosine_table, sine_table).astype(jnp.bfloat16)
    value_rows = mixture[:, :, 2].astype(jnp.bfloat16)
    block_rows = min(512, length)
    block_count = length // block_rows
    score_scale = HD ** (-0.5)

    def block_scores(block_index):
        key_end = (block_index + 1) * block_rows
        query_block = queries[block_index * block_rows : key_end]
        row_index = block_index * block_rows + jnp.arange(block_rows)
        allowed = jnp.arange(key_end)[None, :] <= row_index[:, None]
        scores = score_scale * jnp.einsum(
            "qhd,khd->hqk", query_block, key_rows[:key_end], preferred_element_type=jnp.float32
        )
        return (query_block, jnp.where(allowed[None], scores, masked_score))

    attended_list = []
    log_totals = []
    for block_index in range(block_count):
        query_block, scores = block_scores(block_index)
        key_end = (block_index + 1) * block_rows
        row_max = jnp.max(scores, axis=-1, keepdims=True)
        exp_scores = jnp.exp(scores - row_max)
        row_total = jnp.sum(exp_scores, axis=-1, keepdims=True)
        soft_scores = (exp_scores / row_total).astype(jnp.bfloat16)
        attended_block = jnp.einsum(
            "hqk,khd->qhd", soft_scores, value_rows[:key_end], preferred_element_type=jnp.float32
        )
        attended_list.append(attended_block.astype(jnp.bfloat16))
        log_totals.append(row_max + jnp.log(row_total))
    attended = jnp.concatenate(attended_list, axis=0).reshape(length, heads_local * HD)
    own_start = lax.axis_index("tp") * own_rows
    input_own = layer_input.astype(jnp.float32)
    branch = lax.psum(
        jnp.dot(attended, out_weight, preferred_element_type=jnp.float32).astype(jnp.bfloat16), "tp"
    ).astype(jnp.float32)
    residual = inputs + branch
    normed_second = (residual * rms_scale(residual) * gain_second).astype(jnp.bfloat16)
    resid_own = lax.dynamic_slice_in_dim(residual, own_start, own_rows, 0)
    gate_pre = jnp.dot(normed_second, gate_up_weight[0], preferred_element_type=jnp.float32)
    up_pre = jnp.dot(normed_second, gate_up_weight[1], preferred_element_type=jnp.float32)
    gate_sigmoid = jax.nn.sigmoid(gate_pre)
    activation = (gate_pre * gate_sigmoid * up_pre).astype(jnp.bfloat16)
    layer_output = (
        resid_own
        + lax.psum_scatter(
            jnp.dot(activation, down_weight, preferred_element_type=jnp.float32).astype(
                jnp.bfloat16
            ),
            "tp",
            scatter_dimension=0,
            tiled=True,
        ).astype(jnp.float32)
    ).astype(jnp.bfloat16)
    cot_all = lax.all_gather(cotangent, "tp", axis=0, tiled=True)
    grad_out = (seq_weight * cot_all.astype(jnp.float32)).astype(jnp.bfloat16)
    grad_down = jnp.einsum("tf,td->fd", activation, grad_out, preferred_element_type=jnp.float32)
    grad_act = jnp.einsum("td,fd->tf", grad_out, down_weight, preferred_element_type=jnp.float32)
    grad_gate = (grad_act * up_pre * gate_sigmoid * (1.0 + gate_pre * (1.0 - gate_sigmoid))).astype(
        jnp.bfloat16
    )
    grad_up = (grad_act * gate_pre * gate_sigmoid).astype(jnp.bfloat16)
    grad_gate_up = jnp.stack(
        [
            jnp.einsum("td,tf->df", normed_second, grad_gate, preferred_element_type=jnp.float32),
            jnp.einsum("td,tf->df", normed_second, grad_up, preferred_element_type=jnp.float32),
        ]
    )
    grad_normed_second = lax.psum_scatter(
        (
            jnp.einsum(
                "tf,df->td", grad_gate, gate_up_weight[0], preferred_element_type=jnp.float32
            )
            + jnp.einsum(
                "tf,df->td", grad_up, gate_up_weight[1], preferred_element_type=jnp.float32
            )
        ).astype(jnp.bfloat16),
        "tp",
        scatter_dimension=0,
        tiled=True,
    ).astype(jnp.float32)
    grad_resid_own, gain_second_part = norm_back(resid_own, gain_second, grad_normed_second)
    grad_resid_own = grad_resid_own + seq_weight * cotangent.astype(jnp.float32)
    resid_grad_rows = lax.all_gather(grad_resid_own.astype(jnp.bfloat16), "tp", axis=0, tiled=True)
    grad_out_proj = jnp.einsum(
        "tc,td->cd", attended, resid_grad_rows, preferred_element_type=jnp.float32
    )
    grad_attended = (
        jnp.einsum("td,cd->tc", resid_grad_rows, out_weight, preferred_element_type=jnp.float32)
        .astype(jnp.bfloat16)
        .reshape(length, heads_local, HD)
    )
    grad_keys = jnp.zeros((length, heads_local, HD), jnp.float32)
    grad_values = jnp.zeros((length, heads_local, HD), jnp.float32)
    query_grads = []
    for block_index in range(block_count):
        key_end = (block_index + 1) * block_rows
        query_block, scores = block_scores(block_index)
        soft_scores = jnp.exp(scores - log_totals[block_index])
        grad_block = grad_attended[block_index * block_rows : key_end]
        grad_soft = jnp.einsum(
            "qhd,khd->hqk", grad_block, value_rows[:key_end], preferred_element_type=jnp.float32
        )
        row_delta = jnp.sum(soft_scores * grad_soft, axis=-1, keepdims=True)
        grad_scores = (soft_scores * (grad_soft - row_delta)).astype(jnp.bfloat16)
        query_grads.append(
            score_scale
            * jnp.einsum(
                "hqk,khd->qhd", grad_scores, key_rows[:key_end], preferred_element_type=jnp.float32
            )
        )
        grad_keys = grad_keys.at[:key_end].add(
            score_scale
            * jnp.einsum(
                "hqk,qhd->khd", grad_scores, query_block, preferred_element_type=jnp.float32
            )
        )
        grad_values = grad_values.at[:key_end].add(
            jnp.einsum(
                "hqk,qhd->khd",
                soft_scores.astype(jnp.bfloat16),
                grad_block,
                preferred_element_type=jnp.float32,
            )
        )
    grad_queries = jnp.concatenate(query_grads, axis=0)
    grad_mixture = (
        jnp.stack(
            [
                unrotate(grad_queries, cosine_table, sine_table),
                unrotate(grad_keys, cosine_table, sine_table),
                grad_values,
            ],
            axis=2,
        )
        .astype(jnp.bfloat16)
        .reshape(length, heads_local * 3 * HD)
    )
    grad_qkv = jnp.einsum("td,tc->dc", normed, grad_mixture, preferred_element_type=jnp.float32)
    grad_normed_first = lax.psum_scatter(
        jnp.einsum(
            "tc,dc->td", grad_mixture, qkv_weight, preferred_element_type=jnp.float32
        ).astype(jnp.bfloat16),
        "tp",
        scatter_dimension=0,
        tiled=True,
    ).astype(jnp.float32)
    grad_input_own, gain_first_part = norm_back(input_own, gain_first, grad_normed_first)
    input_grad = grad_resid_own + grad_input_own
    gain_grads = lax.psum(jnp.stack([gain_first_part, gain_second_part]), ("seq", "tp"))
    gain_grad_own = lax.dynamic_slice_in_dim(
        gain_grads, lax.axis_index("seq") * gains_master.shape[1], gains_master.shape[1], 1
    )
    qkv_grad_own, out_grad_own, gate_up_grad_own, down_grad_own = (
        lax.psum_scatter(
            grad_qkv.astype(jnp.bfloat16), "seq", scatter_dimension=0, tiled=True
        ).astype(jnp.float32),
        lax.psum_scatter(
            grad_out_proj.astype(jnp.bfloat16), "seq", scatter_dimension=1, tiled=True
        ).astype(jnp.float32),
        lax.psum_scatter(
            grad_gate_up.astype(jnp.bfloat16), "seq", scatter_dimension=1, tiled=True
        ).astype(jnp.float32),
        lax.psum_scatter(
            grad_down.astype(jnp.bfloat16), "seq", scatter_dimension=1, tiled=True
        ).astype(jnp.float32),
    )
    rate_unit = float(length * seq_size) ** (-0.5)
    qkv_new = apply_update(qkv_master, qkv_grad_own, qkv_moment, qkv_average, rate_qkv * rate_unit)
    out_new = apply_update(out_master, out_grad_own, out_moment, out_average, rate_out * rate_unit)
    gate_up_new = apply_update(
        gate_up_master, gate_up_grad_own, gate_up_moment, gate_up_average, rate_gate_up * rate_unit
    )
    down_new = apply_update(
        down_master, down_grad_own, down_moment, down_average, rate_down * rate_unit
    )
    gains_new = apply_update(
        gains_master, gain_grad_own, gains_moment, gains_average, rate_gains * rate_unit
    )
    return (
        layer_output,
        input_grad,
        qkv_new[0],
        qkv_new[1],
        qkv_new[2],
        qkv_new[3],
        out_new[0],
        out_new[1],
        out_new[2],
        out_new[3],
        gate_up_new[0],
        gate_up_new[1],
        gate_up_new[2],
        gate_up_new[3],
        down_new[0],
        down_new[1],
        down_new[2],
        down_new[3],
        gains_new[0],
        gains_new[1],
        gains_new[2],
        gains_new[3],
    )


def solution(mesh):
    in_specs = (
        P(("seq", "tp"), None),
        P(("seq", "tp"), None),
        P("seq"),
        P("seq"),
        P("seq", "tp"),
        P("seq", "tp"),
        P("seq", "tp"),
        P("tp", "seq"),
        P("tp", "seq"),
        P("tp", "seq"),
        P(None, "seq", "tp"),
        P(None, "seq", "tp"),
        P(None, "seq", "tp"),
        P("tp", "seq"),
        P("tp", "seq"),
        P("tp", "seq"),
        P(None, "seq"),
        P(None, "seq"),
        P(None, "seq"),
    )
    out_specs = (
        P(("seq", "tp"), None),
        P(("seq", "tp"), None),
        P("seq", "tp"),
        P("seq", "tp"),
        P("seq", "tp"),
        P("seq", "tp"),
        P("tp", "seq"),
        P("tp", "seq"),
        P("tp", "seq"),
        P("tp", "seq"),
        P(None, "seq", "tp"),
        P(None, "seq", "tp"),
        P(None, "seq", "tp"),
        P(None, "seq", "tp"),
        P("tp", "seq"),
        P("tp", "seq"),
        P("tp", "seq"),
        P("tp", "seq"),
        P(None, "seq"),
        P(None, "seq"),
        P(None, "seq"),
        P(None, "seq"),
    )
    return jax.shard_map(shards, mesh=mesh, in_specs=in_specs, out_specs=out_specs, check_vma=False)
```

profile of v0, /device:TPU:0, one launch (start us, length us, event | category | flops | bytes accessed | tf_op | source)
XLA Modules:
  0.0 3028.2 jit_solution(8728600308112926493)
XLA Ops:
  35.9 204.6 %all-gather.8.cloned.1.call-done = bf16[4096,2048]{1,0:T(8,128)(2,1)} async-done(((bf16[512,2048]{1,0:T(8,128)(2,1)}), bf16[4096,2048]{1,0:T(8,128)(2,1)}) %all-gather.8.cloned.1.call-update) | async-done | bytes 16777232 | tf_op jit(solution)/shard_map/all_gather | solution.py:111
  247.8 21.6 all-gather.10.cloned.1.call-done
  269.4 21.1 fusion.74
  527.1 495.5 %all-reduce.4.cloned.1.call-done = bf16[4096,2048]{1,0:T(8,128)(2,1)} async-done(((bf16[4096,2048]{1,0:T(8,128)(2,1)}), bf16[4096,2048]{1,0:T(8,128)(2,1)}) %all-reduce.4.cloned.1.call-update) | async-done | bytes 16777232 | tf_op jit(solution)/shard_map/psum | solution.py:152
  1022.6 28.1 convert_add_fusion
  1082.0 24.3 fusion.123
  1106.3 20.9 fusion.122
  1127.1 221.1 %all-gather.18.cloned.1.call-done = bf16[4096,2048]{1,0:T(8,128)(2,1)} async-done(((bf16[512,2048]{1,0:T(8,128)(2,1)}), bf16[4096,2048]{1,0:T(8,128)(2,1)}) %all-gather.18.cloned.1.call-update) | async-done | bytes 16777232 | tf_op jit(solution)/shard_map/all_gather | solution.py:173
  1348.3 36.2 %multiply_convert_fusion.7 = (bf16[4096,1024]{1,0:T(8,128)(2,1)}, bf16[4096,1024]{1,0:T(8,128)(2,1)}, bf16[4096,1024]{1,0:T(8,128)(2,1)}) fusion(f32[4096,1024]{1,0:T(8,128)} %fusion.122, f32[4096,1024]{1,0:T(8,128)} %fusion.123, bf16[1024,2048]{1,0:T(8,128)(2,1)} %all-gather.16.cloned.1.call-done, bf16[4096,2048]{1,0:T(8,128)(2,1)} %all-gather.18.cloned.1.call-done, ...), kind=kOutput, calls=%fused_computation.46 | convolution fusion | flops 17272143872 | bytes 79691776 | tf_op jit(solution)/shard_map/td,fd->tf/dot_general | solution.py:176
  1384.5 25.3 fusion.121
  1409.8 27.5 add_convert_fusion
  1440.0 278.4 %reduce-scatter.10.cloned.1.call-done = bf16[512,2048]{1,0:T(8,128)(2,1)} async-done(((bf16[4096,2048]{1,0:T(8,128)(2,1)}), bf16[512,2048]{1,0:T(8,128)(2,1)}) %reduce-scatter.10.cloned.1.call-update) | async-done | bytes 2097168 | tf_op jit(solution)/shard_map/reduce_scatter | solution.py:187
  1729.2 24.2 fusion.119
  1756.0 22.8 convert_bitcast_fusion
  1778.8 23.7 convert_bitcast_fusion.1
  1808.9 146.9 %all-gather.20.cloned.1.call-done = bf16[4096,2048]{1,0:T(8,128)(2,1)} async-done(((bf16[512,2048]{1,0:T(8,128)(2,1)}), bf16[4096,2048]{1,0:T(8,128)(2,1)}) %all-gather.20.cloned.1.call-update) | async-done | bytes 16777232 | tf_op jit(solution)/shard_map/all_gather | solution.py:202
  2169.5 24.6 multiply_convert_fusion.3
  2204.6 22.9 multiply_reduce_fusion
  2227.6 27.7 multiply_convert_fusion
  2376.0 21.6 fusion.124
  2418.1 24.3 convolution_convert_fusion.1
  2477.2 249.7 %reduce-scatter.12.cloned.1.call-done = bf16[512,2048]{1,0:T(8,128)(2,1)} async-done(((bf16[4096,2048]{1,0:T(8,128)(2,1)}), bf16[512,2048]{1,0:T(8,128)(2,1)}) %reduce-scatter.12.cloned.1.call-update) | async-done | bytes 2097168 | tf_op jit(solution)/shard_map/reduce_scatter | solution.py:258
  2730.0 42.0 %psum.23 = f32[2,2048]{1,0:T(2,128)S(1)} all-reduce(f32[2,2048]{1,0:T(2,128)S(1)} %pad_maximum_fusion.13), channel_id=1, replica_groups=mesh['seq'=4,'tp'=8] {'seq','tp'}, use_global_device_ids=true, to_apply=%region_41.42 | all-reduce | flops 4096 | bytes 32768 | tf_op jit(solution)/shard_map/psum | solution.py:268
  2773.3 239.9 %reduce-scatter.8.cloned.1.call-done = bf16[512,2048]{1,0:T(8,128)(2,1)} async-done(((bf16[4096,2048]{1,0:T(8,128)(2,1)}), bf16[512,2048]{1,0:T(8,128)(2,1)}) %reduce-scatter.8.cloned.1.call-update) | async-done | bytes 2097168 | tf_op jit(solution)/shard_map/reduce_scatter | solution.py:164
  (480 shorter events, 735.8 us)
Async XLA Ops:
  7.2 233.3 %all-gather.8.cloned.1.call-start = ((), (), s32[]{:S(2)}) async-start(), calls=%async_computation.7 | async-start | bytes 18874368 | tf_op jit(solution)/shard_map/all_gather | solution.py:111
  8.0 261.5 %all-gather.10.cloned.1.call-start = ((), (), s32[]{:S(2)}) async-start(), calls=%async_computation.8 | async-start | bytes 3932160 | tf_op jit(solution)/shard_map/all_gather | solution.py:100
  10.4 492.3 %all-gather.12.cloned.1.call-start = ((), (), s32[]{:S(2)}) async-start(), calls=%async_computation.9 | async-start | bytes 1310720 | tf_op jit(solution)/shard_map/all_gather | solution.py:101
  11.2 1011.4 %all-reduce.4.cloned.1.call-start = ((), (), s32[]{:S(2)}) async-start(), calls=%async_computation.10 | async-start | bytes 33554432 | tf_op jit(solution)/shard_map/psum | solution.py:152
  512.9 569.1 %all-gather.14.cloned.1.call-start = ((), (), s32[]{:S(2)}) async-start(), calls=%async_computation.11 | async-start | bytes 10485760 | tf_op jit(solution)/shard_map/all_gather | solution.py:102
  517.0 610.2 %all-gather.16.cloned.1.call-start = ((), (), s32[]{:S(2)}) async-start(), calls=%async_computation.12 | async-start | bytes 5242880 | tf_op jit(solution)/shard_map/all_gather | solution.py:103
  518.2 830.1 %all-gather.18.cloned.1.call-start = ((), (), s32[]{:S(2)}) async-start(), calls=%async_computation.14 | async-start | bytes 18874368 | tf_op jit(solution)/shard_map/all_gather | solution.py:173
  518.9 1199.5 %reduce-scatter.10.cloned.1.call-start = ((), (), s32[]{:S(2)}) async-start(), calls=%async_computation.15 | async-start | bytes 18874368 | tf_op jit(solution)/shard_map/reduce_scatter | solution.py:187
  527.1 523.6 %copy-start.77 = (f32[1,2048]{1,0:T(1,128)S(1)}, f32[1,2048]{1,0:T(1,128)}, u32[]{:S(2)}) copy-start(f32[1,2048]{1,0:T(1,128)} %get-tuple-element.281) | copy-start | bytes 24580
  1437.3 518.5 %all-gather.20.cloned.1.call-start = ((), (), s32[]{:S(2)}) async-start(), calls=%async_computation.16 | async-start | bytes 18874368 | tf_op jit(solution)/shard_map/all_gather | solution.py:202
  1440.0 289.0 %copy-start.98 = (f32[512]{0:T(512)}, f32[512]{0:T(512)S(1)}, u32[]{:S(2)}) copy-start(f32[512]{0:T(512)S(1)} %add_rsqrt_fusion.3) | copy-start | bytes 6148
  1729.0 715.5 %reduce-scatter.20.cloned.1.call-start = ((), (), s32[]{:S(2)}) async-start(), calls=%async_computation.21 | async-start | bytes 5242880 | tf_op jit(solution)/shard_map/reduce_scatter | solution.py:282
  1753.5 699.2 %reduce-scatter.18.cloned.1.call-start = ((), (), s32[]{:S(2)}) async-start(), calls=%async_computation.20 | async-start | bytes 10485760 | tf_op jit(solution)/shard_map/reduce_scatter | solution.py:279
  1754.2 310.2 %copy-start.75 = (f32[4,512]{1,0:T(4,128)}, f32[4,512]{1,0:T(4,128)S(1)}, u32[]{:S(2)}) copy-start(f32[4,512]{1,0:T(4,128)S(1)} %log_add_fusion.3) | copy-start | bytes 24580
  1808.8 657.4 %reduce-scatter.16.cloned.1.call-start = ((), (), s32[]{:S(2)}) async-start(), calls=%async_computation.19 | async-start | bytes 1310720 | tf_op jit(solution)/shard_map/reduce_scatter | solution.py:276
  2375.9 94.7 %reduce-scatter.14.cloned.1.call-start = ((), (), s32[]{:S(2)}) async-start(), calls=%async_computation.18 | async-start | bytes 3932160 | tf_op jit(solution)/shard_map/reduce_scatter | solution.py:273
  2397.6 329.2 %reduce-scatter.12.cloned.1.call-start = ((), (), s32[]{:S(2)}) async-start(), calls=%async_computation.17 | async-start | bytes 18874368 | tf_op jit(solution)/shard_map/reduce_scatter | solution.py:258
  2418.1 595.1 %reduce-scatter.8.cloned.1.call-start = ((), (), s32[]{:S(2)}) async-start(), calls=%async_computation.13 | async-start | bytes 18874368 | tf_op jit(solution)/shard_map/reduce_scatter | solution.py:164
  2475.8 296.2 %copy-start.130 = (f32[2,512]{1,0:T(2,128)S(1)}, f32[2,512]{1,0:T(2,128)}, u32[]{:S(2)}) copy-start(f32[2,512]{1,0:T(2,128)} %param.71) | copy-start | bytes 12292
  2475.8 296.2 %copy-start.132 = (f32[2,512]{1,0:T(2,128)S(1)}, f32[2,512]{1,0:T(2,128)}, u32[]{:S(2)}) copy-start(f32[2,512]{1,0:T(2,128)} %param.72) | copy-start | bytes 12292
  2475.8 296.8 %copy-start.131 = (f32[2,512]{1,0:T(2,128)S(1)}, f32[2,512]{1,0:T(2,128)}, u32[]{:S(2)}) copy-start(f32[2,512]{1,0:T(2,128)} %param.73) | copy-start | bytes 12292
  2475.8 537.3 %copy-start.79 = (f32[1,2048]{1,0:T(1,128)S(1)}, f32[1,2048]{1,0:T(1,128)}, u32[]{:S(2)}) copy-start(f32[1,2048]{1,0:T(1,128)} %get-tuple-element.281) | copy-start | bytes 24580
  2475.9 537.3 %copy-start.99 = (f32[512]{0:T(512)S(1)}, f32[512]{0:T(512)}, u32[]{:S(2)}) copy-start(f32[512]{0:T(512)} %copy-done.98) | copy-start | bytes 6148
  2475.9 537.3 %copy-start.124 = (f32[512]{0:T(512)S(1)}, f32[512]{0:T(512)}, u32[]{:S(2)}) copy-start(f32[512]{0:T(512)} %copy-done.123) | copy-start | bytes 6148
  (141 other events, 3957.0 us)
Sparse Core Ops, SparseCore 0:
  10.2 230.2 all-gather.7
  242.7 26.7 all-gather.9
  271.6 16.7 all-gather.11
  513.0 509.5 all-reduce.3
  1024.6 57.3 all-gather.13
  1084.0 34.4 all-gather.15
  1120.6 227.5 all-gather.17
  1437.5 280.8 reduce-scatter.9
  1729.1 226.6 all-gather.19
  1958.9 42.7 reduce-scatter.19
  2004.3 71.6 reduce-scatter.17
  2376.0 23.3 reduce-scatter.15
  2402.0 37.9 reduce-scatter.13
  2444.1 282.7 reduce-scatter.11
  2730.5 282.6 reduce-scatter.7
where the time goes:
time: 3040 us; the launch traced here: 3030 us
  waiting for transfers between devices  1870 us (62%)
  matrix products  716 us (24%)
  other arithmetic  322 us (11%)
  blocking collectives  54.9 us (2%)
  local copies, waits for them, and re-layouts  44 us (1%)
    psum x1, waiting for transfers between devices, shards(): lax.psum(jnp.dot(attended, out_weight, preferred_element_type=jnp.float32...  495 us
    reduce_scatter x1, waiting for transfers between devices, shards(): lax.psum_scatter((jnp.einsum('tf,df->td', grad_gate, gate_up_weight[0], p...  278 us
    reduce_scatter x1, waiting for transfers between devices, shards(): lax.psum_scatter(jnp.einsum('tc,dc->td', grad_mixture, qkv_weight, prefer...  250 us
    reduce_scatter x1, waiting for transfers between devices, shards(): lax.psum_scatter(jnp.dot(activation, down_weight, preferred_element_type=...  240 us
    all_gather x1, waiting for transfers between devices, shards(): cot_all = lax.all_gather(cotangent, 'tp', axis=0, tiled=True)  221 us
    all_gather x1, waiting for transfers between devices, shards(): gathered = lax.all_gather(layer_input, 'tp', axis=0, tiled=True)  205 us
    all_gather x1, waiting for transfers between devices, shards(): lax.all_gather(grad_resid_own.astype(jnp.bfloat16), 'tp', axis=0, tiled=T...  147 us
    convert_element_type x8, other arithmetic, shards(): grad_scores = (soft_scores * (grad_soft - row_delta)).astype(jnp.bfloat16)  108 us
  transfers between devices with their start and end apart: 15, of which 9 were waited for; matrix products, arithmetic and copies ran while one was open for 31% of the time, Pallas kernels for 0%

commit v1 on v0

--- a/solution.py
+++ b/solution.py
@@ -1,6 +1,8 @@
 import jax
 import jax.numpy as jnp
 from jax import lax
+from jax.experimental import pallas as pl
+from jax.experimental.pallas import tpu as pltpu
 from jax.sharding import PartitionSpec as P
 
 HD = 64
@@ -321,6 +323,642 @@
     )
 
 
+ROW = 512
+BF = jnp.bfloat16
+F32 = jnp.float32
+LOG2E = 1.4426950408889634
+STORED = (0, 4, 1, 5, 2, 6, 3, 7)
+NT = (((1,), (1,)), ((), ()))
+NN = (((1,), (0,)), ((), ()))
+TN = (((0,), (0,)), ((), ()))
+
+
+def ring_plan_fits(mesh):
+    return mesh.shape["seq"] == 4 and mesh.shape["tp"] == 8
+
+
+def device_pairs(target):
+    pairs = []
+    for index in range(32):
+        y, c, h, l, x = (index >> 4) & 1, (index >> 3) & 1, (index >> 2) & 1, (index >> 1) & 1, index & 1
+        goal = target(y, c, h, l, x)
+        if goal is not None:
+            y, c, h, l, x = goal
+            pairs.append((index, 16 * y + 8 * c + 4 * h + 2 * l + x))
+    return pairs
+
+
+def move(values, target):
+    return lax.ppermute(values, ("seq", "tp"), device_pairs(target))
+
+
+def flip(values, bits):
+    return move(
+        values,
+        lambda y, c, h, l, x: (
+            y ^ ("y" in bits),
+            c ^ ("c" in bits),
+            h ^ ("h" in bits),
+            l ^ ("l" in bits),
+            x ^ ("x" in bits),
+        ),
+    )
+
+
+def swap_ch(values):
+    return move(values, lambda y, c, h, l, x: (y, h, c, l, x))
+
+
+def flip_slot(values, slot):
+    return flip(values, ("c" if slot & 4 else "") + ("l" if slot & 2 else "") + ("x" if slot & 1 else ""))
+
+
+def ring_gather(own):
+    half = own.shape[0] // 2
+    s1 = flip(own, "x")
+    s2 = flip(own, "l")
+    s4 = flip(own, "c")
+    s3a = flip(s1[:half], "l")
+    s3b = flip(s2[half:], "x")
+    s5 = flip(s1, "c")
+    s6 = flip(s2, "c")
+    s7a = flip(s3a, "c")
+    s7b = flip(s3b, "c")
+    return (
+        jnp.concatenate([own, s4]),
+        jnp.concatenate([s1, s5]),
+        jnp.concatenate([s2, s6]),
+        jnp.concatenate([s3a, s3b, s7a, s7b]),
+    )
+
+
+def ring_scatter(part):
+    def rounded(values):
+        return values.astype(BF)
+
+    q3 = rounded(part(3) + flip(rounded(part(7)), "c").astype(F32))
+    half = q3.shape[0] // 2
+    ra = flip(q3[:half], "x").astype(F32)
+    rb = flip(q3[half:], "l").astype(F32)
+    q1 = part(1) + flip(rounded(part(5)), "c").astype(F32)
+    q2 = part(2) + flip(rounded(part(6)), "c").astype(F32)
+    r1a = flip(rounded(q1[:half]), "x").astype(F32)
+    r2b = flip(rounded(q2[half:]), "l").astype(F32)
+    r1b = flip(rounded(q1[half:] + rb), "x").astype(F32)
+    r2a = flip(rounded(q2[:half] + ra), "l").astype(F32)
+    q0 = part(0) + flip(rounded(part(4)), "c").astype(F32)
+    return q0 + jnp.concatenate([r1a + r2a, r1b + r2b])
+
+
+def heads_to_rows(blocks):
+    got = []
+    for place, slot in enumerate(STORED):
+        block = blocks[place * ROW : (place + 1) * ROW]
+        got.append(block if slot == 0 else flip_slot(block, slot))
+    return jnp.concatenate(got, axis=1)
+
+
+def rows_to_heads(rows):
+    width = rows.shape[1] // 8
+    got = []
+    for place, slot in enumerate(STORED):
+        block = rows[:, place * width : (place + 1) * width]
+        got.append(block if slot == 0 else flip_slot(block, slot))
+    return jnp.concatenate(got, axis=0)
+
+
+def column_order():
+    column = lax.broadcasted_iota(jnp.int32, (768, 768), 1)
+    row = lax.broadcasted_iota(jnp.int32, (768, 768), 0)
+    part, within = column // 256, column % 256
+    turned = ((within % 128) // 32) * 192 + part * 64 + (within // 128) * 32 + within % 32
+    plain = (within // 64) * 192 + 128 + within % 64
+    return (row == jnp.where(part == 2, plain, turned)).astype(BF)
+
+
+def head_lanes_turned(head):
+    lane = lax.broadcasted_iota(jnp.int32, (1, 256), 1)
+    return (lane % 128) // 32 == head
+
+
+def head_lanes_plain(head):
+    lane = lax.broadcasted_iota(jnp.int32, (1, 256), 1)
+    return lane // 64 == head
+
+
+def stored_place(block, me):
+    slot = block ^ me
+    return (slot & 3) * 2 + (slot >> 2)
+
+
+def picked_block(step, split, splits):
+    half = 4 // splits
+    return jnp.where(step < half, split * half + step, 7 - (split * half + step - half))
+
+
+def attend_kernel(split, splits, me_ref, q_ref, k_ref, v_ref, *refs):
+    o_ref, l_ref, s_scr, m_scr, acc_scr, o_scr = refs[-6:]
+    heads = 4
+    block = picked_block(pl.program_id(0), split, splits)
+    me = me_ref[0]
+    q = q_ref[...]
+    row = lax.broadcasted_iota(jnp.int32, (ROW, ROW), 0)
+    col = lax.broadcasted_iota(jnp.int32, (ROW, ROW), 1)
+
+    def lane_max(s):
+        return jnp.maximum(
+            jnp.maximum(s[:, :128], s[:, 128:256]), jnp.maximum(s[:, 256:384], s[:, 384:])
+        )
+
+    def lane_sum(s):
+        return (s[:, :128] + s[:, 128:256]) + (s[:, 256:384] + s[:, 384:])
+
+    def start_of(key_block):
+        return pl.multiple_of(stored_place(key_block, me) * ROW, ROW)
+
+    for head in range(heads):
+        qh = jnp.where(head_lanes_turned(head), q, jnp.zeros_like(q))
+
+        def scores(key_block):
+            return lax.dot_general(
+                qh, k_ref[pl.ds(start_of(key_block), ROW), :], NT, preferred_element_type=F32
+            )
+
+        s = jnp.where(col <= row, scores(block), masked_score)
+        s_scr[block] = s
+        m_scr[...] = lane_max(s)
+
+        def first_pass(key_block, carry):
+            s = scores(key_block)
+            s_scr[key_block] = s
+            m_scr[...] = jnp.maximum(m_scr[...], lane_max(s))
+            return carry
+
+        lax.fori_loop(0, block, first_pass, 0)
+        top = jnp.max(m_scr[...], axis=1, keepdims=True)
+        m_scr[...] = jnp.zeros_like(m_scr)
+        acc_scr[...] = jnp.zeros_like(acc_scr)
+
+        def second_pass(key_block, carry):
+            e = jnp.exp2(s_scr[key_block] - top)
+            m_scr[...] += lane_sum(e)
+            acc_scr[...] += lax.dot_general(
+                e.astype(BF), v_ref[pl.ds(start_of(key_block), ROW), :], NN, preferred_element_type=F32
+            )
+            return carry
+
+        lax.fori_loop(0, block + 1, second_pass, 0)
+        total = jnp.sum(m_scr[...], axis=1, keepdims=True)
+        part = acc_scr[...] * (1.0 / total)
+        if head == 0:
+            o_scr[...] = part
+        else:
+            o_scr[...] = jnp.where(head_lanes_plain(head), part, o_scr[...])
+        level = jnp.broadcast_to(top + jnp.log2(total), (ROW, 128))
+        l_ref[0, head : head + 1, :] = jnp.transpose(level)[0:1, :]
+    o_ref[...] = o_scr[...].astype(BF)
+
+
+def attend(me, q, k, v, split, splits, earlier):
+    length = q.shape[0]
+    blocks = length // ROW
+
+    def place(step, me):
+        return stored_place(picked_block(step, split, splits), me[0])
+
+    whole = pl.BlockSpec((length, 256), lambda step, me: (0, 0))
+    grid = pltpu.PrefetchScalarGridSpec(
+        num_scalar_prefetch=1,
+        grid=(blocks // splits,),
+        in_specs=[pl.BlockSpec((ROW, 256), lambda step, me: (place(step, me), 0)), whole, whole]
+        + [pl.BlockSpec(memory_space=pl.ANY)] * len(earlier),
+        out_specs=[
+            pl.BlockSpec((ROW, 256), lambda step, me: (place(step, me), 0)),
+            pl.BlockSpec((1, 4, ROW), lambda step, me: (place(step, me), 0, 0)),
+        ],
+        scratch_shapes=[
+            pltpu.VMEM((blocks, ROW, ROW), F32),
+            pltpu.VMEM((ROW, 128), F32),
+            pltpu.VMEM((ROW, 256), F32),
+            pltpu.VMEM((ROW, 256), F32),
+        ],
+    )
+    return pl.pallas_call(
+        lambda *refs: attend_kernel(split, splits, *refs),
+        grid_spec=grid,
+        out_shape=[
+            jax.ShapeDtypeStruct((length, 256), BF),
+            jax.ShapeDtypeStruct((blocks, 4, ROW), F32),
+        ],
+        input_output_aliases={4: 0, 5: 1} if earlier else {},
+        compiler_params=pltpu.CompilerParams(vmem_limit_bytes=48 * 2**20),
+        cost_estimate=pl.CostEstimate(
+            flops=10**11 // splits, bytes_accessed=10 * 2**20, transcendentals=0
+        ),
+    )(me, q, k, v, *earlier)
+
+
+KEYS = 256
+
+
+def attend_back_kernel(split, splits, me_ref, q_ref, k_ref, v_ref, do_ref, o_ref, l_ref, cos_ref, sin_ref, *refs):
+    if split == 0:
+        dq_in = None
+    else:
+        dq_in = refs[0]
+    dkv_ref, dq_out, qm, dom, delta, dq, dk, dv, km, pt, dst = refs[-11:]
+    heads = 4
+    me = me_ref[0]
+    step = pl.program_id(0)
+    blocks = q_ref.shape[0] // ROW
+
+    @pl.when(step == 0)
+    def _():
+        def prepare(place, carry):
+            start = pl.multiple_of(place * ROW, ROW)
+            q = q_ref[pl.ds(start, ROW), :]
+            do = do_ref[pl.ds(start, ROW), :]
+            for head in range(heads):
+                rows = slice(head * ROW, (head + 1) * ROW)
+                qm[place, rows, :] = jnp.where(head_lanes_turned(head), q, jnp.zeros_like(q))
+                dom[place, rows, :] = jnp.where(head_lanes_plain(head), do, jnp.zeros_like(do))
+            product = do.astype(F32) * o_ref[pl.ds(start, ROW), :].astype(F32)
+            high = product.astype(BF)
+            low = (product - high.astype(F32)).astype(BF)
+            head_row = lax.broadcasted_iota(jnp.int32, (8, 256), 0)
+            lane = lax.broadcasted_iota(jnp.int32, (8, 256), 1)
+            pick = jnp.where(lane // 64 == head_row, 1.0, 0.0).astype(BF)
+            sums = lax.dot_general(pick, high, NT, preferred_element_type=F32)
+            sums += lax.dot_general(pick, low, NT, preferred_element_type=F32)
+            delta[place] = sums[:heads, :]
+            if split == 0:
+                dq[pl.ds(start, ROW), :] = jnp.zeros((ROW, 256), F32)
+            else:
+                dq[pl.ds(start, ROW), :] = dq_in[pl.ds(start, ROW), :]
+            return carry
+
+        lax.fori_loop(0, blocks, prepare, 0)
+
+    key_row = lax.broadcasted_iota(jnp.int32, (KEYS, ROW), 0)
+    query_col = lax.broadcasted_iota(jnp.int32, (KEYS, ROW), 1)
+    block = picked_block(step, split, splits)
+    key_place = stored_place(block, me)
+
+    def key_part(sub, carry):
+        inner = pl.multiple_of(sub * KEYS, KEYS)
+        table = pl.ds(pl.multiple_of(key_place * ROW + sub * KEYS, KEYS), KEYS)
+        k = k_ref[pl.ds(inner, KEYS), :]
+        v = v_ref[pl.ds(inner, KEYS), :]
+        for head in range(heads):
+            km[head] = jnp.where(head_lanes_turned(head), k, jnp.zeros_like(k))
+        dk[...] = jnp.zeros_like(dk)
+        dv[...] = jnp.zeros_like(dv)
+
+        def query_part(query_block, diagonal):
+            place = stored_place(query_block, me)
+            rows = pl.ds(pl.multiple_of(place * ROW, ROW), ROW)
+            for head in range(heads):
+                part = slice(head * ROW, (head + 1) * ROW)
+                st = lax.dot_general(k, qm[place, part, :], NT, preferred_element_type=F32)
+                dp = lax.dot_general(v, dom[place, part, :], NT, preferred_element_type=F32)
+                p = jnp.exp2(st - l_ref[place, head : head + 1, :])
+                if diagonal:
+                    p = jnp.where(key_row + inner <= query_col, p, 0.0)
+                ds = p * (dp - delta[place, head : head + 1, :])
+                pt[:, part] = p.astype(BF)
+                dst[:, part] = ds.astype(BF)
+            dv[...] += lax.dot_general(pt[...], dom[place], NN, preferred_element_type=F32)
+            dk[...] += lax.dot_general(dst[...], qm[place], NN, preferred_element_type=F32)
+            total = lax.dot_general(dst[:, 0:ROW], km[0], TN, preferred_element_type=F32)
+            for head in range(1, heads):
+                part = slice(head * ROW, (head + 1) * ROW)
+                total += lax.dot_general(dst[:, part], km[head], TN, preferred_element_type=F32)
+            dq[rows, :] += total
+
+        query_part(block, True)
+
+        def later(query_block, carry):
+            query_part(query_block, False)
+            return carry
+
+        lax.fori_loop(block + 1, blocks, later, 0)
+        cs = cos_ref[table, :]
+        sn = sin_ref[table, :]
+        d = dk[...] * (1.0 / LOG2E)
+        d1, d2 = d[:, :128], d[:, 128:]
+        dkv_ref[pl.ds(inner, KEYS), 0:128] = (d1 * cs + d2 * sn).astype(BF)
+        dkv_ref[pl.ds(inner, KEYS), 128:256] = (d2 * cs - d1 * sn).astype(BF)
+        dkv_ref[pl.ds(inner, KEYS), 256:512] = dv[...].astype(BF)
+        return carry
+
+    lax.fori_loop(0, ROW // KEYS, key_part, 0)
+
+    @pl.when(step == pl.num_programs(0) - 1)
+    def _():
+        def finish(place, carry):
+            rows = pl.ds(pl.multiple_of(place * ROW, ROW), ROW)
+            if split < splits - 1:
+                dq_out[rows, :] = dq[rows, :]
+            else:
+                cs = cos_ref[rows, :]
+                sn = sin_ref[rows, :]
+                d = dq[rows, :] * 0.125
+                d1, d2 = d[:, :128], d[:, 128:]
+                dq_out[rows, 0:128] = (d1 * cs + d2 * sn).astype(BF)
+                dq_out[rows, 128:256] = (d2 * cs - d1 * sn).astype(BF)
+            return carry
+
+        lax.fori_loop(0, blocks, finish, 0)
+
+
+def attend_back(me, q, k, v, do, o, level, cos, sin, split, splits, earlier):
+    length = q.shape[0]
+    blocks = length // ROW
+
+    def place(step, me):
+        return stored_place(picked_block(step, split, splits), me[0])
+
+    def whole(width):
+        return pl.BlockSpec((length, width), lambda step, me: (0, 0))
+
+    key_spec = pl.BlockSpec((ROW, 256), lambda step, me: (place(step, me), 0))
+    more = []
+    if earlier:
+        more = [whole(256), pl.BlockSpec(memory_space=pl.ANY)]
+    grid = pltpu.PrefetchScalarGridSpec(
+        num_scalar_prefetch=1,
+        grid=(blocks // splits,),
+        in_specs=[
+            whole(256),
+            key_spec,
+            key_spec,
+            whole(256),
+            whole(256),
+            pl.BlockSpec((blocks, 4, ROW), lambda step, me: (0, 0, 0)),
+            whole(128),
+            whole(128),
+        ]
+        + more,
+        out_specs=[pl.BlockSpec((ROW, 512), lambda step, me: (place(step, me), 0)), whole(256)],
+        scratch_shapes=[
+            pltpu.VMEM((blocks, 4 * ROW, 256), BF),
+            pltpu.VMEM((blocks, 4 * ROW, 256), BF),
+            pltpu.VMEM((blocks, 4, ROW), F32),
+            pltpu.VMEM((length, 256), F32),
+            pltpu.VMEM((KEYS, 256), F32),
+            pltpu.VMEM((KEYS, 256), F32),
+            pltpu.VMEM((4, KEYS, 256), BF),
+            pltpu.VMEM((KEYS, 4 * ROW), BF),
+            pltpu.VMEM((KEYS, 4 * ROW), BF),
+        ],
+    )
+    last = split == splits - 1
+    return pl.pallas_call(
+        lambda *refs: attend_back_kernel(split, splits, *refs),
+        grid_spec=grid,
+        out_shape=[
+            jax.ShapeDtypeStruct((length, 512), BF),
+            jax.ShapeDtypeStruct((length, 256), BF if last else F32),
+        ],
+        input_output_aliases={10: 0} if earlier else {},
+        compiler_params=pltpu.CompilerParams(vmem_limit_bytes=62 * 2**20),
+        cost_estimate=pl.CostEstimate(
+            flops=14 * 10**10 // splits, bytes_accessed=20 * 2**20, transcendentals=0
+        ),
+    )(me, q, k, v, do, o, level, cos, sin, *earlier)
+
+
+def ring_shards(
+    layer_input,
+    cotangent,
+    counts,
+    positions,
+    qkv_master,
+    qkv_moment,
+    qkv_average,
+    out_master,
+    out_moment,
+    out_average,
+    gate_up_master,
+    gate_up_moment,
+    gate_up_average,
+    down_master,
+    down_moment,
+    down_average,
+    gains_master,
+    gains_moment,
+    gains_average,
+):
+    seq, tp = lax.axis_index("seq"), lax.axis_index("tp")
+    y, c, h = seq >> 1, seq & 1, tp >> 2
+    own = c * 4 + (tp & 3)
+    me = own.astype(jnp.int32).reshape(1)
+    plain_y, plain_c, straight = y == 0, c == 0, c == h
+
+    def features(values):
+        half = values.shape[-1] // 2
+        return jnp.where(
+            plain_y, values, jnp.concatenate([values[..., half:], values[..., :half]], axis=-1)
+        )
+
+    def both_cores(mine, other):
+        return jnp.where(plain_c, mine, other), jnp.where(plain_c, other, mine)
+
+    def gather_weight(shard):
+        r1 = move(shard, lambda y, c, h, l, x: (y, c, 1 - h, l, x) if c == h else None)
+        r2a = move(shard, lambda y, c, h, l, x: (y, 1 - c, h, l, x) if c != h else None)
+        r2b = move(shard, lambda y, c, h, l, x: (y, h, c, l, x) if c != h else None)
+        near = jnp.stack(both_cores(jnp.where(straight, shard, r1), jnp.where(straight, r2a, r2b)))
+        far = flip(near, "y")
+        return near[0], near[1], far[0], far[1]
+
+    def scatter_grad(near, far):
+        total = (near.astype(F32) + flip(far, "y").astype(F32)).astype(BF)
+        kept, other = both_cores(total[0], total[1])
+        r1 = move(kept, lambda y, c, h, l, x: (y, c, 1 - h, l, x) if c != h else None)
+        r2a = move(other, lambda y, c, h, l, x: (y, 1 - c, h, l, x) if c == h else None)
+        r2b = move(other, lambda y, c, h, l, x: (y, h, c, l, x) if c != h else None)
+        return jnp.where(
+            straight,
+            kept.astype(F32) + r1.astype(F32),
+            r2a.astype(F32) + r2b.astype(F32),
+        )
+
+    turn = column_order()
+    qkv_shard = jnp.dot(qkv_master.astype(BF), turn, preferred_element_type=F32).astype(BF)
+    rows_in = features(swap_ch(layer_input)).astype(F32)
+    gains_here = gains_master.astype(BF)
+    gains_near = jnp.concatenate(both_cores(gains_here, flip(gains_here, "c")), axis=1)
+    gains_all = jnp.concatenate([gains_near, flip(gains_near, "y")], axis=1).astype(F32)
+    gain_first, gain_second = gains_all[0], gains_all[1]
+    count_here = counts.astype(F32)
+    count_pair = both_cores(count_here, flip(count_here, "c"))
+    pair_total = count_pair[0] + count_pair[1]
+    count_total = pair_total + flip(pair_total, "y")
+    seq_weight = 4.0 * jnp.where(h == 0, count_pair[0], count_pair[1])[0] / count_total[0]
+
+    scale_first = rms_scale(rows_in)
+    normed_groups = ring_gather((rows_in * scale_first * gain_first).astype(BF))
+    qkv_weight = jnp.concatenate(gather_weight(qkv_shard), axis=0)
+
+    place_order = jnp.stack([own ^ slot for slot in STORED])
+    positions_here = swap_ch(positions).reshape(8, ROW)[place_order].reshape(8 * ROW)
+    frequency = rope_theta ** (
+        -((jnp.arange(128, dtype=jnp.int32) % 32).astype(F32) * 2.0) / HD
+    )
+    angles = positions_here.astype(F32)[:, None] * frequency[None, :]
+    cosine, sine = jnp.cos(angles), jnp.sin(angles)
+
+    queries, keys, values = [], [], []
+    for place, group in enumerate(normed_groups):
+        mixed = jnp.dot(group, qkv_weight, preferred_element_type=F32)
+        rows = slice(place * 2 * ROW, (place + 1) * 2 * ROW)
+        cs, sn = cosine[rows], sine[rows]
+
+        def turned(u1, u2):
+            return jnp.concatenate([u1 * cs - u2 * sn, u2 * cs + u1 * sn], axis=1)
+
+        queries.append((turned(mixed[:, :128], mixed[:, 128:256]) * (0.125 * LOG2E)).astype(BF))
+        keys.append(turned(mixed[:, 256:384], mixed[:, 384:512]).astype(BF))
+        values.append(mixed[:, 512:].astype(BF))
+    queries, keys, values = (jnp.concatenate(v, axis=0) for v in (queries, keys, values))
+
+    gate_up_shard = jnp.concatenate(
+        [gate_up_master[m, :, k * 512 : (k + 1) * 512] for m in range(2) for k in range(2)]
+        + [out_master],
+        axis=0,
+    ).astype(BF)
+    gate_up_blocks = gather_weight(gate_up_shard)
+    gate_up_weight = jnp.concatenate(
+        [
+            jnp.concatenate([block[k * 512 : (k + 1) * 512] for k in range(4)], axis=1)
+            for block in gate_up_blocks
+        ],
+        axis=0,
+    )
+    out_heads = jnp.concatenate([block[2048:] for block in gate_up_blocks], axis=1)
+    out_weight = jnp.concatenate(ring_gather(out_heads), axis=0)
+    down_weight = jnp.concatenate(gather_weight(down_master.astype(BF)), axis=1)
+
+    grad_rows = seq_weight * features(swap_ch(cotangent)).astype(F32)
+    grad_out = jnp.concatenate(ring_gather(grad_rows.astype(BF)), axis=0)
+
+    splits = 4
+    done = ()
+    for split in range(splits):
+        done = tuple(attend(me, queries, keys, values, split, splits, done))
+    attended, level = done
+    attended_own = heads_to_rows(attended)
+    residual = rows_in + jnp.dot(attended_own, out_weight, preferred_element_type=F32)
+    scale_second = rms_scale(residual)
+    second_groups = ring_gather((residual * scale_second * gain_second).astype(BF))
+    gate, up, activation = [], [], []
+    for group in second_groups:
+        g = jnp.dot(group, gate_up_weight[:, :1024], preferred_element_type=F32)
+        u = jnp.dot(group, gate_up_weight[:, 1024:], preferred_element_type=F32)
+        gate.append(g.astype(BF))
+        up.append(u.astype(BF))
+        activation.append((g * jax.nn.sigmoid(g) * u).astype(BF))
+    gate, up, activation = (jnp.concatenate(v, axis=0) for v in (gate, up, activation))
+    normed_second = jnp.concatenate(second_groups, axis=0)
+
+    def rows_of(slot):
+        place = STORED.index(slot)
+        return slice(place * ROW, (place + 1) * ROW)
+
+    grad_act = lax.dot_general(grad_out, down_weight, NT, preferred_element_type=F32)
+    g = gate.astype(F32)
+    sigmoid = jax.nn.sigmoid(g)
+    grad_gate = (grad_act * up.astype(F32) * sigmoid * (1.0 + g * (1.0 - sigmoid))).astype(BF)
+    grad_up = (grad_act * g * sigmoid).astype(BF)
+    grad_gate_up = jnp.concatenate([grad_gate, grad_up], axis=1)
+
+    grad_normed_second = ring_scatter(
+        lambda slot: lax.dot_general(
+            grad_gate_up[rows_of(slot)], gate_up_weight, NT, preferred_element_type=F32
+        )
+    )
+    layer_own = residual + ring_scatter(
+        lambda slot: jnp.dot(activation[rows_of(slot)], down_weight, preferred_element_type=F32)
+    )
+    layer_output = swap_ch(features(layer_own.astype(BF)))
+
+    down_grad = lax.dot_general(activation, grad_out, TN, preferred_element_type=F32).astype(BF)
+    down_grad = down_grad.reshape(1024, 4, 512).transpose(1, 0, 2)
+    down_grad_own = scatter_grad(down_grad[:2], down_grad[2:])
+    gate_up_grad = lax.dot_general(
+        normed_second, grad_gate_up, TN, preferred_element_type=F32
+    ).astype(BF)
+    gate_up_grad = gate_up_grad.reshape(4, 512, 2048)
+    gate_up_grad_own = scatter_grad(gate_up_grad[:2], gate_up_grad[2:])
+
+    def norm_grad(values, scale, gain, grad):
+        scaled = grad * gain
+        back = scale * (
+            scaled - values * scale * scale * jnp.mean(scaled * values, axis=-1, keepdims=True)
+        )
+        return back, jnp.sum(grad * values * scale, axis=0)
+
+    residual_grad, gain_second_part = norm_grad(
+        residual, scale_second, gain_second, grad_normed_second
+    )
+    residual_grad = residual_grad + grad_rows
+    residual_low = residual_grad.astype(BF)
+    grad_attended = rows_to_heads(
+        lax.dot_general(residual_low, out_weight, NT, preferred_element_type=F32).astype(BF)
+    )
+    out_grad = lax.dot_general(attended_own, residual_low, TN, preferred_element_type=F32).astype(BF)
+    out_grad = ring_scatter(
+        lambda slot: out_grad[STORED.index(slot) * 256 : (STORED.index(slot) + 1) * 256].astype(F32)
+    ).astype(BF)
+    out_grad = out_grad.reshape(256, 4, 512).transpose(1, 0, 2)
+    out_grad_own = scatter_grad(out_grad[:2], out_grad[2:])
+
+    splits = 2
+    earlier = ()
+    for split in range(splits):
+        grad_kv, grad_q = attend_back(
+            me, queries, keys, values, grad_attended, attended, level, cosine, sine, split, splits, earlier
+        )
+        earlier = (grad_q, grad_kv)
+    grad_mixture = jnp.concatenate([grad_q, grad_kv], axis=1)
+    grad_normed_first = ring_scatter(
+        lambda slot: lax.dot_general(
+            grad_mixture[rows_of(slot)], qkv_weight, NT, preferred_element_type=F32
+        )
+    )
+    qkv_grad = lax.dot_general(
+        jnp.concatenate(normed_groups, axis=0), grad_mixture, TN, preferred_element_type=F32
+    ).astype(BF)
+    qkv_grad = lax.dot_general(qkv_grad, turn, NT, preferred_element_type=F32).astype(BF)
+    qkv_grad = qkv_grad.reshape(4, 512, 768)
+    qkv_grad_own = scatter_grad(qkv_grad[:2], qkv_grad[2:])
+
+    input_back, gain_first_part = norm_grad(rows_in, scale_first, gain_first, grad_normed_first)
+    input_grad = swap_ch(features(residual_grad + input_back).astype(BF)).astype(F32)
+
+    gain_grads = jnp.stack([gain_first_part, gain_second_part])
+    for bit in "xlch":
+        gain_grads = gain_grads + flip(gain_grads, bit)
+    gain_grads = gain_grads[:, :1024] + flip(gain_grads[:, 1024:], "y")
+    gain_grad_own = jnp.where(plain_c, gain_grads[:, :512], gain_grads[:, 512:])
+
+    rate_unit = float(4 * 8 * ROW) ** (-0.5)
+    qkv_new = apply_update(qkv_master, qkv_grad_own, qkv_moment, qkv_average, rate_qkv * rate_unit)
+    out_new = apply_update(out_master, out_grad_own, out_moment, out_average, rate_out * rate_unit)
+    gate_up_grad_own = jnp.stack([gate_up_grad_own[:, :1024], gate_up_grad_own[:, 1024:]])
+    gate_up_new = apply_update(
+        gate_up_master, gate_up_grad_own, gate_up_moment, gate_up_average, rate_gate_up * rate_unit
+    )
+    down_new = apply_update(
+        down_master, down_grad_own, down_moment, down_average, rate_down * rate_unit
+    )
+    gains_new = apply_update(
+        gains_master, gain_grad_own, gains_moment, gains_average, rate_gains * rate_unit
+    )
+    return (layer_output, input_grad) + qkv_new + out_new + gate_up_new + down_new + gains_new
+
+
 def solution(mesh):
     in_specs = (
         P(("seq", "tp"), None),
@@ -367,4 +1005,5 @@
         P(None, "seq"),
         P(None, "seq"),
     )
-    return jax.shard_map(shards, mesh=mesh, in_specs=in_specs, out_specs=out_specs, check_vma=False)
+    body = ring_shards if ring_plan_fits(mesh) else shards
+    return jax.shard_map(body, mesh=mesh, in_specs=in_specs, out_specs=out_specs, check_vma=False)

time: 3040 us -> 1900 us (0.62)
  waiting for transfers between devices: 1870 us -> 508 us
  starting transfers between devices: 1.02 us -> 455 us
  matrix products: 716 us -> 400 us
  Pallas kernels: 0 us -> 257 us
  other arithmetic: 322 us -> 145 us
  local copies, waits for them, and re-layouts: 44 us -> 117 us
  blocking collectives: 54.9 us -> 0 us
    reduce_scatter x7 -> x0, waiting for transfers between devices: 768 us -> none  [the longest x1 278 us: shards(): lax.psum_scatter((jnp.einsum('tf,df->td', grad_gate, gate_up_weight[0], p...]
    all_gather x7 -> x0, waiting for transfers between devices: 608 us -> none  [the longest x1 221 us: shards(): cot_all = lax.all_gather(cotangent, 'tp', axis=0, tiled=True)]
    ppermute x0 -> x132, waiting for transfers between devices: none -> 508 us  [move(): return lax.ppermute(values, ('seq', 'tp'), device_pairs(target))]
    psum x1 -> x0, waiting for transfers between devices: 495 us -> none  [shards(): lax.psum(jnp.dot(attended, out_weight, preferred_element_type=jnp.float32...]
    ppermute x0 -> x132, starting transfers between devices: none -> 455 us  [move(): return lax.ppermute(values, ('seq', 'tp'), device_pairs(target))]
    dot_general x63 -> x45, matrix products: 716 us -> 400 us  [the longest x8 70.5 us: ring_shards(): lax.dot_general(grad_gate_up[rows_of(slot)], gate_up_weight, NT, preferre...]
    pallas_call x0 -> x6, Pallas kernels: none -> 257 us  [the longest x2 147 us: attend_back(): pl.pallas_call(lambda *refs: attend_back_kernel(split, splits, *refs), gr...]
    convert_element_type x16 -> x22, other arithmetic: 138 us -> 23.7 us  [the longest x9 12.1 us: rounded(): return values.astype(BF)]
  transfers between devices with their start and end apart: 15 -> 132, of which waited for: 9 -> 44; matrix products, arithmetic and copies ran while one was open for 31% -> 23% of each run, Pallas kernels for 0% -> 14%
where the time goes in v1:
time: 1900 us; the launch traced here: 1890 us
  waiting for transfers between devices  508 us (27%)
  starting transfers between devices  455 us (24%)
  matrix products  400 us (21%)
  Pallas kernels  257 us (14%)
  other arithmetic  145 us (8%)
  local copies, waits for them, and re-layouts  117 us (6%)
    ppermute x132, waiting for transfers between devices, move(): return lax.ppermute(values, ('seq', 'tp'), device_pairs(target))  508 us
    ppermute x132, starting transfers between devices, move(): return lax.ppermute(values, ('seq', 'tp'), device_pairs(target))  455 us
    pallas_call x2, Pallas kernels, attend_back(): pl.pallas_call(lambda *refs: attend_back_kernel(split, splits, *refs), gr...  147 us
    pallas_call x4, Pallas kernels, attend(): pl.pallas_call(lambda *refs: attend_kernel(split, splits, *refs), grid_sp...  110 us
    unnamed x321, local copies, waits for them, and re-layouts  75.9 us
    dot_general x8, matrix products, ring_shards(): lax.dot_general(grad_gate_up[rows_of(slot)], gate_up_weight, NT, preferre...  70.5 us
    dot_general x1, matrix products, ring_shards(): lax.dot_general(grad_out, down_weight, NT, preferred_element_type=F32)  49.1 us
    dot_general x8, matrix products, ring_shards(): lax.dot_general(grad_mixture[rows_of(slot)], qkv_weight, NT, preferred_el...  48.8 us
  transfers between devices with their start and end apart: 132, of which 44 were waited for; matrix products, arithmetic and copies ran while one was open for 23% of the time, Pallas kernels for 14%

profile of v1, /device:TPU:0, one launch (start us, length us, event | category | flops | bytes accessed | tf_op | source)
XLA Modules:
  0.0 1888.0 jit_solution(4815241587707250521)
XLA Ops:
  58.5 45.8 %collective-permute-start.24 = (bf16[2304,512]{1,0:T(8,128)(2,1)}, bf16[2304,512]{1,0:T(8,128)(2,1)S(1)}, u32[]{:S(2)}, u32[]{:S(2)}) collective-permute-start(bf16[2304,512]{1,0:T(8,128)(2,1)} %convert_dynamic-update-slice_fusion), channel_id=1, source_target_pairs={{0,4},{1,5},{2,6},{3,7},{12,8},{13,9},{14,10},{15,11},{16,20},{17,... | collective-permute-start | bytes 7077896 | tf_op jit(solution)/shard_map/ppermute | solution.py:352
  150.4 102.8 %collective-permute-start.3 = (bf16[512,2048]{1,0:T(8,128)(2,1)}, bf16[512,2048]{1,0:T(8,128)(2,1)}, u32[]{:S(2)}, u32[]{:S(2)}) collective-permute-start(bf16[512,2048]{1,0:T(8,128)(2,1)} %get-tuple-element.68), channel_id=1, source_target_pairs={{0,8},{1,9},{2,10},{3,11},{4,12},{5,13},{6,14},{7,15},{8,0},{9,1},... | collective-permute-start | bytes 6291464 | tf_op jit(solution)/shard_map/ppermute | solution.py:352
  402.6 27.3 %shard_map.354 = (bf16[4096,256]{1,0:T(8,128)(2,1)S(1)}, f32[8,4,512]{2,1,0:T(4,128)S(1)}) custom-call(s32[1]{0:T(128)} %bitcast.refs_0_, bf16[4096,256]{1,0:T(8,128)(2,1)S(1)} %pad_maximum_fusion.12.refs_1_, bf16[4096,256]{1,0:T(8,128)(2,1)} %maximum_maximum_fusion.1.refs_2_, bf16[4096,256]{1,0:T(8,128)(2,1)} %pad_maximum_fusion.13.refs_3_), custom_call_target="tpu_custom_call" | custom-call | flops 24999999488 | bytes 10485760 | tf_op jit(solution)/shard_map/pallas_call | solution.py:546
  429.9 27.7 %shard_map.355 = (bf16[4096,256]{1,0:T(8,128)(2,1)S(1)}, f32[8,4,512]{2,1,0:T(4,128)S(1)}) custom-call(s32[1]{0:T(128)} %bitcast.refs_0_, bf16[4096,256]{1,0:T(8,128)(2,1)S(1)} %pad_maximum_fusion.12.refs_1_, bf16[4096,256]{1,0:T(8,128)(2,1)} %maximum_maximum_fusion.1.refs_2_, ...), custom_call_target="tpu_custom_call", output_to_operand_aliasing={{0}: (4, {}), {1}: (5, {})} | custom-call | flops 24999999488 | bytes 10485760 | tf_op jit(solution)/shard_map/pallas_call | solution.py:546
  457.6 27.3 %shard_map.356 = (bf16[4096,256]{1,0:T(8,128)(2,1)S(1)}, f32[8,4,512]{2,1,0:T(4,128)S(1)}) custom-call(s32[1]{0:T(128)} %bitcast.refs_0_, bf16[4096,256]{1,0:T(8,128)(2,1)S(1)} %pad_maximum_fusion.12.refs_1_, bf16[4096,256]{1,0:T(8,128)(2,1)} %maximum_maximum_fusion.1.refs_2_, ...), custom_call_target="tpu_custom_call", output_to_operand_aliasing={{0}: (4, {}), {1}: (5, {})} | custom-call | flops 24999999488 | bytes 10485760 | tf_op jit(solution)/shard_map/pallas_call | solution.py:546
  485.0 27.5 %shard_map.357 = (bf16[4096,256]{1,0:T(8,128)(2,1)S(1)}, f32[8,4,512]{2,1,0:T(4,128)S(1)}) custom-call(s32[1]{0:T(128)} %bitcast.refs_0_, bf16[4096,256]{1,0:T(8,128)(2,1)S(1)} %pad_maximum_fusion.12.refs_1_, bf16[4096,256]{1,0:T(8,128)(2,1)} %maximum_maximum_fusion.1.refs_2_, ...), custom_call_target="tpu_custom_call", output_to_operand_aliasing={{0}: (4, {}), {1}: (5, {})} | custom-call | flops 24999999488 | bytes 10485760 | tf_op jit(solution)/shard_map/pallas_call | solution.py:546
  525.1 26.1 %collective-permute-done.18 = bf16[512,256]{1,0:T(8,128)(2,1)S(1)} collective-permute-done((bf16[512,256]{1,0:T(8,128)(2,1)S(1)}, bf16[512,256]{1,0:T(8,128)(2,1)S(1)}, u32[]{:S(2)}, u32[]{:S(2)}) %collective-permute-start.18) | collective-permute-done | bytes 262176 | tf_op jit(solution)/shard_map/ppermute | solution.py:352
  592.8 37.9 %maximum_maximum_fusion = bf16[2048,2048]{1,0:T(8,128)(2,1)S(1)} fusion(bf16[512,512]{1,0:T(8,128)(2,1)} %get-tuple-element.103, bf16[512,512]{1,0:T(8,128)(2,1)} %get-tuple-element.104, bf16[512,512]{1,0:T(8,128)(2,1)} %get-tuple-element.105, bf16[512,512]{1,0:T(8,128)(2,1)} %get-tuple-element.106, bf16[512,512]{1,0:T(8,128)(2,1)} %get-tuple-element.107, ...), kind=kLoop, calls=%fused_computation.30 | loop fusion | flops 134217728 | bytes 16777216 | tf_op jit(solution)/shard_map/concatenate | solution.py:832
  717.9 24.8 %fusion.54 = bf16[1024,2048]{1,0:T(8,128)(2,1)S(1)} fusion(bf16[4096,2048]{1,0:T(8,128)(2,1)} %constant_dynamic-update-slice_fusion.25, bf16[1024,1024]{1,0:T(8,128)(2,1)} %get-tuple-element.126, bf16[1024,1024]{1,0:T(8,128)(2,1)} %get-tuple-element.123, bf16[1024,1024]{1,0:T(8,128)(2,1)} %get-tuple-element.120, bf16[1024,1024]{1,0:T(8,128)(2,1)} %get-tuple-element.117), kind=kOutput, calls=%fused_computation.121 | convolution fusion | flops 17215520768 | bytes 29360128 | tf_op jit(solution)/shard_map/dot_general | solution.py:886
  744.8 46.1 %collective-permute-done.123 = bf16[2,1024,512]{2,1,0:T(8,128)(2,1)S(1)} collective-permute-done((bf16[2,1024,512]{2,1,0:T(8,128)(2,1)S(1)}, bf16[2,1024,512]{2,1,0:T(8,128)(2,1)S(1)}, u32[]{:S(2)}, u32[]{:S(2)}) %collective-permute-start.123) | collective-permute-done | bytes 2097184 | tf_op jit(solution)/shard_map/ppermute | solution.py:352
  800.6 31.1 %collective-permute-done.124 = bf16[1024,512]{1,0:T(8,128)(2,1)S(1)} collective-permute-done((bf16[1024,512]{1,0:T(8,128)(2,1)S(1)}, bf16[1024,512]{1,0:T(8,128)(2,1)S(1)}, u32[]{:S(2)}, u32[]{:S(2)}) %collective-permute-start.124) | collective-permute-done | bytes 1048608 | tf_op jit(solution)/shard_map/ppermute | solution.py:352
  900.2 49.1 %fusion.7 = (bf16[4096,1024]{1,0:T(8,128)(2,1)}, bf16[4096,1024]{1,0:T(8,128)(2,1)}) fusion(bf16[1024,1024]{1,0:T(8,128)(2,1)} %get-tuple-element.125, bf16[1024,1024]{1,0:T(8,128)(2,1)} %get-tuple-element.122, bf16[1024,1024]{1,0:T(8,128)(2,1)} %get-tuple-element.119, bf16[1024,1024]{1,0:T(8,128)(2,1)} %get-tuple-element.116, ...), kind=kOutput, calls=%fused_computation.28 | convolution fusion | flops 17318281216 | bytes 54525952 | tf_op jit(solution)/shard_map/dot_general | solution.py:869
  993.3 44.5 %fusion.18 = bf16[2048,2048]{1,0:T(8,128)(2,1)} fusion(bf16[4096,2048]{1,0:T(8,128)(2,1)} %get-tuple-element.189, bf16[4096,1024]{1,0:T(8,128)(2,1)} %get-tuple-element.73, bf16[4096,1024]{1,0:T(8,128)(2,1)} %get-tuple-element.74), kind=kOutput, calls=%fused_computation.47 | convolution fusion | flops 34397487104 | bytes 41943040 | tf_op jit(solution)/shard_map/dot_general | solution.py:889
  1037.8 20.8 %collective-permute-start.54 = (bf16[512,2048]{1,0:T(8,128)(2,1)}, bf16[512,2048]{1,0:T(8,128)(2,1)S(1)}, u32[]{:S(2)}, u32[]{:S(2)}) collective-permute-start(bf16[512,2048]{1,0:T(8,128)(2,1)} %convolution_convert_fusion.3), channel_id=1, source_target_pairs={{0,8},{1,9},{2,10},{3,11},{4,12},{5,13},{6,14},{7,15},{8,0},{9,1},... | collective-permute-start | bytes 6291464 | tf_op jit(solution)/shard_map/ppermute | solution.py:352
  1176.7 29.0 %collective-permute-done.79 = bf16[256,2048]{1,0:T(8,128)(2,1)S(1)} collective-permute-done((bf16[256,2048]{1,0:T(8,128)(2,1)S(1)}, bf16[256,2048]{1,0:T(8,128)(2,1)S(1)}, u32[]{:S(2)}, u32[]{:S(2)}) %collective-permute-start.79) | collective-permute-done | bytes 1048608 | tf_op jit(solution)/shard_map/ppermute | solution.py:352
  1240.7 57.6 %collective-permute-done.119 = bf16[2,512,2048]{2,1,0:T(8,128)(2,1)} collective-permute-done((bf16[2,512,2048]{2,1,0:T(8,128)(2,1)}, bf16[2,512,2048]{2,1,0:T(8,128)(2,1)}, u32[]{:S(2)}, u32[]{:S(2)}) %collective-permute-start.119) | collective-permute-done | bytes 4194336 | tf_op jit(solution)/shard_map/ppermute | solution.py:352
  1383.9 72.9 %shard_map.358 = (bf16[4096,512]{1,0:T(8,128)(2,1)}, f32[4096,256]{1,0:T(8,128)}) custom-call(s32[1]{0:T(128)} %bitcast.refs_0_, bf16[4096,256]{1,0:T(8,128)(2,1)} %copy-done, bf16[4096,256]{1,0:T(8,128)(2,1)} %maximum_maximum_fusion.1.refs_2_, bf16[4096,256]{1,0:T(8,128)(2,1)} %pad_maximum_fusion.13.refs_3_, bf16[4096,256]{1,0:T(8,128)(2,1)} %copy-done.104, ...), custom_call_target="tpu_custom_call" | custom-call | flops 70000001024 | bytes 20971520 | tf_op jit(solution)/shard_map/pallas_call | solution.py:716
  1456.8 74.3 %shard_map.359 = (bf16[4096,512]{1,0:T(8,128)(2,1)}, bf16[4096,256]{1,0:T(8,128)(2,1)}) custom-call(s32[1]{0:T(128)} %bitcast.refs_0_, bf16[4096,256]{1,0:T(8,128)(2,1)} %copy-done, bf16[4096,256]{1,0:T(8,128)(2,1)} %maximum_maximum_fusion.1.refs_2_, bf16[4096,256]{1,0:T(8,128)(2,1)} %pad_maximum_fusion.13.refs_3_, ...), custom_call_target="tpu_custom_call", output_to_operand_aliasing={{0}: (10, {})} | custom-call | flops 70000001024 | bytes 20971520 | tf_op jit(solution)/shard_map/pallas_call | solution.py:716
  1534.6 19.9 %convolution_convert_fusion.1.clone.5 = bf16[2048,768]{1,0:T(8,128)(2,1)S(1)} fusion(bf16[4096,2048]{1,0:T(8,128)(2,1)} %constant_dynamic-update-slice_fusion.44, bf16[4096,768]{1,0:T(8,128)(2,1)S(1)} %constant_dynamic-update-slice_fusion.42), kind=kOutput, calls=%fused_computation.138.clone.clone.clone.2 | convolution fusion | flops 12886474752 | bytes 26214400 | tf_op jit(solution)/shard_map/dot_general | solution.py:930
  1600.7 27.1 %collective-permute-done.112 = bf16[128,2048]{0,1:T(8,128)(2,1)S(1)} collective-permute-done((bf16[128,2048]{0,1:T(8,128)(2,1)S(1)}, bf16[128,2048]{0,1:T(8,128)(2,1)S(1)}, u32[]{:S(2)}, u32[]{:S(2)}) %collective-permute-start.112) | collective-permute-done | bytes 524320 | tf_op jit(solution)/shard_map/ppermute | solution.py:352
  1662.8 21.8 %collective-permute-done.111 = bf16[128,2048]{0,1:T(8,128)(2,1)} collective-permute-done((bf16[128,2048]{0,1:T(8,128)(2,1)}, bf16[128,2048]{0,1:T(8,128)(2,1)}, u32[]{:S(2)}, u32[]{:S(2)}) %collective-permute-start.111) | collective-permute-done | bytes 524320 | tf_op jit(solution)/shard_map/ppermute | solution.py:352
  1754.1 38.4 %collective-permute-done.96 = bf16[256,2048]{1,0:T(8,128)(2,1)S(1)} collective-permute-done((bf16[256,2048]{1,0:T(8,128)(2,1)S(1)}, bf16[256,2048]{1,0:T(8,128)(2,1)S(1)}, u32[]{:S(2)}, u32[]{:S(2)}) %collective-permute-start.96) | collective-permute-done | bytes 1048608 | tf_op jit(solution)/shard_map/ppermute | solution.py:352
  1828.3 24.2 %collective-permute-start.129 = (f32[2,2048]{1,0:T(2,128)S(1)}, f32[2,2048]{1,0:T(2,128)S(1)}, u32[]{:S(2)}, u32[]{:S(2)}) collective-permute-start(f32[2,2048]{1,0:T(2,128)S(1)} %fusion.239), channel_id=1, source_target_pairs={{0,8},{1,9},{2,10},{3,11},{4,12},{5,13},{6,14},{7,15},{8,0},{9,1},... | collective-permute-start | bytes 49160 | tf_op jit(solution)/shard_map/ppermute | solution.py:352
  1856.5 20.7 %collective-permute-done.130 = f32[2,2048]{1,0:T(2,128)S(1)} collective-permute-done((f32[2,2048]{1,0:T(2,128)S(1)}, f32[2,2048]{1,0:T(2,128)S(1)}, u32[]{:S(2)}, u32[]{:S(2)}) %collective-permute-start.130) | collective-permute-done | bytes 16416 | tf_op jit(solution)/shard_map/ppermute | solution.py:352
  (762 shorter events, 957.2 us)
Async XLA Ops:
  9.3 96.7 %collective-permute-start.63 = (bf16[512,2048]{1,0:T(8,128)(2,1)}, bf16[512,2048]{1,0:T(8,128)(2,1)S(1)}, u32[]{:S(2)}, u32[]{:S(2)}) collective-permute-start(bf16[512,2048]{1,0:T(8,128)(2,1)} %param.20), channel_id=1, source_target_pairs={{0,0},{1,1},{2,2},{3,3},{4,8},{5,9},{6,10},{7,11},{8,4},{9,5},{10,... | collective-permute-start | bytes 6291464 | tf_op jit(solution)/shard_map/ppermute | solution.py:352
  58.5 90.6 %collective-permute-start.24 = (bf16[2304,512]{1,0:T(8,128)(2,1)}, bf16[2304,512]{1,0:T(8,128)(2,1)S(1)}, u32[]{:S(2)}, u32[]{:S(2)}) collective-permute-start(bf16[2304,512]{1,0:T(8,128)(2,1)} %convert_dynamic-update-slice_fusion), channel_id=1, source_target_pairs={{0,4},{1,5},{2,6},{3,7},{12,8},{13,9},{14,10},{15,11},{16,20},{17,... | collective-permute-start | bytes 7077896 | tf_op jit(solution)/shard_map/ppermute | solution.py:352
  106.8 148.6 %collective-permute-start.7 = (bf16[2,512,768]{2,1,0:T(8,128)(2,1)S(1)}, bf16[2,512,768]{2,1,0:T(8,128)(2,1)}, u32[]{:S(2)}, u32[]{:S(2)}) collective-permute-start(bf16[2,512,768]{2,1,0:T(8,128)(2,1)S(1)} %pad_maximum_fusion.15), channel_id=1, source_target_pairs={{0,16},{1,17},{2,18},{3,19},{4,20},{5,21},{6,22},{7,23},{8,24},{9,... | collective-permute-start | bytes 4718600 | tf_op jit(solution)/shard_map/ppermute | solution.py:352
  111.6 145.0 %collective-permute-start.67 = (bf16[512,2048]{1,0:T(8,128)(2,1)}, bf16[512,2048]{1,0:T(8,128)(2,1)S(1)}, u32[]{:S(2)}, u32[]{:S(2)}) collective-permute-start(bf16[512,2048]{1,0:T(8,128)(2,1)} %get-tuple-element.70), channel_id=1, source_target_pairs={{0,2},{1,3},{2,0},{3,1},{4,6},{5,7},{6,4},{7,5},{8,10},{9,11},{10,... | collective-permute-start | bytes 6291464 | tf_op jit(solution)/shard_map/ppermute | solution.py:352
  118.7 157.4 %collective-permute-start.9 = (bf16[512,2048]{1,0:T(8,128)(2,1)}, bf16[512,2048]{1,0:T(8,128)(2,1)S(1)}, u32[]{:S(2)}, u32[]{:S(2)}) collective-permute-start(bf16[512,2048]{1,0:T(8,128)(2,1)} %get-tuple-element.68), channel_id=1, source_target_pairs={{0,1},{1,0},{2,3},{3,2},{4,5},{5,4},{6,7},{7,6},{8,9},{9,8},{10,11... | collective-permute-start | bytes 6291464 | tf_op jit(solution)/shard_map/ppermute | solution.py:352
  127.6 154.1 %collective-permute-start.11 = (bf16[512,2048]{1,0:T(8,128)(2,1)}, bf16[512,2048]{1,0:T(8,128)(2,1)S(1)}, u32[]{:S(2)}, u32[]{:S(2)}) collective-permute-start(bf16[512,2048]{1,0:T(8,128)(2,1)} %get-tuple-element.68), channel_id=1, source_target_pairs={{0,2},{1,3},{2,0},{3,1},{4,6},{5,7},{6,4},{7,5},{8,10},{9,11},{10,... | collective-permute-start | bytes 6291464 | tf_op jit(solution)/shard_map/ppermute | solution.py:352
  150.4 133.6 %collective-permute-start.3 = (bf16[512,2048]{1,0:T(8,128)(2,1)}, bf16[512,2048]{1,0:T(8,128)(2,1)}, u32[]{:S(2)}, u32[]{:S(2)}) collective-permute-start(bf16[512,2048]{1,0:T(8,128)(2,1)} %get-tuple-element.68), channel_id=1, source_target_pairs={{0,8},{1,9},{2,10},{3,11},{4,12},{5,13},{6,14},{7,15},{8,0},{9,1},... | collective-permute-start | bytes 6291464 | tf_op jit(solution)/shard_map/ppermute | solution.py:352
  281.6 82.3 %collective-permute-start.70 = (bf16[256,2048]{1,0:T(8,128)(2,1)}, bf16[256,2048]{1,0:T(8,128)(2,1)}, u32[]{:S(2)}, u32[]{:S(2)}) collective-permute-start(bf16[256,2048]{1,0:T(8,128)(2,1)} %slice.853), channel_id=1, source_target_pairs={{0,1},{1,0},{2,3},{3,2},{4,5},{5,4},{6,7},{7,6},{8,9},{9,8},{10,11... | collective-permute-start | bytes 3145736 | tf_op jit(solution)/shard_map/ppermute | solution.py:352
  364.0 150.7 %collective-permute-start.27 = (bf16[2,2304,512]{2,1,0:T(8,128)(2,1)S(1)}, bf16[2,2304,512]{2,1,0:T(8,128)(2,1)S(1)}, u32[]{:S(2)}, u32[]{:S(2)}) collective-permute-start(bf16[2,2304,512]{2,1,0:T(8,128)(2,1)S(1)} %pad_maximum_fusion.5), channel_id=1, source_target_pairs={{0,16},{1,17},{2,18},{3,19},{4,20},{5,21},{6,22},{7,23},{8,24},{9,... | collective-permute-start | bytes 14155784 | tf_op jit(solution)/shard_map/ppermute | solution.py:352
  367.7 150.4 %collective-permute-start.72 = (bf16[256,2048]{1,0:T(8,128)(2,1)}, bf16[256,2048]{1,0:T(8,128)(2,1)}, u32[]{:S(2)}, u32[]{:S(2)}) collective-permute-start(bf16[256,2048]{1,0:T(8,128)(2,1)} %collective-permute-done.70), channel_id=1, source_target_pairs={{0,8},{1,9},{2,10},{3,11},{4,12},{5,13},{6,14},{7,15},{8,0},{9,1},... | collective-permute-start | bytes 3145736 | tf_op jit(solution)/shard_map/ppermute | solution.py:352
  375.5 139.9 %collective-permute-start.71 = (bf16[256,2048]{1,0:T(8,128)(2,1)}, bf16[256,2048]{1,0:T(8,128)(2,1)S(1)}, u32[]{:S(2)}, u32[]{:S(2)}) collective-permute-start(bf16[256,2048]{1,0:T(8,128)(2,1)} %collective-permute-done.69), channel_id=1, source_target_pairs={{0,8},{1,9},{2,10},{3,11},{4,12},{5,13},{6,14},{7,15},{8,0},{9,1},... | collective-permute-start | bytes 3145736 | tf_op jit(solution)/shard_map/ppermute | solution.py:352
  1079.9 133.0 %collective-permute-start.73 = (bf16[512,2048]{1,0:T(8,128)(2,1)}, bf16[512,2048]{1,0:T(8,128)(2,1)}, u32[]{:S(2)}, u32[]{:S(2)}) collective-permute-start(bf16[512,2048]{1,0:T(8,128)(2,1)} %convolution_convert_fusion.15), channel_id=1, source_target_pairs={{0,8},{1,9},{2,10},{3,11},{4,12},{5,13},{6,14},{7,15},{8,0},{9,1},... | collective-permute-start | bytes 6291464 | tf_op jit(solution)/shard_map/ppermute | solution.py:352
  1176.7 156.2 %collective-permute-start.42 = (bf16[512,2048]{1,0:T(8,128)(2,1)}, bf16[512,2048]{1,0:T(8,128)(2,1)}, u32[]{:S(2)}, u32[]{:S(2)}) collective-permute-start(bf16[512,2048]{1,0:T(8,128)(2,1)} %convolution_convert_fusion.6), channel_id=1, source_target_pairs={{0,8},{1,9},{2,10},{3,11},{4,12},{5,13},{6,14},{7,15},{8,0},{9,1},... | collective-permute-start | bytes 6291464 | tf_op jit(solution)/shard_map/ppermute | solution.py:352
  1205.7 92.5 %collective-permute-start.119 = (bf16[2,512,2048]{2,1,0:T(8,128)(2,1)}, bf16[2,512,2048]{2,1,0:T(8,128)(2,1)}, u32[]{:S(2)}, u32[]{:S(2)}) collective-permute-start(bf16[2,512,2048]{2,1,0:T(8,128)(2,1)} %bitcast.49), channel_id=1, source_target_pairs={{0,16},{1,17},{2,18},{3,19},{4,20},{5,21},{6,22},{7,23},{8,24},{9,... | collective-permute-start | bytes 12582920 | tf_op jit(solution)/shard_map/ppermute | solution.py:352
  1208.9 108.8 %collective-permute-start.59 = (bf16[256,2048]{1,0:T(8,128)(2,1)}, bf16[256,2048]{1,0:T(8,128)(2,1)}, u32[]{:S(2)}, u32[]{:S(2)}) collective-permute-start(bf16[256,2048]{1,0:T(8,128)(2,1)} %slice.1231), channel_id=1, source_target_pairs={{0,2},{1,3},{2,0},{3,1},{4,6},{5,7},{6,4},{7,5},{8,10},{9,11},{10,... | collective-permute-start | bytes 3145736 | tf_op jit(solution)/shard_map/ppermute | solution.py:352
  1210.7 95.9 %collective-permute-start.46 = (bf16[256,2048]{1,0:T(8,128)(2,1)}, bf16[256,2048]{1,0:T(8,128)(2,1)}, u32[]{:S(2)}, u32[]{:S(2)}) collective-permute-start(bf16[256,2048]{1,0:T(8,128)(2,1)} %slice.1232), channel_id=1, source_target_pairs={{0,1},{1,0},{2,3},{3,2},{4,5},{5,4},{6,7},{7,6},{8,9},{9,8},{10,11... | collective-permute-start | bytes 3145736 | tf_op jit(solution)/shard_map/ppermute | solution.py:352
  1212.9 95.7 %collective-permute-start.56 = (bf16[256,2048]{1,0:T(8,128)(2,1)}, bf16[256,2048]{1,0:T(8,128)(2,1)}, u32[]{:S(2)}, u32[]{:S(2)}) collective-permute-start(bf16[256,2048]{1,0:T(8,128)(2,1)} %fusion.125), channel_id=1, source_target_pairs={{0,2},{1,3},{2,0},{3,1},{4,6},{5,7},{6,4},{7,5},{8,10},{9,11},{10,... | collective-permute-start | bytes 3145736 | tf_op jit(solution)/shard_map/ppermute | solution.py:352
  1306.6 341.5 %collective-permute-start.122 = (bf16[512,2048]{1,0:T(8,128)(2,1)}, bf16[512,2048]{1,0:T(8,128)(2,1)}, u32[]{:S(2)}, u32[]{:S(2)}) collective-permute-start(bf16[512,2048]{1,0:T(8,128)(2,1)} %get-tuple-element.115), channel_id=1, source_target_pairs={{4,8},{5,9},{6,10},{7,11},{8,4},{9,5},{10,6},{11,7},{20,24},{21,25... | collective-permute-start | bytes 6291464 | tf_op jit(solution)/shard_map/ppermute | solution.py:352
  1308.6 341.0 %collective-permute-start.121 = (bf16[512,2048]{1,0:T(8,128)(2,1)}, bf16[512,2048]{1,0:T(8,128)(2,1)}, u32[]{:S(2)}, u32[]{:S(2)}) collective-permute-start(bf16[512,2048]{1,0:T(8,128)(2,1)} %get-tuple-element.115), channel_id=1, source_target_pairs={{0,8},{1,9},{2,10},{3,11},{12,4},{13,5},{14,6},{15,7},{16,24},{17,... | collective-permute-start | bytes 6291464 | tf_op jit(solution)/shard_map/ppermute | solution.py:352
  1370.3 202.4 %collective-permute-start.109 = (bf16[256,2048]{0,1:T(8,128)(2,1)}, bf16[256,2048]{0,1:T(8,128)(2,1)}, u32[]{:S(2)}, u32[]{:S(2)}) collective-permute-start(bf16[256,2048]{0,1:T(8,128)(2,1)} %get-tuple-element.80), channel_id=1, source_target_pairs={{0,8},{1,9},{2,10},{3,11},{4,12},{5,13},{6,14},{7,15},{8,0},{9,1},... | collective-permute-start | bytes 3145736 | tf_op jit(solution)/shard_map/ppermute | solution.py:352
  1377.1 197.0 %collective-permute-start.108 = (bf16[256,2048]{0,1:T(8,128)(2,1)}, bf16[256,2048]{0,1:T(8,128)(2,1)}, u32[]{:S(2)}, u32[]{:S(2)}) collective-permute-start(bf16[256,2048]{0,1:T(8,128)(2,1)} %get-tuple-element.81), channel_id=1, source_target_pairs={{0,8},{1,9},{2,10},{3,11},{4,12},{5,13},{6,14},{7,15},{8,0},{9,1},... | collective-permute-start | bytes 3145736 | tf_op jit(solution)/shard_map/ppermute | solution.py:352
  1382.5 193.2 %collective-permute-start.106 = (bf16[256,2048]{0,1:T(8,128)(2,1)}, bf16[256,2048]{0,1:T(8,128)(2,1)}, u32[]{:S(2)}, u32[]{:S(2)}) collective-permute-start(bf16[256,2048]{0,1:T(8,128)(2,1)} %get-tuple-element.82), channel_id=1, source_target_pairs={{0,8},{1,9},{2,10},{3,11},{4,12},{5,13},{6,14},{7,15},{8,0},{9,1},... | collective-permute-start | bytes 3145736 | tf_op jit(solution)/shard_map/ppermute | solution.py:352
  1572.8 74.8 %collective-permute-start.120 = (bf16[512,2048]{1,0:T(8,128)(2,1)S(1)}, bf16[512,2048]{1,0:T(8,128)(2,1)S(1)}, u32[]{:S(2)}, u32[]{:S(2)}) collective-permute-start(bf16[512,2048]{1,0:T(8,128)(2,1)S(1)} %copy-done.23), channel_id=1, source_target_pairs={{4,0},{5,1},{6,2},{7,3},{8,12},{9,13},{10,14},{11,15},{20,16},{21,... | collective-permute-start | bytes 6291464 | tf_op jit(solution)/shard_map/ppermute | solution.py:352
  1695.2 101.6 %collective-permute-start.90 = (bf16[512,2048]{1,0:T(8,128)(2,1)}, bf16[512,2048]{1,0:T(8,128)(2,1)}, u32[]{:S(2)}, u32[]{:S(2)}) collective-permute-start(bf16[512,2048]{1,0:T(8,128)(2,1)} %convolution_convert_fusion.10), channel_id=1, source_target_pairs={{0,8},{1,9},{2,10},{3,11},{4,12},{5,13},{6,14},{7,15},{8,0},{9,1},... | collective-permute-start | bytes 6291464 | tf_op jit(solution)/shard_map/ppermute | solution.py:352
  (243 other events, 7034.5 us)

commit v2 on v1

--- a/solution.py
+++ b/solution.py
@@ -323,11 +323,13 @@
     )
 
 
+AXES = ("y", "c", "h", "l", "x")
+RING = ("c", "l", "x")
+MESH = pl.DeviceIdType.MESH
 ROW = 512
 BF = jnp.bfloat16
 F32 = jnp.float32
 LOG2E = 1.4426950408889634
-STORED = (0, 4, 1, 5, 2, 6, 3, 7)
 NT = (((1,), (1,)), ((), ()))
 NN = (((1,), (0,)), ((), ()))
 TN = (((0,), (0,)), ((), ()))
@@ -349,7 +351,7 @@
 
 
 def move(values, target):
-    return lax.ppermute(values, ("seq", "tp"), device_pairs(target))
+    return lax.ppermute(values, AXES, device_pairs(target))
 
 
 def flip(values, bits):
@@ -369,62 +371,329 @@
     return move(values, lambda y, c, h, l, x: (y, h, c, l, x))
 
 
-def flip_slot(values, slot):
-    return flip(values, ("c" if slot & 4 else "") + ("l" if slot & 2 else "") + ("x" if slot & 1 else ""))
-
-
-def ring_gather(own):
-    half = own.shape[0] // 2
-    s1 = flip(own, "x")
-    s2 = flip(own, "l")
-    s4 = flip(own, "c")
-    s3a = flip(s1[:half], "l")
-    s3b = flip(s2[half:], "x")
-    s5 = flip(s1, "c")
-    s6 = flip(s2, "c")
-    s7a = flip(s3a, "c")
-    s7b = flip(s3b, "c")
-    return (
-        jnp.concatenate([own, s4]),
-        jnp.concatenate([s1, s5]),
-        jnp.concatenate([s2, s6]),
-        jnp.concatenate([s3a, s3b, s7a, s7b]),
-    )
-
-
-def ring_scatter(part):
-    def rounded(values):
-        return values.astype(BF)
-
-    q3 = rounded(part(3) + flip(rounded(part(7)), "c").astype(F32))
-    half = q3.shape[0] // 2
-    ra = flip(q3[:half], "x").astype(F32)
-    rb = flip(q3[half:], "l").astype(F32)
-    q1 = part(1) + flip(rounded(part(5)), "c").astype(F32)
-    q2 = part(2) + flip(rounded(part(6)), "c").astype(F32)
-    r1a = flip(rounded(q1[:half]), "x").astype(F32)
-    r2b = flip(rounded(q2[half:]), "l").astype(F32)
-    r1b = flip(rounded(q1[half:] + rb), "x").astype(F32)
-    r2a = flip(rounded(q2[:half] + ra), "l").astype(F32)
-    q0 = part(0) + flip(rounded(part(4)), "c").astype(F32)
-    return q0 + jnp.concatenate([r1a + r2a, r1b + r2b])
-
-
-def heads_to_rows(blocks):
-    got = []
-    for place, slot in enumerate(STORED):
-        block = blocks[place * ROW : (place + 1) * ROW]
-        got.append(block if slot == 0 else flip_slot(block, slot))
-    return jnp.concatenate(got, axis=1)
-
-
-def rows_to_heads(rows):
-    width = rows.shape[1] // 8
-    got = []
-    for place, slot in enumerate(STORED):
-        block = rows[:, place * width : (place + 1) * width]
-        got.append(block if slot == 0 else flip_slot(block, slot))
-    return jnp.concatenate(got, axis=0)
+def rounded(values):
+    return values.astype(BF)
+
+
+def ring_position():
+    c, l, x = (lax.axis_index(name) for name in RING)
+    partners = ({"x": 1 - x}, {"l": 1 - l}, {"c": 1 - c})
+    return 4 * c + 2 * l + x, partners
+
+
+def enter_ring(partners):
+    barrier = pltpu.get_barrier_semaphore()
+    for partner in partners:
+        pl.semaphore_signal(barrier, inc=1, device_id=partner, device_id_type=MESH)
+    pl.semaphore_wait(barrier, len(partners))
+
+
+def rows_at(block, part=None):
+    if part is None:
+        return pl.ds(pl.multiple_of(block * ROW, ROW), ROW)
+    half = ROW // 2
+    return pl.ds(pl.multiple_of(block * ROW + part * half, half), half)
+
+
+def gather_kernel(finish, width, tables, own_ref, w_ref, *refs):
+    cs_ref, sn_ref = refs[:2] if tables else (None, None)
+    full_ref, *outs = refs[2 if tables else 0 :][:4]
+    buf, res, send, recv, own_sem, full_sem, out_sem = refs[-7:]
+    me, partners = ring_position()
+    to_x, to_l, to_c = partners
+    load = pltpu.make_async_copy(own_ref, buf.at[rows_at(me)], own_sem)
+    load.start()
+    enter_ring(partners)
+    load.wait()
+
+    def copy(index, block, part, partner):
+        place = buf.at[rows_at(block, part)]
+        return pltpu.make_async_remote_copy(
+            src_ref=place,
+            dst_ref=place,
+            send_sem=send.at[index],
+            recv_sem=recv.at[index],
+            device_id=partner,
+            device_id_type=MESH,
+        )
+
+    plan = (
+        (me, 0, to_x, me ^ 1),
+        (me, 1, to_l, me ^ 2),
+        (me, None, to_c, me ^ 4),
+        (me, 1, to_x, me ^ 1),
+        (me, 0, to_l, me ^ 2),
+        (me ^ 1, 0, to_l, me ^ 3),
+        (me ^ 2, 1, to_x, me ^ 3),
+        (me ^ 1, None, to_c, me ^ 5),
+        (me ^ 2, None, to_c, me ^ 6),
+        (me ^ 3, None, to_c, me ^ 7),
+    )
+
+    def start(index):
+        block, part, partner, _ = plan[index]
+        copy(index, block, part, partner).start()
+
+    def arrived(index):
+        _, part, partner, block = plan[index]
+        copy(index, block, part, partner).wait_recv()
+
+    for index in range(5):
+        start(index)
+
+    def step_body(step, carry):
+        block = me ^ ((step >> 1) | ((step & 1) << 2))
+        rows = rows_at(block)
+
+        @pl.when(step == 1)
+        def _():
+            arrived(2)
+
+        @pl.when(step == 2)
+        def _():
+            arrived(0)
+            start(5)
+            arrived(1)
+            start(6)
+            arrived(3)
+            start(7)
+            arrived(4)
+            start(8)
+
+        @pl.when(step == 3)
+        def _():
+            arrived(7)
+
+        @pl.when(step == 5)
+        def _():
+            arrived(8)
+
+        @pl.when(step == 6)
+        def _():
+            arrived(5)
+            arrived(6)
+            start(9)
+
+        @pl.when(step == 7)
+        def _():
+            arrived(9)
+
+        pltpu.make_async_copy(buf.at[rows], full_ref.at[rows], full_sem.at[step]).start()
+        turn = step & 1
+
+        def out_copy(which, rows):
+            return pltpu.make_async_copy(
+                res.at[turn, which], outs[which].at[rows], out_sem.at[turn, which]
+            )
+
+        @pl.when(step >= 2)
+        def _():
+            for which in range(3):
+                out_copy(which, rows).wait()
+
+        finish(buf, rows, w_ref, cs_ref, sn_ref, res, turn)
+        for which in range(3):
+            out_copy(which, rows).start()
+        return carry
+
+    lax.fori_loop(0, 8, step_body, 0)
+    for index in range(10):
+        block, part, partner, _ = plan[index]
+        copy(index, block, part, partner).wait_send()
+
+    def drain(step, carry):
+        rows = rows_at(step)
+        pltpu.make_async_copy(buf.at[rows], full_ref.at[rows], full_sem.at[step]).wait()
+        return carry
+
+    lax.fori_loop(0, 8, drain, 0)
+    for turn in range(2):
+        for which in range(3):
+            pltpu.make_async_copy(
+                res.at[turn, which], outs[which].at[rows_at(0)], out_sem.at[turn, which]
+            ).wait()
+
+
+def feed_forward_finish(buf, rows, w_ref, cs_ref, sn_ref, res, turn):
+    def columns(chunk, carry):
+        here = pl.multiple_of(chunk * 256, 256)
+        block = buf[rows, :]
+        g = jnp.dot(block, w_ref[:, pl.ds(here, 256)], preferred_element_type=F32)
+        u = jnp.dot(block, w_ref[:, pl.ds(here + 1024, 256)], preferred_element_type=F32)
+        res[turn, 0, :, pl.ds(here, 256)] = rounded(g)
+        res[turn, 1, :, pl.ds(here, 256)] = rounded(u)
+        res[turn, 2, :, pl.ds(here, 256)] = rounded(g * (1.0 / (1.0 + jnp.exp(-g))) * u)
+        return carry
+
+    lax.fori_loop(0, 4, columns, 0)
+
+
+def attention_finish(buf, rows, w_ref, cs_ref, sn_ref, res, turn):
+    block = buf[rows, :]
+    cs, sn = cs_ref[rows, :], sn_ref[rows, :]
+    for which in range(2):
+        m = jnp.dot(block, w_ref[:, which * 256 : which * 256 + 256], preferred_element_type=F32)
+        if which == 0:
+            m = m * (0.125 * LOG2E)
+        m1, m2 = m[:, :128], m[:, 128:]
+        res[turn, which, :, 0:128] = rounded(m1 * cs - m2 * sn)
+        res[turn, which, :, 128:256] = rounded(m2 * cs + m1 * sn)
+    res[turn, 2] = rounded(jnp.dot(block, w_ref[:, 512:768], preferred_element_type=F32))
+
+
+def gather_product(own, weight, width, finish, number, tables=()):
+    anywhere = pl.BlockSpec(memory_space=pl.ANY)
+    vmem = pl.BlockSpec(memory_space=pltpu.VMEM)
+    length, depth = 8 * ROW, own.shape[1]
+    return pl.pallas_call(
+        lambda *refs: gather_kernel(finish, width, bool(tables), *refs),
+        in_specs=[anywhere, vmem] + [vmem] * len(tables),
+        out_specs=[anywhere] * 4,
+        out_shape=[jax.ShapeDtypeStruct((length, depth), BF)]
+        + [jax.ShapeDtypeStruct((length, width), BF)] * 3,
+        scratch_shapes=[
+            pltpu.VMEM((length, depth), BF),
+            pltpu.VMEM((2, 3, ROW, width), BF),
+            pltpu.SemaphoreType.DMA((10,)),
+            pltpu.SemaphoreType.DMA((10,)),
+            pltpu.SemaphoreType.DMA,
+            pltpu.SemaphoreType.DMA((8,)),
+            pltpu.SemaphoreType.DMA((2, 3)),
+        ],
+        compiler_params=pltpu.CompilerParams(
+            collective_id=number, has_side_effects=True, vmem_limit_bytes=56 * 2**20
+        ),
+        cost_estimate=pl.CostEstimate(
+            flops=80 * 10**9, bytes_accessed=30 * 2**20, transcendentals=0
+        ),
+    )(own, weight, *tables)
+
+
+def scatter_kernel(dims, a_ref, w_ref, out_ref, abuf, mine, other, sums, ra, rb, near_x, near_l, send, recv, a_sem):
+    me, partners = ring_position()
+    to_x, to_l, to_c = partners
+    order = (7, 3, 5, 6, 1, 2, 4, 0)
+
+    def load(index):
+        return pltpu.make_async_copy(
+            a_ref.at[rows_at(me ^ order[index])], abuf.at[index % 2], a_sem.at[index % 2]
+        )
+
+    load(0).start()
+    enter_ring(partners)
+
+    def copy(index, source, target, partner):
+        return pltpu.make_async_remote_copy(
+            src_ref=source,
+            dst_ref=target,
+            send_sem=send.at[index],
+            recv_sem=recv.at[index],
+            device_id=partner,
+            device_id_type=MESH,
+        )
+
+    half = ROW // 2
+    top, bottom = pl.ds(0, half), pl.ds(half, half)
+    copies = [copy(slot, mine.at[slot], other.at[slot], to_c) for slot in range(4)] + [
+        copy(4, sums.at[2, top], ra, to_x),
+        copy(5, sums.at[2, bottom], rb, to_l),
+        copy(6, sums.at[0, top], near_x.at[top], to_x),
+        copy(7, sums.at[1, bottom], near_l.at[bottom], to_l),
+        copy(8, sums.at[0, bottom], near_x.at[bottom], to_x),
+        copy(9, sums.at[1, top], near_l.at[top], to_l),
+    ]
+
+    def product(index, store):
+        def columns(chunk, carry):
+            here = pl.ds(pl.multiple_of(chunk * 256, 256), 256)
+            w = w_ref[here, :] if dims == NT else w_ref[:, here]
+            store(
+                here, lax.dot_general(abuf[index % 2], w, dims, preferred_element_type=F32)
+            )
+            return carry
+
+        lax.fori_loop(0, 8, columns, 0)
+
+    for index, slot in enumerate(order):
+        load(index).wait()
+        if index + 1 < 8:
+            load(index + 1).start()
+        if slot >= 4:
+
+            def store(here, value, slot=slot):
+                mine[slot - 4, :, here] = rounded(value)
+
+            product(index, store)
+            copies[slot - 4].start()
+        elif slot > 0:
+            copies[slot].wait_recv()
+
+            def store(here, value, slot=slot):
+                sums[slot - 1, :, here] = rounded(value + other[slot, :, here].astype(F32))
+
+            product(index, store)
+            if slot == 3:
+                copies[4].start()
+                copies[5].start()
+            if slot == 1:
+                copies[6].start()
+            if slot == 2:
+                copies[7].start()
+                copies[5].wait_recv()
+                sums[0, bottom, :] = rounded(
+                    sums[0, bottom, :].astype(F32) + rb[...].astype(F32)
+                )
+                copies[8].start()
+                copies[4].wait_recv()
+                sums[1, top, :] = rounded(sums[1, top, :].astype(F32) + ra[...].astype(F32))
+                copies[9].start()
+        else:
+            copies[0].wait_recv()
+
+            def store(here, value):
+                out_ref[:, here] = value + other[0, :, here].astype(F32)
+
+            product(index, store)
+    for part, first, second in ((top, 6, 9), (bottom, 8, 7)):
+        copies[first].wait_recv()
+        copies[second].wait_recv()
+        out_ref[part, :] = out_ref[part, :] + (
+            near_x[part, :].astype(F32) + near_l[part, :].astype(F32)
+        )
+    for each in copies:
+        each.wait_send()
+
+
+def product_scatter(a, weight, dims, number):
+    anywhere = pl.BlockSpec(memory_space=pl.ANY)
+    vmem = pl.BlockSpec(memory_space=pltpu.VMEM)
+    depth = a.shape[1]
+    width = weight.shape[0] if dims == NT else weight.shape[1]
+    return pl.pallas_call(
+        lambda *refs: scatter_kernel(dims, *refs),
+        in_specs=[anywhere, vmem],
+        out_specs=vmem,
+        out_shape=jax.ShapeDtypeStruct((ROW, width), F32),
+        scratch_shapes=[
+            pltpu.VMEM((2, ROW, depth), BF),
+            pltpu.VMEM((4, ROW, width), BF),
+            pltpu.VMEM((4, ROW, width), BF),
+            pltpu.VMEM((3, ROW, width), BF),
+            pltpu.VMEM((ROW // 2, width), BF),
+            pltpu.VMEM((ROW // 2, width), BF),
+            pltpu.VMEM((ROW, width), BF),
+            pltpu.VMEM((ROW, width), BF),
+            pltpu.SemaphoreType.DMA((10,)),
+            pltpu.SemaphoreType.DMA((10,)),
+            pltpu.SemaphoreType.DMA((2,)),
+        ],
+        compiler_params=pltpu.CompilerParams(
+            collective_id=number, has_side_effects=True, vmem_limit_bytes=58 * 2**20
+        ),
+        cost_estimate=pl.CostEstimate(
+            flops=80 * 10**9, bytes_accessed=30 * 2**20, transcendentals=0
+        ),
+    )(a, weight)
 
 
 def column_order():
@@ -446,21 +715,31 @@
     return lane // 64 == head
 
 
-def stored_place(block, me):
-    slot = block ^ me
-    return (slot & 3) * 2 + (slot >> 2)
-
-
-def picked_block(step, split, splits):
-    half = 4 // splits
-    return jnp.where(step < half, split * half + step, 7 - (split * half + step - half))
-
-
-def attend_kernel(split, splits, me_ref, q_ref, k_ref, v_ref, *refs):
+def picked_block(step, blocks):
+    block = jnp.int32(blocks[0])
+    for index in range(1, len(blocks)):
+        block = jnp.where(step == index, blocks[index], block)
+    return block
+
+
+def mark(*values):
+    return sum(value[(0,) * value.ndim].astype(F32) for value in values) * 0.0
+
+
+def after(values, zero):
+    return values + zero.astype(values.dtype)
+
+
+def held(values, zero):
+    if zero is None:
+        return values
+    return after(lax.optimization_barrier(values), zero)
+
+
+def attend_kernel(chosen, me_ref, q_ref, k_ref, v_ref, *refs):
     o_ref, l_ref, s_scr, m_scr, acc_scr, o_scr = refs[-6:]
     heads = 4
-    block = picked_block(pl.program_id(0), split, splits)
-    me = me_ref[0]
+    block = picked_block(pl.program_id(0), chosen)
     q = q_ref[...]
     row = lax.broadcasted_iota(jnp.int32, (ROW, ROW), 0)
     col = lax.broadcasted_iota(jnp.int32, (ROW, ROW), 1)
@@ -474,7 +753,7 @@
         return (s[:, :128] + s[:, 128:256]) + (s[:, 256:384] + s[:, 384:])
 
     def start_of(key_block):
-        return pl.multiple_of(stored_place(key_block, me) * ROW, ROW)
+        return pl.multiple_of(key_block * ROW, ROW)
 
     for head in range(heads):
         qh = jnp.where(head_lanes_turned(head), q, jnp.zeros_like(q))
@@ -519,17 +798,17 @@
     o_ref[...] = o_scr[...].astype(BF)
 
 
-def attend(me, q, k, v, split, splits, earlier):
+def attend(me, q, k, v, chosen, earlier):
     length = q.shape[0]
     blocks = length // ROW
 
     def place(step, me):
-        return stored_place(picked_block(step, split, splits), me[0])
+        return picked_block(step, chosen)
 
     whole = pl.BlockSpec((length, 256), lambda step, me: (0, 0))
     grid = pltpu.PrefetchScalarGridSpec(
         num_scalar_prefetch=1,
-        grid=(blocks // splits,),
+        grid=(len(chosen),),
         in_specs=[pl.BlockSpec((ROW, 256), lambda step, me: (place(step, me), 0)), whole, whole]
         + [pl.BlockSpec(memory_space=pl.ANY)] * len(earlier),
         out_specs=[
@@ -544,7 +823,7 @@
         ],
     )
     return pl.pallas_call(
-        lambda *refs: attend_kernel(split, splits, *refs),
+        lambda *refs: attend_kernel(chosen, *refs),
         grid_spec=grid,
         out_shape=[
             jax.ShapeDtypeStruct((length, 256), BF),
@@ -553,7 +832,7 @@
         input_output_aliases={4: 0, 5: 1} if earlier else {},
         compiler_params=pltpu.CompilerParams(vmem_limit_bytes=48 * 2**20),
         cost_estimate=pl.CostEstimate(
-            flops=10**11 // splits, bytes_accessed=10 * 2**20, transcendentals=0
+            flops=14 * 10**9 * len(chosen), bytes_accessed=10 * 2**20, transcendentals=0
         ),
     )(me, q, k, v, *earlier)
 
@@ -561,14 +840,18 @@
 KEYS = 256
 
 
-def attend_back_kernel(split, splits, me_ref, q_ref, k_ref, v_ref, do_ref, o_ref, l_ref, cos_ref, sin_ref, *refs):
-    if split == 0:
-        dq_in = None
+def attend_back_kernel(chosen, first, last, me_ref, q_ref, k_ref, v_ref, do_ref, l_ref, cos_ref, sin_ref, *refs):
+    if first:
+        o_ref, dkv_ref, dq_out, delta = refs[:4]
+        rest = refs[4:]
     else:
-        dq_in = refs[0]
-    dkv_ref, dq_out, qm, dom, delta, dq, dk, dv, km, pt, dst = refs[-11:]
+        if last:
+            all_cos, all_sin = refs[:2]
+            refs = refs[2:]
+        delta, dq_in, _, dkv_ref, dq_out = refs[:5]
+        rest = refs[5:]
+    qm, dom, dq, dk, dv, km, pt, dst = rest
     heads = 4
-    me = me_ref[0]
     step = pl.program_id(0)
     blocks = q_ref.shape[0] // ROW
 
@@ -582,16 +865,16 @@
                 rows = slice(head * ROW, (head + 1) * ROW)
                 qm[place, rows, :] = jnp.where(head_lanes_turned(head), q, jnp.zeros_like(q))
                 dom[place, rows, :] = jnp.where(head_lanes_plain(head), do, jnp.zeros_like(do))
-            product = do.astype(F32) * o_ref[pl.ds(start, ROW), :].astype(F32)
-            high = product.astype(BF)
-            low = (product - high.astype(F32)).astype(BF)
-            head_row = lax.broadcasted_iota(jnp.int32, (8, 256), 0)
-            lane = lax.broadcasted_iota(jnp.int32, (8, 256), 1)
-            pick = jnp.where(lane // 64 == head_row, 1.0, 0.0).astype(BF)
-            sums = lax.dot_general(pick, high, NT, preferred_element_type=F32)
-            sums += lax.dot_general(pick, low, NT, preferred_element_type=F32)
-            delta[place] = sums[:heads, :]
-            if split == 0:
+            if first:
+                product = do.astype(F32) * o_ref[pl.ds(start, ROW), :].astype(F32)
+                high = product.astype(BF)
+                low = (product - high.astype(F32)).astype(BF)
+                head_row = lax.broadcasted_iota(jnp.int32, (8, 256), 0)
+                lane = lax.broadcasted_iota(jnp.int32, (8, 256), 1)
+                pick = jnp.where(lane // 64 == head_row, 1.0, 0.0).astype(BF)
+                sums = lax.dot_general(pick, high, NT, preferred_element_type=F32)
+                sums += lax.dot_general(pick, low, NT, preferred_element_type=F32)
+                delta[place] = sums[:heads, :]
                 dq[pl.ds(start, ROW), :] = jnp.zeros((ROW, 256), F32)
             else:
                 dq[pl.ds(start, ROW), :] = dq_in[pl.ds(start, ROW), :]
@@ -601,12 +884,10 @@
 
     key_row = lax.broadcasted_iota(jnp.int32, (KEYS, ROW), 0)
     query_col = lax.broadcasted_iota(jnp.int32, (KEYS, ROW), 1)
-    block = picked_block(step, split, splits)
-    key_place = stored_place(block, me)
+    block = picked_block(step, chosen)
 
     def key_part(sub, carry):
         inner = pl.multiple_of(sub * KEYS, KEYS)
-        table = pl.ds(pl.multiple_of(key_place * ROW + sub * KEYS, KEYS), KEYS)
         k = k_ref[pl.ds(inner, KEYS), :]
         v = v_ref[pl.ds(inner, KEYS), :]
         for head in range(heads):
@@ -615,7 +896,7 @@
         dv[...] = jnp.zeros_like(dv)
 
         def query_part(query_block, diagonal):
-            place = stored_place(query_block, me)
+            place = query_block
             rows = pl.ds(pl.multiple_of(place * ROW, ROW), ROW)
             for head in range(heads):
                 part = slice(head * ROW, (head + 1) * ROW)
@@ -642,8 +923,8 @@
             return carry
 
         lax.fori_loop(block + 1, blocks, later, 0)
-        cs = cos_ref[table, :]
-        sn = sin_ref[table, :]
+        cs = cos_ref[pl.ds(inner, KEYS), :]
+        sn = sin_ref[pl.ds(inner, KEYS), :]
         d = dk[...] * (1.0 / LOG2E)
         d1, d2 = d[:, :128], d[:, 128:]
         dkv_ref[pl.ds(inner, KEYS), 0:128] = (d1 * cs + d2 * sn).astype(BF)
@@ -657,11 +938,11 @@
     def _():
         def finish(place, carry):
             rows = pl.ds(pl.multiple_of(place * ROW, ROW), ROW)
-            if split < splits - 1:
+            if not last:
                 dq_out[rows, :] = dq[rows, :]
             else:
-                cs = cos_ref[rows, :]
-                sn = sin_ref[rows, :]
+                cs = all_cos[rows, :]
+                sn = all_sin[rows, :]
                 d = dq[rows, :] * 0.125
                 d1, d2 = d[:, :128], d[:, 128:]
                 dq_out[rows, 0:128] = (d1 * cs + d2 * sn).astype(BF)
@@ -671,39 +952,50 @@
         lax.fori_loop(0, blocks, finish, 0)
 
 
-def attend_back(me, q, k, v, do, o, level, cos, sin, split, splits, earlier):
+def attend_back(me, q, k, v, do, o, level, cos, sin, chosen, last, earlier):
     length = q.shape[0]
     blocks = length // ROW
 
     def place(step, me):
-        return stored_place(picked_block(step, split, splits), me[0])
+        return picked_block(step, chosen)
 
     def whole(width):
         return pl.BlockSpec((length, width), lambda step, me: (0, 0))
 
-    key_spec = pl.BlockSpec((ROW, 256), lambda step, me: (place(step, me), 0))
-    more = []
-    if earlier:
-        more = [whole(256), pl.BlockSpec(memory_space=pl.ANY)]
+    def key_spec(width):
+        return pl.BlockSpec((ROW, width), lambda step, me: (place(step, me), 0))
+
+    head_rows = pl.BlockSpec((blocks, 4, ROW), lambda step, me: (0, 0, 0))
+    out_specs = [key_spec(512), whole(256)]
+    out_shape = [
+        jax.ShapeDtypeStruct((length, 512), BF),
+        jax.ShapeDtypeStruct((length, 256), BF if last else F32),
+    ]
+    if not earlier:
+        more = [(whole(256), o)]
+        out_specs.append(head_rows)
+        out_shape.append(jax.ShapeDtypeStruct((blocks, 4, ROW), F32))
+    else:
+        delta, dq, dkv = earlier
+        more = [(whole(128), cos), (whole(128), sin)] if last else []
+        more += [(head_rows, delta), (whole(256), dq), (pl.BlockSpec(memory_space=pl.ANY), dkv)]
     grid = pltpu.PrefetchScalarGridSpec(
         num_scalar_prefetch=1,
-        grid=(blocks // splits,),
+        grid=(len(chosen),),
         in_specs=[
             whole(256),
-            key_spec,
-            key_spec,
+            key_spec(256),
+            key_spec(256),
             whole(256),
-            whole(256),
-            pl.BlockSpec((blocks, 4, ROW), lambda step, me: (0, 0, 0)),
-            whole(128),
-            whole(128),
+            head_rows,
+            key_spec(128),
+            key_spec(128),
         ]
-        + more,
-        out_specs=[pl.BlockSpec((ROW, 512), lambda step, me: (place(step, me), 0)), whole(256)],
+        + [spec for spec, _ in more],
+        out_specs=out_specs,
         scratch_shapes=[
             pltpu.VMEM((blocks, 4 * ROW, 256), BF),
             pltpu.VMEM((blocks, 4 * ROW, 256), BF),
-            pltpu.VMEM((blocks, 4, ROW), F32),
             pltpu.VMEM((length, 256), F32),
             pltpu.VMEM((KEYS, 256), F32),
             pltpu.VMEM((KEYS, 256), F32),
@@ -712,20 +1004,16 @@
             pltpu.VMEM((KEYS, 4 * ROW), BF),
         ],
     )
-    last = split == splits - 1
     return pl.pallas_call(
-        lambda *refs: attend_back_kernel(split, splits, *refs),
+        lambda *refs: attend_back_kernel(chosen, not earlier, last, *refs),
         grid_spec=grid,
-        out_shape=[
-            jax.ShapeDtypeStruct((length, 512), BF),
-            jax.ShapeDtypeStruct((length, 256), BF if last else F32),
-        ],
-        input_output_aliases={10: 0} if earlier else {},
+        out_shape=out_shape,
+        input_output_aliases={7 + len(more): 0} if earlier else {},
         compiler_params=pltpu.CompilerParams(vmem_limit_bytes=62 * 2**20),
         cost_estimate=pl.CostEstimate(
-            flops=14 * 10**10 // splits, bytes_accessed=20 * 2**20, transcendentals=0
+            flops=19 * 10**9 * len(chosen), bytes_accessed=20 * 2**20, transcendentals=0
         ),
-    )(me, q, k, v, do, o, level, cos, sin, *earlier)
+    )(me, q, k, v, do, level, cos, sin, *[value for _, value in more])
 
 
 def ring_shards(
@@ -749,11 +1037,10 @@
     gains_moment,
     gains_average,
 ):
-    seq, tp = lax.axis_index("seq"), lax.axis_index("tp")
-    y, c, h = seq >> 1, seq & 1, tp >> 2
-    own = c * 4 + (tp & 3)
-    me = own.astype(jnp.int32).reshape(1)
+    y, c, h, l, x = (lax.axis_index(name) for name in AXES)
+    own = 4 * c + 2 * l + x
     plain_y, plain_c, straight = y == 0, c == 0, c == h
+    idle = jnp.zeros((1,), jnp.int32)
 
     def features(values):
         half = values.shape[-1] // 2
@@ -764,20 +1051,25 @@
     def both_cores(mine, other):
         return jnp.where(plain_c, mine, other), jnp.where(plain_c, other, mine)
 
-    def gather_weight(shard):
+    def gather_near(shard):
         r1 = move(shard, lambda y, c, h, l, x: (y, c, 1 - h, l, x) if c == h else None)
         r2a = move(shard, lambda y, c, h, l, x: (y, 1 - c, h, l, x) if c != h else None)
         r2b = move(shard, lambda y, c, h, l, x: (y, h, c, l, x) if c != h else None)
         near = jnp.stack(both_cores(jnp.where(straight, shard, r1), jnp.where(straight, r2a, r2b)))
-        far = flip(near, "y")
-        return near[0], near[1], far[0], far[1]
-
-    def scatter_grad(near, far):
-        total = (near.astype(F32) + flip(far, "y").astype(F32)).astype(BF)
+        return near, mark(r1, r2a, r2b)
+
+    def scatter_y(blocks, zero=None):
+        return blocks[:2], flip(held(blocks[2:], zero), "y")
+
+    def scatter_ch(near, far):
+        total = (near.astype(F32) + far.astype(F32)).astype(BF)
         kept, other = both_cores(total[0], total[1])
         r1 = move(kept, lambda y, c, h, l, x: (y, c, 1 - h, l, x) if c != h else None)
         r2a = move(other, lambda y, c, h, l, x: (y, 1 - c, h, l, x) if c == h else None)
         r2b = move(other, lambda y, c, h, l, x: (y, h, c, l, x) if c != h else None)
+        return kept, r1, r2a, r2b
+
+    def scatter_own(kept, r1, r2a, r2b):
         return jnp.where(
             straight,
             kept.astype(F32) + r1.astype(F32),
@@ -785,86 +1077,70 @@
         )
 
     turn = column_order()
-    qkv_shard = jnp.dot(qkv_master.astype(BF), turn, preferred_element_type=F32).astype(BF)
-    rows_in = features(swap_ch(layer_input)).astype(F32)
+    rows_moved = swap_ch(layer_input)
+    rows_in = features(rows_moved).astype(F32)
     gains_here = gains_master.astype(BF)
     gains_near = jnp.concatenate(both_cores(gains_here, flip(gains_here, "c")), axis=1)
     gains_all = jnp.concatenate([gains_near, flip(gains_near, "y")], axis=1).astype(F32)
     gain_first, gain_second = gains_all[0], gains_all[1]
+    qkv_shard = jnp.dot(qkv_master.astype(BF), turn, preferred_element_type=F32).astype(BF)
+    scale_first = rms_scale(rows_in)
+    normed_own = (rows_in * scale_first * gain_first).astype(BF)
+    qkv_near, near_there = gather_near(held(qkv_shard, mark(rows_moved)))
+    qkv_far = flip(qkv_near, "y")
+    grad_moved = swap_ch(held(cotangent, near_there))
+    qkv_weight = jnp.concatenate([qkv_near, qkv_far]).reshape(2048, 768)
+
+    frequency = rope_theta ** (
+        -((jnp.arange(128, dtype=jnp.int32) % 32).astype(F32) * 2.0) / HD
+    )
+    angles = swap_ch(positions).astype(F32)[:, None] * frequency[None, :]
+    cosine, sine = jnp.cos(angles), jnp.sin(angles)
+    normed, queries, keys, values = gather_product(
+        normed_own, qkv_weight, 256, attention_finish, 1, (cosine, sine)
+    )
+
     count_here = counts.astype(F32)
     count_pair = both_cores(count_here, flip(count_here, "c"))
     pair_total = count_pair[0] + count_pair[1]
     count_total = pair_total + flip(pair_total, "y")
     seq_weight = 4.0 * jnp.where(h == 0, count_pair[0], count_pair[1])[0] / count_total[0]
 
-    scale_first = rms_scale(rows_in)
-    normed_groups = ring_gather((rows_in * scale_first * gain_first).astype(BF))
-    qkv_weight = jnp.concatenate(gather_weight(qkv_shard), axis=0)
-
-    place_order = jnp.stack([own ^ slot for slot in STORED])
-    positions_here = swap_ch(positions).reshape(8, ROW)[place_order].reshape(8 * ROW)
-    frequency = rope_theta ** (
-        -((jnp.arange(128, dtype=jnp.int32) % 32).astype(F32) * 2.0) / HD
-    )
-    angles = positions_here.astype(F32)[:, None] * frequency[None, :]
-    cosine, sine = jnp.cos(angles), jnp.sin(angles)
-
-    queries, keys, values = [], [], []
-    for place, group in enumerate(normed_groups):
-        mixed = jnp.dot(group, qkv_weight, preferred_element_type=F32)
-        rows = slice(place * 2 * ROW, (place + 1) * 2 * ROW)
-        cs, sn = cosine[rows], sine[rows]
-
-        def turned(u1, u2):
-            return jnp.concatenate([u1 * cs - u2 * sn, u2 * cs + u1 * sn], axis=1)
-
-        queries.append((turned(mixed[:, :128], mixed[:, 128:256]) * (0.125 * LOG2E)).astype(BF))
-        keys.append(turned(mixed[:, 256:384], mixed[:, 384:512]).astype(BF))
-        values.append(mixed[:, 512:].astype(BF))
-    queries, keys, values = (jnp.concatenate(v, axis=0) for v in (queries, keys, values))
-
-    gate_up_shard = jnp.concatenate(
-        [gate_up_master[m, :, k * 512 : (k + 1) * 512] for m in range(2) for k in range(2)]
-        + [out_master],
-        axis=0,
-    ).astype(BF)
-    gate_up_blocks = gather_weight(gate_up_shard)
-    gate_up_weight = jnp.concatenate(
-        [
-            jnp.concatenate([block[k * 512 : (k + 1) * 512] for k in range(4)], axis=1)
-            for block in gate_up_blocks
-        ],
-        axis=0,
-    )
-    out_heads = jnp.concatenate([block[2048:] for block in gate_up_blocks], axis=1)
-    out_weight = jnp.concatenate(ring_gather(out_heads), axis=0)
-    down_weight = jnp.concatenate(gather_weight(down_master.astype(BF)), axis=1)
-
-    grad_rows = seq_weight * features(swap_ch(cotangent)).astype(F32)
-    grad_out = jnp.concatenate(ring_gather(grad_rows.astype(BF)), axis=0)
-
-    splits = 4
-    done = ()
-    for split in range(splits):
-        done = tuple(attend(me, queries, keys, values, split, splits, done))
+    first_there = mark(values)
+    grad_rows = seq_weight * features(grad_moved).astype(F32)
+    grad_out = lax.all_gather(
+        held(grad_rows.astype(BF), first_there), RING, axis=0, tiled=True
+    )
+    out_near, out_there = gather_near(held(out_master.astype(BF), first_there))
+    gate_up_shard = jnp.concatenate([gate_up_master[0], gate_up_master[1]], axis=1).astype(BF)
+    gate_up_near, gate_up_there = gather_near(held(gate_up_shard, first_there))
+    done = attend(idle, queries, keys, values, (7, 0, 6, 1), ())
+    stage = out_there + gate_up_there
+    out_far = flip(out_near, "y")
+    gate_up_far = flip(gate_up_near, "y")
+    down_near, down_there = gather_near(held(down_master.astype(BF), gate_up_there))
+    out_heads = jnp.concatenate([out_near, out_far]).transpose(1, 0, 2).reshape(256, 2048)
+    out_weight = lax.all_gather(out_heads, RING, axis=0, tiled=True)
+    done = attend(idle + stage.astype(jnp.int32), queries, keys, values, (5, 2, 4, 3), tuple(done))
     attended, level = done
-    attended_own = heads_to_rows(attended)
+    gate_up_weight = jnp.concatenate([gate_up_near, gate_up_far]).reshape(2048, 2048)
+    down_far = flip(down_near, "y")
+    down_weight = jnp.concatenate([down_near, down_far]).transpose(1, 0, 2).reshape(1024, 2048)
+
+    attended_own = (
+        lax.all_to_all(attended.reshape(8, ROW, 256), RING, 0, 0)
+        .transpose(1, 0, 2)
+        .reshape(ROW, 2048)
+    )
     residual = rows_in + jnp.dot(attended_own, out_weight, preferred_element_type=F32)
     scale_second = rms_scale(residual)
-    second_groups = ring_gather((residual * scale_second * gain_second).astype(BF))
-    gate, up, activation = [], [], []
-    for group in second_groups:
-        g = jnp.dot(group, gate_up_weight[:, :1024], preferred_element_type=F32)
-        u = jnp.dot(group, gate_up_weight[:, 1024:], preferred_element_type=F32)
-        gate.append(g.astype(BF))
-        up.append(u.astype(BF))
-        activation.append((g * jax.nn.sigmoid(g) * u).astype(BF))
-    gate, up, activation = (jnp.concatenate(v, axis=0) for v in (gate, up, activation))
-    normed_second = jnp.concatenate(second_groups, axis=0)
-
-    def rows_of(slot):
-        place = STORED.index(slot)
-        return slice(place * ROW, (place + 1) * ROW)
+    normed_second, gate, up, activation = gather_product(
+        (residual * scale_second * gain_second).astype(BF),
+        gate_up_weight,
+        1024,
+        feed_forward_finish,
+        2,
+    )
 
     grad_act = lax.dot_general(grad_out, down_weight, NT, preferred_element_type=F32)
     g = gate.astype(F32)
@@ -872,25 +1148,15 @@
     grad_gate = (grad_act * up.astype(F32) * sigmoid * (1.0 + g * (1.0 - sigmoid))).astype(BF)
     grad_up = (grad_act * g * sigmoid).astype(BF)
     grad_gate_up = jnp.concatenate([grad_gate, grad_up], axis=1)
-
-    grad_normed_second = ring_scatter(
-        lambda slot: lax.dot_general(
-            grad_gate_up[rows_of(slot)], gate_up_weight, NT, preferred_element_type=F32
-        )
-    )
-    layer_own = residual + ring_scatter(
-        lambda slot: jnp.dot(activation[rows_of(slot)], down_weight, preferred_element_type=F32)
-    )
-    layer_output = swap_ch(features(layer_own.astype(BF)))
-
-    down_grad = lax.dot_general(activation, grad_out, TN, preferred_element_type=F32).astype(BF)
-    down_grad = down_grad.reshape(1024, 4, 512).transpose(1, 0, 2)
-    down_grad_own = scatter_grad(down_grad[:2], down_grad[2:])
+    grad_normed_second = product_scatter(grad_gate_up, gate_up_weight, NT, 3)
     gate_up_grad = lax.dot_general(
         normed_second, grad_gate_up, TN, preferred_element_type=F32
     ).astype(BF)
-    gate_up_grad = gate_up_grad.reshape(4, 512, 2048)
-    gate_up_grad_own = scatter_grad(gate_up_grad[:2], gate_up_grad[2:])
+    gate_up_y = scatter_y(gate_up_grad.reshape(4, 512, 2048))
+    down_grad = lax.dot_general(activation, grad_out, TN, preferred_element_type=F32).astype(BF)
+    down_y = scatter_y(down_grad.reshape(1024, 4, 512).transpose(1, 0, 2))
+    layer_own = residual + product_scatter(activation, down_weight, NN, 4)
+    layer_output = swap_ch(features(layer_own.astype(BF)))
 
     def norm_grad(values, scale, gain, grad):
         scaled = grad * gain
@@ -904,35 +1170,35 @@
     )
     residual_grad = residual_grad + grad_rows
     residual_low = residual_grad.astype(BF)
-    grad_attended = rows_to_heads(
-        lax.dot_general(residual_low, out_weight, NT, preferred_element_type=F32).astype(BF)
-    )
-    out_grad = lax.dot_general(attended_own, residual_low, TN, preferred_element_type=F32).astype(BF)
-    out_grad = ring_scatter(
-        lambda slot: out_grad[STORED.index(slot) * 256 : (STORED.index(slot) + 1) * 256].astype(F32)
-    ).astype(BF)
-    out_grad = out_grad.reshape(256, 4, 512).transpose(1, 0, 2)
-    out_grad_own = scatter_grad(out_grad[:2], out_grad[2:])
-
-    splits = 2
-    earlier = ()
-    for split in range(splits):
-        grad_kv, grad_q = attend_back(
-            me, queries, keys, values, grad_attended, attended, level, cosine, sine, split, splits, earlier
-        )
-        earlier = (grad_q, grad_kv)
+    grad_heads = lax.dot_general(residual_low, out_weight, NT, preferred_element_type=F32)
+    grad_attended = lax.all_to_all(
+        grad_heads.astype(BF).reshape(ROW, 8, 256).transpose(1, 0, 2), RING, 0, 0
+    ).reshape(8 * ROW, 256)
+
+    def back(zero, chosen, last, earlier):
+        grad_kv, grad_q, *delta = attend_back(
+            idle + zero.astype(jnp.int32),
+            queries, keys, values, grad_attended, attended, level, cosine, sine, chosen, last, earlier,
+        )
+        return (delta[0] if delta else earlier[0], grad_q, grad_kv)
+
+    earlier = back(mark(gate_up_y[1]), (0, 7, 1, 6), False, ())
+    gate_up_ch = scatter_ch(*gate_up_y)
+    down_ch = scatter_ch(*down_y)
+    _, grad_q, grad_kv = back(mark(*gate_up_ch[1:]), (2, 5, 3, 4), True, earlier)
+
     grad_mixture = jnp.concatenate([grad_q, grad_kv], axis=1)
-    grad_normed_first = ring_scatter(
-        lambda slot: lax.dot_general(
-            grad_mixture[rows_of(slot)], qkv_weight, NT, preferred_element_type=F32
-        )
-    )
-    qkv_grad = lax.dot_general(
-        jnp.concatenate(normed_groups, axis=0), grad_mixture, TN, preferred_element_type=F32
-    ).astype(BF)
+    grad_normed_first = product_scatter(grad_mixture, qkv_weight, NT, 5)
+    qkv_grad = lax.dot_general(normed, grad_mixture, TN, preferred_element_type=F32).astype(BF)
     qkv_grad = lax.dot_general(qkv_grad, turn, NT, preferred_element_type=F32).astype(BF)
-    qkv_grad = qkv_grad.reshape(4, 512, 768)
-    qkv_grad_own = scatter_grad(qkv_grad[:2], qkv_grad[2:])
+    qkv_y = scatter_y(qkv_grad.reshape(4, 512, 768))
+    out_grad = lax.dot_general(attended_own, residual_low, TN, preferred_element_type=F32)
+    out_grad = lax.psum_scatter(out_grad.astype(BF), RING, scatter_dimension=0, tiled=True)
+    out_y = scatter_y(out_grad.reshape(256, 4, 512).transpose(1, 0, 2))
+    qkv_grad_own = scatter_own(*scatter_ch(*qkv_y))
+    out_grad_own = scatter_own(*scatter_ch(*out_y))
+    gate_up_grad_own = scatter_own(*gate_up_ch)
+    down_grad_own = scatter_own(*down_ch)
 
     input_back, gain_first_part = norm_grad(rows_in, scale_first, gain_first, grad_normed_first)
     input_grad = swap_ch(features(residual_grad + input_back).astype(BF)).astype(F32)
@@ -1005,5 +1271,22 @@
         P(None, "seq"),
         P(None, "seq"),
     )
-    body = ring_shards if ring_plan_fits(mesh) else shards
-    return jax.shard_map(body, mesh=mesh, in_specs=in_specs, out_specs=out_specs, check_vma=False)
+    if ring_plan_fits(mesh):
+        fine = jax.sharding.Mesh(mesh.devices.reshape(2, 2, 2, 2, 2), AXES)
+        names = {"seq": ("y", "c"), "tp": ("h", "l", "x")}
+
+        def finer(spec):
+            parts = []
+            for entry in spec:
+                entry = (entry,) if isinstance(entry, str) else (entry or ())
+                parts.append(sum((names[name] for name in entry), ()) or None)
+            return P(*parts)
+
+        return jax.shard_map(
+            ring_shards,
+            mesh=fine,
+            in_specs=tuple(finer(spec) for spec in in_specs),
+            out_specs=tuple(finer(spec) for spec in out_specs),
+            check_vma=False,
+        )
+    return jax.shard_map(shards, mesh=mesh, in_specs=in_specs, out_specs=out_specs, check_vma=False)

time: 1900 us -> 1660 us (0.87)
  Pallas kernels: 257 us -> 789 us
  matrix products: 400 us -> 136 us
  starting transfers between devices: 455 us -> 225 us
  waiting for transfers between devices: 508 us -> 293 us
  local copies, waits for them, and re-layouts: 117 us -> 56.9 us
  other arithmetic: 145 us -> 118 us
  between operations: 6.12 us -> 27.8 us
    pallas_call x6 -> x9, Pallas kernels: 257 us -> 789 us  [the longest x3 325 us: product_scatter(): pl.pallas_call(lambda *refs: scatter_kernel(dims, *refs), in_specs=[anywh...]
    ppermute x132 -> x46, starting transfers between devices: 455 us -> 190 us  [move(): return lax.ppermute(values, AXES, device_pairs(target))]
    ppermute x132 -> x46, waiting for transfers between devices: 508 us -> 274 us  [move(): return lax.ppermute(values, AXES, device_pairs(target))]
    dot_general x37 -> x1, matrix products: 251 us -> 19 us  [ring_shards(): lax.dot_general(normed, grad_mixture, TN, preferred_element_type=F32)]
    unnamed x321 -> x158, local copies, waits for them, and re-layouts: 75.9 us -> 19.6 us
    all_to_all x0 -> x2, starting transfers between devices: none -> 35 us  [the longest x1 30.5 us: ring_shards(): lax.all_to_all(attended.reshape(8, ROW, 256), RING, 0, 0).transpose(1, 0, 2)]
    concatenate x6 -> x4, other arithmetic: 50.9 us -> 16.3 us  [the longest x1 7.33 us: ring_shards(): jnp.concatenate([gate_up_near, gate_up_far]).reshape(2048, 2048)]
    dot_general x1, matrix products: 49.1 us -> 22.3 us  [ring_shards(): lax.dot_general(grad_out, down_weight, NT, preferred_element_type=F32)]
  transfers between devices with their start and end apart: 132 -> 51, of which waited for: 44 -> 17; matrix products, arithmetic and copies ran while one was open for 23% -> 9% of each run, Pallas kernels for 14% -> 27%
where the time goes in v2:
time: 1660 us; the launch traced here: 1650 us
  Pallas kernels  789 us (48%)
  waiting for transfers between devices  293 us (18%)
  starting transfers between devices  225 us (14%)
  matrix products  136 us (8%)
  other arithmetic  118 us (7%)
  local copies, waits for them, and re-layouts  56.9 us (3%)
  between operations  27.8 us (2%)
    pallas_call x3, Pallas kernels, product_scatter(): pl.pallas_call(lambda *refs: scatter_kernel(dims, *refs), in_specs=[anywh...  325 us
    ppermute x46, waiting for transfers between devices, move(): return lax.ppermute(values, AXES, device_pairs(target))  274 us
    pallas_call x2, Pallas kernels, gather_product(): pl.pallas_call(lambda *refs: gather_kernel(finish, width, bool(tables), *...  215 us
    ppermute x46, starting transfers between devices, move(): return lax.ppermute(values, AXES, device_pairs(target))  190 us
    pallas_call x2, Pallas kernels, attend_back(): pl.pallas_call(lambda *refs: attend_back_kernel(chosen, not earlier, last...  144 us
    pallas_call x2, Pallas kernels, attend(): pl.pallas_call(lambda *refs: attend_kernel(chosen, *refs), grid_spec=grid...  105 us
    dot_general x1, matrix products, ring_shards(): lax.dot_general(normed_second, grad_gate_up, TN, preferred_element_type=F32)  44.5 us
  transfers between devices with their start and end apart: 51, of which 17 were waited for; matrix products, arithmetic and copies ran while one was open for 9% of the time, Pallas kernels for 27%

profile of v2, /device:TPU:0, one launch (start us, length us, event | category | flops | bytes accessed | tf_op | source)
XLA Modules:
  0.0 1646.1 jit_solution(13911251170181028268)
XLA Ops:
  20.6 44.0 %collective-permute-start.3 = (bf16[512,768]{1,0:T(8,128)(2,1)}, bf16[512,768]{1,0:T(8,128)(2,1)}, u32[]{:S(2)}, u32[]{:S(2)}) collective-permute-start(bf16[512,768]{1,0:T(8,128)(2,1)} %broadcast_add_fusion.4), channel_id=1, source_target_pairs={{0,4},{1,5},{2,6},{3,7},{12,8},{13,9},{14,10},{15,11},{16,20},{17,... | collective-permute-start | bytes 2359304 | tf_op jit(solution)/shard_map/ppermute | solution.py:354
  98.0 120.8 %shard_map.354 = (bf16[4096,2048]{1,0:T(8,128)(2,1)}, bf16[4096,256]{1,0:T(8,128)(2,1)}, bf16[4096,256]{1,0:T(8,128)(2,1)}, bf16[4096,256]{1,0:T(8,128)(2,1)}) custom-call(bf16[512,2048]{1,0:T(8,128)(2,1)} %fusion.11.refs_0_, bf16[2048,768]{1,0:T(8,128)(2,1)} %bitcast.127, f32[4096,128]{1,0:T(8,128)} %get-tuple-element.115.refs_2_.refs_6_.refs_8_, ...), custom_call_target="tpu_custom_call" | custom-call | flops 80000000000 | bytes 31457280 | tf_op jit(solution)/shard_map/pallas_call | solution.py:548
  278.6 34.0 %collective-permute-start.11 = (bf16[512,2048]{1,0:T(8,128)(2,1)}, bf16[512,2048]{1,0:T(8,128)(2,1)S(1)}, u32[]{:S(2)}, u32[]{:S(2)}) collective-permute-start(bf16[512,2048]{1,0:T(8,128)(2,1)} %broadcast_add_fusion.2), channel_id=1, source_target_pairs={{0,4},{1,5},{2,6},{3,7},{12,8},{13,9},{14,10},{15,11},{16,20},{17,... | collective-permute-start | bytes 6291464 | tf_op jit(solution)/shard_map/ppermute | solution.py:354
  314.9 52.2 %shard_map.355 = (bf16[4096,256]{1,0:T(8,128)(2,1)S(1)}, f32[8,4,512]{2,1,0:T(4,128)S(1)}) custom-call(s32[1]{0:T(128)} %constant.168.clone.1.refs_0_, bf16[4096,256]{1,0:T(8,128)(2,1)S(1)} %copy-done.1, bf16[4096,256]{1,0:T(8,128)(2,1)} %get-tuple-element.41.refs_2_, bf16[4096,256]{1,0:T(8,128)(2,1)} %get-tuple-element.39.refs_3_), custom_call_target="tpu_custom_call" | custom-call | flops 56000000000 | bytes 10485760 | tf_op jit(solution)/shard_map/pallas_call | solution.py:825
  390.6 52.8 %shard_map.356 = (bf16[4096,256]{1,0:T(8,128)(2,1)S(1)}, f32[8,4,512]{2,1,0:T(4,128)S(1)}) custom-call(s32[1]{0:T(128)} %bitcast.9.refs_0_, bf16[4096,256]{1,0:T(8,128)(2,1)S(1)} %copy-done.1, bf16[4096,256]{1,0:T(8,128)(2,1)} %get-tuple-element.41.refs_2_, ...), custom_call_target="tpu_custom_call", output_to_operand_aliasing={{0}: (4, {}), {1}: (5, {})} | custom-call | flops 56000000000 | bytes 10485760 | tf_op jit(solution)/shard_map/pallas_call | solution.py:825
  446.7 30.5 %all-to-all-start = ((bf16[8,512,256]{1,2,0:T(8,128)(2,1)}), bf16[8,512,256]{1,2,0:T(8,128)(2,1)}, u32[]{:S(2)}, u32[]{:S(2)}) async-start(bf16[8,512,256]{1,2,0:T(8,128)(2,1)} %copy.51), calls=%async_computation | async-start | bytes 4194304 | tf_op jit(solution)/shard_map/all_to_all | solution.py:1131
  484.6 18.8 %all-to-all-done = bf16[8,512,256]{1,2,0:T(8,128)(2,1)} async-done(((bf16[8,512,256]{1,2,0:T(8,128)(2,1)}), bf16[8,512,256]{1,2,0:T(8,128)(2,1)}, u32[]{:S(2)}, u32[]{:S(2)}) %all-to-all-start) | async-done | bytes 2097184 | tf_op jit(solution)/shard_map/all_to_all | solution.py:1131
  513.9 94.3 %shard_map.357 = (bf16[4096,2048]{1,0:T(8,128)(2,1)}, bf16[4096,1024]{1,0:T(8,128)(2,1)}, bf16[4096,1024]{1,0:T(8,128)(2,1)}, bf16[4096,1024]{1,0:T(8,128)(2,1)}) custom-call(bf16[512,2048]{1,0:T(8,128)(2,1)} %multiply_convert_fusion.refs_0_, bf16[2048,2048]{1,0:T(8,128)(2,1)} %bitcast.116), custom_call_target="tpu_custom_call" | custom-call | flops 80000000000 | bytes 31457280 | tf_op jit(solution)/shard_map/pallas_call | solution.py:548
  608.2 22.8 %convolution_convert_fusion.2 = bf16[1024,2048]{1,0:T(8,128)(2,1)S(1)} fusion(bf16[4096,1024]{1,0:T(8,128)(2,1)} %get-tuple-element.45.refs_0_, bf16[4096,2048]{1,0:T(8,128)(2,1)} %all-gather.5.cloned.1.call-done), kind=kOutput, calls=%fused_computation.56 | convolution fusion | flops 17181966336 | bytes 29360128 | tf_op jit(solution)/shard_map/dot_general | solution.py:1156
  633.4 44.8 %collective-permute-done.37 = bf16[2,1024,512]{2,1,0:T(8,128)(2,1)S(1)} collective-permute-done((bf16[2,1024,512]{2,1,0:T(8,128)(2,1)S(1)}, bf16[2,1024,512]{2,1,0:T(8,128)(2,1)S(1)}, u32[]{:S(2)}, u32[]{:S(2)}) %collective-permute-start.37) | collective-permute-done | bytes 2097184 | tf_op jit(solution)/shard_map/ppermute | solution.py:354
  682.6 36.6 %collective-permute-done.38 = bf16[1024,512]{1,0:T(8,128)(2,1)S(1)} collective-permute-done((bf16[1024,512]{1,0:T(8,128)(2,1)S(1)}, bf16[1024,512]{1,0:T(8,128)(2,1)S(1)}, u32[]{:S(2)}, u32[]{:S(2)}) %collective-permute-start.38) | collective-permute-done | bytes 1048608 | tf_op jit(solution)/shard_map/ppermute | solution.py:354
  755.0 24.3 %collective-permute-done.19 = bf16[2,1024,512]{2,1,0:T(8,128)(2,1)S(1)} collective-permute-done((bf16[2,1024,512]{2,1,0:T(8,128)(2,1)S(1)}, bf16[2,1024,512]{2,1,0:T(8,128)(2,1)S(1)}, u32[]{:S(2)}, u32[]{:S(2)}) %collective-permute-start.19) | collective-permute-done | bytes 2097184 | tf_op jit(solution)/shard_map/ppermute | solution.py:354
  782.8 129.8 %shard_map.358 = f32[512,2048]{1,0:T(8,128)} custom-call(bf16[4096,1024]{1,0:T(8,128)(2,1)} %get-tuple-element.45.refs_0_, bf16[1024,2048]{1,0:T(8,128)(2,1)} %bitcast.122), custom_call_target="tpu_custom_call" | custom-call | flops 80000000000 | bytes 31457280 | tf_op jit(solution)/shard_map/pallas_call | solution.py:672
  912.7 22.3 %fusion.71 = f32[4096,1024]{1,0:T(8,128)} fusion(bf16[4096,2048]{1,0:T(8,128)(2,1)} %all-gather.5.cloned.1.call-done, bf16[1024,2048]{1,0:T(8,128)(2,1)S(1)} %bitcast.123), kind=kOutput, calls=%fused_computation.206 | convolution fusion | flops 17179869184 | bytes 37748736 | tf_op jit(solution)/shard_map/dot_general | solution.py:1145
  961.3 93.7 %shard_map.359 = f32[512,2048]{1,0:T(8,128)} custom-call(bf16[4096,2048]{1,0:T(8,128)(2,1)} %pad_maximum_fusion.refs_0_, bf16[2048,2048]{1,0:T(8,128)(2,1)} %bitcast.117), custom_call_target="tpu_custom_call" | custom-call | flops 80000000000 | bytes 31457280 | tf_op jit(solution)/shard_map/pallas_call | solution.py:672
  1058.8 44.5 %convolution_convert_fusion.1 = bf16[2048,2048]{1,0:T(8,128)(2,1)} fusion(bf16[4096,2048]{1,0:T(8,128)(2,1)} %get-tuple-element.48, bf16[4096,1024]{1,0:T(8,128)(2,1)} %copy-done.9, bf16[4096,1024]{1,0:T(8,128)(2,1)} %copy-done.8), kind=kOutput, calls=%fused_computation.21 | convolution fusion | flops 34397487104 | bytes 41943040 | tf_op jit(solution)/shard_map/dot_general | solution.py:1152
  1144.1 60.1 %collective-permute-done.24 = bf16[2,512,2048]{2,1,0:T(8,128)(2,1)} collective-permute-done((bf16[2,512,2048]{2,1,0:T(8,128)(2,1)}, bf16[2,512,2048]{2,1,0:T(8,128)(2,1)}, u32[]{:S(2)}, u32[]{:S(2)}) %collective-permute-start.24) | collective-permute-done | bytes 4194336 | tf_op jit(solution)/shard_map/ppermute | solution.py:354
  1220.4 72.3 %shard_map.360 = (bf16[4096,512]{1,0:T(8,128)(2,1)}, f32[4096,256]{1,0:T(8,128)}, f32[8,4,512]{2,1,0:T(4,128)}) custom-call(s32[1]{0:T(128)} %bitcast.36.refs_0_, bf16[4096,256]{1,0:T(8,128)(2,1)} %get-tuple-element.40.refs_1_, bf16[4096,256]{1,0:T(8,128)(2,1)} %get-tuple-element.41.refs_2_, bf16[4096,256]{1,0:T(8,128)(2,1)} %get-tuple-element.39.refs_3_, ...), custom_call_target="tpu_custom_call" | custom-call | flops 76000002048 | bytes 20971520 | tf_op jit(solution)/shard_map/pallas_call | solution.py:1007
  1302.4 71.6 %shard_map.361 = (bf16[4096,512]{1,0:T(8,128)(2,1)}, bf16[4096,256]{1,0:T(8,128)(2,1)}) custom-call(s32[1]{0:T(128)} %bitcast.33.refs_0_, bf16[4096,256]{1,0:T(8,128)(2,1)} %get-tuple-element.40.refs_1_, bf16[4096,256]{1,0:T(8,128)(2,1)} %get-tuple-element.41.refs_2_, bf16[4096,256]{1,0:T(8,128)(2,1)} %get-tuple-element.39.refs_3_, ...), custom_call_target="tpu_custom_call", output_to_operand_aliasing={{0}: (12, {})} | custom-call | flops 76000002048 | bytes 20971520 | tf_op jit(solution)/shard_map/pallas_call | solution.py:1007
  1379.6 101.7 %shard_map.362 = f32[512,2048]{1,0:T(8,128)} custom-call(bf16[4096,768]{1,0:T(8,128)(2,1)} %constant_dynamic-update-slice_fusion.refs_0_, bf16[2048,768]{1,0:T(8,128)(2,1)} %bitcast.128), custom_call_target="tpu_custom_call" | custom-call | flops 80000000000 | bytes 31457280 | tf_op jit(solution)/shard_map/pallas_call | solution.py:672
  1486.0 19.0 %convolution_convert_fusion.3.clone.5 = bf16[2048,768]{1,0:T(8,128)(2,1)S(1)} fusion(bf16[4096,2048]{1,0:T(8,128)(2,1)} %get-tuple-element.55, bf16[4096,768]{1,0:T(8,128)(2,1)} %constant_dynamic-update-slice_fusion.refs_0_), kind=kOutput, calls=%fused_computation.73.clone.clone.clone.2 | convolution fusion | flops 12886474752 | bytes 26214400 | tf_op jit(solution)/shard_map/dot_general | solution.py:1192
  1524.0 17.8 %collective-permute-start.28 = (bf16[512,2048]{1,0:T(8,128)(2,1)}, bf16[512,2048]{1,0:T(8,128)(2,1)}, u32[]{:S(2)}, u32[]{:S(2)}) collective-permute-start(bf16[512,2048]{1,0:T(8,128)(2,1)} %fusion.20), channel_id=1, source_target_pairs={{0,0},{1,1},{2,2},{3,3},{4,8},{5,9},{6,10},{7,11},{8,4},{9,5},{10,... | collective-permute-start | bytes 6291464 | tf_op jit(solution)/shard_map/ppermute | solution.py:354
  1545.4 31.1 %collective-permute-done.44 = f32[2,2048]{1,0:T(2,128)S(1)} collective-permute-done((f32[2,2048]{1,0:T(2,128)S(1)}, f32[2,2048]{1,0:T(2,128)S(1)}, u32[]{:S(2)}, u32[]{:S(2)}) %collective-permute-start.44) | collective-permute-done | bytes 16416 | tf_op jit(solution)/shard_map/ppermute | solution.py:354
  1595.9 20.5 %collective-permute-done.30 = bf16[512,768]{1,0:T(8,128)(2,1)} collective-permute-done((bf16[512,768]{1,0:T(8,128)(2,1)S(1)}, bf16[512,768]{1,0:T(8,128)(2,1)}, u32[]{:S(2)}, u32[]{:S(2)}) %collective-permute-start.30) | collective-permute-done | bytes 786464 | tf_op jit(solution)/shard_map/ppermute | solution.py:354
  (366 shorter events, 357.7 us)
Async XLA Ops:
  7.2 496.2 %all-gather.3.cloned.1.call-start = ((), (), s32[]{:S(2)}) async-start(), calls=%async_computation.3 | async-start | bytes 9437184 | tf_op jit(solution)/shard_map/all_gather | solution.py:1123
  14.0 57.7 %collective-permute-start.7 = (s32[4096]{0:T(1024)}, s32[4096]{0:T(1024)S(1)}, u32[]{:S(2)}, u32[]{:S(2)}) collective-permute-start(s32[4096]{0:T(1024)} %param.22), channel_id=1, source_target_pairs={{0,0},{1,1},{2,2},{3,3},{4,8},{5,9},{6,10},{7,11},{8,4},{9,5},{10,... | collective-permute-start | bytes 49160 | tf_op jit(solution)/shard_map/ppermute | solution.py:354
  20.6 53.5 %collective-permute-start.3 = (bf16[512,768]{1,0:T(8,128)(2,1)}, bf16[512,768]{1,0:T(8,128)(2,1)}, u32[]{:S(2)}, u32[]{:S(2)}) collective-permute-start(bf16[512,768]{1,0:T(8,128)(2,1)} %broadcast_add_fusion.4), channel_id=1, source_target_pairs={{0,4},{1,5},{2,6},{3,7},{12,8},{13,9},{14,10},{15,11},{16,20},{17,... | collective-permute-start | bytes 2359304 | tf_op jit(solution)/shard_map/ppermute | solution.py:354
  244.0 364.2 %all-gather.5.cloned.1.call-start = ((), (), s32[]{:S(2)}) async-start(), calls=%async_computation.4 | async-start | bytes 18874368 | tf_op jit(solution)/shard_map/all_gather | solution.py:1111
  278.6 99.9 %collective-permute-start.11 = (bf16[512,2048]{1,0:T(8,128)(2,1)}, bf16[512,2048]{1,0:T(8,128)(2,1)S(1)}, u32[]{:S(2)}, u32[]{:S(2)}) collective-permute-start(bf16[512,2048]{1,0:T(8,128)(2,1)} %broadcast_add_fusion.2), channel_id=1, source_target_pairs={{0,4},{1,5},{2,6},{3,7},{12,8},{13,9},{14,10},{15,11},{16,20},{17,... | collective-permute-start | bytes 6291464 | tf_op jit(solution)/shard_map/ppermute | solution.py:354
  312.6 65.9 %collective-permute-start.12 = (bf16[512,2048]{1,0:T(8,128)(2,1)}, bf16[512,2048]{1,0:T(8,128)(2,1)S(1)}, u32[]{:S(2)}, u32[]{:S(2)}) collective-permute-start(bf16[512,2048]{1,0:T(8,128)(2,1)} %broadcast_add_fusion.2), channel_id=1, source_target_pairs={{4,12},{5,13},{6,14},{7,15},{8,0},{9,1},{10,2},{11,3},{20,28},{21,... | collective-permute-start | bytes 6291464 | tf_op jit(solution)/shard_map/ppermute | solution.py:354
  313.9 66.0 %collective-permute-start.13 = (bf16[512,2048]{1,0:T(8,128)(2,1)}, bf16[512,2048]{1,0:T(8,128)(2,1)S(1)}, u32[]{:S(2)}, u32[]{:S(2)}) collective-permute-start(bf16[512,2048]{1,0:T(8,128)(2,1)} %broadcast_add_fusion.2), channel_id=1, source_target_pairs={{4,8},{5,9},{6,10},{7,11},{8,4},{9,5},{10,6},{11,7},{20,24},{21,25... | collective-permute-start | bytes 6291464 | tf_op jit(solution)/shard_map/ppermute | solution.py:354
  385.2 92.1 %collective-permute-start.15 = (bf16[2,512,2048]{2,1,0:T(8,128)(2,1)}, bf16[2,512,2048]{2,1,0:T(8,128)(2,1)}, u32[]{:S(2)}, u32[]{:S(2)}) collective-permute-start(bf16[2,512,2048]{2,1,0:T(8,128)(2,1)} %pad_maximum_fusion.2), channel_id=1, source_target_pairs={{0,16},{1,17},{2,18},{3,19},{4,20},{5,21},{6,22},{7,23},{8,24},{9,... | collective-permute-start | bytes 12582920 | tf_op jit(solution)/shard_map/ppermute | solution.py:354
  446.7 56.7 %all-to-all-start = ((bf16[8,512,256]{1,2,0:T(8,128)(2,1)}), bf16[8,512,256]{1,2,0:T(8,128)(2,1)}, u32[]{:S(2)}, u32[]{:S(2)}) async-start(bf16[8,512,256]{1,2,0:T(8,128)(2,1)} %copy.51), calls=%async_computation | async-start | bytes 4194304 | tf_op jit(solution)/shard_map/all_to_all | solution.py:1131
  631.6 46.6 %collective-permute-start.37 = (bf16[2,1024,512]{2,1,0:T(8,128)(2,1)S(1)}, bf16[2,1024,512]{2,1,0:T(8,128)(2,1)S(1)}, u32[]{:S(2)}, u32[]{:S(2)}) collective-permute-start(bf16[2,1024,512]{2,1,0:T(8,128)(2,1)S(1)} %slice.249), channel_id=1, source_target_pairs={{0,16},{1,17},{2,18},{3,19},{4,20},{5,21},{6,22},{7,23},{8,24},{9,... | collective-permute-start | bytes 6291464 | tf_op jit(solution)/shard_map/ppermute | solution.py:354
  679.0 40.2 %collective-permute-start.38 = (bf16[1024,512]{1,0:T(8,128)(2,1)S(1)}, bf16[1024,512]{1,0:T(8,128)(2,1)S(1)}, u32[]{:S(2)}, u32[]{:S(2)}) collective-permute-start(bf16[1024,512]{1,0:T(8,128)(2,1)S(1)} %get-tuple-element.96), channel_id=1, source_target_pairs={{4,0},{5,1},{6,2},{7,3},{8,12},{9,13},{10,14},{11,15},{20,16},{21,... | collective-permute-start | bytes 3145736 | tf_op jit(solution)/shard_map/ppermute | solution.py:354
  680.5 38.7 %collective-permute-start.39 = (bf16[1024,512]{1,0:T(8,128)(2,1)S(1)}, bf16[1024,512]{1,0:T(8,128)(2,1)S(1)}, u32[]{:S(2)}, u32[]{:S(2)}) collective-permute-start(bf16[1024,512]{1,0:T(8,128)(2,1)S(1)} %get-tuple-element.97), channel_id=1, source_target_pairs={{0,8},{1,9},{2,10},{3,11},{12,4},{13,5},{14,6},{15,7},{16,24},{17,... | collective-permute-start | bytes 3145736 | tf_op jit(solution)/shard_map/ppermute | solution.py:354
  681.9 37.3 %collective-permute-start.40 = (bf16[1024,512]{1,0:T(8,128)(2,1)S(1)}, bf16[1024,512]{1,0:T(8,128)(2,1)S(1)}, u32[]{:S(2)}, u32[]{:S(2)}) collective-permute-start(bf16[1024,512]{1,0:T(8,128)(2,1)S(1)} %get-tuple-element.97), channel_id=1, source_target_pairs={{4,8},{5,9},{6,10},{7,11},{8,4},{9,5},{10,6},{11,7},{20,24},{21,25... | collective-permute-start | bytes 3145736 | tf_op jit(solution)/shard_map/ppermute | solution.py:354
  1110.5 93.7 %collective-permute-start.24 = (bf16[2,512,2048]{2,1,0:T(8,128)(2,1)}, bf16[2,512,2048]{2,1,0:T(8,128)(2,1)}, u32[]{:S(2)}, u32[]{:S(2)}) collective-permute-start(bf16[2,512,2048]{2,1,0:T(8,128)(2,1)} %bitcast.30), channel_id=1, source_target_pairs={{0,16},{1,17},{2,18},{3,19},{4,20},{5,21},{6,22},{7,23},{8,24},{9,... | collective-permute-start | bytes 12582920 | tf_op jit(solution)/shard_map/ppermute | solution.py:354
  1123.6 96.8 %all-to-all-start.1 = ((bf16[8,512,256]{2,1,0:T(8,128)(2,1)}), bf16[8,512,256]{2,1,0:T(8,128)(2,1)}, u32[]{:S(2)}, u32[]{:S(2)}) async-start(bf16[8,512,256]{2,1,0:T(8,128)(2,1)} %bitcast.118), calls=%async_computation.1 | async-start | bytes 4194304 | tf_op jit(solution)/shard_map/all_to_all | solution.py:1174
  1128.1 458.8 %reduce-scatter.2.cloned.1.call-start = ((), (), s32[]{:S(2)}) async-start(), calls=%async_computation.5 | async-start | bytes 9437184 | tf_op jit(solution)/shard_map/reduce_scatter | solution.py:1196
  1212.0 86.0 %collective-permute-start.26 = (bf16[512,2048]{1,0:T(8,128)(2,1)}, bf16[512,2048]{1,0:T(8,128)(2,1)}, u32[]{:S(2)}, u32[]{:S(2)}) collective-permute-start(bf16[512,2048]{1,0:T(8,128)(2,1)} %get-tuple-element.85), channel_id=1, source_target_pairs={{0,8},{1,9},{2,10},{3,11},{12,4},{13,5},{14,6},{15,7},{16,24},{17,... | collective-permute-start | bytes 6291464 | tf_op jit(solution)/shard_map/ppermute | solution.py:354
  1215.3 85.3 %collective-permute-start.27 = (bf16[512,2048]{1,0:T(8,128)(2,1)}, bf16[512,2048]{1,0:T(8,128)(2,1)}, u32[]{:S(2)}, u32[]{:S(2)}) collective-permute-start(bf16[512,2048]{1,0:T(8,128)(2,1)} %get-tuple-element.85), channel_id=1, source_target_pairs={{4,8},{5,9},{6,10},{7,11},{8,4},{9,5},{10,6},{11,7},{20,24},{21,25... | collective-permute-start | bytes 6291464 | tf_op jit(solution)/shard_map/ppermute | solution.py:354
  1219.1 77.8 %collective-permute-start.25 = (bf16[512,2048]{1,0:T(8,128)(2,1)}, bf16[512,2048]{1,0:T(8,128)(2,1)}, u32[]{:S(2)}, u32[]{:S(2)}) collective-permute-start(bf16[512,2048]{1,0:T(8,128)(2,1)} %get-tuple-element.86), channel_id=1, source_target_pairs={{4,0},{5,1},{6,2},{7,3},{8,12},{9,13},{10,14},{11,15},{20,16},{21,... | collective-permute-start | bytes 6291464 | tf_op jit(solution)/shard_map/ppermute | solution.py:354
  1508.8 67.9 %collective-permute-start.29 = (bf16[2,512,768]{2,1,0:T(8,128)(2,1)S(1)}, bf16[2,512,768]{2,1,0:T(8,128)(2,1)S(1)}, u32[]{:S(2)}, u32[]{:S(2)}) collective-permute-start(bf16[2,512,768]{2,1,0:T(8,128)(2,1)S(1)} %bitcast.130), channel_id=1, source_target_pairs={{0,16},{1,17},{2,18},{3,19},{4,20},{5,21},{6,22},{7,23},{8,24},{9,... | collective-permute-start | bytes 4718600 | tf_op jit(solution)/shard_map/ppermute | solution.py:354
  1524.0 67.7 %collective-permute-start.28 = (bf16[512,2048]{1,0:T(8,128)(2,1)}, bf16[512,2048]{1,0:T(8,128)(2,1)}, u32[]{:S(2)}, u32[]{:S(2)}) collective-permute-start(bf16[512,2048]{1,0:T(8,128)(2,1)} %fusion.20), channel_id=1, source_target_pairs={{0,0},{1,1},{2,2},{3,3},{4,8},{5,9},{6,10},{7,11},{8,4},{9,5},{10,... | collective-permute-start | bytes 6291464 | tf_op jit(solution)/shard_map/ppermute | solution.py:354
  1541.8 34.7 %collective-permute-start.44 = (f32[2,2048]{1,0:T(2,128)S(1)}, f32[2,2048]{1,0:T(2,128)S(1)}, u32[]{:S(2)}, u32[]{:S(2)}) collective-permute-start(f32[2,2048]{1,0:T(2,128)S(1)} %add.361), channel_id=1, source_target_pairs={{0,4},{1,5},{2,6},{3,7},{4,0},{5,1},{6,2},{7,3},{8,12},{9,13},{10,... | collective-permute-start | bytes 49160 | tf_op jit(solution)/shard_map/ppermute | solution.py:354
  1578.1 38.4 %collective-permute-start.31 = (bf16[512,768]{1,0:T(8,128)(2,1)}, bf16[512,768]{1,0:T(8,128)(2,1)}, u32[]{:S(2)}, u32[]{:S(2)}) collective-permute-start(bf16[512,768]{1,0:T(8,128)(2,1)} %get-tuple-element.109), channel_id=1, source_target_pairs={{0,8},{1,9},{2,10},{3,11},{12,4},{13,5},{14,6},{15,7},{16,24},{17,... | collective-permute-start | bytes 2359304 | tf_op jit(solution)/shard_map/ppermute | solution.py:354
  1580.4 36.1 %collective-permute-start.32 = (bf16[512,768]{1,0:T(8,128)(2,1)}, bf16[512,768]{1,0:T(8,128)(2,1)}, u32[]{:S(2)}, u32[]{:S(2)}) collective-permute-start(bf16[512,768]{1,0:T(8,128)(2,1)} %get-tuple-element.109), channel_id=1, source_target_pairs={{4,8},{5,9},{6,10},{7,11},{8,4},{9,5},{10,6},{11,7},{20,24},{21,25... | collective-permute-start | bytes 2359304 | tf_op jit(solution)/shard_map/ppermute | solution.py:354
  (105 other events, 1900.0 us)
Sparse Core Ops, SparseCore 0:
  244.1 89.4 all-gather.2
  335.7 119.7 all-gather.4
  1144.2 180.3 reduce-scatter.1

commit v3 on v2

--- a/solution.py
+++ b/solution.py
@@ -395,89 +395,306 @@
     return pl.ds(pl.multiple_of(block * ROW + part * half, half), half)
 
 
-def gather_kernel(finish, width, tables, own_ref, w_ref, *refs):
-    cs_ref, sn_ref = refs[:2] if tables else (None, None)
-    full_ref, *outs = refs[2 if tables else 0 :][:4]
-    buf, res, send, recv, own_sem, full_sem, out_sem = refs[-7:]
-    me, partners = ring_position()
-    to_x, to_l, to_c = partners
+def remote(source, target, sent, received, device):
+    return pltpu.make_async_remote_copy(
+        src_ref=source,
+        dst_ref=target,
+        send_sem=sent,
+        recv_sem=received,
+        device_id=device,
+        device_id_type=MESH,
+    )
+
+
+def places():
+    y, c, h, l, x = (lax.axis_index(name) for name in AXES)
+    return y, c, h, 4 * c + 2 * l + x
+
+
+def wide_partners():
+    y, c, h, _ = places()
+    _, (to_x, to_l, to_c) = ring_position()
+    mixed = ({**to_x, **to_l}, {**to_x, **to_c}, {**to_l, **to_c}, {**to_x, **to_l, **to_c})
+    across = ({"c": 0, "h": 1 - h}, {"c": 1, "h": 1 - h})
+    return (to_x, to_l, to_c) + mixed + ({"y": 1 - y},) + across
+
+
+class Ring:
+    def __init__(self, buffer, size, send, recv):
+        self.buffer, self.size, self.send, self.recv = buffer, size, send, recv
+        me, (to_x, to_l, to_c) = ring_position()
+        self.plan = (
+            (me, 0, to_x, me ^ 1),
+            (me, 1, to_l, me ^ 2),
+            (me, None, to_c, me ^ 4),
+            (me, 1, to_x, me ^ 1),
+            (me, 0, to_l, me ^ 2),
+            (me ^ 1, 0, to_l, me ^ 3),
+            (me ^ 2, 1, to_x, me ^ 3),
+            (me ^ 1, None, to_c, me ^ 5),
+            (me ^ 2, None, to_c, me ^ 6),
+            (me ^ 3, None, to_c, me ^ 7),
+        )
+
+    def copy(self, index, block):
+        _, part, partner, _ = self.plan[index]
+        size = self.size if part is None else self.size // 2
+        first = block * self.size + (size if part == 1 else 0)
+        place = self.buffer.at[pl.ds(pl.multiple_of(first, size), size)]
+        return remote(place, place, self.send.at[index], self.recv.at[index], partner)
+
+    def start(self, *indices):
+        for index in indices:
+            self.copy(index, self.plan[index][0]).start()
+
+    def arrived(self, *indices):
+        for index in indices:
+            self.copy(index, self.plan[index][3]).wait_recv()
+
+    def sent(self):
+        for index in range(10):
+            self.copy(index, self.plan[index][0]).wait_send()
+
+
+class Spread:
+    def __init__(self, source, target, near, far, keep):
+        self.source, self.target, self.near, self.far, self.keep = source, target, near, far, keep
+        _, self.c, self.h, _ = places()
+
+    def local(self):
+        return pltpu.make_async_copy(self.source, self.target, self.keep)
+
+    def beside(self):
+        return remote(self.source, self.target, self.near.at[0], self.near.at[1], {"c": self.h})
+
+    def across(self, core):
+        return remote(
+            self.source, self.target, self.far.at[2], self.far.at[core], {"c": self.h, "h": 1 - self.h}
+        )
+
+    def start(self):
+        self.across(self.c).start()
+
+        @pl.when(self.c == self.h)
+        def _():
+            self.local().start()
+
+        @pl.when(self.c != self.h)
+        def _():
+            self.beside().start()
+
+    def arrived(self):
+        @pl.when(self.c == self.h)
+        def _():
+            self.local().wait()
+            self.beside().wait_recv()
+
+        @pl.when(self.c != self.h)
+        def _():
+            self.across(0).wait_recv()
+            self.across(1).wait_recv()
+
+    def sent(self):
+        self.across(self.c).wait_send()
+
+        @pl.when(self.c != self.h)
+        def _():
+            self.beside().wait_send()
+
+
+SPREAD_SEMAPHORES = [
+    pltpu.SemaphoreType.DMA((4, 2)),
+    pltpu.SemaphoreType.DMA((4, 3)),
+    pltpu.SemaphoreType.DMA((4,)),
+    pltpu.SemaphoreType.DMA((4, 2)),
+    pltpu.SemaphoreType.DMA((4, 2)),
+]
+
+
+class First:
+    def __init__(self, refs):
+        (self.shard, self.grad), (self.whole, self.moved) = refs[:2], refs[2:4]
+        self.w, near, far, keep, self.y_send, self.y_recv, self.grad_sems = refs[4:]
+        self.y, self.c, self.h, _ = places()
+        first = (2 * self.y + self.c) * 512
+        self.pieces = [
+            Spread(
+                self.shard.at[pl.ds(k * 256, 256)],
+                self.w.at[pl.ds(pl.multiple_of(first + k * 256, 256), 256)],
+                near.at[k],
+                far.at[k],
+                keep.at[k],
+            )
+            for k in range(2)
+        ]
+
+    def over_y(self, k, core, y):
+        first = (2 * y + core) * 512 + k * 256
+        place = self.w.at[pl.ds(pl.multiple_of(first, 256), 256)]
+        return remote(place, place, self.y_send.at[k, core], self.y_recv.at[k, core], {"y": 1 - self.y})
+
+    def grad_local(self):
+        return pltpu.make_async_copy(self.grad, self.moved, self.grad_sems.at[2])
+
+    def grad_remote(self):
+        return remote(
+            self.grad, self.moved, self.grad_sems.at[0], self.grad_sems.at[1], {"c": self.h, "h": self.c}
+        )
+
+    def run(self, ring):
+        for piece in self.pieces:
+            piece.start()
+        for k in range(2):
+            self.pieces[k].arrived()
+            for core in range(2):
+                self.over_y(k, core, self.y).start()
+            if k == 0:
+                ring.arrived(0)
+                ring.start(5)
+                ring.arrived(1)
+                ring.start(6)
+
+        @pl.when(self.c == self.h)
+        def _():
+            self.grad_local().start()
+
+        @pl.when(self.c != self.h)
+        def _():
+            self.grad_remote().start()
+
+        ring.arrived(2, 3)
+        ring.start(7)
+        ring.arrived(4)
+        ring.start(8)
+        for k in range(2):
+            for core in range(2):
+                self.over_y(k, core, 1 - self.y).wait_recv()
+        pltpu.make_async_copy(self.w, self.whole, self.grad_sems.at[3]).start()
+
+    def poll(self, step):
+        pass
+
+    def finish(self):
+        for piece in self.pieces:
+            piece.sent()
+        for k in range(2):
+            for core in range(2):
+                self.over_y(k, core, self.y).wait_send()
+        pltpu.make_async_copy(self.w, self.whole, self.grad_sems.at[3]).wait()
+
+        @pl.when(self.c == self.h)
+        def _():
+            self.grad_local().wait()
+
+        @pl.when(self.c != self.h)
+        def _():
+            self.grad_remote().wait_recv()
+            self.grad_remote().wait_send()
+
+
+class Second:
+    def __init__(self, refs):
+        self.shard, self.whole = refs[:2]
+        near, far, keep, self.y_send, self.y_recv = refs[2:]
+        self.y, c, _, _ = places()
+        columns = pl.ds(pl.multiple_of((2 * self.y + c) * 512, 512), 512)
+        self.pieces = [
+            Spread(
+                self.shard.at[pl.ds(k * 512, 512)],
+                self.whole.at[pl.ds(k * 512, 512), columns],
+                near.at[k],
+                far.at[k],
+                keep.at[k],
+            )
+            for k in range(2)
+        ]
+
+    def over_y(self, k, y):
+        place = self.whole.at[pl.ds(k * 512, 512), pl.ds(pl.multiple_of(y * 1024, 1024), 1024)]
+        return remote(place, place, self.y_send.at[k, 0], self.y_recv.at[k, 0], {"y": 1 - self.y})
+
+    def run(self, ring):
+        for piece in self.pieces:
+            piece.start()
+
+    def poll(self, step):
+        @pl.when(step == 1)
+        def _():
+            self.pieces[0].arrived()
+            self.over_y(0, self.y).start()
+
+        @pl.when(step == 4)
+        def _():
+            self.pieces[1].arrived()
+            self.over_y(1, self.y).start()
+
+    def finish(self):
+        for k in range(2):
+            self.pieces[k].sent()
+            self.over_y(k, 1 - self.y).wait_recv()
+            self.over_y(k, self.y).wait_send()
+
+
+def gather_kernel(finish, beside, inputs, outputs, *refs):
+    own_ref, refs = refs[0], refs[1:]
+    given, refs = refs[:inputs], refs[inputs:]
+    full_ref, outs, refs = refs[0], refs[1:4], refs[4:]
+    extra_outs, refs = refs[:outputs], refs[outputs:]
+    buf, res, send, recv, own_sem, full_sem, out_sem = refs[:7]
+    me, _ = ring_position()
     load = pltpu.make_async_copy(own_ref, buf.at[rows_at(me)], own_sem)
     load.start()
-    enter_ring(partners)
+    enter_ring(wide_partners())
     load.wait()
-
-    def copy(index, block, part, partner):
-        place = buf.at[rows_at(block, part)]
-        return pltpu.make_async_remote_copy(
-            src_ref=place,
-            dst_ref=place,
-            send_sem=send.at[index],
-            recv_sem=recv.at[index],
-            device_id=partner,
-            device_id_type=MESH,
-        )
-
-    plan = (
-        (me, 0, to_x, me ^ 1),
-        (me, 1, to_l, me ^ 2),
-        (me, None, to_c, me ^ 4),
-        (me, 1, to_x, me ^ 1),
-        (me, 0, to_l, me ^ 2),
-        (me ^ 1, 0, to_l, me ^ 3),
-        (me ^ 2, 1, to_x, me ^ 3),
-        (me ^ 1, None, to_c, me ^ 5),
-        (me ^ 2, None, to_c, me ^ 6),
-        (me ^ 3, None, to_c, me ^ 7),
-    )
-
-    def start(index):
-        block, part, partner, _ = plan[index]
-        copy(index, block, part, partner).start()
-
-    def arrived(index):
-        _, part, partner, block = plan[index]
-        copy(index, block, part, partner).wait_recv()
-
-    for index in range(5):
-        start(index)
+    ring = Ring(buf, ROW, send, recv)
+    ring.start(0, 1, 2, 3, 4)
+    early = beside is First
+    if early:
+        more = First(given[2:] + extra_outs + refs[7:])
+        w_ref, tables = more.w, given[:2]
+    else:
+        more = Second(given[1:] + extra_outs + refs[7:])
+        w_ref, tables = given[0], ()
+    more.run(ring)
 
     def step_body(step, carry):
         block = me ^ ((step >> 1) | ((step & 1) << 2))
         rows = rows_at(block)
-
-        @pl.when(step == 1)
-        def _():
-            arrived(2)
-
-        @pl.when(step == 2)
-        def _():
-            arrived(0)
-            start(5)
-            arrived(1)
-            start(6)
-            arrived(3)
-            start(7)
-            arrived(4)
-            start(8)
+        if not early:
+
+            @pl.when(step == 1)
+            def _():
+                ring.arrived(2)
+
+            @pl.when(step == 2)
+            def _():
+                ring.arrived(0)
+                ring.start(5)
+                ring.arrived(1)
+                ring.start(6)
+                ring.arrived(3)
+                ring.start(7)
+                ring.arrived(4)
+                ring.start(8)
 
         @pl.when(step == 3)
         def _():
-            arrived(7)
+            ring.arrived(7)
 
         @pl.when(step == 5)
         def _():
-            arrived(8)
+            ring.arrived(8)
 
         @pl.when(step == 6)
         def _():
-            arrived(5)
-            arrived(6)
-            start(9)
+            ring.arrived(5, 6)
+            ring.start(9)
 
         @pl.when(step == 7)
         def _():
-            arrived(9)
-
+            ring.arrived(9)
+
+        more.poll(step)
         pltpu.make_async_copy(buf.at[rows], full_ref.at[rows], full_sem.at[step]).start()
         turn = step & 1
 
@@ -491,15 +708,14 @@
             for which in range(3):
                 out_copy(which, rows).wait()
 
-        finish(buf, rows, w_ref, cs_ref, sn_ref, res, turn)
+        finish(buf, rows, w_ref, tables, res, turn)
         for which in range(3):
             out_copy(which, rows).start()
         return carry
 
     lax.fori_loop(0, 8, step_body, 0)
-    for index in range(10):
-        block, part, partner, _ = plan[index]
-        copy(index, block, part, partner).wait_send()
+    ring.sent()
+    more.finish()
 
     def drain(step, carry):
         rows = rows_at(step)
@@ -514,7 +730,7 @@
             ).wait()
 
 
-def feed_forward_finish(buf, rows, w_ref, cs_ref, sn_ref, res, turn):
+def feed_forward_finish(buf, rows, w_ref, tables, res, turn):
     def columns(chunk, carry):
         here = pl.multiple_of(chunk * 256, 256)
         block = buf[rows, :]
@@ -528,9 +744,9 @@
     lax.fori_loop(0, 4, columns, 0)
 
 
-def attention_finish(buf, rows, w_ref, cs_ref, sn_ref, res, turn):
+def attention_finish(buf, rows, w_ref, tables, res, turn):
     block = buf[rows, :]
-    cs, sn = cs_ref[rows, :], sn_ref[rows, :]
+    cs, sn = tables[0][rows, :], tables[1][rows, :]
     for which in range(2):
         m = jnp.dot(block, w_ref[:, which * 256 : which * 256 + 256], preferred_element_type=F32)
         if which == 0:
@@ -541,16 +757,18 @@
     res[turn, 2] = rounded(jnp.dot(block, w_ref[:, 512:768], preferred_element_type=F32))
 
 
-def gather_product(own, weight, width, finish, number, tables=()):
+def gather_product(own, given, anywhere_given, extra_shapes, width, finish, beside, scratch, number):
     anywhere = pl.BlockSpec(memory_space=pl.ANY)
     vmem = pl.BlockSpec(memory_space=pltpu.VMEM)
     length, depth = 8 * ROW, own.shape[1]
+    inputs = len(given) + len(anywhere_given)
     return pl.pallas_call(
-        lambda *refs: gather_kernel(finish, width, bool(tables), *refs),
-        in_specs=[anywhere, vmem] + [vmem] * len(tables),
-        out_specs=[anywhere] * 4,
+        lambda *refs: gather_kernel(finish, beside, inputs, len(extra_shapes), *refs),
+        in_specs=[anywhere] + [vmem] * len(given) + [anywhere] * len(anywhere_given),
+        out_specs=[anywhere] * (4 + len(extra_shapes)),
         out_shape=[jax.ShapeDtypeStruct((length, depth), BF)]
-        + [jax.ShapeDtypeStruct((length, width), BF)] * 3,
+        + [jax.ShapeDtypeStruct((length, width), BF)] * 3
+        + [jax.ShapeDtypeStruct(shape, BF) for shape in extra_shapes],
         scratch_shapes=[
             pltpu.VMEM((length, depth), BF),
             pltpu.VMEM((2, 3, ROW, width), BF),
@@ -559,14 +777,15 @@
             pltpu.SemaphoreType.DMA,
             pltpu.SemaphoreType.DMA((8,)),
             pltpu.SemaphoreType.DMA((2, 3)),
-        ],
+        ]
+        + scratch,
         compiler_params=pltpu.CompilerParams(
             collective_id=number, has_side_effects=True, vmem_limit_bytes=56 * 2**20
         ),
         cost_estimate=pl.CostEstimate(
             flops=80 * 10**9, bytes_accessed=30 * 2**20, transcendentals=0
         ),
-    )(own, weight, *tables)
+    )(own, *given, *anywhere_given)
 
 
 def scatter_kernel(dims, a_ref, w_ref, out_ref, abuf, mine, other, sums, ra, rb, near_x, near_l, send, recv, a_sem):
@@ -736,11 +955,180 @@
     return after(lax.optimization_barrier(values), zero)
 
 
-def attend_kernel(chosen, me_ref, q_ref, k_ref, v_ref, *refs):
-    o_ref, l_ref, s_scr, m_scr, acc_scr, o_scr = refs[-6:]
-    heads = 4
-    block = picked_block(pl.program_id(0), chosen)
-    q = q_ref[...]
+class Beside:
+    def __init__(self, refs):
+        self.out_shard, self.gate_up_shard, self.grad_own = refs[:3]
+        self.out_full, self.gate_up, self.grad_full, self.rows_own = refs[3:7]
+        (
+            near,
+            far,
+            keep,
+            self.y_send,
+            self.y_recv,
+            out_near,
+            out_far,
+            out_keep,
+            self.out_y,
+            grad_send,
+            grad_recv,
+            out_send,
+            out_recv,
+            self.row_send,
+            self.row_recv,
+            self.own_sem,
+        ) = refs[7:]
+        self.y, self.c, self.h, self.me = places()
+        _, _, _, l, x = (lax.axis_index(name) for name in AXES)
+        s = 2 * self.y + self.c
+        self.pieces = [
+            Spread(
+                self.gate_up_shard.at[pl.ds(k * 128, 128)],
+                self.gate_up.at[pl.ds(pl.multiple_of(s * 512 + k * 128, 128), 128)],
+                near.at[k],
+                far.at[k],
+                keep.at[k],
+            )
+            for k in range(4)
+        ]
+        heads = 4 * self.h + 2 * l + x
+        self.out_piece = Spread(
+            self.out_shard,
+            self.out_full.at[
+                pl.ds(pl.multiple_of(heads * 256, 256), 256), pl.ds(pl.multiple_of(s * 512, 512), 512)
+            ],
+            out_near,
+            out_far,
+            out_keep,
+        )
+        self.grad_ring = Ring(self.grad_full, ROW, grad_send, grad_recv)
+        self.out_ring = Ring(self.out_full, 256, out_send, out_recv)
+
+    def over_y(self, k, core, y):
+        first = (2 * y + core) * 512 + k * 128
+        place = self.gate_up.at[pl.ds(pl.multiple_of(first, 128), 128)]
+        return remote(place, place, self.y_send.at[k, core], self.y_recv.at[k, core], {"y": 1 - self.y})
+
+    def out_over_y(self, y):
+        place = self.out_full.at[
+            pl.ds(pl.multiple_of(self.me * 256, 256), 256), pl.ds(pl.multiple_of(y * 1024, 1024), 1024)
+        ]
+        return remote(place, place, self.out_y.at[0], self.out_y.at[1], {"y": 1 - self.y})
+
+    def piece_over_y(self, k):
+        self.pieces[k].arrived()
+        for core in range(2):
+            self.over_y(k, core, self.y).start()
+
+    def begin(self):
+        own = pltpu.make_async_copy(self.grad_own, self.grad_full.at[rows_at(self.me)], self.own_sem.at[0])
+        own.start()
+        enter_ring(wide_partners())
+        self.out_piece.start()
+        self.pieces[0].start()
+        own.wait()
+        self.grad_ring.start(0, 1, 2, 3, 4)
+
+    def at(self, step):
+        def when(number, *actions):
+            @pl.when(step == number)
+            def _():
+                for action in actions:
+                    action()
+
+        def out_on():
+            self.out_piece.arrived()
+            self.out_over_y(self.y).start()
+
+        def out_ring_on():
+            self.out_over_y(1 - self.y).wait_recv()
+            self.out_ring.start(0, 1, 2, 3, 4)
+
+        def relay(ring):
+            ring.arrived(0)
+            ring.start(5)
+            ring.arrived(1)
+            ring.start(6)
+
+        def relay_core(ring):
+            ring.arrived(3)
+            ring.start(7)
+            ring.arrived(4)
+            ring.start(8)
+
+        def relay_last(ring):
+            ring.arrived(5, 6)
+            ring.start(9)
+
+        when(0, self.begin)
+        when(3, out_on, self.pieces[1].start)
+        when(6, out_ring_on, lambda: relay(self.grad_ring))
+        when(9, lambda: self.piece_over_y(0), self.pieces[2].start)
+        when(12, lambda: relay_core(self.grad_ring), lambda: relay(self.out_ring))
+        when(14, lambda: self.piece_over_y(1), self.pieces[3].start)
+        when(18, lambda: relay_core(self.out_ring), lambda: relay_last(self.grad_ring))
+        when(20, lambda: self.piece_over_y(2))
+        when(25, lambda: relay_last(self.out_ring))
+        when(29, lambda: self.piece_over_y(3))
+
+    def row_local(self, block, o_all):
+        columns = pl.ds(pl.multiple_of(self.me * 256, 256), 256)
+        return pltpu.make_async_copy(
+            o_all.at[rows_at(block)], self.rows_own.at[:, columns], self.own_sem.at[1]
+        )
+
+    def row_remote(self, block, o_all, sender):
+        columns = pl.ds(pl.multiple_of(sender * 256, 256), 256)
+        return remote(
+            o_all.at[rows_at(block)],
+            self.rows_own.at[:, columns],
+            self.row_send.at[block],
+            self.row_recv.at[sender],
+            {"c": block >> 2, "l": (block >> 1) & 1, "x": block & 1},
+        )
+
+    def send_rows(self, block, o_all):
+        @pl.when(block == self.me)
+        def _():
+            self.row_local(block, o_all).start()
+
+        @pl.when(block != self.me)
+        def _():
+            self.row_remote(block, o_all, self.me).start()
+
+    def end(self, o_all):
+        self.out_piece.sent()
+        self.out_over_y(self.y).wait_send()
+        for k in range(4):
+            self.pieces[k].sent()
+            for core in range(2):
+                self.over_y(k, core, self.y).wait_send()
+                self.over_y(k, core, 1 - self.y).wait_recv()
+        for ring in (self.grad_ring, self.out_ring):
+            ring.arrived(2, 7, 8, 9)
+            ring.sent()
+
+        def each(block, carry):
+            @pl.when(block == self.me)
+            def _():
+                self.row_local(block, o_all).wait()
+
+            @pl.when(block != self.me)
+            def _():
+                self.row_remote(block, o_all, self.me).wait_send()
+                self.row_remote(block, o_all, block).wait_recv()
+
+            return carry
+
+        lax.fori_loop(0, 8, each, 0)
+
+
+def attend_kernel(q_ref, k_ref, v_ref, out_shard, gate_up_shard, grad_own, o_ref, l_ref, *refs):
+    beside = Beside((out_shard, gate_up_shard, grad_own) + refs[:4] + refs[8:])
+    s_scr, m_scr, acc_scr, o_all = refs[4:8]
+    head = pl.program_id(1)
+    step = pl.program_id(0) * 4 + head
+    block = 7 - pl.program_id(0)
+    beside.at(step)
     row = lax.broadcasted_iota(jnp.int32, (ROW, ROW), 0)
     col = lax.broadcasted_iota(jnp.int32, (ROW, ROW), 1)
 
@@ -752,89 +1140,105 @@
     def lane_sum(s):
         return (s[:, :128] + s[:, 128:256]) + (s[:, 256:384] + s[:, 384:])
 
-    def start_of(key_block):
-        return pl.multiple_of(key_block * ROW, ROW)
-
-    for head in range(heads):
-        qh = jnp.where(head_lanes_turned(head), q, jnp.zeros_like(q))
-
-        def scores(key_block):
-            return lax.dot_general(
-                qh, k_ref[pl.ds(start_of(key_block), ROW), :], NT, preferred_element_type=F32
-            )
-
-        s = jnp.where(col <= row, scores(block), masked_score)
-        s_scr[block] = s
-        m_scr[...] = lane_max(s)
-
-        def first_pass(key_block, carry):
-            s = scores(key_block)
-            s_scr[key_block] = s
-            m_scr[...] = jnp.maximum(m_scr[...], lane_max(s))
-            return carry
-
-        lax.fori_loop(0, block, first_pass, 0)
-        top = jnp.max(m_scr[...], axis=1, keepdims=True)
-        m_scr[...] = jnp.zeros_like(m_scr)
-        acc_scr[...] = jnp.zeros_like(acc_scr)
-
-        def second_pass(key_block, carry):
-            e = jnp.exp2(s_scr[key_block] - top)
-            m_scr[...] += lane_sum(e)
-            acc_scr[...] += lax.dot_general(
-                e.astype(BF), v_ref[pl.ds(start_of(key_block), ROW), :], NN, preferred_element_type=F32
-            )
-            return carry
-
-        lax.fori_loop(0, block + 1, second_pass, 0)
-        total = jnp.sum(m_scr[...], axis=1, keepdims=True)
-        part = acc_scr[...] * (1.0 / total)
-        if head == 0:
-            o_scr[...] = part
-        else:
-            o_scr[...] = jnp.where(head_lanes_plain(head), part, o_scr[...])
-        level = jnp.broadcast_to(top + jnp.log2(total), (ROW, 128))
-        l_ref[0, head : head + 1, :] = jnp.transpose(level)[0:1, :]
-    o_ref[...] = o_scr[...].astype(BF)
-
-
-def attend(me, q, k, v, chosen, earlier):
+    def keys_at(key_block):
+        return pl.ds(pl.multiple_of(key_block * ROW, ROW), ROW)
+
+    q = q_ref[...]
+    qh = jnp.where(head_lanes_turned(head), q, jnp.zeros_like(q))
+
+    def scores(key_block):
+        return lax.dot_general(qh, k_ref[keys_at(key_block), :], NT, preferred_element_type=F32)
+
+    s = jnp.where(col <= row, scores(block), masked_score)
+    s_scr[block] = s
+    m_scr[...] = lane_max(s)
+
+    def first_pass(key_block, carry):
+        s = scores(key_block)
+        s_scr[key_block] = s
+        m_scr[...] = jnp.maximum(m_scr[...], lane_max(s))
+        return carry
+
+    lax.fori_loop(0, block, first_pass, 0)
+    top = jnp.max(m_scr[...], axis=1, keepdims=True)
+    m_scr[...] = jnp.zeros_like(m_scr)
+    acc_scr[...] = jnp.zeros_like(acc_scr)
+
+    def second_pass(key_block, carry):
+        e = jnp.exp2(s_scr[key_block] - top)
+        m_scr[...] += lane_sum(e)
+        acc_scr[...] += lax.dot_general(
+            e.astype(BF), v_ref[keys_at(key_block), :], NN, preferred_element_type=F32
+        )
+        return carry
+
+    lax.fori_loop(0, block + 1, second_pass, 0)
+    total = jnp.sum(m_scr[...], axis=1, keepdims=True)
+    part = rounded(acc_scr[...] * (1.0 / total))
+    rows = rows_at(block)
+
+    @pl.when(head == 0)
+    def _():
+        o_all[rows, :] = part
+
+    @pl.when(head > 0)
+    def _():
+        o_all[rows, :] = jnp.where(head_lanes_plain(head), part, o_all[rows, :])
+
+    level = jnp.transpose(jnp.broadcast_to(top + jnp.log2(total), (ROW, 128)))[0:4, :]
+    row4 = lax.broadcasted_iota(jnp.int32, (4, ROW), 0)
+    l_ref[0] = jnp.where(row4 == head, level, l_ref[0])
+
+    @pl.when(head == 3)
+    def _():
+        o_ref[...] = o_all[rows, :]
+        beside.send_rows(block, o_all)
+
+    @pl.when(step == 31)
+    def _():
+        beside.end(o_all)
+
+
+def attend(q, k, v, out_shard, gate_up_shard, grad_own):
     length = q.shape[0]
     blocks = length // ROW
-
-    def place(step, me):
-        return picked_block(step, chosen)
-
-    whole = pl.BlockSpec((length, 256), lambda step, me: (0, 0))
-    grid = pltpu.PrefetchScalarGridSpec(
-        num_scalar_prefetch=1,
-        grid=(len(chosen),),
-        in_specs=[pl.BlockSpec((ROW, 256), lambda step, me: (place(step, me), 0)), whole, whole]
-        + [pl.BlockSpec(memory_space=pl.ANY)] * len(earlier),
+    whole = pl.BlockSpec((length, 256), lambda i, head: (0, 0))
+    anywhere = pl.BlockSpec(memory_space=pl.ANY)
+    dma = pltpu.SemaphoreType.DMA
+    return pl.pallas_call(
+        attend_kernel,
+        grid=(blocks, 4),
+        in_specs=[pl.BlockSpec((ROW, 256), lambda i, head: (7 - i, 0)), whole, whole] + [anywhere] * 3,
         out_specs=[
-            pl.BlockSpec((ROW, 256), lambda step, me: (place(step, me), 0)),
-            pl.BlockSpec((1, 4, ROW), lambda step, me: (place(step, me), 0, 0)),
+            pl.BlockSpec((ROW, 256), lambda i, head: (7 - i, 0)),
+            pl.BlockSpec((1, 4, ROW), lambda i, head: (7 - i, 0, 0)),
+        ]
+        + [anywhere] * 4,
+        out_shape=[
+            jax.ShapeDtypeStruct((length, 256), BF),
+            jax.ShapeDtypeStruct((blocks, 4, ROW), F32),
+            jax.ShapeDtypeStruct((2048, 2048), BF),
+            jax.ShapeDtypeStruct((2048, 2048), BF),
+            jax.ShapeDtypeStruct((length, 2048), BF),
+            jax.ShapeDtypeStruct((ROW, 2048), BF),
         ],
         scratch_shapes=[
             pltpu.VMEM((blocks, ROW, ROW), F32),
             pltpu.VMEM((ROW, 128), F32),
             pltpu.VMEM((ROW, 256), F32),
-            pltpu.VMEM((ROW, 256), F32),
-        ],
-    )
-    return pl.pallas_call(
-        lambda *refs: attend_kernel(chosen, *refs),
-        grid_spec=grid,
-        out_shape=[
-            jax.ShapeDtypeStruct((length, 256), BF),
-            jax.ShapeDtypeStruct((blocks, 4, ROW), F32),
-        ],
-        input_output_aliases={4: 0, 5: 1} if earlier else {},
-        compiler_params=pltpu.CompilerParams(vmem_limit_bytes=48 * 2**20),
+            pltpu.VMEM((length, 256), BF),
+        ]
+        + SPREAD_SEMAPHORES
+        + [dma((2,)), dma((3,)), dma, dma((2,))]
+        + [dma((10,))] * 4
+        + [dma((8,)), dma((8,)), dma((2,))],
+        compiler_params=pltpu.CompilerParams(
+            collective_id=6, has_side_effects=True, vmem_limit_bytes=48 * 2**20
+        ),
         cost_estimate=pl.CostEstimate(
-            flops=14 * 10**9 * len(chosen), bytes_accessed=10 * 2**20, transcendentals=0
+            flops=14 * 10**9 * blocks, bytes_accessed=10 * 2**20, transcendentals=0
         ),
-    )(me, q, k, v, *earlier)
+    )(q, k, v, out_shard, gate_up_shard, grad_own)
 
 
 KEYS = 256
@@ -1042,24 +1446,19 @@
     plain_y, plain_c, straight = y == 0, c == 0, c == h
     idle = jnp.zeros((1,), jnp.int32)
 
-    def features(values):
-        half = values.shape[-1] // 2
+    def both_y(mine, other, axis):
         return jnp.where(
-            plain_y, values, jnp.concatenate([values[..., half:], values[..., :half]], axis=-1)
+            plain_y,
+            jnp.concatenate([mine, other], axis=axis),
+            jnp.concatenate([other, mine], axis=axis),
         )
 
     def both_cores(mine, other):
         return jnp.where(plain_c, mine, other), jnp.where(plain_c, other, mine)
 
-    def gather_near(shard):
-        r1 = move(shard, lambda y, c, h, l, x: (y, c, 1 - h, l, x) if c == h else None)
-        r2a = move(shard, lambda y, c, h, l, x: (y, 1 - c, h, l, x) if c != h else None)
-        r2b = move(shard, lambda y, c, h, l, x: (y, h, c, l, x) if c != h else None)
-        near = jnp.stack(both_cores(jnp.where(straight, shard, r1), jnp.where(straight, r2a, r2b)))
-        return near, mark(r1, r2a, r2b)
-
     def scatter_y(blocks, zero=None):
-        return blocks[:2], flip(held(blocks[2:], zero), "y")
+        mine = lax.dynamic_slice_in_dim(blocks, 2 * y, 2, 0)
+        return mine, flip(held(lax.dynamic_slice_in_dim(blocks, 2 * (1 - y), 2, 0), zero), "y")
 
     def scatter_ch(near, far):
         total = (near.astype(F32) + far.astype(F32)).astype(BF)
@@ -1077,68 +1476,51 @@
         )
 
     turn = column_order()
-    rows_moved = swap_ch(layer_input)
-    rows_in = features(rows_moved).astype(F32)
+    rows_in = swap_ch(layer_input).astype(F32)
     gains_here = gains_master.astype(BF)
     gains_near = jnp.concatenate(both_cores(gains_here, flip(gains_here, "c")), axis=1)
-    gains_all = jnp.concatenate([gains_near, flip(gains_near, "y")], axis=1).astype(F32)
+    gains_all = both_y(gains_near, flip(gains_near, "y"), 1).astype(F32)
     gain_first, gain_second = gains_all[0], gains_all[1]
     qkv_shard = jnp.dot(qkv_master.astype(BF), turn, preferred_element_type=F32).astype(BF)
     scale_first = rms_scale(rows_in)
     normed_own = (rows_in * scale_first * gain_first).astype(BF)
-    qkv_near, near_there = gather_near(held(qkv_shard, mark(rows_moved)))
-    qkv_far = flip(qkv_near, "y")
-    grad_moved = swap_ch(held(cotangent, near_there))
-    qkv_weight = jnp.concatenate([qkv_near, qkv_far]).reshape(2048, 768)
-
     frequency = rope_theta ** (
         -((jnp.arange(128, dtype=jnp.int32) % 32).astype(F32) * 2.0) / HD
     )
-    angles = swap_ch(positions).astype(F32)[:, None] * frequency[None, :]
+    positions_here = jnp.where(straight, positions, flip(positions, "c"))
+    angles = positions_here.astype(F32)[:, None] * frequency[None, :]
     cosine, sine = jnp.cos(angles), jnp.sin(angles)
-    normed, queries, keys, values = gather_product(
-        normed_own, qkv_weight, 256, attention_finish, 1, (cosine, sine)
-    )
-
     count_here = counts.astype(F32)
-    count_pair = both_cores(count_here, flip(count_here, "c"))
-    pair_total = count_pair[0] + count_pair[1]
-    count_total = pair_total + flip(pair_total, "y")
-    seq_weight = 4.0 * jnp.where(h == 0, count_pair[0], count_pair[1])[0] / count_total[0]
-
-    first_there = mark(values)
-    grad_rows = seq_weight * features(grad_moved).astype(F32)
-    grad_out = lax.all_gather(
-        held(grad_rows.astype(BF), first_there), RING, axis=0, tiled=True
-    )
-    out_near, out_there = gather_near(held(out_master.astype(BF), first_there))
+    count_total = count_here + flip(count_here, "c")
+    count_total = count_total + flip(count_total, "y")
+    grad_here = (4.0 * count_here[0] / count_total[0] * cotangent.astype(F32)).astype(BF)
+    normed, queries, keys, values, qkv_weight, grad_own = gather_product(
+        normed_own,
+        (cosine, sine),
+        (qkv_shard, grad_here),
+        ((2048, 768), (ROW, 2048)),
+        256,
+        attention_finish,
+        First,
+        [pltpu.VMEM((2048, 768), BF)] + SPREAD_SEMAPHORES + [pltpu.SemaphoreType.DMA((4,))],
+        1,
+    )
     gate_up_shard = jnp.concatenate([gate_up_master[0], gate_up_master[1]], axis=1).astype(BF)
-    gate_up_near, gate_up_there = gather_near(held(gate_up_shard, first_there))
-    done = attend(idle, queries, keys, values, (7, 0, 6, 1), ())
-    stage = out_there + gate_up_there
-    out_far = flip(out_near, "y")
-    gate_up_far = flip(gate_up_near, "y")
-    down_near, down_there = gather_near(held(down_master.astype(BF), gate_up_there))
-    out_heads = jnp.concatenate([out_near, out_far]).transpose(1, 0, 2).reshape(256, 2048)
-    out_weight = lax.all_gather(out_heads, RING, axis=0, tiled=True)
-    done = attend(idle + stage.astype(jnp.int32), queries, keys, values, (5, 2, 4, 3), tuple(done))
-    attended, level = done
-    gate_up_weight = jnp.concatenate([gate_up_near, gate_up_far]).reshape(2048, 2048)
-    down_far = flip(down_near, "y")
-    down_weight = jnp.concatenate([down_near, down_far]).transpose(1, 0, 2).reshape(1024, 2048)
-
-    attended_own = (
-        lax.all_to_all(attended.reshape(8, ROW, 256), RING, 0, 0)
-        .transpose(1, 0, 2)
-        .reshape(ROW, 2048)
-    )
+    attended, level, out_weight, gate_up_weight, grad_out, attended_own = attend(
+        queries, keys, values, out_master.astype(BF), gate_up_shard, grad_own
+    )
+    grad_rows = grad_own.astype(F32)
     residual = rows_in + jnp.dot(attended_own, out_weight, preferred_element_type=F32)
     scale_second = rms_scale(residual)
-    normed_second, gate, up, activation = gather_product(
+    normed_second, gate, up, activation, down_weight = gather_product(
         (residual * scale_second * gain_second).astype(BF),
-        gate_up_weight,
+        (gate_up_weight,),
+        (down_master.astype(BF),),
+        ((1024, 2048),),
         1024,
         feed_forward_finish,
+        Second,
+        SPREAD_SEMAPHORES,
         2,
     )
 
@@ -1156,7 +1538,7 @@
     down_grad = lax.dot_general(activation, grad_out, TN, preferred_element_type=F32).astype(BF)
     down_y = scatter_y(down_grad.reshape(1024, 4, 512).transpose(1, 0, 2))
     layer_own = residual + product_scatter(activation, down_weight, NN, 4)
-    layer_output = swap_ch(features(layer_own.astype(BF)))
+    layer_output = swap_ch(layer_own.astype(BF))
 
     def norm_grad(values, scale, gain, grad):
         scaled = grad * gain
@@ -1201,13 +1583,12 @@
     down_grad_own = scatter_own(*down_ch)
 
     input_back, gain_first_part = norm_grad(rows_in, scale_first, gain_first, grad_normed_first)
-    input_grad = swap_ch(features(residual_grad + input_back).astype(BF)).astype(F32)
+    input_grad = swap_ch((residual_grad + input_back).astype(BF)).astype(F32)
 
     gain_grads = jnp.stack([gain_first_part, gain_second_part])
-    for bit in "xlch":
+    for bit in "xlchy":
         gain_grads = gain_grads + flip(gain_grads, bit)
-    gain_grads = gain_grads[:, :1024] + flip(gain_grads[:, 1024:], "y")
-    gain_grad_own = jnp.where(plain_c, gain_grads[:, :512], gain_grads[:, 512:])
+    gain_grad_own = lax.dynamic_slice_in_dim(gain_grads, (2 * y + c) * 512, 512, 1)
 
     rate_unit = float(4 * 8 * ROW) ** (-0.5)
     qkv_new = apply_update(qkv_master, qkv_grad_own, qkv_moment, qkv_average, rate_qkv * rate_unit)

time: 1660 us -> 1440 us (0.87)
  waiting for transfers between devices: 293 us -> 135 us
  starting transfers between devices: 225 us -> 81.1 us
  Pallas kernels: 789 us -> 907 us
  local copies, waits for them, and re-layouts: 56.9 us -> 39.4 us
    pallas_call x4 -> x3, Pallas kernels: 320 us -> 488 us  [the longest x2 257 us: gather_product(): pl.pallas_call(lambda *refs: gather_kernel(finish, beside, inputs, len(ex...]
    ppermute x46 -> x29, waiting for transfers between devices: 274 us -> 135 us  [move(): return lax.ppermute(values, AXES, device_pairs(target))]
    ppermute x46 -> x29, starting transfers between devices: 190 us -> 76.7 us  [move(): return lax.ppermute(values, AXES, device_pairs(target))]
    pallas_call x3, Pallas kernels: 325 us -> 274 us  [product_scatter(): pl.pallas_call(lambda *refs: scatter_kernel(dims, *refs), in_specs=[anywh...]
    all_to_all x1 -> x0, starting transfers between devices: 30.5 us -> none  [ring_shards(): lax.all_to_all(attended.reshape(8, ROW, 256), RING, 0, 0).transpose(1, 0, 2)]
    all_to_all x1 -> x0, waiting for transfers between devices: 18.8 us -> none  [ring_shards(): lax.all_to_all(attended.reshape(8, ROW, 256), RING, 0, 0).transpose(1, 0, 2)]
  transfers between devices with their start and end apart: 51 -> 31, of which waited for: 17 -> 8; matrix products, arithmetic and copies ran while one was open for 9% -> 9% of each run, Pallas kernels for 27% -> 17%
where the time goes in v3:
time: 1440 us; the launch traced here: 1430 us
  Pallas kernels  907 us (63%)
  matrix products  140 us (10%)
  waiting for transfers between devices  135 us (9%)
  other arithmetic  109 us (8%)
  starting transfers between devices  81.1 us (6%)
  local copies, waits for them, and re-layouts  39.4 us (3%)
  between operations  20 us (1%)
    pallas_call x3, Pallas kernels, product_scatter(): pl.pallas_call(lambda *refs: scatter_kernel(dims, *refs), in_specs=[anywh...  274 us
    pallas_call x2, Pallas kernels, gather_product(): pl.pallas_call(lambda *refs: gather_kernel(finish, beside, inputs, len(ex...  257 us
    pallas_call x1, Pallas kernels, attend(): pl.pallas_call(attend_kernel, grid=(blocks, 4), in_specs=[pl.BlockSpec((R...  232 us
    pallas_call x2, Pallas kernels, attend_back(): pl.pallas_call(lambda *refs: attend_back_kernel(chosen, not earlier, last...  144 us
    ppermute x29, waiting for transfers between devices, move(): return lax.ppermute(values, AXES, device_pairs(target))  135 us
    ppermute x29, starting transfers between devices, move(): return lax.ppermute(values, AXES, device_pairs(target))  76.7 us
    dot_general x1, matrix products, ring_shards(): lax.dot_general(normed_second, grad_gate_up, TN, preferred_element_type=F32)  44.5 us
  transfers between devices with their start and end apart: 31, of which 8 were waited for; matrix products, arithmetic and copies ran while one was open for 9% of the time, Pallas kernels for 17%

profile of v3, /device:TPU:0, one launch (start us, length us, event | category | flops | bytes accessed | tf_op | source)
XLA Modules:
  0.0 1430.7 jit_solution(6298895720654449254)
XLA Ops:
  34.3 9.3 multiply_sine_fusion
  46.0 137.8 %shard_map.354 = (bf16[4096,2048]{1,0:T(8,128)(2,1)}, bf16[4096,256]{1,0:T(8,128)(2,1)}, bf16[4096,256]{1,0:T(8,128)(2,1)}, bf16[4096,256]{1,0:T(8,128)(2,1)}, b...) custom-call(bf16[512,2048]{1,0:T(8,128)(2,1)} %fusion.10.refs_0_, ...), custom_call_target="tpu_custom_call" | custom-call | flops 80000000000 | bytes 31457280 | tf_op jit(solution)/shard_map/pallas_call | solution.py:765
  183.8 231.7 %shard_map.355 = (bf16[4096,256]{1,0:T(8,128)(2,1)S(1)}, f32[8,4,512]{2,1,0:T(4,128)S(1)}, bf16[2048,2048]{1,0:T(8,128)(2,1)}, bf16[2048,2048]{1,0:T(8,128)(2,1)...) custom-call(bf16[4096,256]{1,0:T(8,128)(2,1)} %get-tuple-element.44.q_ref.refs_1_, ...), custom_call_target="tpu_custom_call" | custom-call | flops 112000000000 | bytes 10485760 | tf_op jit(solution)/shard_map/pallas_call | solution.py:1208
  415.5 8.6 multiply_reduce_fusion.2
  426.8 119.0 %shard_map.356 = (bf16[4096,2048]{1,0:T(8,128)(2,1)}, bf16[4096,1024]{1,0:T(8,128)(2,1)}, bf16[4096,1024]{1,0:T(8,128)(2,1)}, bf16[4096,1024]{1,0:T(8,128)(2,1)}, bf16[1024,2048]{1,0:T(8,128)(2,1)}) custom-call(bf16[512,2048]{1,0:T(8,128)(2,1)} %multiply_convert_fusion.refs_0_, bf16[2048,2048]{1,0:T(8,128)(2,1)} %get-tuple-element.50.refs_1_, ...), custom_call_target="tpu_custom_call" | custom-call | flops 80000000000 | bytes 31457280 | tf_op jit(solution)/shard_map/pallas_call | solution.py:765
  545.8 24.2 %convolution_convert_fusion.2 = bf16[1024,2048]{1,0:T(8,128)(2,1)} fusion(bf16[4096,1024]{1,0:T(8,128)(2,1)} %get-tuple-element.51.refs_0_, bf16[4096,2048]{1,0:T(8,128)(2,1)} %get-tuple-element.53), kind=kOutput, calls=%fused_computation.50 | convolution fusion | flops 17181966336 | bytes 29360128 | tf_op jit(solution)/shard_map/dot_general | solution.py:1538
  570.0 86.7 %shard_map.357 = f32[512,2048]{1,0:T(8,128)} custom-call(bf16[4096,1024]{1,0:T(8,128)(2,1)} %get-tuple-element.51.refs_0_, bf16[1024,2048]{1,0:T(8,128)(2,1)} %get-tuple-element.52.refs_1_), custom_call_target="tpu_custom_call" | custom-call | flops 80000000000 | bytes 31457280 | tf_op jit(solution)/shard_map/pallas_call | solution.py:891
  656.7 23.8 %fusion.65 = f32[4096,1024]{1,0:T(8,128)} fusion(bf16[4096,2048]{1,0:T(8,128)(2,1)} %get-tuple-element.53, bf16[1024,2048]{1,0:T(8,128)(2,1)} %get-tuple-element.52.refs_1_), kind=kOutput, calls=%fused_computation.173 | convolution fusion | flops 17179869184 | bytes 37748736 | tf_op jit(solution)/shard_map/dot_general | solution.py:1527
  680.4 12.2 fusion.5
  692.6 9.8 pad_maximum_fusion.refs_0_
  703.6 44.5 %convolution_convert_fusion.1 = bf16[2048,2048]{1,0:T(8,128)(2,1)} fusion(bf16[4096,2048]{1,0:T(8,128)(2,1)} %get-tuple-element.56, bf16[4096,1024]{1,0:T(8,128)(2,1)} %copy-done.10, bf16[4096,1024]{1,0:T(8,128)(2,1)} %copy-done.9), kind=kOutput, calls=%fused_computation.19 | convolution fusion | flops 34397487104 | bytes 41943040 | tf_op jit(solution)/shard_map/dot_general | solution.py:1534
  748.1 94.6 %shard_map.358 = f32[512,2048]{1,0:T(8,128)} custom-call(bf16[4096,2048]{1,0:T(8,128)(2,1)} %pad_maximum_fusion.refs_0_, bf16[2048,2048]{1,0:T(8,128)(2,1)} %get-tuple-element.50.refs_1_), custom_call_target="tpu_custom_call" | custom-call | flops 80000000000 | bytes 31457280 | tf_op jit(solution)/shard_map/pallas_call | solution.py:891
  869.5 17.2 %collective-permute-start.6 = (bf16[512,2048]{1,0:T(8,128)(2,1)}, bf16[512,2048]{1,0:T(8,128)(2,1)}, u32[]{:S(2)}, u32[]{:S(2)}) collective-permute-start(bf16[512,2048]{1,0:T(8,128)(2,1)} %get-tuple-element.94), channel_id=1, source_target_pairs={{0,0},{1,1},{2,2},{3,3},{4,8},{5,9},{6,10},{7,11},{8,4},{9,5},{10,... | collective-permute-start | bytes 6291464 | tf_op jit(solution)/shard_map/ppermute | solution.py:354
  890.0 8.2 convolution_convert_fusion.5
  928.8 36.8 %collective-permute-done.21 = bf16[1024,512]{1,0:T(8,128)(2,1)} collective-permute-done((bf16[1024,512]{1,0:T(8,128)(2,1)S(1)}, bf16[1024,512]{1,0:T(8,128)(2,1)}, u32[]{:S(2)}, u32[]{:S(2)}) %collective-permute-start.21) | collective-permute-done | bytes 1048608 | tf_op jit(solution)/shard_map/ppermute | solution.py:354
  973.0 26.4 %collective-permute-done.7 = bf16[2,512,2048]{2,1,0:T(8,128)(2,1)} collective-permute-done((bf16[2,512,2048]{2,1,0:T(8,128)(2,1)}, bf16[2,512,2048]{2,1,0:T(8,128)(2,1)}, u32[]{:S(2)}, u32[]{:S(2)}) %collective-permute-start.7) | collective-permute-done | bytes 4194336 | tf_op jit(solution)/shard_map/ppermute | solution.py:354
  1016.8 72.2 %shard_map.359 = (bf16[4096,512]{1,0:T(8,128)(2,1)}, f32[4096,256]{1,0:T(8,128)}, f32[8,4,512]{2,1,0:T(4,128)}) custom-call(s32[1]{0:T(128)} %bitcast.12.refs_0_, bf16[4096,256]{1,0:T(8,128)(2,1)} %get-tuple-element.44.q_ref.refs_1_, bf16[4096,256]{1,0:T(8,128)(2,1)} %get-tuple-element.45.k_ref.refs_2_, bf16[4096,256]{1,0:T(8,128)(2,1)} %get-tuple-element.46.v_ref.refs_3_, ...), custom_call_target="tpu_custom_call" | custom-call | flops 76000002048 | bytes 20971520 | tf_op jit(solution)/shard_map/pallas_call | solution.py:1411
  1100.6 71.8 %shard_map.360 = (bf16[4096,512]{1,0:T(8,128)(2,1)}, bf16[4096,256]{1,0:T(8,128)(2,1)}) custom-call(s32[1]{0:T(128)} %bitcast.9.refs_0_, bf16[4096,256]{1,0:T(8,128)(2,1)} %get-tuple-element.44.q_ref.refs_1_, bf16[4096,256]{1,0:T(8,128)(2,1)} %get-tuple-element.45.k_ref.refs_2_, ...), custom_call_target="tpu_custom_call", output_to_operand_aliasing={{0}: (12, {})} | custom-call | flops 76000002048 | bytes 20971520 | tf_op jit(solution)/shard_map/pallas_call | solution.py:1411
  1178.4 93.1 %shard_map.361 = f32[512,2048]{1,0:T(8,128)} custom-call(bf16[4096,768]{1,0:T(8,128)(2,1)} %copy-done.34, bf16[2048,768]{1,0:T(8,128)(2,1)} %get-tuple-element.64.refs_1_), custom_call_target="tpu_custom_call" | custom-call | flops 80000000000 | bytes 31457280 | tf_op jit(solution)/shard_map/pallas_call | solution.py:891
  1276.0 17.4 %convolution_convert_fusion.3.clone.5 = bf16[2048,768]{1,0:T(8,128)(2,1)S(1)} fusion(bf16[4096,2048]{1,0:T(8,128)(2,1)} %get-tuple-element.65, bf16[4096,768]{1,0:T(8,128)(2,1)S(1)} %copy-done.35), kind=kOutput, calls=%fused_computation.67.clone.clone.clone.2 | convolution fusion | flops 12886474752 | bytes 26214400 | tf_op jit(solution)/shard_map/dot_general | solution.py:1574
  1307.7 17.9 %collective-permute-start.11 = (bf16[512,2048]{1,0:T(8,128)(2,1)}, bf16[512,2048]{1,0:T(8,128)(2,1)}, u32[]{:S(2)}, u32[]{:S(2)}) collective-permute-start(bf16[512,2048]{1,0:T(8,128)(2,1)} %fusion.15), channel_id=1, source_target_pairs={{0,0},{1,1},{2,2},{3,3},{4,8},{5,9},{6,10},{7,11},{8,4},{9,5},{10,... | collective-permute-start | bytes 6291464 | tf_op jit(solution)/shard_map/ppermute | solution.py:354
  1329.4 30.7 %collective-permute-done.27 = f32[2,2048]{1,0:T(2,128)S(1)} collective-permute-done((f32[2,2048]{1,0:T(2,128)S(1)}, f32[2,2048]{1,0:T(2,128)S(1)}, u32[]{:S(2)}, u32[]{:S(2)}) %collective-permute-start.27) | collective-permute-done | bytes 16416 | tf_op jit(solution)/shard_map/ppermute | solution.py:354
  1380.2 19.9 %collective-permute-done.13 = bf16[512,768]{1,0:T(8,128)(2,1)} collective-permute-done((bf16[512,768]{1,0:T(8,128)(2,1)S(1)}, bf16[512,768]{1,0:T(8,128)(2,1)}, u32[]{:S(2)}, u32[]{:S(2)}) %collective-permute-start.13) | collective-permute-done | bytes 786464 | tf_op jit(solution)/shard_map/ppermute | solution.py:354
  1410.0 8.2 collective-permute-done.17
  (263 shorter events, 188.9 us)
Async XLA Ops:
  7.8 14.8 %collective-permute-start.4 = (f32[1]{0:T(128)}, f32[1]{0:T(128)}, u32[]{:S(2)}, u32[]{:S(2)}) collective-permute-start(f32[1]{0:T(128)} %convert_element_type.232), channel_id=1, source_target_pairs={{0,8},{1,9},{2,10},{3,11},{4,12},{5,13},{6,14},{7,15},{8,0},{9,1},... | collective-permute-start | bytes 20 | tf_op jit(solution)/shard_map/ppermute | solution.py:354
  10.0 18.1 %collective-permute-start.1 = (bf16[2,512]{1,0:T(2,128)(2,1)S(1)}, bf16[2,512]{1,0:T(2,128)(2,1)S(1)}, u32[]{:S(2)}, u32[]{:S(2)}) collective-permute-start(bf16[2,512]{1,0:T(2,128)(2,1)S(1)} %convert_element_type.224), channel_id=1, source_target_pairs={{0,8},{1,9},{2,10},{3,11},{4,12},{5,13},{6,14},{7,15},{8,0},{9,1},... | collective-permute-start | bytes 6152 | tf_op jit(solution)/shard_map/ppermute | solution.py:354
  10.1 24.3 %collective-permute-start.3 = (s32[4096]{0:T(1024)}, s32[4096]{0:T(1024)S(1)}, u32[]{:S(2)}, u32[]{:S(2)}) collective-permute-start(s32[4096]{0:T(1024)} %param.22), channel_id=1, source_target_pairs={{0,8},{1,9},{2,10},{3,11},{4,12},{5,13},{6,14},{7,15},{8,0},{9,1},... | collective-permute-start | bytes 49160 | tf_op jit(solution)/shard_map/ppermute | solution.py:354
  10.5 33.1 %collective-permute-start = (bf16[512,2048]{1,0:T(8,128)(2,1)}, bf16[512,2048]{1,0:T(8,128)(2,1)S(1)}, u32[]{:S(2)}, u32[]{:S(2)}) collective-permute-start(bf16[512,2048]{1,0:T(8,128)(2,1)} %param.19), channel_id=1, source_target_pairs={{0,0},{1,1},{2,2},{3,3},{4,8},{5,9},{6,10},{7,11},{8,4},{9,5},{10,... | collective-permute-start | bytes 6291464 | tf_op jit(solution)/shard_map/ppermute | solution.py:354
  861.8 48.8 %collective-permute-start.20 = (bf16[2,1024,512]{2,1,0:T(8,128)(2,1)}, bf16[2,1024,512]{2,1,0:T(8,128)(2,1)}, u32[]{:S(2)}, u32[]{:S(2)}) collective-permute-start(bf16[2,1024,512]{2,1,0:T(8,128)(2,1)} %bitcast.75), channel_id=1, source_target_pairs={{0,16},{1,17},{2,18},{3,19},{4,20},{5,21},{6,22},{7,23},{8,24},{9,... | collective-permute-start | bytes 6291464 | tf_op jit(solution)/shard_map/ppermute | solution.py:354
  869.5 59.3 %collective-permute-start.6 = (bf16[512,2048]{1,0:T(8,128)(2,1)}, bf16[512,2048]{1,0:T(8,128)(2,1)}, u32[]{:S(2)}, u32[]{:S(2)}) collective-permute-start(bf16[512,2048]{1,0:T(8,128)(2,1)} %get-tuple-element.94), channel_id=1, source_target_pairs={{0,0},{1,1},{2,2},{3,3},{4,8},{5,9},{6,10},{7,11},{8,4},{9,5},{10,... | collective-permute-start | bytes 6291464 | tf_op jit(solution)/shard_map/ppermute | solution.py:354
  889.2 110.2 %collective-permute-start.7 = (bf16[2,512,2048]{2,1,0:T(8,128)(2,1)}, bf16[2,512,2048]{2,1,0:T(8,128)(2,1)}, u32[]{:S(2)}, u32[]{:S(2)}) collective-permute-start(bf16[2,512,2048]{2,1,0:T(8,128)(2,1)} %constant_dynamic-slice_fusion.5), channel_id=1, source_target_pairs={{0,16},{1,17},{2,18},{3,19},{4,20},{5,21},{6,22},{7,23},{8,24},{9,... | collective-permute-start | bytes 12582920 | tf_op jit(solution)/shard_map/ppermute | solution.py:354
  899.6 117.1 %all-to-all-start = ((bf16[8,512,256]{2,1,0:T(8,128)(2,1)}), bf16[8,512,256]{2,1,0:T(8,128)(2,1)}, u32[]{:S(2)}, u32[]{:S(2)}) async-start(bf16[8,512,256]{2,1,0:T(8,128)(2,1)} %bitcast.81), calls=%async_computation | async-start | bytes 4194304 | tf_op jit(solution)/shard_map/all_to_all | solution.py:1556
  904.0 467.6 %reduce-scatter.2.cloned.1.call-start = ((), (), s32[]{:S(2)}) async-start(), calls=%async_computation.2 | async-start | bytes 9437184 | tf_op jit(solution)/shard_map/reduce_scatter | solution.py:1578
  914.1 51.5 %collective-permute-start.23 = (bf16[1024,512]{1,0:T(8,128)(2,1)}, bf16[1024,512]{1,0:T(8,128)(2,1)}, u32[]{:S(2)}, u32[]{:S(2)}) collective-permute-start(bf16[1024,512]{1,0:T(8,128)(2,1)} %get-tuple-element.96), channel_id=1, source_target_pairs={{4,8},{5,9},{6,10},{7,11},{8,4},{9,5},{10,6},{11,7},{20,24},{21,25... | collective-permute-start | bytes 3145736 | tf_op jit(solution)/shard_map/ppermute | solution.py:354
  915.8 49.8 %collective-permute-start.22 = (bf16[1024,512]{1,0:T(8,128)(2,1)}, bf16[1024,512]{1,0:T(8,128)(2,1)}, u32[]{:S(2)}, u32[]{:S(2)}) collective-permute-start(bf16[1024,512]{1,0:T(8,128)(2,1)} %get-tuple-element.96), channel_id=1, source_target_pairs={{0,8},{1,9},{2,10},{3,11},{12,4},{13,5},{14,6},{15,7},{16,24},{17,... | collective-permute-start | bytes 3145736 | tf_op jit(solution)/shard_map/ppermute | solution.py:354
  920.4 45.1 %collective-permute-start.21 = (bf16[1024,512]{1,0:T(8,128)(2,1)S(1)}, bf16[1024,512]{1,0:T(8,128)(2,1)}, u32[]{:S(2)}, u32[]{:S(2)}) collective-permute-start(bf16[1024,512]{1,0:T(8,128)(2,1)S(1)} %get-tuple-element.95), channel_id=1, source_target_pairs={{4,0},{5,1},{6,2},{7,3},{8,12},{9,13},{10,14},{11,15},{20,16},{21,... | collective-permute-start | bytes 3145736 | tf_op jit(solution)/shard_map/ppermute | solution.py:354
  1007.0 91.7 %collective-permute-start.10 = (bf16[512,2048]{1,0:T(8,128)(2,1)}, bf16[512,2048]{1,0:T(8,128)(2,1)}, u32[]{:S(2)}, u32[]{:S(2)}) collective-permute-start(bf16[512,2048]{1,0:T(8,128)(2,1)} %get-tuple-element.91), channel_id=1, source_target_pairs={{4,8},{5,9},{6,10},{7,11},{8,4},{9,5},{10,6},{11,7},{20,24},{21,25... | collective-permute-start | bytes 6291464 | tf_op jit(solution)/shard_map/ppermute | solution.py:354
  1009.0 79.9 %collective-permute-start.9 = (bf16[512,2048]{1,0:T(8,128)(2,1)}, bf16[512,2048]{1,0:T(8,128)(2,1)}, u32[]{:S(2)}, u32[]{:S(2)}) collective-permute-start(bf16[512,2048]{1,0:T(8,128)(2,1)} %get-tuple-element.91), channel_id=1, source_target_pairs={{0,8},{1,9},{2,10},{3,11},{12,4},{13,5},{14,6},{15,7},{16,24},{17,... | collective-permute-start | bytes 6291464 | tf_op jit(solution)/shard_map/ppermute | solution.py:354
  1015.4 80.9 %collective-permute-start.8 = (bf16[512,2048]{1,0:T(8,128)(2,1)}, bf16[512,2048]{1,0:T(8,128)(2,1)}, u32[]{:S(2)}, u32[]{:S(2)}) collective-permute-start(bf16[512,2048]{1,0:T(8,128)(2,1)} %get-tuple-element.92), channel_id=1, source_target_pairs={{4,0},{5,1},{6,2},{7,3},{8,12},{9,13},{10,14},{11,15},{20,16},{21,... | collective-permute-start | bytes 6291464 | tf_op jit(solution)/shard_map/ppermute | solution.py:354
  1275.2 25.4 %collective-permute-start.24 = (f32[2,2048]{1,0:T(2,128)S(1)}, f32[2,2048]{1,0:T(2,128)S(1)}, u32[]{:S(2)}, u32[]{:S(2)}) collective-permute-start(f32[2,2048]{1,0:T(2,128)S(1)} %pad_maximum_fusion.3), channel_id=1, source_target_pairs={{0,1},{1,0},{2,3},{3,2},{4,5},{5,4},{6,7},{7,6},{8,9},{9,8},{10,11... | collective-permute-start | bytes 49160 | tf_op jit(solution)/shard_map/ppermute | solution.py:354
  1297.2 64.3 %collective-permute-start.12 = (bf16[2,512,768]{2,1,0:T(8,128)(2,1)S(1)}, bf16[2,512,768]{2,1,0:T(8,128)(2,1)S(1)}, u32[]{:S(2)}, u32[]{:S(2)}) collective-permute-start(bf16[2,512,768]{2,1,0:T(8,128)(2,1)S(1)} %constant_dynamic-slice_fusion.4), channel_id=1, source_target_pairs={{0,16},{1,17},{2,18},{3,19},{4,20},{5,21},{6,22},{7,23},{8,24},{9,... | collective-permute-start | bytes 4718600 | tf_op jit(solution)/shard_map/ppermute | solution.py:354
  1307.0 18.6 %collective-permute-start.26 = (f32[2,2048]{1,0:T(2,128)S(1)}, f32[2,2048]{1,0:T(2,128)S(1)}, u32[]{:S(2)}, u32[]{:S(2)}) collective-permute-start(f32[2,2048]{1,0:T(2,128)S(1)} %fusion.77), channel_id=1, source_target_pairs={{0,8},{1,9},{2,10},{3,11},{4,12},{5,13},{6,14},{7,15},{8,0},{9,1},... | collective-permute-start | bytes 49160 | tf_op jit(solution)/shard_map/ppermute | solution.py:354
  1307.7 68.3 %collective-permute-start.11 = (bf16[512,2048]{1,0:T(8,128)(2,1)}, bf16[512,2048]{1,0:T(8,128)(2,1)}, u32[]{:S(2)}, u32[]{:S(2)}) collective-permute-start(bf16[512,2048]{1,0:T(8,128)(2,1)} %fusion.15), channel_id=1, source_target_pairs={{0,0},{1,1},{2,2},{3,3},{4,8},{5,9},{6,10},{7,11},{8,4},{9,5},{10,... | collective-permute-start | bytes 6291464 | tf_op jit(solution)/shard_map/ppermute | solution.py:354
  1325.6 34.5 %collective-permute-start.27 = (f32[2,2048]{1,0:T(2,128)S(1)}, f32[2,2048]{1,0:T(2,128)S(1)}, u32[]{:S(2)}, u32[]{:S(2)}) collective-permute-start(f32[2,2048]{1,0:T(2,128)S(1)} %add.298), channel_id=1, source_target_pairs={{0,4},{1,5},{2,6},{3,7},{4,0},{5,1},{6,2},{7,3},{8,12},{9,13},{10,... | collective-permute-start | bytes 49160 | tf_op jit(solution)/shard_map/ppermute | solution.py:354
  1363.0 37.1 %collective-permute-start.15 = (bf16[512,768]{1,0:T(8,128)(2,1)}, bf16[512,768]{1,0:T(8,128)(2,1)S(1)}, u32[]{:S(2)}, u32[]{:S(2)}) collective-permute-start(bf16[512,768]{1,0:T(8,128)(2,1)} %get-tuple-element.100), channel_id=1, source_target_pairs={{4,8},{5,9},{6,10},{7,11},{8,4},{9,5},{10,6},{11,7},{20,24},{21,25... | collective-permute-start | bytes 2359304 | tf_op jit(solution)/shard_map/ppermute | solution.py:354
  1363.8 36.3 %collective-permute-start.14 = (bf16[512,768]{1,0:T(8,128)(2,1)}, bf16[512,768]{1,0:T(8,128)(2,1)S(1)}, u32[]{:S(2)}, u32[]{:S(2)}) collective-permute-start(bf16[512,768]{1,0:T(8,128)(2,1)} %get-tuple-element.100), channel_id=1, source_target_pairs={{0,8},{1,9},{2,10},{3,11},{12,4},{13,5},{14,6},{15,7},{16,24},{17,... | collective-permute-start | bytes 2359304 | tf_op jit(solution)/shard_map/ppermute | solution.py:354
  1366.6 33.5 %collective-permute-start.13 = (bf16[512,768]{1,0:T(8,128)(2,1)S(1)}, bf16[512,768]{1,0:T(8,128)(2,1)}, u32[]{:S(2)}, u32[]{:S(2)}) collective-permute-start(bf16[512,768]{1,0:T(8,128)(2,1)S(1)} %get-tuple-element.99), channel_id=1, source_target_pairs={{4,0},{5,1},{6,2},{7,3},{8,12},{9,13},{10,14},{11,15},{20,16},{21,... | collective-permute-start | bytes 2359304 | tf_op jit(solution)/shard_map/ppermute | solution.py:354
  1374.6 28.8 %collective-permute-start.16 = (bf16[2,256,512]{2,1,0:T(8,128)(2,1)S(1)}, bf16[2,256,512]{2,1,0:T(8,128)(2,1)S(1)}, u32[]{:S(2)}, u32[]{:S(2)}) collective-permute-start(bf16[2,256,512]{2,1,0:T(8,128)(2,1)S(1)} %bitcast.85), channel_id=1, source_target_pairs={{0,16},{1,17},{2,18},{3,19},{4,20},{5,21},{6,22},{7,23},{8,24},{9,... | collective-permute-start | bytes 1572872 | tf_op jit(solution)/shard_map/ppermute | solution.py:354
  (74 other events, 1242.9 us)
Sparse Core Ops, SparseCore 0:
  928.9 181.3 reduce-scatter.1

commit v4 on v3

--- a/solution.py
+++ b/solution.py
@@ -1244,180 +1244,481 @@
 KEYS = 256
 
 
-def attend_back_kernel(chosen, first, last, me_ref, q_ref, k_ref, v_ref, do_ref, l_ref, cos_ref, sin_ref, *refs):
-    if first:
-        o_ref, dkv_ref, dq_out, delta = refs[:4]
-        rest = refs[4:]
-    else:
-        if last:
-            all_cos, all_sin = refs[:2]
-            refs = refs[2:]
-        delta, dq_in, _, dkv_ref, dq_out = refs[:5]
-        rest = refs[5:]
-    qm, dom, dq, dk, dv, km, pt, dst = rest
+HALF = ROW // 2
+
+
+class BesideBack:
+    DUE = {"a": 8, "b": 9, "c": 11, "d": 12, "D0": 15, "e": 24, "f": 25, "D1": 27, "G0": 37, "g": 48, "h": 49, "G1": 51, "G2": 61, "G3": 70}
+
+    def __init__(self, refs):
+        self.heads_own, self.parts, self.gate_up, self.down, self.residual, self.cos, self.sin = refs[:7]
+        self.gate_up_sums, self.down_sums, self.layer = refs[7:10]
+        (
+            self.do,
+            self.cs,
+            self.sn,
+            self.other,
+            self.near_x,
+            self.near_l,
+            self.ra,
+            self.rb,
+            self.land,
+            self.stage,
+            self.rest,
+            self.row_send,
+            self.row_recv,
+            self.core_send,
+            self.core_recv,
+            self.far_send,
+            self.far_recv,
+            self.y_send,
+            self.y_recv,
+            self.z_send,
+            self.z_recv,
+            self.stage_sem,
+            self.own_sem,
+        ) = refs[10:]
+        self.y, self.c, self.h, self.me = places()
+        _, (self.to_x, self.to_l, self.to_c) = ring_position()
+        self.names = list(self.DUE)
+        self.where = {
+            "a": (3, 0), "b": (3, 1), "c": (1, 0), "d": (2, 1), "e": (1, 1), "f": (2, 0), "g": (0, 0), "h": (0, 1)
+        }
+
+    def far(self, name):
+        top, bottom = pl.ds(0, HALF), pl.ds(HALF, HALF)
+        other = self.other
+        index = "abcdef".index(name)
+        source, target, device = (
+            (other.at[3, top], self.ra, self.to_x),
+            (other.at[3, bottom], self.rb, self.to_l),
+            (other.at[1, top], self.near_x.at[top], self.to_x),
+            (other.at[2, bottom], self.near_l.at[bottom], self.to_l),
+            (other.at[1, bottom], self.near_x.at[bottom], self.to_x),
+            (other.at[2, top], self.near_l.at[top], self.to_l),
+        )[index]
+        return remote(source, target, self.far_send.at[index], self.far_recv.at[index], device)
+
+    def tables(self):
+        return (
+            pltpu.make_async_copy(self.cos, self.cs, self.own_sem.at[0]),
+            pltpu.make_async_copy(self.sin, self.sn, self.own_sem.at[1]),
+        )
+
+    def row_local(self):
+        columns = pl.ds(pl.multiple_of(self.me * 256, 256), 256)
+        return pltpu.make_async_copy(
+            self.heads_own.at[:, columns], self.do.at[rows_at(self.me)], self.own_sem.at[2]
+        )
+
+    def row_remote(self, block, sender):
+        columns = pl.ds(pl.multiple_of(block * 256, 256), 256)
+        return remote(
+            self.heads_own.at[:, columns],
+            self.do.at[rows_at(sender)],
+            self.row_send.at[block],
+            self.row_recv.at[sender],
+            {"c": block >> 2, "l": (block >> 1) & 1, "x": block & 1},
+        )
+
+    def core(self, slot):
+        return remote(
+            self.parts.at[rows_at(self.me ^ (slot | 4))],
+            self.other.at[slot],
+            self.core_send.at[slot],
+            self.core_recv.at[slot],
+            self.to_c,
+        )
+
+    def piece(self, name, y):
+        k = int(name[1])
+        if name[0] == "G":
+            first = (2 * y + (k >> 1)) * 512 + (k & 1) * 256
+            return self.gate_up.at[pl.ds(pl.multiple_of(first, 256), 256)]
+        return self.down.at[:, pl.ds(pl.multiple_of((2 * y + k) * 512, 512), 512)]
+
+    def over_y(self, name):
+        index = ("D0", "D1", "G0", "G1", "G2", "G3").index(name)
+        target = self.land_d.at[int(name[1])] if name[0] == "D" else self.land.at[int(name[1])]
+        return remote(
+            self.piece(name, 1 - self.y), target, self.y_send.at[index], self.y_recv.at[index], {"y": 1 - self.y}
+        )
+
+    def owner(self, name):
+        k = int(name[1])
+        return k >> 1 if name[0] == "G" else k
+
+    def sum_place(self, name, h):
+        k = int(name[1])
+        if name[0] == "G":
+            return self.gate_up_sums.at[h, pl.ds((k & 1) * 256, 256)]
+        return self.down_sums.at[h]
+
+    def over_z(self, name, h):
+        index = ("D0", "D1", "G0", "G1", "G2", "G3").index(name)
+        source = self.land_d.at[int(name[1])] if name[0] == "D" else self.land.at[int(name[1])]
+        group = (0, 0, 1, 2, 1, 2)[index]
+        return (
+            remote(
+                source,
+                self.sum_place(name, h),
+                self.z_send.at[index],
+                self.z_recv.at[group, h],
+                {"c": self.owner(name), "h": self.c},
+            ),
+            pltpu.make_async_copy(source, self.sum_place(name, h), self.z_send.at[index]),
+        )
+
+    def stage_copy(self, index):
+        name = self.names[index]
+        sem = self.stage_sem.at[index % 2]
+        if name in self.where:
+            slot, half = self.where[name]
+            return pltpu.make_async_copy(
+                self.parts.at[rows_at(self.me ^ slot, half)], self.stage.at[index % 2], sem
+            )
+        if name[0] == "G":
+            return pltpu.make_async_copy(self.piece(name, self.y), self.stage.at[index % 2], sem)
+        return pltpu.make_async_copy(self.piece(name, self.y), self.stage_d.at[index % 2], sem)
+
+    def rest_copy(self, half):
+        return pltpu.make_async_copy(self.residual.at[pl.ds(half * HALF, HALF)], self.rest, self.own_sem.at[3])
+
+    def layer_remote(self, half):
+        part = pl.ds(half * HALF, HALF)
+        return (
+            remote(
+                self.other.at[0, part],
+                self.layer.at[part],
+                self.far_send.at[6 + half],
+                self.far_recv.at[6 + half],
+                {"c": self.h, "h": self.c},
+            ),
+            pltpu.make_async_copy(self.other.at[0, part], self.layer.at[part], self.far_send.at[6 + half]),
+        )
+
+    def either(self, here, pair, method):
+        away, local = pair
+
+        @pl.when(here)
+        def _():
+            getattr(local, method)()
+
+        @pl.when(jnp.logical_not(here))
+        def _():
+            getattr(away, method)()
+
+    def begin(self):
+        for copy in self.tables():
+            copy.start()
+        self.row_local().start()
+        self.stage_copy(0).start()
+        self.stage_copy(1).start()
+        enter_ring(wide_partners())
+
+        def send(index, carry):
+            block = 7 - index
+
+            @pl.when(block != self.me)
+            def _():
+                self.row_remote(block, self.me).start()
+
+            return carry
+
+        lax.fori_loop(0, 8, send, 0)
+        for slot in (3, 1, 2, 0):
+            self.core(slot).start()
+        self.over_y("D0").start()
+        self.over_y("D1").start()
+        for copy in self.tables():
+            copy.wait()
+
+    def rows_there(self, block):
+        @pl.when(block == self.me)
+        def _():
+            self.row_local().wait()
+
+        @pl.when(block != self.me)
+        def _():
+            self.row_remote(block, block).wait_recv()
+
+    def add(self, target, terms, count):
+        size = target.shape[0] // count
+
+        def chunk(index, carry):
+            rows = pl.ds(pl.multiple_of(index * size, size), size)
+            total = terms[0][rows, :].astype(F32)
+            for term in terms[1:]:
+                total += term[rows, :].astype(F32)
+            target[rows, :] = rounded(total)
+            return carry
+
+        lax.fori_loop(0, count, chunk, 0)
+
+    def work(self, name):
+        index = self.names.index(name)
+        order = ("D0", "D1", "G0", "G1", "G2", "G3")
+        self.stage_copy(index).wait()
+        if name in self.where:
+            slot, half = self.where[name]
+            part = pl.ds(half * HALF, HALF)
+            if name in "acd" or name == "g":
+                self.core(slot).wait_recv()
+            terms = [self.stage.at[index % 2], self.other.at[slot, part]]
+            if name == "e":
+                self.far("b").wait_recv()
+                terms.append(self.rb)
+            if name == "f":
+                self.far("a").wait_recv()
+                terms.append(self.ra)
+            if name in "gh":
+                for each in ("c", "f") if name == "g" else ("e", "d"):
+                    self.far(each).wait_recv()
+                self.rest_copy(half).start()
+                self.rest_copy(half).wait()
+                terms += [self.near_x.at[part], self.near_l.at[part], self.rest]
+            self.add(self.other.at[slot, part], terms, 8)
+            if name in "gh":
+                self.either(self.c == self.h, self.layer_remote(half), "start")
+            else:
+                self.far(name).start()
+        else:
+            self.over_y(name).wait_recv()
+            if name[0] == "D":
+                source, mine = self.land_d.at[int(name[1])], self.stage_d.at[index % 2]
+            else:
+                source, mine = self.land.at[int(name[1])], self.stage.at[index % 2]
+            self.add(source, [mine, source], 8)
+            here = jnp.logical_and(self.owner(name) == self.c, self.h == self.c)
+            self.either(here, self.over_z(name, self.h), "start")
+            place = order.index(name)
+            if place + 2 < 6:
+                self.over_y(order[place + 2]).start()
+        if index + 2 < len(self.names):
+            self.stage_copy(index + 2).start()
+
+    def poll(self, unit):
+        for name, due in self.DUE.items():
+
+            @pl.when(unit == due)
+            def _(name=name):
+                self.work(name)
+
+    def end(self):
+        def each(block, carry):
+            @pl.when(block != self.me)
+            def _():
+                self.row_remote(block, self.me).wait_send()
+
+            return carry
+
+        lax.fori_loop(0, 8, each, 0)
+        for slot in range(4):
+            self.core(slot).wait_send()
+        for name in "abcdef":
+            self.far(name).wait_send()
+        for half in range(2):
+            pair = self.layer_remote(half)
+
+            @pl.when(self.c == self.h)
+            def _(pair=pair):
+                pair[1].wait()
+
+            @pl.when(self.c != self.h)
+            def _(pair=pair):
+                pair[0].wait_send()
+                pair[0].wait_recv()
+
+        for name in ("D0", "D1", "G0", "G1", "G2", "G3"):
+            self.over_y(name).wait_send()
+            here = jnp.logical_and(self.owner(name) == self.c, self.h == self.c)
+            pair = self.over_z(name, self.h)
+
+            @pl.when(here)
+            def _(pair=pair):
+                pair[1].wait()
+
+            @pl.when(jnp.logical_not(here))
+            def _(pair=pair):
+                pair[0].wait_send()
+
+        for h in range(2):
+            here = jnp.logical_and(h == self.h, self.c == self.h)
+            for name in ("D0", "G0", "G1"):
+
+                @pl.when(jnp.logical_not(here))
+                def _(name=name, h=h):
+                    self.over_z(name, h)[0].wait_recv()
+
+
+def attend_back_kernel(q_ref, k_ref, v_ref, o_ref, l_ref, *refs):
+    given, (dkv_ref, dq_out), outs = refs[:7], refs[7:9], refs[9:12]
+    qm, dom, delta, dq, dk, dv, km, pt, dst = refs[12:21]
+    land_d, stage_d = refs[21:23]
+    beside = BesideBack(given + outs + refs[23:])
+    beside.land_d, beside.stage_d = land_d, stage_d
     heads = 4
-    step = pl.program_id(0)
-    blocks = q_ref.shape[0] // ROW
-
-    @pl.when(step == 0)
+    i, sub = pl.program_id(0), pl.program_id(1)
+    block = 7 - i
+    blocks = 8
+    unit = i * (i + 1) + sub * (i + 1)
+    rows_here = rows_at(block)
+
+    @pl.when(jnp.logical_and(i == 0, sub == 0))
     def _():
-        def prepare(place, carry):
-            start = pl.multiple_of(place * ROW, ROW)
-            q = q_ref[pl.ds(start, ROW), :]
-            do = do_ref[pl.ds(start, ROW), :]
-            for head in range(heads):
-                rows = slice(head * ROW, (head + 1) * ROW)
-                qm[place, rows, :] = jnp.where(head_lanes_turned(head), q, jnp.zeros_like(q))
-                dom[place, rows, :] = jnp.where(head_lanes_plain(head), do, jnp.zeros_like(do))
-            if first:
-                product = do.astype(F32) * o_ref[pl.ds(start, ROW), :].astype(F32)
-                high = product.astype(BF)
-                low = (product - high.astype(F32)).astype(BF)
-                head_row = lax.broadcasted_iota(jnp.int32, (8, 256), 0)
-                lane = lax.broadcasted_iota(jnp.int32, (8, 256), 1)
-                pick = jnp.where(lane // 64 == head_row, 1.0, 0.0).astype(BF)
-                sums = lax.dot_general(pick, high, NT, preferred_element_type=F32)
-                sums += lax.dot_general(pick, low, NT, preferred_element_type=F32)
-                delta[place] = sums[:heads, :]
-                dq[pl.ds(start, ROW), :] = jnp.zeros((ROW, 256), F32)
-            else:
-                dq[pl.ds(start, ROW), :] = dq_in[pl.ds(start, ROW), :]
-            return carry
-
-        lax.fori_loop(0, blocks, prepare, 0)
-
+        beside.begin()
+
+    @pl.when(sub == 0)
+    def _():
+        beside.rows_there(block)
+        q = q_ref[...]
+        do = beside.do[rows_here, :]
+        for head in range(heads):
+            part = slice(head * ROW, (head + 1) * ROW)
+            qm[block, part, :] = jnp.where(head_lanes_turned(head), q, jnp.zeros_like(q))
+            dom[block, part, :] = jnp.where(head_lanes_plain(head), do, jnp.zeros_like(do))
+        product = do.astype(F32) * o_ref[...].astype(F32)
+        high = rounded(product)
+        low = rounded(product - high.astype(F32))
+        head_row = lax.broadcasted_iota(jnp.int32, (8, 256), 0)
+        lane = lax.broadcasted_iota(jnp.int32, (8, 256), 1)
+        pick = jnp.where(lane // 64 == head_row, 1.0, 0.0).astype(BF)
+        sums = lax.dot_general(pick, high, NT, preferred_element_type=F32)
+        sums += lax.dot_general(pick, low, NT, preferred_element_type=F32)
+        delta[block] = sums[:heads, :]
+        dq[rows_here, :] = jnp.zeros((ROW, 256), F32)
+
+    beside.poll(unit)
     key_row = lax.broadcasted_iota(jnp.int32, (KEYS, ROW), 0)
     query_col = lax.broadcasted_iota(jnp.int32, (KEYS, ROW), 1)
-    block = picked_block(step, chosen)
-
-    def key_part(sub, carry):
-        inner = pl.multiple_of(sub * KEYS, KEYS)
-        k = k_ref[pl.ds(inner, KEYS), :]
-        v = v_ref[pl.ds(inner, KEYS), :]
+    inner = pl.multiple_of(sub * KEYS, KEYS)
+    k = k_ref[pl.ds(inner, KEYS), :]
+    v = v_ref[pl.ds(inner, KEYS), :]
+    for head in range(heads):
+        km[head] = jnp.where(head_lanes_turned(head), k, jnp.zeros_like(k))
+    dk[...] = jnp.zeros_like(dk)
+    dv[...] = jnp.zeros_like(dv)
+
+    def query_part(place, diagonal):
+        rows = rows_at(place)
         for head in range(heads):
-            km[head] = jnp.where(head_lanes_turned(head), k, jnp.zeros_like(k))
-        dk[...] = jnp.zeros_like(dk)
-        dv[...] = jnp.zeros_like(dv)
-
-        def query_part(query_block, diagonal):
-            place = query_block
-            rows = pl.ds(pl.multiple_of(place * ROW, ROW), ROW)
-            for head in range(heads):
-                part = slice(head * ROW, (head + 1) * ROW)
-                st = lax.dot_general(k, qm[place, part, :], NT, preferred_element_type=F32)
-                dp = lax.dot_general(v, dom[place, part, :], NT, preferred_element_type=F32)
-                p = jnp.exp2(st - l_ref[place, head : head + 1, :])
-                if diagonal:
-                    p = jnp.where(key_row + inner <= query_col, p, 0.0)
-                ds = p * (dp - delta[place, head : head + 1, :])
-                pt[:, part] = p.astype(BF)
-                dst[:, part] = ds.astype(BF)
-            dv[...] += lax.dot_general(pt[...], dom[place], NN, preferred_element_type=F32)
-            dk[...] += lax.dot_general(dst[...], qm[place], NN, preferred_element_type=F32)
-            total = lax.dot_general(dst[:, 0:ROW], km[0], TN, preferred_element_type=F32)
-            for head in range(1, heads):
-                part = slice(head * ROW, (head + 1) * ROW)
-                total += lax.dot_general(dst[:, part], km[head], TN, preferred_element_type=F32)
-            dq[rows, :] += total
-
-        query_part(block, True)
-
-        def later(query_block, carry):
-            query_part(query_block, False)
-            return carry
-
-        lax.fori_loop(block + 1, blocks, later, 0)
-        cs = cos_ref[pl.ds(inner, KEYS), :]
-        sn = sin_ref[pl.ds(inner, KEYS), :]
-        d = dk[...] * (1.0 / LOG2E)
-        d1, d2 = d[:, :128], d[:, 128:]
-        dkv_ref[pl.ds(inner, KEYS), 0:128] = (d1 * cs + d2 * sn).astype(BF)
-        dkv_ref[pl.ds(inner, KEYS), 128:256] = (d2 * cs - d1 * sn).astype(BF)
-        dkv_ref[pl.ds(inner, KEYS), 256:512] = dv[...].astype(BF)
+            part = slice(head * ROW, (head + 1) * ROW)
+            st = lax.dot_general(k, qm[place, part, :], NT, preferred_element_type=F32)
+            dp = lax.dot_general(v, dom[place, part, :], NT, preferred_element_type=F32)
+            p = jnp.exp2(st - l_ref[place, head : head + 1, :])
+            if diagonal:
+                p = jnp.where(key_row + inner <= query_col, p, 0.0)
+            ds = p * (dp - delta[place, head : head + 1, :])
+            pt[:, part] = p.astype(BF)
+            dst[:, part] = ds.astype(BF)
+        dv[...] += lax.dot_general(pt[...], dom[place], NN, preferred_element_type=F32)
+        dk[...] += lax.dot_general(dst[...], qm[place], NN, preferred_element_type=F32)
+        total = lax.dot_general(dst[:, 0:ROW], km[0], TN, preferred_element_type=F32)
+        for head in range(1, heads):
+            part = slice(head * ROW, (head + 1) * ROW)
+            total += lax.dot_general(dst[:, part], km[head], TN, preferred_element_type=F32)
+        dq[rows, :] += total
+
+    query_part(block, True)
+
+    def later(query_block, carry):
+        beside.poll(unit + query_block - block)
+        query_part(query_block, False)
         return carry
 
-    lax.fori_loop(0, ROW // KEYS, key_part, 0)
-
-    @pl.when(step == pl.num_programs(0) - 1)
+    lax.fori_loop(block + 1, blocks, later, 0)
+    table = pl.ds(pl.multiple_of(block * ROW + inner, KEYS), KEYS)
+    cs, sn = beside.cs[table, :], beside.sn[table, :]
+    d = dk[...] * (1.0 / LOG2E)
+    d1, d2 = d[:, :128], d[:, 128:]
+    dkv_ref[pl.ds(inner, KEYS), 0:128] = rounded(d1 * cs + d2 * sn)
+    dkv_ref[pl.ds(inner, KEYS), 128:256] = rounded(d2 * cs - d1 * sn)
+    dkv_ref[pl.ds(inner, KEYS), 256:512] = rounded(dv[...])
+
+    @pl.when(jnp.logical_and(i == 7, sub == 1))
     def _():
         def finish(place, carry):
-            rows = pl.ds(pl.multiple_of(place * ROW, ROW), ROW)
-            if not last:
-                dq_out[rows, :] = dq[rows, :]
-            else:
-                cs = all_cos[rows, :]
-                sn = all_sin[rows, :]
-                d = dq[rows, :] * 0.125
-                d1, d2 = d[:, :128], d[:, 128:]
-                dq_out[rows, 0:128] = (d1 * cs + d2 * sn).astype(BF)
-                dq_out[rows, 128:256] = (d2 * cs - d1 * sn).astype(BF)
+            rows = rows_at(place)
+            cs, sn = beside.cs[rows, :], beside.sn[rows, :]
+            d = dq[rows, :] * 0.125
+            d1, d2 = d[:, :128], d[:, 128:]
+            beside.do[rows, 0:128] = rounded(d1 * cs + d2 * sn)
+            beside.do[rows, 128:256] = rounded(d2 * cs - d1 * sn)
             return carry
 
         lax.fori_loop(0, blocks, finish, 0)
-
-
-def attend_back(me, q, k, v, do, o, level, cos, sin, chosen, last, earlier):
+        copy = pltpu.make_async_copy(beside.do, dq_out, beside.own_sem.at[4])
+        copy.start()
+        copy.wait()
+        beside.end()
+
+
+def attend_back(q, k, v, o, level, heads_own, parts, gate_up, down, residual, cos, sin):
     length = q.shape[0]
     blocks = length // ROW
-
-    def place(step, me):
-        return picked_block(step, chosen)
-
-    def whole(width):
-        return pl.BlockSpec((length, width), lambda step, me: (0, 0))
+    dma = pltpu.SemaphoreType.DMA
+    anywhere = pl.BlockSpec(memory_space=pl.ANY)
 
     def key_spec(width):
-        return pl.BlockSpec((ROW, width), lambda step, me: (place(step, me), 0))
-
-    head_rows = pl.BlockSpec((blocks, 4, ROW), lambda step, me: (0, 0, 0))
-    out_specs = [key_spec(512), whole(256)]
-    out_shape = [
-        jax.ShapeDtypeStruct((length, 512), BF),
-        jax.ShapeDtypeStruct((length, 256), BF if last else F32),
-    ]
-    if not earlier:
-        more = [(whole(256), o)]
-        out_specs.append(head_rows)
-        out_shape.append(jax.ShapeDtypeStruct((blocks, 4, ROW), F32))
-    else:
-        delta, dq, dkv = earlier
-        more = [(whole(128), cos), (whole(128), sin)] if last else []
-        more += [(head_rows, delta), (whole(256), dq), (pl.BlockSpec(memory_space=pl.ANY), dkv)]
-    grid = pltpu.PrefetchScalarGridSpec(
-        num_scalar_prefetch=1,
-        grid=(len(chosen),),
-        in_specs=[
-            whole(256),
-            key_spec(256),
-            key_spec(256),
-            whole(256),
-            head_rows,
-            key_spec(128),
-            key_spec(128),
-        ]
-        + [spec for spec, _ in more],
-        out_specs=out_specs,
+        return pl.BlockSpec((ROW, width), lambda i, sub: (7 - i, 0))
+
+    return pl.pallas_call(
+        attend_back_kernel,
+        grid=(blocks, 2),
+        in_specs=[key_spec(256)] * 4
+        + [pl.BlockSpec((blocks, 4, ROW), lambda i, sub: (0, 0, 0))]
+        + [anywhere] * 7,
+        out_specs=[key_spec(512)] + [anywhere] * 4,
+        out_shape=[
+            jax.ShapeDtypeStruct((length, 512), BF),
+            jax.ShapeDtypeStruct((length, 256), BF),
+            jax.ShapeDtypeStruct((2, 512, 2048), BF),
+            jax.ShapeDtypeStruct((2, 1024, 512), BF),
+            jax.ShapeDtypeStruct((ROW, 2048), BF),
+        ],
         scratch_shapes=[
             pltpu.VMEM((blocks, 4 * ROW, 256), BF),
             pltpu.VMEM((blocks, 4 * ROW, 256), BF),
+            pltpu.VMEM((blocks, 4, ROW), F32),
             pltpu.VMEM((length, 256), F32),
             pltpu.VMEM((KEYS, 256), F32),
             pltpu.VMEM((KEYS, 256), F32),
             pltpu.VMEM((4, KEYS, 256), BF),
             pltpu.VMEM((KEYS, 4 * ROW), BF),
             pltpu.VMEM((KEYS, 4 * ROW), BF),
+            pltpu.VMEM((2, 1024, 512), BF),
+            pltpu.VMEM((2, 1024, 512), BF),
+            pltpu.VMEM((length, 256), BF),
+            pltpu.VMEM((length, 128), F32),
+            pltpu.VMEM((length, 128), F32),
+            pltpu.VMEM((4, ROW, 2048), BF),
+            pltpu.VMEM((ROW, 2048), BF),
+            pltpu.VMEM((ROW, 2048), BF),
+            pltpu.VMEM((HALF, 2048), BF),
+            pltpu.VMEM((HALF, 2048), BF),
+            pltpu.VMEM((4, 256, 2048), BF),
+            pltpu.VMEM((2, 256, 2048), BF),
+            pltpu.VMEM((HALF, 2048), F32),
+            dma((8,)),
+            dma((8,)),
+            dma((4,)),
+            dma((4,)),
+            dma((8,)),
+            dma((8,)),
+            dma((6,)),
+            dma((6,)),
+            dma((6,)),
+            dma((3, 2)),
+            dma((2,)),
+            dma((5,)),
         ],
-    )
-    return pl.pallas_call(
-        lambda *refs: attend_back_kernel(chosen, not earlier, last, *refs),
-        grid_spec=grid,
-        out_shape=out_shape,
-        input_output_aliases={7 + len(more): 0} if earlier else {},
-        compiler_params=pltpu.CompilerParams(vmem_limit_bytes=62 * 2**20),
+        compiler_params=pltpu.CompilerParams(
+            collective_id=7, has_side_effects=True, vmem_limit_bytes=63 * 2**20
+        ),
         cost_estimate=pl.CostEstimate(
-            flops=19 * 10**9 * len(chosen), bytes_accessed=20 * 2**20, transcendentals=0
+            flops=19 * 10**9 * blocks, bytes_accessed=20 * 2**20, transcendentals=0
         ),
-    )(me, q, k, v, do, level, cos, sin, *[value for _, value in more])
+    )(q, k, v, o, level, heads_own, parts, gate_up, down, residual, cos, sin)
 
 
 def ring_shards(
@@ -1444,7 +1745,6 @@
     y, c, h, l, x = (lax.axis_index(name) for name in AXES)
     own = 4 * c + 2 * l + x
     plain_y, plain_c, straight = y == 0, c == 0, c == h
-    idle = jnp.zeros((1,), jnp.int32)
 
     def both_y(mine, other, axis):
         return jnp.where(
@@ -1534,11 +1834,8 @@
     gate_up_grad = lax.dot_general(
         normed_second, grad_gate_up, TN, preferred_element_type=F32
     ).astype(BF)
-    gate_up_y = scatter_y(gate_up_grad.reshape(4, 512, 2048))
     down_grad = lax.dot_general(activation, grad_out, TN, preferred_element_type=F32).astype(BF)
-    down_y = scatter_y(down_grad.reshape(1024, 4, 512).transpose(1, 0, 2))
-    layer_own = residual + product_scatter(activation, down_weight, NN, 4)
-    layer_output = swap_ch(layer_own.astype(BF))
+    layer_parts = jnp.dot(activation, down_weight, preferred_element_type=F32).astype(BF)
 
     def norm_grad(values, scale, gain, grad):
         scaled = grad * gain
@@ -1552,22 +1849,12 @@
     )
     residual_grad = residual_grad + grad_rows
     residual_low = residual_grad.astype(BF)
-    grad_heads = lax.dot_general(residual_low, out_weight, NT, preferred_element_type=F32)
-    grad_attended = lax.all_to_all(
-        grad_heads.astype(BF).reshape(ROW, 8, 256).transpose(1, 0, 2), RING, 0, 0
-    ).reshape(8 * ROW, 256)
-
-    def back(zero, chosen, last, earlier):
-        grad_kv, grad_q, *delta = attend_back(
-            idle + zero.astype(jnp.int32),
-            queries, keys, values, grad_attended, attended, level, cosine, sine, chosen, last, earlier,
-        )
-        return (delta[0] if delta else earlier[0], grad_q, grad_kv)
-
-    earlier = back(mark(gate_up_y[1]), (0, 7, 1, 6), False, ())
-    gate_up_ch = scatter_ch(*gate_up_y)
-    down_ch = scatter_ch(*down_y)
-    _, grad_q, grad_kv = back(mark(*gate_up_ch[1:]), (2, 5, 3, 4), True, earlier)
+    grad_heads = lax.dot_general(residual_low, out_weight, NT, preferred_element_type=F32).astype(BF)
+    grad_kv, grad_q, gate_up_sums, down_sums, layer_output = attend_back(
+        queries, keys, values, attended, level, grad_heads, layer_parts, gate_up_grad, down_grad, residual, cosine, sine
+    )
+    gate_up_grad_own = gate_up_sums[0].astype(F32) + gate_up_sums[1].astype(F32)
+    down_grad_own = down_sums[0].astype(F32) + down_sums[1].astype(F32)
 
     grad_mixture = jnp.concatenate([grad_q, grad_kv], axis=1)
     grad_normed_first = product_scatter(grad_mixture, qkv_weight, NT, 5)
@@ -1579,8 +1866,6 @@
     out_y = scatter_y(out_grad.reshape(256, 4, 512).transpose(1, 0, 2))
     qkv_grad_own = scatter_own(*scatter_ch(*qkv_y))
     out_grad_own = scatter_own(*scatter_ch(*out_y))
-    gate_up_grad_own = scatter_own(*gate_up_ch)
-    down_grad_own = scatter_own(*down_ch)
 
     input_back, gain_first_part = norm_grad(rows_in, scale_first, gain_first, grad_normed_first)
     input_grad = swap_ch((residual_grad + input_back).astype(BF)).astype(F32)

time: 1440 us -> 1450 us (level)
  Pallas kernels: 907 us -> 1050 us
  waiting for transfers between devices: 135 us -> 46.2 us
  starting transfers between devices: 81.1 us -> 51.6 us
  matrix products: 140 us -> 166 us
  other arithmetic: 109 us -> 83 us
    pallas_call x2 -> x1, Pallas kernels: 144 us -> 234 us  [attend_back(): pl.pallas_call(attend_back_kernel, grid=(blocks, 2), in_specs=[key_spec(2...]
    ppermute x29 -> x20, waiting for transfers between devices: 135 us -> 46.2 us  [move(): return lax.ppermute(values, AXES, device_pairs(target))]
    pallas_call x3 -> x2, Pallas kernels: 274 us -> 332 us  [product_scatter(): pl.pallas_call(lambda *refs: scatter_kernel(dims, *refs), in_specs=[anywh...]
    ppermute x29 -> x20, starting transfers between devices: 76.7 us -> 51.6 us  [move(): return lax.ppermute(values, AXES, device_pairs(target))]
    dot_general x0 -> x1, matrix products: none -> 22.3 us  [ring_shards(): jnp.dot(activation, down_weight, preferred_element_type=F32).astype(BF)]
  transfers between devices with their start and end apart: 31 -> 21, of which waited for: 8 -> 4; matrix products, arithmetic and copies ran while one was open for 9% -> 6% of each run, Pallas kernels for 17% -> 17%
where the time goes in v4:
time: 1450 us; the launch traced here: 1440 us
  Pallas kernels  1050 us (72%)
  matrix products  166 us (11%)
  other arithmetic  83 us (6%)
  starting transfers between devices  51.6 us (4%)
  waiting for transfers between devices  46.2 us (3%)
  local copies, waits for them, and re-layouts  25.1 us (2%)
  between operations  17.3 us (1%)
    pallas_call x2, Pallas kernels, product_scatter(): pl.pallas_call(lambda *refs: scatter_kernel(dims, *refs), in_specs=[anywh...  332 us
    pallas_call x2, Pallas kernels, gather_product(): pl.pallas_call(lambda *refs: gather_kernel(finish, beside, inputs, len(ex...  253 us
    pallas_call x1, Pallas kernels, attend_back(): pl.pallas_call(attend_back_kernel, grid=(blocks, 2), in_specs=[key_spec(2...  234 us
    pallas_call x1, Pallas kernels, attend(): pl.pallas_call(attend_kernel, grid=(blocks, 4), in_specs=[pl.BlockSpec((R...  232 us
    ppermute x20, starting transfers between devices, move(): return lax.ppermute(values, AXES, device_pairs(target))  51.6 us
    ppermute x20, waiting for transfers between devices, move(): return lax.ppermute(values, AXES, device_pairs(target))  46.2 us
    dot_general x1, matrix products, ring_shards(): lax.dot_general(normed_second, grad_gate_up, TN, preferred_element_type=F32)  44.6 us
  transfers between devices with their start and end apart: 21, of which 4 were waited for; matrix products, arithmetic and copies ran while one was open for 6% of the time, Pallas kernels for 17%

profile of v4, /device:TPU:0, one launch (start us, length us, event | category | flops | bytes accessed | tf_op | source)
XLA Modules:
  0.0 1439.0 jit_solution(12957144297975802045)
XLA Ops:
  11.3 4.4 collective-permute-start.4
  36.3 9.3 multiply_sine_fusion
  48.0 133.7 %shard_map.354 = (bf16[4096,2048]{1,0:T(8,128)(2,1)}, bf16[4096,256]{1,0:T(8,128)(2,1)}, bf16[4096,256]{1,0:T(8,128)(2,1)}, bf16[4096,256]{1,0:T(8,128)(2,1)}, b...) custom-call(bf16[512,2048]{1,0:T(8,128)(2,1)} %fusion.10.refs_0_, f32[4096,128]{1,0:T(8,128)} %get-tuple-element.98.refs_1_.refs_5_, ...), custom_call_target="tpu_custom_call" | custom-call | flops 80000000000 | bytes 31457280 | tf_op jit(solution)/shard_map/pallas_call | solution.py:765
  181.7 231.7 %shard_map.355 = (bf16[4096,256]{1,0:T(8,128)(2,1)S(1)}, f32[8,4,512]{2,1,0:T(4,128)S(1)}, bf16[2048,2048]{1,0:T(8,128)(2,1)}, bf16[2048,2048]{1,0:T(8,128)(2,1)...) custom-call(bf16[4096,256]{1,0:T(8,128)(2,1)} %get-tuple-element.44.q_ref, ...), custom_call_target="tpu_custom_call" | custom-call | flops 112000000000 | bytes 10485760 | tf_op jit(solution)/shard_map/pallas_call | solution.py:1208
  413.4 8.6 multiply_reduce_fusion.2
  424.7 118.8 %shard_map.356 = (bf16[4096,2048]{1,0:T(8,128)(2,1)}, bf16[4096,1024]{1,0:T(8,128)(2,1)}, bf16[4096,1024]{1,0:T(8,128)(2,1)}, bf16[4096,1024]{1,0:T(8,128)(2,1)}, bf16[1024,2048]{1,0:T(8,128)(2,1)}) custom-call(bf16[512,2048]{1,0:T(8,128)(2,1)} %multiply_convert_fusion.refs_0_, bf16[2048,2048]{1,0:T(8,128)(2,1)} %get-tuple-element.53.refs_1_, ...), custom_call_target="tpu_custom_call" | custom-call | flops 80000000000 | bytes 31457280 | tf_op jit(solution)/shard_map/pallas_call | solution.py:765
  543.5 25.1 %convolution_convert_fusion.3.refs_3_ = bf16[1024,2048]{1,0:T(8,128)(2,1)} fusion(bf16[4096,1024]{1,0:T(8,128)(2,1)} %get-tuple-element.57, bf16[4096,2048]{1,0:T(8,128)(2,1)} %get-tuple-element.52), kind=kOutput, calls=%fused_computation.47 | convolution fusion | flops 17181966336 | bytes 29360128 | tf_op jit(solution)/shard_map/dot_general | solution.py:1837
  568.6 23.7 %fusion.67 = f32[4096,1024]{1,0:T(8,128)} fusion(bf16[4096,2048]{1,0:T(8,128)(2,1)} %get-tuple-element.52, bf16[1024,2048]{1,0:T(8,128)(2,1)} %get-tuple-element.54), kind=kOutput, calls=%fused_computation.163 | convolution fusion | flops 17179869184 | bytes 37748736 | tf_op jit(solution)/shard_map/dot_general | solution.py:1827
  592.4 22.3 %convolution_convert_fusion.refs_1_ = bf16[4096,2048]{1,0:T(8,128)(2,1)} fusion(bf16[4096,1024]{1,0:T(8,128)(2,1)S(1)} %bitcast.82, bf16[1024,2048]{1,0:T(8,128)(2,1)} %get-tuple-element.54), kind=kOutput, calls=%fused_computation.12 | convolution fusion | flops 17188257792 | bytes 29360128 | tf_op jit(solution)/shard_map/dot_general | solution.py:1838
  614.7 12.2 fusion.5
  632.8 6.8 pad_maximum_fusion.refs_0_
  639.6 93.4 %shard_map.357 = f32[512,2048]{1,0:T(8,128)} custom-call(bf16[4096,2048]{1,0:T(8,128)(2,1)} %pad_maximum_fusion.refs_0_, bf16[2048,2048]{1,0:T(8,128)(2,1)} %get-tuple-element.53.refs_1_), custom_call_target="tpu_custom_call" | custom-call | flops 80000000000 | bytes 31457280 | tf_op jit(solution)/shard_map/pallas_call | solution.py:891
  738.5 11.3 convolution_convert_fusion.6.refs_0_
  749.8 6.9 convolution_convert_fusion.1
  756.6 44.6 %convolution_convert_fusion.2.refs_2_ = bf16[2048,2048]{1,0:T(8,128)(2,1)} fusion(bf16[4096,2048]{1,0:T(8,128)(2,1)} %get-tuple-element.58, bf16[4096,1024]{1,0:T(8,128)(2,1)} %copy-done.10, bf16[4096,1024]{1,0:T(8,128)(2,1)} %copy-done.9), kind=kOutput, calls=%fused_computation.19 | convolution fusion | flops 34397487104 | bytes 41943040 | tf_op jit(solution)/shard_map/dot_general | solution.py:1834
  801.2 233.6 %shard_map.358 = (bf16[4096,512]{1,0:T(8,128)(2,1)}, bf16[4096,256]{1,0:T(8,128)(2,1)}, bf16[2,512,2048]{2,1,0:T(8,128)(2,1)}, bf16[2,1024,512]{2,1,0:T(8,128)(2,1)}, bf16[512,2048]{1,0:T(8,128)(2,1)}) custom-call(bf16[4096,256]{1,0:T(8,128)(2,1)} %get-tuple-element.44.q_ref, bf16[4096,256]{1,0:T(8,128)(2,1)} %get-tuple-element.45.k_ref, ...), custom_call_target="tpu_custom_call" | custom-call | flops 152000004096 | bytes 20971520 | tf_op jit(solution)/shard_map/pallas_call | solution.py:1665
  1038.0 4.5 constant_dynamic-update-slice_fusion.refs_0_
  1042.5 238.8 %shard_map.359 = f32[512,2048]{1,0:T(8,128)} custom-call(bf16[4096,768]{1,0:T(8,128)(2,1)} %constant_dynamic-update-slice_fusion.refs_0_, bf16[2048,768]{1,0:T(8,128)(2,1)} %get-tuple-element.62.refs_1_), custom_call_target="tpu_custom_call" | custom-call | flops 80000000000 | bytes 31457280 | tf_op jit(solution)/shard_map/pallas_call | solution.py:891
  1287.0 17.7 %convolution_convert_fusion.4.clone.5 = bf16[2048,768]{1,0:T(8,128)(2,1)S(1)} fusion(bf16[4096,2048]{1,0:T(8,128)(2,1)} %get-tuple-element.63, bf16[4096,768]{1,0:T(8,128)(2,1)S(1)} %copy-done.37), kind=kOutput, calls=%fused_computation.64.clone.clone.clone.2 | convolution fusion | flops 12886474752 | bytes 26214400 | tf_op jit(solution)/shard_map/dot_general | solution.py:1861
  1317.2 17.3 %collective-permute-start.6 = (bf16[512,2048]{1,0:T(8,128)(2,1)}, bf16[512,2048]{1,0:T(8,128)(2,1)}, u32[]{:S(2)}, u32[]{:S(2)}) collective-permute-start(bf16[512,2048]{1,0:T(8,128)(2,1)} %fusion.15), channel_id=1, source_target_pairs={{0,0},{1,1},{2,2},{3,3},{4,8},{5,9},{6,10},{7,11},{8,4},{9,5},{10,... | collective-permute-start | bytes 6291464 | tf_op jit(solution)/shard_map/ppermute | solution.py:354
  1345.9 4.6 collective-permute-start.18
  1352.9 14.8 %collective-permute-done.18 = f32[2,2048]{1,0:T(2,128)S(1)} collective-permute-done((f32[2,2048]{1,0:T(2,128)S(1)}, f32[2,2048]{1,0:T(2,128)S(1)}, u32[]{:S(2)}, u32[]{:S(2)}) %collective-permute-start.18) | collective-permute-done | bytes 16416 | tf_op jit(solution)/shard_map/ppermute | solution.py:354
  1388.8 19.8 %collective-permute-done.8 = bf16[512,768]{1,0:T(8,128)(2,1)} collective-permute-done((bf16[512,768]{1,0:T(8,128)(2,1)S(1)}, bf16[512,768]{1,0:T(8,128)(2,1)}, u32[]{:S(2)}, u32[]{:S(2)}) %collective-permute-start.8) | collective-permute-done | bytes 786464 | tf_op jit(solution)/shard_map/ppermute | solution.py:354
  1417.5 10.7 collective-permute-done.12
  (238 shorter events, 107.2 us)
Async XLA Ops:
  7.2 1372.5 %reduce-scatter.2.cloned.1.call-start = ((), (), s32[]{:S(2)}) async-start(), calls=%async_computation.1 | async-start | bytes 9437184 | tf_op jit(solution)/shard_map/reduce_scatter | solution.py:1865
  7.9 22.7 %collective-permute-start.1 = (bf16[2,512]{1,0:T(2,128)(2,1)S(1)}, bf16[2,512]{1,0:T(2,128)(2,1)S(1)}, u32[]{:S(2)}, u32[]{:S(2)}) collective-permute-start(bf16[2,512]{1,0:T(2,128)(2,1)S(1)} %convert_element_type.172), channel_id=1, source_target_pairs={{0,8},{1,9},{2,10},{3,11},{4,12},{5,13},{6,14},{7,15},{8,0},{9,1},... | collective-permute-start | bytes 6152 | tf_op jit(solution)/shard_map/ppermute | solution.py:354
  8.4 37.2 %collective-permute-start = (bf16[512,2048]{1,0:T(8,128)(2,1)}, bf16[512,2048]{1,0:T(8,128)(2,1)S(1)}, u32[]{:S(2)}, u32[]{:S(2)}) collective-permute-start(bf16[512,2048]{1,0:T(8,128)(2,1)} %param.19), channel_id=1, source_target_pairs={{0,0},{1,1},{2,2},{3,3},{4,8},{5,9},{6,10},{7,11},{8,4},{9,5},{10,... | collective-permute-start | bytes 6291464 | tf_op jit(solution)/shard_map/ppermute | solution.py:354
  11.3 14.3 collective-permute-start.4
  15.7 20.6 %collective-permute-start.3 = (s32[4096]{0:T(1024)}, s32[4096]{0:T(1024)S(1)}, u32[]{:S(2)}, u32[]{:S(2)}) collective-permute-start(s32[4096]{0:T(1024)} %param.22), channel_id=1, source_target_pairs={{0,8},{1,9},{2,10},{3,11},{4,12},{5,13},{6,14},{7,15},{8,0},{9,1},... | collective-permute-start | bytes 49160 | tf_op jit(solution)/shard_map/ppermute | solution.py:354
  26.2 3.7 collective-permute-start.5
  30.6 5.0 collective-permute-start.2
  1042.5 238.8 %copy-start.8 = (bf16[512,2048]{1,0:T(8,128)(2,1)S(1)}, bf16[512,2048]{1,0:T(8,128)(2,1)}, u32[]{:S(2)}) copy-start(bf16[512,2048]{1,0:T(8,128)(2,1)} %copy-done.6) | copy-start | bytes 6291460
  1042.5 238.9 %copy-start.41 = (f32[1,2048]{1,0:T(1,128)S(1)}, f32[1,2048]{1,0:T(1,128)}, u32[]{:S(2)}) copy-start(f32[1,2048]{1,0:T(1,128)} %copy-done.40) | copy-start | bytes 24580
  1042.5 238.9 %copy-start.48 = (f32[512]{0:T(512)S(1)}, f32[512]{0:T(512)}, u32[]{:S(2)}) copy-start(f32[512]{0:T(512)} %copy-done.47) | copy-start | bytes 6148
  1285.0 49.4 %collective-permute-start.15 = (f32[2,2048]{1,0:T(2,128)S(1)}, f32[2,2048]{1,0:T(2,128)S(1)}, u32[]{:S(2)}, u32[]{:S(2)}) collective-permute-start(f32[2,2048]{1,0:T(2,128)S(1)} %pad_maximum_fusion.3), channel_id=1, source_target_pairs={{0,1},{1,0},{2,3},{3,2},{4,5},{5,4},{6,7},{7,6},{8,9},{9,8},{10,11... | collective-permute-start | bytes 49160 | tf_op jit(solution)/shard_map/ppermute | solution.py:354
  1309.5 59.3 %collective-permute-start.7 = (bf16[2,512,768]{2,1,0:T(8,128)(2,1)}, bf16[2,512,768]{2,1,0:T(8,128)(2,1)}, u32[]{:S(2)}, u32[]{:S(2)}) collective-permute-start(bf16[2,512,768]{2,1,0:T(8,128)(2,1)} %constant_dynamic-slice_fusion.2), channel_id=1, source_target_pairs={{0,16},{1,17},{2,18},{3,19},{4,20},{5,21},{6,22},{7,23},{8,24},{9,... | collective-permute-start | bytes 4718600 | tf_op jit(solution)/shard_map/ppermute | solution.py:354
  1317.2 67.4 %collective-permute-start.6 = (bf16[512,2048]{1,0:T(8,128)(2,1)}, bf16[512,2048]{1,0:T(8,128)(2,1)}, u32[]{:S(2)}, u32[]{:S(2)}) collective-permute-start(bf16[512,2048]{1,0:T(8,128)(2,1)} %fusion.15), channel_id=1, source_target_pairs={{0,0},{1,1},{2,2},{3,3},{4,8},{5,9},{6,10},{7,11},{8,4},{9,5},{10,... | collective-permute-start | bytes 6291464 | tf_op jit(solution)/shard_map/ppermute | solution.py:354
  1334.4 6.4 collective-permute-start.16
  1340.9 5.0 collective-permute-start.17
  1345.9 21.9 %collective-permute-start.18 = (f32[2,2048]{1,0:T(2,128)S(1)}, f32[2,2048]{1,0:T(2,128)S(1)}, u32[]{:S(2)}, u32[]{:S(2)}) collective-permute-start(f32[2,2048]{1,0:T(2,128)S(1)} %add.264), channel_id=1, source_target_pairs={{0,4},{1,5},{2,6},{3,7},{4,0},{5,1},{6,2},{7,3},{8,12},{9,13},{10,... | collective-permute-start | bytes 49160 | tf_op jit(solution)/shard_map/ppermute | solution.py:354
  1367.7 11.3 collective-permute-start.19
  1371.6 17.2 %collective-permute-start.10 = (bf16[512,768]{1,0:T(8,128)(2,1)}, bf16[512,768]{1,0:T(8,128)(2,1)}, u32[]{:S(2)}, u32[]{:S(2)}) collective-permute-start(bf16[512,768]{1,0:T(8,128)(2,1)} %get-tuple-element.92), channel_id=1, source_target_pairs={{4,8},{5,9},{6,10},{7,11},{8,4},{9,5},{10,6},{11,7},{20,24},{21,25... | collective-permute-start | bytes 2359304 | tf_op jit(solution)/shard_map/ppermute | solution.py:354
  1373.1 35.5 %collective-permute-start.9 = (bf16[512,768]{1,0:T(8,128)(2,1)}, bf16[512,768]{1,0:T(8,128)(2,1)}, u32[]{:S(2)}, u32[]{:S(2)}) collective-permute-start(bf16[512,768]{1,0:T(8,128)(2,1)} %get-tuple-element.92), channel_id=1, source_target_pairs={{0,8},{1,9},{2,10},{3,11},{12,4},{13,5},{14,6},{15,7},{16,24},{17,... | collective-permute-start | bytes 2359304 | tf_op jit(solution)/shard_map/ppermute | solution.py:354
  1375.9 32.6 %collective-permute-start.8 = (bf16[512,768]{1,0:T(8,128)(2,1)S(1)}, bf16[512,768]{1,0:T(8,128)(2,1)}, u32[]{:S(2)}, u32[]{:S(2)}) collective-permute-start(bf16[512,768]{1,0:T(8,128)(2,1)S(1)} %get-tuple-element.91), channel_id=1, source_target_pairs={{4,0},{5,1},{6,2},{7,3},{8,12},{9,13},{10,14},{11,15},{20,16},{21,... | collective-permute-start | bytes 2359304 | tf_op jit(solution)/shard_map/ppermute | solution.py:354
  1382.7 29.6 %collective-permute-start.11 = (bf16[2,256,512]{2,1,0:T(8,128)(2,1)S(1)}, bf16[2,256,512]{2,1,0:T(8,128)(2,1)S(1)}, u32[]{:S(2)}, u32[]{:S(2)}) collective-permute-start(bf16[2,256,512]{2,1,0:T(8,128)(2,1)S(1)} %bitcast.68), channel_id=1, source_target_pairs={{0,16},{1,17},{2,18},{3,19},{4,20},{5,21},{6,22},{7,23},{8,24},{9,... | collective-permute-start | bytes 1572872 | tf_op jit(solution)/shard_map/ppermute | solution.py:354
  1412.5 15.7 %collective-permute-start.13 = (bf16[256,512]{1,0:T(8,128)(2,1)S(1)}, bf16[256,512]{1,0:T(8,128)(2,1)S(1)}, u32[]{:S(2)}, u32[]{:S(2)}) collective-permute-start(bf16[256,512]{1,0:T(8,128)(2,1)S(1)} %get-tuple-element.96), channel_id=1, source_target_pairs={{0,8},{1,9},{2,10},{3,11},{12,4},{13,5},{14,6},{15,7},{16,24},{17,... | collective-permute-start | bytes 786440 | tf_op jit(solution)/shard_map/ppermute | solution.py:354
  1414.1 14.1 collective-permute-start.14
  1414.8 13.4 collective-permute-start.12
  (68 other events, 1221.7 us)
Sparse Core Ops, SparseCore 0:
  1038.1 252.5 reduce-scatter.1

commit v5 on v4

--- a/solution.py
+++ b/solution.py
@@ -788,7 +788,11 @@
     )(own, *given, *anywhere_given)
 
 
-def scatter_kernel(dims, a_ref, w_ref, out_ref, abuf, mine, other, sums, ra, rb, near_x, near_l, send, recv, a_sem):
+def scatter_kernel(dims, beside, a_ref, w_ref, *refs):
+    given, refs = refs[:beside], refs[beside:]
+    out_ref, refs = refs[0], refs[1:]
+    more_outs, refs = refs[: 2 * beside], refs[2 * beside :]
+    abuf, mine, other, sums, ra, rb, near_x, near_l, send, recv, a_sem = refs[:11]
     me, partners = ring_position()
     to_x, to_l, to_c = partners
     order = (7, 3, 5, 6, 1, 2, 4, 0)
@@ -799,7 +803,10 @@
         )
 
     load(0).start()
-    enter_ring(partners)
+    enter_ring(wide_partners() if beside else partners)
+    if beside:
+        tail = WeightTail(given + more_outs + refs[11:])
+        tail.begin()
 
     def copy(index, source, target, partner):
         return pltpu.make_async_remote_copy(
@@ -873,6 +880,8 @@
                 out_ref[:, here] = value + other[0, :, here].astype(F32)
 
             product(index, store)
+    if beside:
+        tail.run()
     for part, first, second in ((top, 6, 9), (bottom, 8, 7)):
         copies[first].wait_recv()
         copies[second].wait_recv()
@@ -881,18 +890,61 @@
         )
     for each in copies:
         each.wait_send()
-
-
-def product_scatter(a, weight, dims, number):
+    if beside:
+        tail.end()
+
+
+class WeightTail:
+    def __init__(self, refs):
+        self.grad, self.totals, self.landing, stage, result, y_sems, z_sems, stage_sems = refs
+        self.y, _, _, _ = places()
+        self.names = [("Q", 0, 0), ("Q", 1, 0)]
+        self.pieces = PieceSums(
+            self.names,
+            self.piece,
+            lambda name: self.landing.at[name[1]],
+            lambda name, h: self.totals.at[h],
+            y_sems,
+            z_sems,
+        )
+        self.sums = Sums(stage, result, stage_sems)
+        for name in self.names:
+            self.sums.item(
+                0,
+                512,
+                [self.piece(name, self.y), self.landing.at[name[1]]],
+                self.pieces.sends(name),
+                [lambda name=name: self.pieces.over_y(name).wait_recv()],
+            )
+
+    def piece(self, name, y):
+        return self.grad.at[pl.ds(pl.multiple_of((2 * y + name[1]) * 512, 512), 512)]
+
+    def begin(self):
+        for name in self.names:
+            self.pieces.over_y(name).start()
+
+    def run(self):
+        for k in range(2):
+            self.sums.load(k)
+            self.sums.add(k)
+
+    def end(self):
+        self.sums.last_sent()
+        self.pieces.end()
+
+
+def product_scatter(a, weight, dims, number, *grad):
     anywhere = pl.BlockSpec(memory_space=pl.ANY)
     vmem = pl.BlockSpec(memory_space=pltpu.VMEM)
     depth = a.shape[1]
     width = weight.shape[0] if dims == NT else weight.shape[1]
     return pl.pallas_call(
-        lambda *refs: scatter_kernel(dims, *refs),
-        in_specs=[anywhere, vmem],
-        out_specs=vmem,
-        out_shape=jax.ShapeDtypeStruct((ROW, width), F32),
+        lambda *refs: scatter_kernel(dims, len(grad), *refs),
+        in_specs=[anywhere, vmem] + [anywhere] * len(grad),
+        out_specs=[vmem] + [anywhere] * (2 * len(grad)),
+        out_shape=[jax.ShapeDtypeStruct((ROW, width), F32)]
+        + [jax.ShapeDtypeStruct((2, 512, 768), BF)] * (2 * len(grad)),
         scratch_shapes=[
             pltpu.VMEM((2, ROW, depth), BF),
             pltpu.VMEM((4, ROW, width), BF),
@@ -905,14 +957,22 @@
             pltpu.SemaphoreType.DMA((10,)),
             pltpu.SemaphoreType.DMA((10,)),
             pltpu.SemaphoreType.DMA((2,)),
-        ],
+        ]
+        + [
+            pltpu.VMEM((2, 2, 512, 768), BF),
+            pltpu.VMEM((2, 512, 768), BF),
+            pltpu.SemaphoreType.DMA((2, 2)),
+            pltpu.SemaphoreType.DMA((3, 2)),
+            pltpu.SemaphoreType.DMA((2, 5)),
+        ]
+        * len(grad),
         compiler_params=pltpu.CompilerParams(
             collective_id=number, has_side_effects=True, vmem_limit_bytes=58 * 2**20
         ),
         cost_estimate=pl.CostEstimate(
             flops=80 * 10**9, bytes_accessed=30 * 2**20, transcendentals=0
         ),
-    )(a, weight)
+    )(a, weight, *grad)
 
 
 def column_order():
@@ -1244,60 +1304,349 @@
 KEYS = 256
 
 
-HALF = ROW // 2
+class Sums:
+    def __init__(self, stage, result, stage_sems):
+        self.stage, self.result, self.stage_sems = stage, result, stage_sems
+        self.items = []
+
+    def item(self, due, rows, terms, sends, waits=(), extra=None, then=None):
+        self.items.append((due, rows, terms, sends, waits, extra, then))
+
+    def loads(self, k):
+        _, rows, terms, _, _, extra, _ = self.items[k]
+        turn = k % 2
+        copies = [
+            pltpu.make_async_copy(
+                term, self.stage.at[turn, index, pl.ds(0, rows)], self.stage_sems.at[turn, index]
+            )
+            for index, term in enumerate(terms)
+        ]
+        if extra is not None:
+            copies.append(pltpu.make_async_copy(extra[0], extra[1], self.stage_sems.at[turn, 4]))
+        return copies
+
+    def load(self, k):
+        for wait in self.items[k][4]:
+            wait()
+        for copy in self.loads(k):
+            copy.start()
+
+    def add(self, k):
+        _, rows, terms, sends, _, extra, then = self.items[k]
+        turn = k % 2
+        for copy in self.loads(k):
+            copy.wait()
+        if k >= 2:
+            self.sent(k - 2)
+        target = self.result.at[turn]
+        size = rows // 8
+
+        def chunk(index, carry):
+            here = pl.ds(pl.multiple_of(index * size, size), size)
+            total = self.stage[turn, 0, here, :].astype(F32)
+            for term in range(1, len(terms)):
+                total += self.stage[turn, term, here, :].astype(F32)
+            if extra is not None:
+                total += extra[1][here, :]
+            target[here, :] = rounded(total)
+            return carry
+
+        lax.fori_loop(0, 8, chunk, 0)
+        for here, away, local in sends(self.result.at[turn, pl.ds(0, rows)]):
+            self.either(here, away, local, "start")
+        if then is not None:
+            then()
+
+    def either(self, here, away, local, method):
+        if here is None:
+            getattr(away(), method)()
+            return
+
+        @pl.when(here)
+        def _():
+            getattr(local(), "wait" if method == "wait_send" else method)()
+
+        @pl.when(jnp.logical_not(here))
+        def _():
+            getattr(away(), method)()
+
+    def sent(self, k):
+        _, rows, _, sends, _, _, _ = self.items[k]
+        for here, away, local in sends(self.result.at[k % 2, pl.ds(0, rows)]):
+            self.either(here, away, local, "wait_send")
+
+    def poll(self, unit):
+        for k, item in enumerate(self.items):
+
+            @pl.when(unit == item[0])
+            def _(k=k):
+                self.load(k)
+
+            @pl.when(unit == item[0] + 1)
+            def _(k=k):
+                self.add(k)
+
+    def last_sent(self):
+        for k in range(len(self.items) - 2, len(self.items)):
+            self.sent(k)
+
+
+def half_columns(half):
+    return pl.ds(half * 1024, 1024)
+
+
+class RingSum:
+    def __init__(self, parts, size, core_land, far_land, core_sems, far_sems):
+        self.parts, self.size, self.core_land, self.far_land = parts, size, core_land, far_land
+        self.core_sems, self.far_sems = core_sems, far_sems
+        self.me, (self.to_x, self.to_l, self.to_c) = ring_position()
+
+    def block(self, slot):
+        return pl.ds(pl.multiple_of((self.me ^ slot) * self.size, self.size), self.size)
+
+    def core(self, slot):
+        return remote(
+            self.parts.at[self.block(slot | 4)],
+            self.core_land.at[slot],
+            self.core_sems.at[0, slot],
+            self.core_sems.at[1, slot],
+            self.to_c,
+        )
+
+    def begin(self):
+        for slot in (3, 1, 2, 0):
+            self.core(slot).start()
+
+    def far(self, index, source):
+        device = self.to_x if index in (0, 2, 4) else self.to_l
+        return remote(
+            source, self.far_land.at[index], self.far_sems.at[0, index], self.far_sems.at[1, index], device
+        )
+
+    def landed(self, index):
+        return lambda: self.far(index, self.far_land.at[index]).wait_recv()
+
+    def terms(self, slot, half):
+        return [
+            self.parts.at[self.block(slot), half_columns(half)],
+            self.core_land.at[slot, :, half_columns(half)],
+        ]
+
+    def add_to(self, sums, due, last_sends, extra):
+        def items():
+            core = lambda slot: (lambda: self.core(slot).wait_recv())
+            send = lambda index: (lambda source: [(None, lambda: self.far(index, source), None)])
+            yield 0, self.terms(3, 0), send(0), [core(3)], None
+            yield 1, self.terms(3, 1), send(1), [], None
+            yield 2, self.terms(1, 0), send(2), [core(1)], None
+            yield 3, self.terms(2, 1), send(3), [core(2)], None
+            yield 4, self.terms(1, 1) + [self.far_land.at[1]], send(4), [self.landed(1)], None
+            yield 5, self.terms(2, 0) + [self.far_land.at[0]], send(5), [self.landed(0)], None
+            yield (
+                6,
+                self.terms(0, 0) + [self.far_land.at[2], self.far_land.at[5]],
+                last_sends(0),
+                [core(0), self.landed(2), self.landed(5)],
+                extra(0),
+            )
+            yield (
+                7,
+                self.terms(0, 1) + [self.far_land.at[4], self.far_land.at[3]],
+                last_sends(1),
+                [self.landed(4), self.landed(3)],
+                extra(1),
+            )
+
+        return [
+            (due[index], self.size, terms, sends, waits, more) for index, terms, sends, waits, more in items()
+        ]
+
+    def end(self):
+        for slot in range(4):
+            self.core(slot).wait_send()
+
+
+class PieceSums:
+    def __init__(self, names, piece, landing, sums_at, y_sems, z_sems):
+        self.names, self.piece, self.landing, self.sums_at = names, piece, landing, sums_at
+        self.y_sems, self.z_sems = y_sems, z_sems
+        self.y, self.c, self.h, _ = places()
+
+    def core_of(self, name):
+        return name[1]
+
+    def over_y(self, name):
+        index = self.names.index(name)
+        return remote(
+            self.piece(name, 1 - self.y),
+            self.landing(name),
+            self.y_sems.at[0, index],
+            self.y_sems.at[1, index],
+            {"y": 1 - self.y},
+        )
+
+    def group(self, name):
+        groups = []
+        for each in self.names:
+            key = (each[0], each[2])
+            if key not in groups:
+                groups.append(key)
+        return groups.index((name[0], name[2])), groups
+
+    def over_z(self, name, h, source):
+        index = self.names.index(name)
+        target = self.sums_at(name, h)
+        return (
+            lambda: remote(
+                source,
+                target,
+                self.z_sems.at[0, index],
+                self.z_sems.at[1 + h, self.group(name)[0]],
+                {"c": self.core_of(name), "h": self.c},
+            ),
+            lambda: pltpu.make_async_copy(source, target, self.z_sems.at[0, index]),
+        )
+
+    def sends(self, name):
+        here = jnp.logical_and(self.core_of(name) == self.c, self.h == self.c)
+        return lambda source: [(here, *self.over_z(name, self.h, source))]
+
+    def end(self):
+        for name in self.names:
+            self.over_y(name).wait_send()
+        self.owned()
+
+    def owned(self):
+        seen = []
+        for name in self.names:
+            group, _ = self.group(name)
+            if group in seen:
+                continue
+            seen.append(group)
+            for h in range(2):
+                here = jnp.logical_and(h == self.h, self.c == self.h)
+
+                @pl.when(jnp.logical_not(here))
+                def _(name=name, h=h):
+                    self.over_z(name, h, self.sums_at(name, h))[0]().wait_recv()
 
 
 class BesideBack:
-    DUE = {"a": 8, "b": 9, "c": 11, "d": 12, "D0": 15, "e": 24, "f": 25, "D1": 27, "G0": 37, "g": 48, "h": 49, "G1": 51, "G2": 61, "G3": 70}
-
     def __init__(self, refs):
-        self.heads_own, self.parts, self.gate_up, self.down, self.residual, self.cos, self.sin = refs[:7]
-        self.gate_up_sums, self.down_sums, self.layer = refs[7:10]
+        self.heads_own, self.parts, self.gate_up, self.down, self.out, self.residual, self.cos, self.sin = refs[:8]
+        (
+            self.gate_up_sums,
+            self.down_sums,
+            self.out_sums,
+            self.layer,
+            core_land,
+            far_land,
+            self.y_land,
+            out_core_land,
+            out_far_land,
+            self.out_own,
+            self.out_y_land,
+        ) = refs[8:19]
         (
             self.do,
             self.cs,
             self.sn,
-            self.other,
-            self.near_x,
-            self.near_l,
-            self.ra,
-            self.rb,
-            self.land,
-            self.stage,
+            stage,
+            result,
             self.rest,
             self.row_send,
             self.row_recv,
-            self.core_send,
-            self.core_recv,
-            self.far_send,
-            self.far_recv,
-            self.y_send,
-            self.y_recv,
-            self.z_send,
-            self.z_recv,
-            self.stage_sem,
+            core_sems,
+            far_sems,
+            out_core_sems,
+            out_far_sems,
+            self.layer_sems,
+            y_sems,
+            z_sems,
+            self.out_sems,
+            out_y_sems,
+            out_z_sems,
+            stage_sems,
             self.own_sem,
-        ) = refs[10:]
+        ) = refs[19:]
         self.y, self.c, self.h, self.me = places()
-        _, (self.to_x, self.to_l, self.to_c) = ring_position()
-        self.names = list(self.DUE)
-        self.where = {
-            "a": (3, 0), "b": (3, 1), "c": (1, 0), "d": (2, 1), "e": (1, 1), "f": (2, 0), "g": (0, 0), "h": (0, 1)
-        }
-
-    def far(self, name):
-        top, bottom = pl.ds(0, HALF), pl.ds(HALF, HALF)
-        other = self.other
-        index = "abcdef".index(name)
-        source, target, device = (
-            (other.at[3, top], self.ra, self.to_x),
-            (other.at[3, bottom], self.rb, self.to_l),
-            (other.at[1, top], self.near_x.at[top], self.to_x),
-            (other.at[2, bottom], self.near_l.at[bottom], self.to_l),
-            (other.at[1, bottom], self.near_x.at[bottom], self.to_x),
-            (other.at[2, top], self.near_l.at[top], self.to_l),
-        )[index]
-        return remote(source, target, self.far_send.at[index], self.far_recv.at[index], device)
+        self.sums = Sums(stage, result, stage_sems)
+        self.layer_ring = RingSum(self.parts, ROW, core_land, far_land, core_sems, far_sems)
+        self.out_ring = RingSum(self.out, 256, out_core_land, out_far_land, out_core_sems, out_far_sems)
+        names = [("D", 0, 0), ("D", 1, 0), ("G", 0, 0), ("G", 0, 1), ("G", 1, 0), ("G", 1, 1)]
+        self.pieces = PieceSums(names, self.piece, lambda name: self.y_land.at[names.index(name)], self.sums_at, y_sems, z_sems)
+        self.names = names
+        out_names = [("O", 0, 0), ("O", 1, 0)]
+        self.out_pieces = PieceSums(out_names, None, None, self.sums_at, out_y_sems, out_z_sems)
+        work = self.layer_ring.add_to(
+            self.sums, (8, 9, 10, 11, 25, 26, 46, 47), self.layer_sends, self.residual_half
+        )
+        work += self.out_ring.add_to(
+            self.sums, (28, 29, 30, 31, 51, 52, 63, 64), self.out_sends, lambda half: None
+        )
+        for name, due in zip(names, (13, 24, 36, 48, 58, 69)):
+            work.append((due, ROW, [self.piece(name, self.y), self.y_land.at[names.index(name)]], self.pieces.sends(name), [self.arrived(name)], None))
+        work.sort(key=lambda item: item[0])
+        for item in work:
+            self.sums.item(*item)
+
+    def arrived(self, name):
+        def wait():
+            self.pieces.over_y(name).wait_recv()
+            place = self.names.index(name) + 2
+            if place < 6:
+                self.pieces.over_y(self.names[place]).start()
+
+        return wait
+
+    def residual_half(self, half):
+        return (self.residual.at[:, half_columns(half)], self.rest)
+
+    def layer_sends(self, half):
+        def sends(source):
+            target = self.layer.at[:, half_columns(half)]
+            return [
+                (
+                    self.c == self.h,
+                    lambda: remote(
+                        source,
+                        target,
+                        self.layer_sems.at[0, half],
+                        self.layer_sems.at[1, half],
+                        {"c": self.h, "h": self.c},
+                    ),
+                    lambda: pltpu.make_async_copy(source, target, self.layer_sems.at[0, half]),
+                )
+            ]
+
+        return sends
+
+    def out_sends(self, half):
+        def sends(source):
+            return [
+                (
+                    self.y == half,
+                    lambda: remote(
+                        source, self.out_y_land, self.out_sems.at[half], self.out_sems.at[2], {"y": 1 - self.y}
+                    ),
+                    lambda: pltpu.make_async_copy(source, self.out_own, self.out_sems.at[half]),
+                )
+            ]
+
+        return sends
+
+    def piece(self, name, y):
+        kind, core, half = name
+        rows = pl.ds(pl.multiple_of((2 * y + core) * 512, 512), 512)
+        if kind == "G":
+            return self.gate_up.at[rows, half_columns(half)]
+        return self.down.at[rows]
+
+    def sums_at(self, name, h):
+        kind, _, half = name
+        if kind == "G":
+            return self.gate_up_sums.at[h, :, half_columns(half)]
+        return self.down_sums.at[h] if kind == "D" else self.out_sums.at[h]
 
     def tables(self):
         return (
@@ -1321,99 +1670,10 @@
             {"c": block >> 2, "l": (block >> 1) & 1, "x": block & 1},
         )
 
-    def core(self, slot):
-        return remote(
-            self.parts.at[rows_at(self.me ^ (slot | 4))],
-            self.other.at[slot],
-            self.core_send.at[slot],
-            self.core_recv.at[slot],
-            self.to_c,
-        )
-
-    def piece(self, name, y):
-        k = int(name[1])
-        if name[0] == "G":
-            first = (2 * y + (k >> 1)) * 512 + (k & 1) * 256
-            return self.gate_up.at[pl.ds(pl.multiple_of(first, 256), 256)]
-        return self.down.at[:, pl.ds(pl.multiple_of((2 * y + k) * 512, 512), 512)]
-
-    def over_y(self, name):
-        index = ("D0", "D1", "G0", "G1", "G2", "G3").index(name)
-        target = self.land_d.at[int(name[1])] if name[0] == "D" else self.land.at[int(name[1])]
-        return remote(
-            self.piece(name, 1 - self.y), target, self.y_send.at[index], self.y_recv.at[index], {"y": 1 - self.y}
-        )
-
-    def owner(self, name):
-        k = int(name[1])
-        return k >> 1 if name[0] == "G" else k
-
-    def sum_place(self, name, h):
-        k = int(name[1])
-        if name[0] == "G":
-            return self.gate_up_sums.at[h, pl.ds((k & 1) * 256, 256)]
-        return self.down_sums.at[h]
-
-    def over_z(self, name, h):
-        index = ("D0", "D1", "G0", "G1", "G2", "G3").index(name)
-        source = self.land_d.at[int(name[1])] if name[0] == "D" else self.land.at[int(name[1])]
-        group = (0, 0, 1, 2, 1, 2)[index]
-        return (
-            remote(
-                source,
-                self.sum_place(name, h),
-                self.z_send.at[index],
-                self.z_recv.at[group, h],
-                {"c": self.owner(name), "h": self.c},
-            ),
-            pltpu.make_async_copy(source, self.sum_place(name, h), self.z_send.at[index]),
-        )
-
-    def stage_copy(self, index):
-        name = self.names[index]
-        sem = self.stage_sem.at[index % 2]
-        if name in self.where:
-            slot, half = self.where[name]
-            return pltpu.make_async_copy(
-                self.parts.at[rows_at(self.me ^ slot, half)], self.stage.at[index % 2], sem
-            )
-        if name[0] == "G":
-            return pltpu.make_async_copy(self.piece(name, self.y), self.stage.at[index % 2], sem)
-        return pltpu.make_async_copy(self.piece(name, self.y), self.stage_d.at[index % 2], sem)
-
-    def rest_copy(self, half):
-        return pltpu.make_async_copy(self.residual.at[pl.ds(half * HALF, HALF)], self.rest, self.own_sem.at[3])
-
-    def layer_remote(self, half):
-        part = pl.ds(half * HALF, HALF)
-        return (
-            remote(
-                self.other.at[0, part],
-                self.layer.at[part],
-                self.far_send.at[6 + half],
-                self.far_recv.at[6 + half],
-                {"c": self.h, "h": self.c},
-            ),
-            pltpu.make_async_copy(self.other.at[0, part], self.layer.at[part], self.far_send.at[6 + half]),
-        )
-
-    def either(self, here, pair, method):
-        away, local = pair
-
-        @pl.when(here)
-        def _():
-            getattr(local, method)()
-
-        @pl.when(jnp.logical_not(here))
-        def _():
-            getattr(away, method)()
-
     def begin(self):
         for copy in self.tables():
             copy.start()
         self.row_local().start()
-        self.stage_copy(0).start()
-        self.stage_copy(1).start()
         enter_ring(wide_partners())
 
         def send(index, carry):
@@ -1426,10 +1686,10 @@
             return carry
 
         lax.fori_loop(0, 8, send, 0)
-        for slot in (3, 1, 2, 0):
-            self.core(slot).start()
-        self.over_y("D0").start()
-        self.over_y("D1").start()
+        self.layer_ring.begin()
+        self.out_ring.begin()
+        for name in self.names[:2]:
+            self.pieces.over_y(name).start()
         for copy in self.tables():
             copy.wait()
 
@@ -1442,67 +1702,8 @@
         def _():
             self.row_remote(block, block).wait_recv()
 
-    def add(self, target, terms, count):
-        size = target.shape[0] // count
-
-        def chunk(index, carry):
-            rows = pl.ds(pl.multiple_of(index * size, size), size)
-            total = terms[0][rows, :].astype(F32)
-            for term in terms[1:]:
-                total += term[rows, :].astype(F32)
-            target[rows, :] = rounded(total)
-            return carry
-
-        lax.fori_loop(0, count, chunk, 0)
-
-    def work(self, name):
-        index = self.names.index(name)
-        order = ("D0", "D1", "G0", "G1", "G2", "G3")
-        self.stage_copy(index).wait()
-        if name in self.where:
-            slot, half = self.where[name]
-            part = pl.ds(half * HALF, HALF)
-            if name in "acd" or name == "g":
-                self.core(slot).wait_recv()
-            terms = [self.stage.at[index % 2], self.other.at[slot, part]]
-            if name == "e":
-                self.far("b").wait_recv()
-                terms.append(self.rb)
-            if name == "f":
-                self.far("a").wait_recv()
-                terms.append(self.ra)
-            if name in "gh":
-                for each in ("c", "f") if name == "g" else ("e", "d"):
-                    self.far(each).wait_recv()
-                self.rest_copy(half).start()
-                self.rest_copy(half).wait()
-                terms += [self.near_x.at[part], self.near_l.at[part], self.rest]
-            self.add(self.other.at[slot, part], terms, 8)
-            if name in "gh":
-                self.either(self.c == self.h, self.layer_remote(half), "start")
-            else:
-                self.far(name).start()
-        else:
-            self.over_y(name).wait_recv()
-            if name[0] == "D":
-                source, mine = self.land_d.at[int(name[1])], self.stage_d.at[index % 2]
-            else:
-                source, mine = self.land.at[int(name[1])], self.stage.at[index % 2]
-            self.add(source, [mine, source], 8)
-            here = jnp.logical_and(self.owner(name) == self.c, self.h == self.c)
-            self.either(here, self.over_z(name, self.h), "start")
-            place = order.index(name)
-            if place + 2 < 6:
-                self.over_y(order[place + 2]).start()
-        if index + 2 < len(self.names):
-            self.stage_copy(index + 2).start()
-
     def poll(self, unit):
-        for name, due in self.DUE.items():
-
-            @pl.when(unit == due)
-            def _(name=name):
-                self.work(name)
+        self.sums.poll(unit)
 
     def end(self):
         def each(block, carry):
@@ -1513,50 +1714,52 @@
             return carry
 
         lax.fori_loop(0, 8, each, 0)
-        for slot in range(4):
-            self.core(slot).wait_send()
-        for name in "abcdef":
-            self.far(name).wait_send()
-        for half in range(2):
-            pair = self.layer_remote(half)
-
-            @pl.when(self.c == self.h)
-            def _(pair=pair):
-                pair[1].wait()
-
-            @pl.when(self.c != self.h)
-            def _(pair=pair):
-                pair[0].wait_send()
-                pair[0].wait_recv()
-
-        for name in ("D0", "D1", "G0", "G1", "G2", "G3"):
-            self.over_y(name).wait_send()
-            here = jnp.logical_and(self.owner(name) == self.c, self.h == self.c)
-            pair = self.over_z(name, self.h)
-
-            @pl.when(here)
-            def _(pair=pair):
-                pair[1].wait()
-
-            @pl.when(jnp.logical_not(here))
-            def _(pair=pair):
-                pair[0].wait_send()
-
-        for h in range(2):
-            here = jnp.logical_and(h == self.h, self.c == self.h)
-            for name in ("D0", "G0", "G1"):
-
-                @pl.when(jnp.logical_not(here))
-                def _(name=name, h=h):
-                    self.over_z(name, h)[0].wait_recv()
+        self.sums.last_sent()
+        remote(
+            self.out_own, self.out_y_land, self.out_sems.at[0], self.out_sems.at[2], {"y": 1 - self.y}
+        ).wait_recv()
+        terms = [self.out_own, self.out_y_land]
+        count = len(self.sums.items)
+
+        def owners(source):
+            sends = []
+            for name in self.out_pieces.names:
+                part = source.at[:, pl.ds(name[1] * 512, 512)]
+                sends += self.out_pieces.sends(name)(part)
+            return sends
+
+        self.sums.item(0, 256, terms, owners)
+        self.sums.load(count)
+        for copy in self.sums.loads(count):
+            copy.wait()
+        turn = count % 2
+        total = self.sums.stage[turn, 0, 0:256, :].astype(F32) + self.sums.stage[turn, 1, 0:256, :].astype(F32)
+        self.sums.result[turn, 0:256, :] = rounded(total)
+        for here, away, local in owners(self.sums.result.at[turn, pl.ds(0, 256)]):
+            self.sums.either(here, away, local, "start")
+        self.layer_ring.end()
+        self.out_ring.end()
+        self.pieces.end()
+        for here, away, local in owners(self.sums.result.at[turn, pl.ds(0, 256)]):
+            self.sums.either(here, away, local, "wait_send")
+        self.out_pieces.owned()
+
+        @pl.when(self.c != self.h)
+        def _():
+            for half in range(2):
+                remote(
+                    self.layer.at[:, half_columns(half)],
+                    self.layer.at[:, half_columns(half)],
+                    self.layer_sems.at[0, half],
+                    self.layer_sems.at[1, half],
+                    {"c": self.h, "h": self.c},
+                ).wait_recv()
 
 
 def attend_back_kernel(q_ref, k_ref, v_ref, o_ref, l_ref, *refs):
-    given, (dkv_ref, dq_out), outs = refs[:7], refs[7:9], refs[9:12]
-    qm, dom, delta, dq, dk, dv, km, pt, dst = refs[12:21]
-    land_d, stage_d = refs[21:23]
-    beside = BesideBack(given + outs + refs[23:])
-    beside.land_d, beside.stage_d = land_d, stage_d
+    given, (dkv_ref, dq_out), outs = refs[:8], refs[8:10], refs[10:21]
+    qm, dom, delta, dq, dk, dv, km, pt, dst = refs[21:30]
+    beside = BesideBack(given + outs + refs[30:])
     heads = 4
     i, sub = pl.program_id(0), pl.program_id(1)
     block = 7 - i
@@ -1653,7 +1856,7 @@
         beside.end()
 
 
-def attend_back(q, k, v, o, level, heads_own, parts, gate_up, down, residual, cos, sin):
+def attend_back(q, k, v, o, level, heads_own, parts, gate_up, down, out, residual, cos, sin):
     length = q.shape[0]
     blocks = length // ROW
     dma = pltpu.SemaphoreType.DMA
@@ -1662,20 +1865,28 @@
     def key_spec(width):
         return pl.BlockSpec((ROW, width), lambda i, sub: (7 - i, 0))
 
+    shapes = [
+        (2, 512, 2048),
+        (2, 512, 1024),
+        (2, 256, 512),
+        (ROW, 2048),
+        (4, ROW, 2048),
+        (6, ROW, 1024),
+        (6, 512, 1024),
+        (4, 256, 2048),
+        (6, 256, 1024),
+        (256, 1024),
+        (256, 1024),
+    ]
     return pl.pallas_call(
         attend_back_kernel,
         grid=(blocks, 2),
         in_specs=[key_spec(256)] * 4
         + [pl.BlockSpec((blocks, 4, ROW), lambda i, sub: (0, 0, 0))]
-        + [anywhere] * 7,
-        out_specs=[key_spec(512)] + [anywhere] * 4,
-        out_shape=[
-            jax.ShapeDtypeStruct((length, 512), BF),
-            jax.ShapeDtypeStruct((length, 256), BF),
-            jax.ShapeDtypeStruct((2, 512, 2048), BF),
-            jax.ShapeDtypeStruct((2, 1024, 512), BF),
-            jax.ShapeDtypeStruct((ROW, 2048), BF),
-        ],
+        + [anywhere] * 8,
+        out_specs=[key_spec(512)] + [anywhere] * (1 + len(shapes)),
+        out_shape=[jax.ShapeDtypeStruct((length, 512), BF), jax.ShapeDtypeStruct((length, 256), BF)]
+        + [jax.ShapeDtypeStruct(shape, BF) for shape in shapes],
         scratch_shapes=[
             pltpu.VMEM((blocks, 4 * ROW, 256), BF),
             pltpu.VMEM((blocks, 4 * ROW, 256), BF),
@@ -1686,39 +1897,34 @@
             pltpu.VMEM((4, KEYS, 256), BF),
             pltpu.VMEM((KEYS, 4 * ROW), BF),
             pltpu.VMEM((KEYS, 4 * ROW), BF),
-            pltpu.VMEM((2, 1024, 512), BF),
-            pltpu.VMEM((2, 1024, 512), BF),
             pltpu.VMEM((length, 256), BF),
             pltpu.VMEM((length, 128), F32),
             pltpu.VMEM((length, 128), F32),
-            pltpu.VMEM((4, ROW, 2048), BF),
-            pltpu.VMEM((ROW, 2048), BF),
-            pltpu.VMEM((ROW, 2048), BF),
-            pltpu.VMEM((HALF, 2048), BF),
-            pltpu.VMEM((HALF, 2048), BF),
-            pltpu.VMEM((4, 256, 2048), BF),
-            pltpu.VMEM((2, 256, 2048), BF),
-            pltpu.VMEM((HALF, 2048), F32),
+            pltpu.VMEM((2, 4, ROW, 1024), BF),
+            pltpu.VMEM((2, ROW, 1024), BF),
+            pltpu.VMEM((ROW, 1024), F32),
             dma((8,)),
             dma((8,)),
-            dma((4,)),
-            dma((4,)),
-            dma((8,)),
-            dma((8,)),
-            dma((6,)),
-            dma((6,)),
-            dma((6,)),
+            dma((2, 4)),
+            dma((2, 6)),
+            dma((2, 4)),
+            dma((2, 6)),
+            dma((2, 2)),
+            dma((2, 6)),
+            dma((3, 6)),
+            dma((3,)),
+            dma((2, 2)),
             dma((3, 2)),
-            dma((2,)),
+            dma((2, 5)),
             dma((5,)),
         ],
         compiler_params=pltpu.CompilerParams(
-            collective_id=7, has_side_effects=True, vmem_limit_bytes=63 * 2**20
+            collective_id=7, has_side_effects=True, vmem_limit_bytes=60 * 2**20
         ),
         cost_estimate=pl.CostEstimate(
             flops=19 * 10**9 * blocks, bytes_accessed=20 * 2**20, transcendentals=0
         ),
-    )(q, k, v, o, level, heads_own, parts, gate_up, down, residual, cos, sin)
+    )(q, k, v, o, level, heads_own, parts, gate_up, down, out, residual, cos, sin)
 
 
 def ring_shards(
@@ -1756,25 +1962,6 @@
     def both_cores(mine, other):
         return jnp.where(plain_c, mine, other), jnp.where(plain_c, other, mine)
 
-    def scatter_y(blocks, zero=None):
-        mine = lax.dynamic_slice_in_dim(blocks, 2 * y, 2, 0)
-        return mine, flip(held(lax.dynamic_slice_in_dim(blocks, 2 * (1 - y), 2, 0), zero), "y")
-
-    def scatter_ch(near, far):
-        total = (near.astype(F32) + far.astype(F32)).astype(BF)
-        kept, other = both_cores(total[0], total[1])
-        r1 = move(kept, lambda y, c, h, l, x: (y, c, 1 - h, l, x) if c != h else None)
-        r2a = move(other, lambda y, c, h, l, x: (y, 1 - c, h, l, x) if c == h else None)
-        r2b = move(other, lambda y, c, h, l, x: (y, h, c, l, x) if c != h else None)
-        return kept, r1, r2a, r2b
-
-    def scatter_own(kept, r1, r2a, r2b):
-        return jnp.where(
-            straight,
-            kept.astype(F32) + r1.astype(F32),
-            r2a.astype(F32) + r2b.astype(F32),
-        )
-
     turn = column_order()
     rows_in = swap_ch(layer_input).astype(F32)
     gains_here = gains_master.astype(BF)
@@ -1830,11 +2017,11 @@
     grad_gate = (grad_act * up.astype(F32) * sigmoid * (1.0 + g * (1.0 - sigmoid))).astype(BF)
     grad_up = (grad_act * g * sigmoid).astype(BF)
     grad_gate_up = jnp.concatenate([grad_gate, grad_up], axis=1)
-    grad_normed_second = product_scatter(grad_gate_up, gate_up_weight, NT, 3)
+    grad_normed_second = product_scatter(grad_gate_up, gate_up_weight, NT, 3)[0]
     gate_up_grad = lax.dot_general(
         normed_second, grad_gate_up, TN, preferred_element_type=F32
     ).astype(BF)
-    down_grad = lax.dot_general(activation, grad_out, TN, preferred_element_type=F32).astype(BF)
+    down_grad = lax.dot_general(grad_out, activation, TN, preferred_element_type=F32).astype(BF)
     layer_parts = jnp.dot(activation, down_weight, preferred_element_type=F32).astype(BF)
 
     def norm_grad(values, scale, gain, grad):
@@ -1850,22 +2037,19 @@
     residual_grad = residual_grad + grad_rows
     residual_low = residual_grad.astype(BF)
     grad_heads = lax.dot_general(residual_low, out_weight, NT, preferred_element_type=F32).astype(BF)
-    grad_kv, grad_q, gate_up_sums, down_sums, layer_output = attend_back(
-        queries, keys, values, attended, level, grad_heads, layer_parts, gate_up_grad, down_grad, residual, cosine, sine
+    out_grad = lax.dot_general(attended_own, residual_low, TN, preferred_element_type=F32).astype(BF)
+    grad_kv, grad_q, gate_up_sums, down_sums, out_sums, layer_output, *_ = attend_back(
+        queries, keys, values, attended, level, grad_heads, layer_parts, gate_up_grad, down_grad, out_grad, residual, cosine, sine
     )
     gate_up_grad_own = gate_up_sums[0].astype(F32) + gate_up_sums[1].astype(F32)
-    down_grad_own = down_sums[0].astype(F32) + down_sums[1].astype(F32)
+    down_grad_own = (down_sums[0].astype(F32) + down_sums[1].astype(F32)).T
+    out_grad_own = out_sums[0].astype(F32) + out_sums[1].astype(F32)
 
     grad_mixture = jnp.concatenate([grad_q, grad_kv], axis=1)
-    grad_normed_first = product_scatter(grad_mixture, qkv_weight, NT, 5)
     qkv_grad = lax.dot_general(normed, grad_mixture, TN, preferred_element_type=F32).astype(BF)
     qkv_grad = lax.dot_general(qkv_grad, turn, NT, preferred_element_type=F32).astype(BF)
-    qkv_y = scatter_y(qkv_grad.reshape(4, 512, 768))
-    out_grad = lax.dot_general(attended_own, residual_low, TN, preferred_element_type=F32)
-    out_grad = lax.psum_scatter(out_grad.astype(BF), RING, scatter_dimension=0, tiled=True)
-    out_y = scatter_y(out_grad.reshape(256, 4, 512).transpose(1, 0, 2))
-    qkv_grad_own = scatter_own(*scatter_ch(*qkv_y))
-    out_grad_own = scatter_own(*scatter_ch(*out_y))
+    grad_normed_first, qkv_sums, _ = product_scatter(grad_mixture, qkv_weight, NT, 5, qkv_grad)
+    qkv_grad_own = qkv_sums[0].astype(F32) + qkv_sums[1].astype(F32)
 
     input_back, gain_first_part = norm_grad(rows_in, scale_first, gain_first, grad_normed_first)
     input_grad = swap_ch((residual_grad + input_back).astype(BF)).astype(F32)

time: 1450 us -> 1350 us (0.931)
  Pallas kernels: 1050 us -> 1000 us
  waiting for transfers between devices: 46.2 us -> 20.8 us
  starting transfers between devices: 51.6 us -> 29.2 us
    pallas_call x2, Pallas kernels: 332 us -> 199 us  [product_scatter(): pl.pallas_call(lambda *refs: scatter_kernel(dims, len(grad), *refs), in_s...]
    pallas_call x1, Pallas kernels: 234 us -> 325 us  [attend_back(): pl.pallas_call(attend_back_kernel, grid=(blocks, 2), in_specs=[key_spec(2...]
    ppermute x20 -> x12, waiting for transfers between devices: 46.2 us -> 20.8 us  [move(): return lax.ppermute(values, AXES, device_pairs(target))]
    ppermute x20 -> x12, starting transfers between devices: 51.6 us -> 29.2 us  [move(): return lax.ppermute(values, AXES, device_pairs(target))]
    unnamed x145 -> x153, local copies, waits for them, and re-layouts: 15.2 us -> 31.4 us
  transfers between devices with their start and end apart: 21 -> 12, of which waited for: 4 -> 3; matrix products, arithmetic and copies ran while one was open for 6% -> 5% of each run, Pallas kernels for 17% -> 0%
where the time goes in v5:
time: 1350 us; the launch traced here: 1340 us
  Pallas kernels  1000 us (74%)
  matrix products  169 us (13%)
  other arithmetic  81.7 us (6%)
  local copies, waits for them, and re-layouts  34.4 us (3%)
  starting transfers between devices  29.2 us (2%)
  waiting for transfers between devices  20.8 us (2%)
    pallas_call x1, Pallas kernels, attend_back(): pl.pallas_call(attend_back_kernel, grid=(blocks, 2), in_specs=[key_spec(2...  325 us
    pallas_call x2, Pallas kernels, gather_product(): pl.pallas_call(lambda *refs: gather_kernel(finish, beside, inputs, len(ex...  248 us
    pallas_call x1, Pallas kernels, attend(): pl.pallas_call(attend_kernel, grid=(blocks, 4), in_specs=[pl.BlockSpec((R...  232 us
    pallas_call x2, Pallas kernels, product_scatter(): pl.pallas_call(lambda *refs: scatter_kernel(dims, len(grad), *refs), in_s...  199 us
    dot_general x1, matrix products, ring_shards(): lax.dot_general(normed_second, grad_gate_up, TN, preferred_element_type=F32)  44.5 us
    unnamed x153, local copies, waits for them, and re-layouts  31.4 us
    ppermute x12, starting transfers between devices, move(): return lax.ppermute(values, AXES, device_pairs(target))  29.2 us
  transfers between devices with their start and end apart: 12, of which 3 were waited for; matrix products, arithmetic and copies ran while one was open for 5% of the time, Pallas kernels for 0%

profile of v5, /device:TPU:0, one launch (start us, length us, event | category | flops | bytes accessed | tf_op | source)
XLA Modules:
  0.0 1342.9 jit_solution(9413253961255367107)
XLA Ops:
  25.5 3.9 collective-permute-start.5
  36.7 9.3 multiply_sine_fusion
  48.3 128.9 %shard_map.354 = (bf16[4096,2048]{1,0:T(8,128)(2,1)}, bf16[4096,256]{1,0:T(8,128)(2,1)}, bf16[4096,256]{1,0:T(8,128)(2,1)}, bf16[4096,256]{1,0:T(8,128)(2,1)}, b...) custom-call(bf16[512,2048]{1,0:T(8,128)(2,1)} %fusion.10.refs_0_, f32[4096,128]{1,0:T(8,128)} %get-tuple-element.120.refs_1_.refs_6_, ...), custom_call_target="tpu_custom_call" | custom-call | flops 80000000000 | bytes 31457280 | tf_op jit(solution)/shard_map/pallas_call | solution.py:765
  177.2 231.7 %shard_map.355 = (bf16[4096,256]{1,0:T(8,128)(2,1)S(1)}, f32[8,4,512]{2,1,0:T(4,128)S(1)}, bf16[2048,2048]{1,0:T(8,128)(2,1)}, bf16[2048,2048]{1,0:T(8,128)(2,1)...) custom-call(bf16[4096,256]{1,0:T(8,128)(2,1)} %get-tuple-element.47.q_ref, ...), custom_call_target="tpu_custom_call" | custom-call | flops 112000000000 | bytes 10485760 | tf_op jit(solution)/shard_map/pallas_call | solution.py:1268
  409.0 8.6 multiply_reduce_fusion.2
  420.3 118.9 %shard_map.356 = (bf16[4096,2048]{1,0:T(8,128)(2,1)}, bf16[4096,1024]{1,0:T(8,128)(2,1)}, bf16[4096,1024]{1,0:T(8,128)(2,1)}, bf16[4096,1024]{1,0:T(8,128)(2,1)}, bf16[1024,2048]{1,0:T(8,128)(2,1)}) custom-call(bf16[512,2048]{1,0:T(8,128)(2,1)} %multiply_convert_fusion.refs_0_, bf16[2048,2048]{1,0:T(8,128)(2,1)} %get-tuple-element.56.refs_1_, ...), custom_call_target="tpu_custom_call" | custom-call | flops 80000000000 | bytes 31457280 | tf_op jit(solution)/shard_map/pallas_call | solution.py:765
  539.1 25.0 %convolution_convert_fusion.3.refs_3_ = bf16[2048,1024]{1,0:T(8,128)(2,1)} fusion(bf16[4096,2048]{1,0:T(8,128)(2,1)} %get-tuple-element.55, bf16[4096,1024]{1,0:T(8,128)(2,1)} %get-tuple-element.60), kind=kOutput, calls=%fused_computation.47 | convolution fusion | flops 17181966336 | bytes 29360128 | tf_op jit(solution)/shard_map/dot_general | solution.py:2024
  564.1 23.8 %fusion.72 = f32[4096,1024]{1,0:T(8,128)} fusion(bf16[4096,2048]{1,0:T(8,128)(2,1)} %get-tuple-element.55, bf16[1024,2048]{1,0:T(8,128)(2,1)} %get-tuple-element.57), kind=kOutput, calls=%fused_computation.156 | convolution fusion | flops 17179869184 | bytes 37748736 | tf_op jit(solution)/shard_map/dot_general | solution.py:2014
  587.9 22.3 %convolution_convert_fusion.refs_1_ = bf16[4096,2048]{1,0:T(8,128)(2,1)} fusion(bf16[4096,1024]{1,0:T(8,128)(2,1)S(1)} %bitcast.83, bf16[1024,2048]{1,0:T(8,128)(2,1)} %get-tuple-element.57), kind=kOutput, calls=%fused_computation.12 | convolution fusion | flops 17188257792 | bytes 29360128 | tf_op jit(solution)/shard_map/dot_general | solution.py:2025
  610.2 12.0 fusion.5
  628.0 6.8 pad_maximum_fusion.refs_0_
  634.8 93.6 %shard_map.357 = f32[512,2048]{1,0:T(8,128)} custom-call(bf16[4096,2048]{1,0:T(8,128)(2,1)} %pad_maximum_fusion.refs_0_, bf16[2048,2048]{1,0:T(8,128)(2,1)} %get-tuple-element.56.refs_1_), custom_call_target="tpu_custom_call" | custom-call | flops 80000000000 | bytes 31457280 | tf_op jit(solution)/shard_map/pallas_call | solution.py:942
  728.5 4.0 multiply_reduce_fusion
  733.9 10.7 convolution_convert_fusion.6.refs_0_
  744.6 7.3 convolution_convert_fusion.1.refs_4_
  751.9 44.5 %convolution_convert_fusion.2.refs_2_ = bf16[2048,2048]{1,0:T(8,128)(2,1)} fusion(bf16[4096,2048]{1,0:T(8,128)(2,1)} %get-tuple-element.61, bf16[4096,1024]{1,0:T(8,128)(2,1)} %copy-done.10, bf16[4096,1024]{1,0:T(8,128)(2,1)} %copy-done.9), kind=kOutput, calls=%fused_computation.19 | convolution fusion | flops 34397487104 | bytes 41943040 | tf_op jit(solution)/shard_map/dot_general | solution.py:2021
  796.4 325.5 %shard_map.358 = (bf16[4096,512]{1,0:T(8,128)(2,1)}, bf16[4096,256]{1,0:T(8,128)(2,1)}, bf16[2,512,2048]{2,1,0:T(8,128)(2,1)}, bf16[2,512,1024]{2,1,0:T(8,128)(2...) custom-call(bf16[4096,256]{1,0:T(8,128)(2,1)} %get-tuple-element.47., ...), custom_call_target="tpu_custom_call" | custom-call | flops 152000004096 | bytes 20971520 | tf_op jit(solution)/shard_map/pallas_call | solution.py:1881
  1129.5 19.7 %convolution_convert_fusion.4.clone.5 = bf16[2048,768]{1,0:T(8,128)(2,1)S(1)} fusion(bf16[4096,2048]{1,0:T(8,128)(2,1)} %get-tuple-element.66, bf16[4096,768]{1,0:T(8,128)(2,1)S(1)} %constant_dynamic-update-slice_fusion.refs_0_), kind=kOutput, calls=%fused_computation.64.clone.clone.clone.2 | convolution fusion | flops 12886474752 | bytes 26214400 | tf_op jit(solution)/shard_map/dot_general | solution.py:2049
  1149.3 4.9 convolution_convert_fusion.5.refs_2_
  1154.2 105.4 %shard_map.359 = (f32[512,2048]{1,0:T(8,128)}, bf16[2,512,768]{2,1,0:T(8,128)(2,1)}, bf16[2,512,768]{2,1,0:T(8,128)(2,1)}) custom-call(bf16[4096,768]{1,0:T(8,128)(2,1)} %copy-done.37, bf16[2048,768]{1,0:T(8,128)(2,1)} %get-tuple-element.65.refs_1_, bf16[2048,768]{1,0:T(8,128)(2,1)} %convolution_convert_fusion.5.refs_2_), custom_call_target="tpu_custom_call" | custom-call | flops 80000000000 | bytes 31457280 | tf_op jit(solution)/shard_map/pallas_call | solution.py:942
  1264.6 4.9 fusion.15
  1269.5 17.2 %collective-permute-start.6 = (bf16[512,2048]{1,0:T(8,128)(2,1)}, bf16[512,2048]{1,0:T(8,128)(2,1)}, u32[]{:S(2)}, u32[]{:S(2)}) collective-permute-start(bf16[512,2048]{1,0:T(8,128)(2,1)} %fusion.15), channel_id=1, source_target_pairs={{0,0},{1,1},{2,2},{3,3},{4,8},{5,9},{6,10},{7,11},{8,4},{9,5},{10,... | collective-permute-start | bytes 6291464 | tf_op jit(solution)/shard_map/ppermute | solution.py:354
  1303.1 16.9 %collective-permute-done.8 = f32[2,2048]{1,0:T(2,128)S(1)} collective-permute-done((f32[2,2048]{1,0:T(2,128)S(1)}, f32[2,2048]{1,0:T(2,128)S(1)}, u32[]{:S(2)}, u32[]{:S(2)}) %collective-permute-start.8) | collective-permute-done | bytes 16416 | tf_op jit(solution)/shard_map/ppermute | solution.py:354
  1336.8 4.3 convert_element_type.171
  (220 shorter events, 89.1 us)
Async XLA Ops:
  1.3 23.6 %collective-permute-start.4 = (f32[1]{0:T(128)}, f32[1]{0:T(128)}, u32[]{:S(2)}, u32[]{:S(2)}) collective-permute-start(f32[1]{0:T(128)} %convert_element_type.151), channel_id=1, source_target_pairs={{0,8},{1,9},{2,10},{3,11},{4,12},{5,13},{6,14},{7,15},{8,0},{9,1},... | collective-permute-start | bytes 20 | tf_op jit(solution)/shard_map/ppermute | solution.py:354
  3.5 27.0 %collective-permute-start.1 = (bf16[2,512]{1,0:T(2,128)(2,1)S(1)}, bf16[2,512]{1,0:T(2,128)(2,1)S(1)}, u32[]{:S(2)}, u32[]{:S(2)}) collective-permute-start(bf16[2,512]{1,0:T(2,128)(2,1)S(1)} %convert_element_type.143), channel_id=1, source_target_pairs={{0,8},{1,9},{2,10},{3,11},{4,12},{5,13},{6,14},{7,15},{8,0},{9,1},... | collective-permute-start | bytes 6152 | tf_op jit(solution)/shard_map/ppermute | solution.py:354
  3.5 33.1 %collective-permute-start.3 = (s32[4096]{0:T(1024)}, s32[4096]{0:T(1024)S(1)}, u32[]{:S(2)}, u32[]{:S(2)}) collective-permute-start(s32[4096]{0:T(1024)} %param.22), channel_id=1, source_target_pairs={{0,8},{1,9},{2,10},{3,11},{4,12},{5,13},{6,14},{7,15},{8,0},{9,1},... | collective-permute-start | bytes 49160 | tf_op jit(solution)/shard_map/ppermute | solution.py:354
  4.0 42.0 %collective-permute-start = (bf16[512,2048]{1,0:T(8,128)(2,1)}, bf16[512,2048]{1,0:T(8,128)(2,1)S(1)}, u32[]{:S(2)}, u32[]{:S(2)}) collective-permute-start(bf16[512,2048]{1,0:T(8,128)(2,1)} %param.19), channel_id=1, source_target_pairs={{0,0},{1,1},{2,2},{3,3},{4,8},{5,9},{6,10},{7,11},{8,4},{9,5},{10,... | collective-permute-start | bytes 6291464 | tf_op jit(solution)/shard_map/ppermute | solution.py:354
  25.5 4.2 collective-permute-start.5
  30.5 5.5 collective-permute-start.2
  177.2 231.7 %copy-start.7 = (bf16[512,2048]{1,0:T(8,128)(2,1)S(1)}, bf16[512,2048]{1,0:T(8,128)(2,1)}, u32[]{:S(2)}) copy-start(bf16[512,2048]{1,0:T(8,128)(2,1)} %copy-done.6) | copy-start | bytes 6291460
  539.1 48.7 %slice-start.2 = ((s8[8388608]{0:T(1024)(128)(4,1)}), s8[4194304]{0:T(1024)(128)(4,1)S(1)}, s32[]{:S(2)}) async-start(s8[8388608]{0:T(1024)(128)(4,1)} %bitcast.82), calls=%async_computation.2 | async-start | bytes 8388608
  539.1 71.0 %slice-start = ((s8[8388608]{0:T(1024)(128)(4,1)}), s8[4194304]{0:T(1024)(128)(4,1)S(1)}, s32[]{:S(2)}) async-start(s8[8388608]{0:T(1024)(128)(4,1)} %bitcast.68), calls=%async_computation | async-start | bytes 8388608
  564.1 23.8 %slice-start.3 = ((s8[8388608]{0:T(1024)(128)(4,1)}), s8[4194304]{0:T(1024)(128)(4,1)S(1)}, s32[]{:S(2)}) async-start(s8[8388608]{0:T(1024)(128)(4,1)} %bitcast.82), calls=%async_computation.3 | async-start | bytes 8388608
  564.1 46.0 %slice-start.1 = ((s8[8388608]{0:T(1024)(128)(4,1)}), s8[4194304]{0:T(1024)(128)(4,1)S(1)}, s32[]{:S(2)}) async-start(s8[8388608]{0:T(1024)(128)(4,1)} %bitcast.68), calls=%async_computation.1 | async-start | bytes 8388608
  634.8 93.6 %copy-start.5 = (f32[512,2048]{1,0:T(8,128)S(1)}, f32[512,2048]{1,0:T(8,128)}, u32[]{:S(2)}) copy-start(f32[512,2048]{1,0:T(8,128)} %copy-done.4) | copy-start | bytes 12582916
  634.8 93.6 %copy-start.44 = (f32[1,2048]{1,0:T(1,128)S(1)}, f32[1,2048]{1,0:T(1,128)}, u32[]{:S(2)}) copy-start(f32[1,2048]{1,0:T(1,128)} %get-tuple-element.121) | copy-start | bytes 24580
  634.8 93.6 %copy-start.51 = (f32[512]{0:T(512)S(1)}, f32[512]{0:T(512)}, u32[]{:S(2)}) copy-start(f32[512]{0:T(512)} %copy-done.50) | copy-start | bytes 6148
  1154.2 105.4 %copy-start.8 = (bf16[512,2048]{1,0:T(8,128)(2,1)S(1)}, bf16[512,2048]{1,0:T(8,128)(2,1)}, u32[]{:S(2)}) copy-start(bf16[512,2048]{1,0:T(8,128)(2,1)} %copy-done.6) | copy-start | bytes 6291460
  1154.2 105.4 %copy-start.42 = (f32[1,2048]{1,0:T(1,128)S(1)}, f32[1,2048]{1,0:T(1,128)}, u32[]{:S(2)}) copy-start(f32[1,2048]{1,0:T(1,128)} %copy-done.41) | copy-start | bytes 24580
  1154.2 105.4 %copy-start.49 = (f32[512]{0:T(512)S(1)}, f32[512]{0:T(512)}, u32[]{:S(2)}) copy-start(f32[512]{0:T(512)} %copy-done.48) | copy-start | bytes 6148
  1263.3 23.3 %copy-start.20 = (f32[1,512,1024]{2,1,0:T(8,128)S(1)}, f32[1,512,1024]{2,1,0:T(8,128)}, u32[]{:S(2)}) copy-start(f32[1,512,1024]{2,1,0:T(8,128)} %get-tuple-element.116) | copy-start | bytes 6291460
  1263.4 37.9 %collective-permute-start.7 = (f32[2,2048]{1,0:T(2,128)S(1)}, f32[2,2048]{1,0:T(2,128)S(1)}, u32[]{:S(2)}, u32[]{:S(2)}) collective-permute-start(f32[2,2048]{1,0:T(2,128)S(1)} %pad_maximum_fusion.3), channel_id=1, source_target_pairs={{0,1},{1,0},{2,3},{3,2},{4,5},{5,4},{6,7},{7,6},{8,9},{9,8},{10,11... | collective-permute-start | bytes 49160 | tf_op jit(solution)/shard_map/ppermute | solution.py:354
  1269.5 67.3 %collective-permute-start.6 = (bf16[512,2048]{1,0:T(8,128)(2,1)}, bf16[512,2048]{1,0:T(8,128)(2,1)}, u32[]{:S(2)}, u32[]{:S(2)}) collective-permute-start(bf16[512,2048]{1,0:T(8,128)(2,1)} %fusion.15), channel_id=1, source_target_pairs={{0,0},{1,1},{2,2},{3,3},{4,8},{5,9},{6,10},{7,11},{8,4},{9,5},{10,... | collective-permute-start | bytes 6291464 | tf_op jit(solution)/shard_map/ppermute | solution.py:354
  1301.2 18.7 %collective-permute-start.8 = (f32[2,2048]{1,0:T(2,128)S(1)}, f32[2,2048]{1,0:T(2,128)S(1)}, u32[]{:S(2)}, u32[]{:S(2)}) collective-permute-start(f32[2,2048]{1,0:T(2,128)S(1)} %fusion.60), channel_id=1, source_target_pairs={{0,2},{1,3},{2,0},{3,1},{4,6},{5,7},{6,4},{7,5},{8,10},{9,11},{10,... | collective-permute-start | bytes 49160 | tf_op jit(solution)/shard_map/ppermute | solution.py:354
  1320.0 1.6 collective-permute-start.9
  1321.6 4.7 collective-permute-start.10
  1326.4 9.2 collective-permute-start.11
  (60 other events, 459.3 us)

commit v6 on v5

--- a/solution.py
+++ b/solution.py
@@ -420,8 +420,9 @@
 
 
 class Ring:
-    def __init__(self, buffer, size, send, recv):
-        self.buffer, self.size, self.send, self.recv = buffer, size, send, recv
+    def __init__(self, buffer, size, send, recv, lean=False, own=None, cut=None):
+        self.buffer, self.size, self.send, self.recv, self.own = buffer, size, send, recv, own
+        self.cut = size // 2 if cut is None else cut
         me, (to_x, to_l, to_c) = ring_position()
         self.plan = (
             (me, 0, to_x, me ^ 1),
@@ -435,13 +436,18 @@
             (me ^ 2, None, to_c, me ^ 6),
             (me ^ 3, None, to_c, me ^ 7),
         )
+        if lean:
+            self.plan = self.plan[:5] + ((me ^ 2, 0, to_x, me ^ 3),) + self.plan[6:]
 
     def copy(self, index, block):
         _, part, partner, _ = self.plan[index]
-        size = self.size if part is None else self.size // 2
-        first = block * self.size + (size if part == 1 else 0)
-        place = self.buffer.at[pl.ds(pl.multiple_of(first, size), size)]
-        return remote(place, place, self.send.at[index], self.recv.at[index], partner)
+        size = (self.cut, self.size - self.cut, self.size)[2 if part is None else part]
+        offset = self.cut if part == 1 else 0
+        place = self.buffer.at[pl.ds(pl.multiple_of(block * self.size + offset, 128), size)]
+        source = place
+        if self.own is not None and index < 5:
+            source = self.own.at[pl.ds(offset, size)]
+        return remote(source, place, self.send.at[index], self.recv.at[index], partner)
 
     def start(self, *indices):
         for index in indices:
@@ -457,12 +463,15 @@
 
 
 class Spread:
-    def __init__(self, source, target, near, far, keep):
+    def __init__(self, source, target, near, far, keep, stage=None):
         self.source, self.target, self.near, self.far, self.keep = source, target, near, far, keep
+        self.stage = stage
         _, self.c, self.h, _ = places()
 
     def local(self):
-        return pltpu.make_async_copy(self.source, self.target, self.keep)
+        return pltpu.make_async_copy(
+            self.source, self.target if self.stage is None else self.stage, self.keep
+        )
 
     def beside(self):
         return remote(self.source, self.target, self.near.at[0], self.near.at[1], {"c": self.h})
@@ -487,6 +496,10 @@
         @pl.when(self.c == self.h)
         def _():
             self.local().wait()
+            if self.stage is not None:
+                copy = pltpu.make_async_copy(self.stage, self.target, self.keep)
+                copy.start()
+                copy.wait()
             self.beside().wait_recv()
 
         @pl.when(self.c != self.h)
@@ -514,7 +527,7 @@
 class First:
     def __init__(self, refs):
         (self.shard, self.grad), (self.whole, self.moved) = refs[:2], refs[2:4]
-        self.w, near, far, keep, self.y_send, self.y_recv, self.grad_sems = refs[4:]
+        self.w, near, far, keep, self.y_send, self.y_recv, self.grad_sems, self.stage = refs[4:]
         self.y, self.c, self.h, _ = places()
         first = (2 * self.y + self.c) * 512
         self.pieces = [
@@ -533,8 +546,11 @@
         place = self.w.at[pl.ds(pl.multiple_of(first, 256), 256)]
         return remote(place, place, self.y_send.at[k, core], self.y_recv.at[k, core], {"y": 1 - self.y})
 
+    def grad_load(self):
+        return pltpu.make_async_copy(self.grad, self.stage, self.grad_sems.at[2])
+
     def grad_local(self):
-        return pltpu.make_async_copy(self.grad, self.moved, self.grad_sems.at[2])
+        return pltpu.make_async_copy(self.stage, self.moved, self.grad_sems.at[2])
 
     def grad_remote(self):
         return remote(
@@ -544,35 +560,36 @@
     def run(self, ring):
         for piece in self.pieces:
             piece.start()
+
+        @pl.when(self.c == self.h)
+        def _():
+            self.grad_load().start()
+
         for k in range(2):
             self.pieces[k].arrived()
             for core in range(2):
                 self.over_y(k, core, self.y).start()
             if k == 0:
-                ring.arrived(0)
-                ring.start(5)
                 ring.arrived(1)
                 ring.start(6)
 
         @pl.when(self.c == self.h)
         def _():
+            self.grad_load().wait()
             self.grad_local().start()
 
         @pl.when(self.c != self.h)
         def _():
             self.grad_remote().start()
 
-        ring.arrived(2, 3)
+        ring.arrived(4)
+        ring.start(5, 8)
+        ring.arrived(2, 0, 3)
         ring.start(7)
-        ring.arrived(4)
-        ring.start(8)
         for k in range(2):
             for core in range(2):
                 self.over_y(k, core, 1 - self.y).wait_recv()
         pltpu.make_async_copy(self.w, self.whole, self.grad_sems.at[3]).start()
-
-    def poll(self, step):
-        pass
 
     def finish(self):
         for piece in self.pieces:
@@ -595,7 +612,7 @@
 class Second:
     def __init__(self, refs):
         self.shard, self.whole = refs[:2]
-        near, far, keep, self.y_send, self.y_recv = refs[2:]
+        near, far, keep, self.y_send, self.y_recv, stage = refs[2:]
         self.y, c, _, _ = places()
         columns = pl.ds(pl.multiple_of((2 * self.y + c) * 512, 512), 512)
         self.pieces = [
@@ -605,6 +622,7 @@
                 near.at[k],
                 far.at[k],
                 keep.at[k],
+                stage.at[k],
             )
             for k in range(2)
         ]
@@ -617,16 +635,9 @@
         for piece in self.pieces:
             piece.start()
 
-    def poll(self, step):
-        @pl.when(step == 1)
-        def _():
-            self.pieces[0].arrived()
-            self.over_y(0, self.y).start()
-
-        @pl.when(step == 4)
-        def _():
-            self.pieces[1].arrived()
-            self.over_y(1, self.y).start()
+    def on(self, k):
+        self.pieces[k].arrived()
+        self.over_y(k, self.y).start()
 
     def finish(self):
         for k in range(2):
@@ -646,9 +657,9 @@
     load.start()
     enter_ring(wide_partners())
     load.wait()
-    ring = Ring(buf, ROW, send, recv)
+    early = beside is First
+    ring = Ring(buf, ROW, send, recv, lean=early, cut=256 if early else 128)
     ring.start(0, 1, 2, 3, 4)
-    early = beside is First
     if early:
         more = First(given[2:] + extra_outs + refs[7:])
         w_ref, tables = more.w, given[:2]
@@ -672,8 +683,10 @@
                 ring.start(5)
                 ring.arrived(1)
                 ring.start(6)
+                more.on(0)
                 ring.arrived(3)
                 ring.start(7)
+                more.on(1)
                 ring.arrived(4)
                 ring.start(8)
 
@@ -694,7 +707,6 @@
         def _():
             ring.arrived(9)
 
-        more.poll(step)
         pltpu.make_async_copy(buf.at[rows], full_ref.at[rows], full_sem.at[step]).start()
         turn = step & 1
 
@@ -788,21 +800,59 @@
     )(own, *given, *anywhere_given)
 
 
-def scatter_kernel(dims, beside, a_ref, w_ref, *refs):
-    given, refs = refs[:beside], refs[beside:]
-    out_ref, refs = refs[0], refs[1:]
-    more_outs, refs = refs[: 2 * beside], refs[2 * beside :]
+def scatter_kernel(dims, cut, kind, *refs):
+    beside = 2 if kind == 2 else 0
+    if kind == 3:
+        grad_ref, gate_ref, up_ref, down_ref, w_ref, out_ref, a_ref = refs[:7]
+        refs = refs[7:]
+        grad_buf, gate_buf, up_buf, made_sem = refs[11:]
+    else:
+        a_ref, w_ref, refs = refs[0], refs[1], refs[2:]
+        given, refs = refs[:beside], refs[beside:]
+        out_ref, refs = refs[0], refs[1:]
+        more_outs, refs = refs[: 3 if beside else 0], refs[3 if beside else 0 :]
     abuf, mine, other, sums, ra, rb, near_x, near_l, send, recv, a_sem = refs[:11]
     me, partners = ring_position()
     to_x, to_l, to_c = partners
     order = (7, 3, 5, 6, 1, 2, 4, 0)
 
     def load(index):
+        rows, turn = rows_at(me ^ order[index]), index % 2
+        if kind == 3:
+            pairs = ((grad_ref, grad_buf), (gate_ref, gate_buf), (up_ref, up_buf))
+        else:
+            pairs = ((a_ref, abuf),)
+        return [
+            pltpu.make_async_copy(ref.at[rows], buf.at[turn], a_sem.at[turn, k])
+            for k, (ref, buf) in enumerate(pairs)
+        ]
+
+    def made(index):
         return pltpu.make_async_copy(
-            a_ref.at[rows_at(me ^ order[index])], abuf.at[index % 2], a_sem.at[index % 2]
-        )
-
-    load(0).start()
+            abuf.at[index % 2], a_ref.at[rows_at(me ^ order[index])], made_sem.at[index % 2]
+        )
+
+    def make(index):
+        turn = index % 2
+        if index >= 2:
+            made(index - 2).wait()
+
+        def columns(chunk, carry):
+            start = pl.multiple_of(chunk * 256, 256)
+            here, there = pl.ds(start, 256), pl.ds(start + 1024, 256)
+            d = lax.dot_general(grad_buf[turn], down_ref[here, :], NT, preferred_element_type=F32)
+            g = gate_buf[turn, :, here].astype(F32)
+            u = up_buf[turn, :, here].astype(F32)
+            sigmoid = 1.0 / (1.0 + jnp.exp(-g))
+            abuf[turn, :, here] = rounded(d * u * sigmoid * (1.0 + g * (1.0 - sigmoid)))
+            abuf[turn, :, there] = rounded(d * g * sigmoid)
+            return carry
+
+        lax.fori_loop(0, 4, columns, 0)
+        made(index).start()
+
+    for each in load(0):
+        each.start()
     enter_ring(wide_partners() if beside else partners)
     if beside:
         tail = WeightTail(given + more_outs + refs[11:])
@@ -818,9 +868,9 @@
             device_id_type=MESH,
         )
 
-    half = ROW // 2
-    top, bottom = pl.ds(0, half), pl.ds(half, half)
-    copies = [copy(slot, mine.at[slot], other.at[slot], to_c) for slot in range(4)] + [
+    top, bottom = pl.ds(0, cut), pl.ds(cut, ROW - cut)
+    turns = {3: 0, 1: 1, 2: 0, 0: 1}
+    copies = [copy(slot, mine.at[turns[slot]], other.at[slot], to_c) for slot in range(4)] + [
         copy(4, sums.at[2, top], ra, to_x),
         copy(5, sums.at[2, bottom], rb, to_l),
         copy(6, sums.at[0, top], near_x.at[top], to_x),
@@ -841,13 +891,19 @@
         lax.fori_loop(0, 8, columns, 0)
 
     for index, slot in enumerate(order):
-        load(index).wait()
+        for each in load(index):
+            each.wait()
         if index + 1 < 8:
-            load(index + 1).start()
+            for each in load(index + 1):
+                each.start()
+        if kind == 3:
+            make(index)
         if slot >= 4:
+            if slot in (6, 4):
+                copies[3 if slot == 6 else 1].wait_send()
 
             def store(here, value, slot=slot):
-                mine[slot - 4, :, here] = rounded(value)
+                mine[turns[slot - 4], :, here] = rounded(value)
 
             product(index, store)
             copies[slot - 4].start()
@@ -888,16 +944,21 @@
         out_ref[part, :] = out_ref[part, :] + (
             near_x[part, :].astype(F32) + near_l[part, :].astype(F32)
         )
-    for each in copies:
-        each.wait_send()
+    for index, each in enumerate(copies):
+        if index not in (1, 3):
+            each.wait_send()
+    if kind == 3:
+        made(6).wait()
+        made(7).wait()
     if beside:
         tail.end()
 
 
 class WeightTail:
     def __init__(self, refs):
-        self.grad, self.totals, self.landing, stage, result, y_sems, z_sems, stage_sems = refs
-        self.y, _, _, _ = places()
+        self.grad, self.layer, self.totals, self.landing, self.layer_out = refs[:5]
+        stage, result, y_sems, z_sems, stage_sems, self.layer_stage, self.layer_sems = refs[5:]
+        self.y, self.c, self.h, _ = places()
         self.names = [("Q", 0, 0), ("Q", 1, 0)]
         self.pieces = PieceSums(
             self.names,
@@ -920,11 +981,35 @@
     def piece(self, name, y):
         return self.grad.at[pl.ds(pl.multiple_of((2 * y + name[1]) * 512, 512), 512)]
 
+    def layer_load(self):
+        return pltpu.make_async_copy(self.layer, self.layer_stage, self.layer_sems.at[2])
+
+    def layer_local(self):
+        return pltpu.make_async_copy(self.layer_stage, self.layer_out, self.layer_sems.at[2])
+
+    def layer_remote(self):
+        return remote(
+            self.layer, self.layer_out, self.layer_sems.at[0], self.layer_sems.at[1], {"c": self.h, "h": self.c}
+        )
+
     def begin(self):
         for name in self.names:
             self.pieces.over_y(name).start()
 
+        @pl.when(self.c == self.h)
+        def _():
+            self.layer_load().start()
+
+        @pl.when(self.c != self.h)
+        def _():
+            self.layer_remote().start()
+
     def run(self):
+        @pl.when(self.c == self.h)
+        def _():
+            self.layer_load().wait()
+            self.layer_local().start()
+
         for k in range(2):
             self.sums.load(k)
             self.sums.add(k)
@@ -933,46 +1018,94 @@
         self.sums.last_sent()
         self.pieces.end()
 
-
-def product_scatter(a, weight, dims, number, *grad):
+        @pl.when(self.c == self.h)
+        def _():
+            self.layer_local().wait()
+
+        @pl.when(self.c != self.h)
+        def _():
+            self.layer_remote().wait_recv()
+            self.layer_remote().wait_send()
+
+
+def scatter_scratch(depth, width, cut):
+    return [
+        pltpu.VMEM((2, ROW, depth), BF),
+        pltpu.VMEM((2, ROW, width), BF),
+        pltpu.VMEM((4, ROW, width), BF),
+        pltpu.VMEM((3, ROW, width), BF),
+        pltpu.VMEM((cut, width), BF),
+        pltpu.VMEM((ROW - cut, width), BF),
+        pltpu.VMEM((ROW, width), BF),
+        pltpu.VMEM((ROW, width), BF),
+        pltpu.SemaphoreType.DMA((10,)),
+        pltpu.SemaphoreType.DMA((10,)),
+        pltpu.SemaphoreType.DMA((2, 3)),
+    ]
+
+
+def feed_forward_back(grad, gate, up, down_weight, gate_up_weight, number):
+    anywhere = pl.BlockSpec(memory_space=pl.ANY)
+    vmem = pl.BlockSpec(memory_space=pltpu.VMEM)
+    return pl.pallas_call(
+        lambda *refs: scatter_kernel(NT, ROW // 2, 3, *refs),
+        in_specs=[anywhere] * 3 + [vmem] * 2,
+        out_specs=[vmem, anywhere],
+        out_shape=[
+            jax.ShapeDtypeStruct((ROW, 2048), F32),
+            jax.ShapeDtypeStruct((8 * ROW, 2048), BF),
+        ],
+        scratch_shapes=scatter_scratch(2048, 2048, ROW // 2)
+        + [
+            pltpu.VMEM((2, ROW, 2048), BF),
+            pltpu.VMEM((2, ROW, 1024), BF),
+            pltpu.VMEM((2, ROW, 1024), BF),
+            pltpu.SemaphoreType.DMA((2,)),
+        ],
+        compiler_params=pltpu.CompilerParams(
+            collective_id=number, has_side_effects=True, vmem_limit_bytes=62 * 2**20
+        ),
+        cost_estimate=pl.CostEstimate(
+            flops=80 * 10**9, bytes_accessed=60 * 2**20, transcendentals=0
+        ),
+    )(grad, gate, up, down_weight, gate_up_weight)
+
+
+def product_scatter(a, weight, dims, number, *more):
     anywhere = pl.BlockSpec(memory_space=pl.ANY)
     vmem = pl.BlockSpec(memory_space=pltpu.VMEM)
     depth = a.shape[1]
     width = weight.shape[0] if dims == NT else weight.shape[1]
+    cut = 384 if more else 256
     return pl.pallas_call(
-        lambda *refs: scatter_kernel(dims, len(grad), *refs),
-        in_specs=[anywhere, vmem] + [anywhere] * len(grad),
-        out_specs=[vmem] + [anywhere] * (2 * len(grad)),
+        lambda *refs: scatter_kernel(dims, cut, len(more), *refs),
+        in_specs=[anywhere, vmem] + [anywhere] * len(more),
+        out_specs=[vmem] + [anywhere] * (3 if more else 0),
         out_shape=[jax.ShapeDtypeStruct((ROW, width), F32)]
-        + [jax.ShapeDtypeStruct((2, 512, 768), BF)] * (2 * len(grad)),
-        scratch_shapes=[
-            pltpu.VMEM((2, ROW, depth), BF),
-            pltpu.VMEM((4, ROW, width), BF),
-            pltpu.VMEM((4, ROW, width), BF),
-            pltpu.VMEM((3, ROW, width), BF),
-            pltpu.VMEM((ROW // 2, width), BF),
-            pltpu.VMEM((ROW // 2, width), BF),
-            pltpu.VMEM((ROW, width), BF),
-            pltpu.VMEM((ROW, width), BF),
-            pltpu.SemaphoreType.DMA((10,)),
-            pltpu.SemaphoreType.DMA((10,)),
-            pltpu.SemaphoreType.DMA((2,)),
+        + [
+            jax.ShapeDtypeStruct((2, 512, 768), BF),
+            jax.ShapeDtypeStruct((2, 512, 768), BF),
+            jax.ShapeDtypeStruct((ROW, 2048), BF),
         ]
+        * bool(more),
+        scratch_shapes=scatter_scratch(depth, width, cut)
         + [
             pltpu.VMEM((2, 2, 512, 768), BF),
             pltpu.VMEM((2, 512, 768), BF),
             pltpu.SemaphoreType.DMA((2, 2)),
             pltpu.SemaphoreType.DMA((3, 2)),
             pltpu.SemaphoreType.DMA((2, 5)),
+            pltpu.VMEM((ROW, 2048), BF),
+            pltpu.SemaphoreType.DMA((3,)),
         ]
-        * len(grad),
+        * bool(more),
         compiler_params=pltpu.CompilerParams(
             collective_id=number, has_side_effects=True, vmem_limit_bytes=58 * 2**20
         ),
         cost_estimate=pl.CostEstimate(
             flops=80 * 10**9, bytes_accessed=30 * 2**20, transcendentals=0
         ),
-    )(a, weight, *grad)
+    )(a, weight, *more)
 
 
 def column_order():
@@ -1036,6 +1169,9 @@
             self.row_send,
             self.row_recv,
             self.own_sem,
+            stage,
+            out_stage,
+            self.grad_stage,
         ) = refs[7:]
         self.y, self.c, self.h, self.me = places()
         _, _, _, l, x = (lax.axis_index(name) for name in AXES)
@@ -1047,6 +1183,7 @@
                 near.at[k],
                 far.at[k],
                 keep.at[k],
+                stage.at[k],
             )
             for k in range(4)
         ]
@@ -1059,8 +1196,9 @@
             out_near,
             out_far,
             out_keep,
-        )
-        self.grad_ring = Ring(self.grad_full, ROW, grad_send, grad_recv)
+            out_stage,
+        )
+        self.grad_ring = Ring(self.grad_full, ROW, grad_send, grad_recv, lean=True, own=self.grad_stage)
         self.out_ring = Ring(self.out_full, 256, out_send, out_recv)
 
     def over_y(self, k, core, y):
@@ -1079,14 +1217,19 @@
         for core in range(2):
             self.over_y(k, core, self.y).start()
 
+    def own_out(self):
+        return pltpu.make_async_copy(
+            self.grad_stage, self.grad_full.at[rows_at(self.me)], self.own_sem.at[0]
+        )
+
     def begin(self):
-        own = pltpu.make_async_copy(self.grad_own, self.grad_full.at[rows_at(self.me)], self.own_sem.at[0])
+        own = pltpu.make_async_copy(self.grad_own, self.grad_stage, self.own_sem.at[0])
         own.start()
         enter_ring(wide_partners())
         self.out_piece.start()
-        self.pieces[0].start()
         own.wait()
         self.grad_ring.start(0, 1, 2, 3, 4)
+        self.own_out().start()
 
     def at(self, step):
         def when(number, *actions):
@@ -1098,37 +1241,46 @@
         def out_on():
             self.out_piece.arrived()
             self.out_over_y(self.y).start()
+            self.pieces[0].start()
 
         def out_ring_on():
             self.out_over_y(1 - self.y).wait_recv()
             self.out_ring.start(0, 1, 2, 3, 4)
-
-        def relay(ring):
-            ring.arrived(0)
-            ring.start(5)
-            ring.arrived(1)
-            ring.start(6)
-
-        def relay_core(ring):
-            ring.arrived(3)
-            ring.start(7)
-            ring.arrived(4)
-            ring.start(8)
-
-        def relay_last(ring):
-            ring.arrived(5, 6)
-            ring.start(9)
+            self.pieces[1].start()
+
+        def grad_one():
+            self.grad_ring.arrived(1)
+            self.grad_ring.start(6)
+
+        def grad_two():
+            self.grad_ring.arrived(4)
+            self.grad_ring.start(5, 8)
+            self.grad_ring.arrived(0, 3)
+            self.grad_ring.start(7)
+
+        def out_one():
+            self.out_ring.arrived(0)
+            self.out_ring.start(5)
+            self.out_ring.arrived(1)
+            self.out_ring.start(6)
+
+        def out_two():
+            self.out_ring.arrived(3)
+            self.out_ring.start(7)
+            self.out_ring.arrived(4)
+            self.out_ring.start(8)
 
         when(0, self.begin)
-        when(3, out_on, self.pieces[1].start)
-        when(6, out_ring_on, lambda: relay(self.grad_ring))
+        when(3, out_on)
+        when(6, out_ring_on)
+        when(7, grad_one)
         when(9, lambda: self.piece_over_y(0), self.pieces[2].start)
-        when(12, lambda: relay_core(self.grad_ring), lambda: relay(self.out_ring))
+        when(11, grad_two)
         when(14, lambda: self.piece_over_y(1), self.pieces[3].start)
-        when(18, lambda: relay_core(self.out_ring), lambda: relay_last(self.grad_ring))
-        when(20, lambda: self.piece_over_y(2))
-        when(25, lambda: relay_last(self.out_ring))
-        when(29, lambda: self.piece_over_y(3))
+        when(16, out_one)
+        when(19, lambda: self.piece_over_y(2))
+        when(22, out_two)
+        when(28, lambda: self.piece_over_y(3))
 
     def row_local(self, block, o_all):
         columns = pl.ds(pl.multiple_of(self.me * 256, 256), 256)
@@ -1156,6 +1308,10 @@
             self.row_remote(block, o_all, self.me).start()
 
     def end(self, o_all):
+        for ring in (self.out_ring, self.grad_ring):
+            ring.arrived(5, 6)
+            ring.start(9)
+        self.own_out().wait()
         self.out_piece.sent()
         self.out_over_y(self.y).wait_send()
         for k in range(4):
@@ -1291,7 +1447,8 @@
         + SPREAD_SEMAPHORES
         + [dma((2,)), dma((3,)), dma, dma((2,))]
         + [dma((10,))] * 4
-        + [dma((8,)), dma((8,)), dma((2,))],
+        + [dma((8,)), dma((8,)), dma((2,))]
+        + [pltpu.VMEM((4, 128, 2048), BF), pltpu.VMEM((256, 512), BF), pltpu.VMEM((ROW, 2048), BF)],
         compiler_params=pltpu.CompilerParams(
             collective_id=6, has_side_effects=True, vmem_limit_bytes=48 * 2**20
         ),
@@ -1358,8 +1515,11 @@
             then()
 
     def either(self, here, away, local, method):
-        if here is None:
+        if local is None:
             getattr(away(), method)()
+            return
+        if away is None:
+            getattr(local(), "wait" if method == "wait_send" else method)()
             return
 
         @pl.when(here)
@@ -1396,7 +1556,8 @@
 
 
 class RingSum:
-    def __init__(self, parts, size, core_land, far_land, core_sems, far_sems):
+    def __init__(self, parts, size, core_land, far_land, core_sems, far_sems, lean):
+        self.lean = lean
         self.parts, self.size, self.core_land, self.far_land = parts, size, core_land, far_land
         self.core_sems, self.far_sems = core_sems, far_sems
         self.me, (self.to_x, self.to_l, self.to_c) = ring_position()
@@ -1418,7 +1579,7 @@
             self.core(slot).start()
 
     def far(self, index, source):
-        device = self.to_x if index in (0, 2, 4) else self.to_l
+        device = self.to_x if index in ((0, 1, 2, 3) if self.lean else (0, 2, 4)) else self.to_l
         return remote(
             source, self.far_land.at[index], self.far_sems.at[0, index], self.far_sems.at[1, index], device
         )
@@ -1432,34 +1593,26 @@
             self.core_land.at[slot, :, half_columns(half)],
         ]
 
-    def add_to(self, sums, due, last_sends, extra):
-        def items():
-            core = lambda slot: (lambda: self.core(slot).wait_recv())
-            send = lambda index: (lambda source: [(None, lambda: self.far(index, source), None)])
-            yield 0, self.terms(3, 0), send(0), [core(3)], None
-            yield 1, self.terms(3, 1), send(1), [], None
-            yield 2, self.terms(1, 0), send(2), [core(1)], None
-            yield 3, self.terms(2, 1), send(3), [core(2)], None
-            yield 4, self.terms(1, 1) + [self.far_land.at[1]], send(4), [self.landed(1)], None
-            yield 5, self.terms(2, 0) + [self.far_land.at[0]], send(5), [self.landed(0)], None
-            yield (
-                6,
-                self.terms(0, 0) + [self.far_land.at[2], self.far_land.at[5]],
-                last_sends(0),
-                [core(0), self.landed(2), self.landed(5)],
-                extra(0),
-            )
-            yield (
-                7,
-                self.terms(0, 1) + [self.far_land.at[4], self.far_land.at[3]],
-                last_sends(1),
-                [self.landed(4), self.landed(3)],
-                extra(1),
-            )
-
-        return [
-            (due[index], self.size, terms, sends, waits, more) for index, terms, sends, waits, more in items()
-        ]
+    def work(self, due, last_sends, extra):
+        if self.lean:
+            plan = ((3, 0), (3, 1), (1, 0), (1, 1), (2, 0, 0), (2, 1, 1), (0, 0, 2, 4), (0, 1, 3, 5))
+        else:
+            plan = ((3, 0), (3, 1), (1, 0), (2, 1), (1, 1, 1), (2, 0, 0), (0, 0, 2, 5), (0, 1, 4, 3))
+        first = {}
+        for index in sorted(range(8), key=lambda index: due[index]):
+            first.setdefault(plan[index][0], index)
+        items = []
+        for index, (slot, half, *landings) in enumerate(plan):
+            waits = [self.landed(landing) for landing in landings]
+            if first[slot] == index:
+                waits.append(lambda slot=slot: self.core(slot).wait_recv())
+            if index < 6:
+                sends = lambda source, index=index: [(None, lambda: self.far(index, source), None)]
+            else:
+                sends = last_sends(half)
+            terms = self.terms(slot, half) + [self.far_land.at[landing] for landing in landings]
+            items.append((due[index], self.size, terms, sends, waits, extra(half) if index >= 6 else None))
+        return items
 
     def end(self):
         for slot in range(4):
@@ -1571,21 +1724,21 @@
         ) = refs[19:]
         self.y, self.c, self.h, self.me = places()
         self.sums = Sums(stage, result, stage_sems)
-        self.layer_ring = RingSum(self.parts, ROW, core_land, far_land, core_sems, far_sems)
-        self.out_ring = RingSum(self.out, 256, out_core_land, out_far_land, out_core_sems, out_far_sems)
+        self.layer_ring = RingSum(self.parts, ROW, core_land, far_land, core_sems, far_sems, True)
+        self.out_ring = RingSum(
+            self.out, 256, out_core_land, out_far_land, out_core_sems, out_far_sems, False
+        )
         names = [("D", 0, 0), ("D", 1, 0), ("G", 0, 0), ("G", 0, 1), ("G", 1, 0), ("G", 1, 1)]
         self.pieces = PieceSums(names, self.piece, lambda name: self.y_land.at[names.index(name)], self.sums_at, y_sems, z_sems)
         self.names = names
         out_names = [("O", 0, 0), ("O", 1, 0)]
         self.out_pieces = PieceSums(out_names, None, None, self.sums_at, out_y_sems, out_z_sems)
-        work = self.layer_ring.add_to(
-            self.sums, (8, 9, 10, 11, 25, 26, 46, 47), self.layer_sends, self.residual_half
-        )
-        work += self.out_ring.add_to(
-            self.sums, (28, 29, 30, 31, 51, 52, 63, 64), self.out_sends, lambda half: None
-        )
-        for name, due in zip(names, (13, 24, 36, 48, 58, 69)):
-            work.append((due, ROW, [self.piece(name, self.y), self.y_land.at[names.index(name)]], self.pieces.sends(name), [self.arrived(name)], None))
+        work = self.layer_ring.work((22, 35, 48, 61, 36, 56, 62, 70), self.layer_sends, self.residual_half)
+        work += self.out_ring.work((1, 2, 8, 14, 15, 25, 37, 26), self.out_sends, lambda half: None)
+        for name, due in zip(names, (3, 16, 29, 44, 57, 69)):
+            terms = [self.piece(name, self.y), self.y_land.at[names.index(name)]]
+            work.append((due, ROW, terms, self.pieces.sends(name), [self.arrived(name)], None))
+        work.append((64, 256, [self.out_own, self.out_y_land], self.out_owners, [self.out_landed], None))
         work.sort(key=lambda item: item[0])
         for item in work:
             self.sums.item(*item)
@@ -1593,29 +1746,35 @@
     def arrived(self, name):
         def wait():
             self.pieces.over_y(name).wait_recv()
-            place = self.names.index(name) + 2
+            place = self.names.index(name) + 1
             if place < 6:
                 self.pieces.over_y(self.names[place]).start()
 
         return wait
 
+    def out_landed(self):
+        remote(
+            self.out_own, self.out_y_land, self.out_sems.at[0], self.out_sems.at[2], {"y": 1 - self.y}
+        ).wait_recv()
+
+    def out_owners(self, source):
+        sends = []
+        for name in self.out_pieces.names:
+            sends += self.out_pieces.sends(name)(source.at[:, pl.ds(name[1] * 512, 512)])
+        return sends
+
     def residual_half(self, half):
         return (self.residual.at[:, half_columns(half)], self.rest)
 
     def layer_sends(self, half):
         def sends(source):
-            target = self.layer.at[:, half_columns(half)]
             return [
                 (
-                    self.c == self.h,
-                    lambda: remote(
-                        source,
-                        target,
-                        self.layer_sems.at[0, half],
-                        self.layer_sems.at[1, half],
-                        {"c": self.h, "h": self.c},
+                    None,
+                    None,
+                    lambda: pltpu.make_async_copy(
+                        source, self.layer.at[:, half_columns(half)], self.layer_sems.at[half]
                     ),
-                    lambda: pltpu.make_async_copy(source, target, self.layer_sems.at[0, half]),
                 )
             ]
 
@@ -1688,8 +1847,7 @@
         lax.fori_loop(0, 8, send, 0)
         self.layer_ring.begin()
         self.out_ring.begin()
-        for name in self.names[:2]:
-            self.pieces.over_y(name).start()
+        self.pieces.over_y(self.names[0]).start()
         for copy in self.tables():
             copy.wait()
 
@@ -1715,45 +1873,10 @@
 
         lax.fori_loop(0, 8, each, 0)
         self.sums.last_sent()
-        remote(
-            self.out_own, self.out_y_land, self.out_sems.at[0], self.out_sems.at[2], {"y": 1 - self.y}
-        ).wait_recv()
-        terms = [self.out_own, self.out_y_land]
-        count = len(self.sums.items)
-
-        def owners(source):
-            sends = []
-            for name in self.out_pieces.names:
-                part = source.at[:, pl.ds(name[1] * 512, 512)]
-                sends += self.out_pieces.sends(name)(part)
-            return sends
-
-        self.sums.item(0, 256, terms, owners)
-        self.sums.load(count)
-        for copy in self.sums.loads(count):
-            copy.wait()
-        turn = count % 2
-        total = self.sums.stage[turn, 0, 0:256, :].astype(F32) + self.sums.stage[turn, 1, 0:256, :].astype(F32)
-        self.sums.result[turn, 0:256, :] = rounded(total)
-        for here, away, local in owners(self.sums.result.at[turn, pl.ds(0, 256)]):
-            self.sums.either(here, away, local, "start")
         self.layer_ring.end()
         self.out_ring.end()
         self.pieces.end()
-        for here, away, local in owners(self.sums.result.at[turn, pl.ds(0, 256)]):
-            self.sums.either(here, away, local, "wait_send")
         self.out_pieces.owned()
-
-        @pl.when(self.c != self.h)
-        def _():
-            for half in range(2):
-                remote(
-                    self.layer.at[:, half_columns(half)],
-                    self.layer.at[:, half_columns(half)],
-                    self.layer_sems.at[0, half],
-                    self.layer_sems.at[1, half],
-                    {"c": self.h, "h": self.c},
-                ).wait_recv()
 
 
 def attend_back_kernel(q_ref, k_ref, v_ref, o_ref, l_ref, *refs):
@@ -1909,7 +2032,7 @@
             dma((2, 6)),
             dma((2, 4)),
             dma((2, 6)),
-            dma((2, 2)),
+            dma((2,)),
             dma((2, 6)),
             dma((3, 6)),
             dma((3,)),
@@ -1989,7 +2112,9 @@
         256,
         attention_finish,
         First,
-        [pltpu.VMEM((2048, 768), BF)] + SPREAD_SEMAPHORES + [pltpu.SemaphoreType.DMA((4,))],
+        [pltpu.VMEM((2048, 768), BF)]
+        + SPREAD_SEMAPHORES
+        + [pltpu.SemaphoreType.DMA((4,)), pltpu.VMEM((ROW, 2048), BF)],
         1,
     )
     gate_up_shard = jnp.concatenate([gate_up_master[0], gate_up_master[1]], axis=1).astype(BF)
@@ -2007,17 +2132,13 @@
         1024,
         feed_forward_finish,
         Second,
-        SPREAD_SEMAPHORES,
+        SPREAD_SEMAPHORES + [pltpu.VMEM((2, 512, 512), BF)],
         2,
     )
 
-    grad_act = lax.dot_general(grad_out, down_weight, NT, preferred_element_type=F32)
-    g = gate.astype(F32)
-    sigmoid = jax.nn.sigmoid(g)
-    grad_gate = (grad_act * up.astype(F32) * sigmoid * (1.0 + g * (1.0 - sigmoid))).astype(BF)
-    grad_up = (grad_act * g * sigmoid).astype(BF)
-    grad_gate_up = jnp.concatenate([grad_gate, grad_up], axis=1)
-    grad_normed_second = product_scatter(grad_gate_up, gate_up_weight, NT, 3)[0]
+    grad_normed_second, grad_gate_up = feed_forward_back(
+        grad_out, gate, up, down_weight, gate_up_weight, 3
+    )
     gate_up_grad = lax.dot_general(
         normed_second, grad_gate_up, TN, preferred_element_type=F32
     ).astype(BF)
@@ -2038,17 +2159,22 @@
     residual_low = residual_grad.astype(BF)
     grad_heads = lax.dot_general(residual_low, out_weight, NT, preferred_element_type=F32).astype(BF)
     out_grad = lax.dot_general(attended_own, residual_low, TN, preferred_element_type=F32).astype(BF)
-    grad_kv, grad_q, gate_up_sums, down_sums, out_sums, layer_output, *_ = attend_back(
+    grad_kv, grad_q, gate_up_sums, down_sums, out_sums, layer_own, *_ = attend_back(
         queries, keys, values, attended, level, grad_heads, layer_parts, gate_up_grad, down_grad, out_grad, residual, cosine, sine
     )
     gate_up_grad_own = gate_up_sums[0].astype(F32) + gate_up_sums[1].astype(F32)
-    down_grad_own = (down_sums[0].astype(F32) + down_sums[1].astype(F32)).T
+    unit = jnp.eye(512, dtype=BF)
+    down_grad_own = lax.dot_general(
+        down_sums.reshape(1024, 1024), jnp.concatenate([unit, unit]), TN, preferred_element_type=F32
+    )
     out_grad_own = out_sums[0].astype(F32) + out_sums[1].astype(F32)
 
     grad_mixture = jnp.concatenate([grad_q, grad_kv], axis=1)
     qkv_grad = lax.dot_general(normed, grad_mixture, TN, preferred_element_type=F32).astype(BF)
     qkv_grad = lax.dot_general(qkv_grad, turn, NT, preferred_element_type=F32).astype(BF)
-    grad_normed_first, qkv_sums, _ = product_scatter(grad_mixture, qkv_weight, NT, 5, qkv_grad)
+    grad_normed_first, qkv_sums, _, layer_output = product_scatter(
+        grad_mixture, qkv_weight, NT, 5, qkv_grad, layer_own
+    )
     qkv_grad_own = qkv_sums[0].astype(F32) + qkv_sums[1].astype(F32)
 
     input_back, gain_first_part = norm_grad(rows_in, scale_first, gain_first, grad_normed_first)

time: 1350 us -> 1190 us (0.88)
  Pallas kernels: 1000 us -> 912 us
  matrix products: 169 us -> 145 us
  local copies, waits for them, and re-layouts: 34.4 us -> 11.5 us
  other arithmetic: 81.7 us -> 59.2 us
    pallas_call x1, Pallas kernels: 325 us -> 233 us  [attend_back(): pl.pallas_call(attend_back_kernel, grid=(blocks, 2), in_specs=[key_spec(2...]
    pallas_call x2, Pallas kernels: 199 us -> 261 us  [the longest x1 148 us: product_scatter(): pl.pallas_call(lambda *refs: scatter_kernel(dims, cut, len(more), *refs),...]
    pallas_call x1, Pallas kernels: 232 us -> 191 us  [attend(): pl.pallas_call(attend_kernel, grid=(blocks, 4), in_specs=[pl.BlockSpec((R...]
    unnamed x153 -> x134, local copies, waits for them, and re-layouts: 31.4 us -> 9.83 us
    dot_general x1, matrix products: 23.8 us -> 3.32 us  [ring_shards(): lax.dot_general(down_sums.reshape(1024, 1024), jnp.concatenate([unit, uni...]
    pallas_call x2, Pallas kernels: 248 us -> 227 us  [gather_product(): pl.pallas_call(lambda *refs: gather_kernel(finish, beside, inputs, len(ex...]
  transfers between devices with their start and end apart: 12 -> 12, of which waited for: 3 -> 4; matrix products, arithmetic and copies ran while one was open for 5% -> 4% of each run, Pallas kernels for 0% -> 0%
where the time goes in v6:
time: 1190 us; the launch traced here: 1180 us
  Pallas kernels  912 us (77%)
  matrix products  145 us (12%)
  other arithmetic  59.2 us (5%)
  starting transfers between devices  23.8 us (2%)
  waiting for transfers between devices  22.2 us (2%)
    pallas_call x1, Pallas kernels, attend_back(): pl.pallas_call(attend_back_kernel, grid=(blocks, 2), in_specs=[key_spec(2...  233 us
    pallas_call x2, Pallas kernels, gather_product(): pl.pallas_call(lambda *refs: gather_kernel(finish, beside, inputs, len(ex...  227 us
    pallas_call x1, Pallas kernels, attend(): pl.pallas_call(attend_kernel, grid=(blocks, 4), in_specs=[pl.BlockSpec((R...  191 us
    pallas_call x1, Pallas kernels, product_scatter(): pl.pallas_call(lambda *refs: scatter_kernel(dims, cut, len(more), *refs),...  148 us
    pallas_call x1, Pallas kernels, feed_forward_back(): pl.pallas_call(lambda *refs: scatter_kernel(NT, ROW // 2, 3, *refs), in_s...  113 us
    dot_general x1, matrix products, ring_shards(): lax.dot_general(normed_second, grad_gate_up, TN, preferred_element_type=F32)  43.3 us
    dot_general x1, matrix products, ring_shards(): jnp.dot(activation, down_weight, preferred_element_type=F32).astype(BF)  23.8 us
  transfers between devices with their start and end apart: 12, of which 4 were waited for; matrix products, arithmetic and copies ran while one was open for 4% of the time, Pallas kernels for 0%

profile of v6, /device:TPU:0, one launch (start us, length us, event | category | flops | bytes accessed | tf_op | source)
XLA Modules:
  0.0 1178.1 jit_solution(6449319471947098203)
XLA Ops:
  3.6 3.8 collective-permute-start.1
  26.9 3.4 multiply_convert_fusion.1.refs_4_
  30.9 9.3 multiply_sine_fusion
  42.6 115.4 %shard_map.354 = (bf16[4096,2048]{1,0:T(8,128)(2,1)}, bf16[4096,256]{1,0:T(8,128)(2,1)}, bf16[4096,256]{1,0:T(8,128)(2,1)}, bf16[4096,256]{1,0:T(8,128)(2,1)}, b...) custom-call(bf16[512,2048]{1,0:T(8,128)(2,1)} %fusion.2.refs_0_, f32[4096,128]{1,0:T(8,128)} %get-tuple-element.102.refs_1_.refs_6_, ...), custom_call_target="tpu_custom_call" | custom-call | flops 80000000000 | bytes 31457280 | tf_op jit(solution)/shard_map/pallas_call | solution.py:777
  158.0 191.4 %shard_map.355 = (bf16[4096,256]{1,0:T(8,128)(2,1)S(1)}, f32[8,4,512]{2,1,0:T(4,128)S(1)}, bf16[2048,2048]{1,0:T(8,128)(2,1)}, bf16[2048,2048]{1,0:T(8,128)(2,1)...) custom-call(bf16[4096,256]{1,0:T(8,128)(2,1)} %get-tuple-element.50.q_ref, ...), custom_call_target="tpu_custom_call" | custom-call | flops 112000000000 | bytes 10485760 | tf_op jit(solution)/shard_map/pallas_call | solution.py:1424
  349.5 8.6 multiply_reduce_fusion.2
  360.7 112.0 %shard_map.356 = (bf16[4096,2048]{1,0:T(8,128)(2,1)}, bf16[4096,1024]{1,0:T(8,128)(2,1)}, bf16[4096,1024]{1,0:T(8,128)(2,1)}, bf16[4096,1024]{1,0:T(8,128)(2,1)}, bf16[1024,2048]{1,0:T(8,128)(2,1)}) custom-call(bf16[512,2048]{1,0:T(8,128)(2,1)} %multiply_convert_fusion.refs_0_, bf16[2048,2048]{1,0:T(8,128)(2,1)} %get-tuple-element.59.refs_1_.refs_4_, ...), custom_call_target="tpu_custom_call" | custom-call | flops 80000000000 | bytes 31457280 | tf_op jit(solution)/shard_map/pallas_call | solution.py:777
  472.8 23.8 %convolution_convert_fusion.refs_1_ = bf16[4096,2048]{1,0:T(8,128)(2,1)} fusion(bf16[4096,1024]{1,0:T(8,128)(2,1)} %get-tuple-element.64, bf16[1024,2048]{1,0:T(8,128)(2,1)} %get-tuple-element.62.refs_3_), kind=kOutput, calls=%fused_computation | convolution fusion | flops 17188257792 | bytes 29360128 | tf_op jit(solution)/shard_map/dot_general | solution.py:2146
  496.6 21.4 %convolution_convert_fusion.3.refs_3_ = bf16[2048,1024]{1,0:T(8,128)(2,1)} fusion(bf16[4096,2048]{1,0:T(8,128)(2,1)} %get-tuple-element.58.refs_0_, bf16[4096,1024]{1,0:T(8,128)(2,1)S(1)} %copy-done.65), kind=kOutput, calls=%fused_computation.35 | convolution fusion | flops 17181966336 | bytes 29360128 | tf_op jit(solution)/shard_map/dot_general | solution.py:2145
  518.0 113.1 %shard_map.357 = (f32[512,2048]{1,0:T(8,128)}, bf16[4096,2048]{1,0:T(8,128)(2,1)}) custom-call(bf16[4096,2048]{1,0:T(8,128)(2,1)} %get-tuple-element.58.refs_0_, bf16[4096,1024]{1,0:T(8,128)(2,1)} %get-tuple-element.60.refs_1_, bf16[4096,1024]{1,0:T(8,128)(2,1)} %get-tuple-element.61.refs_2_, bf16[1024,2048]{1,0:T(8,128)(2,1)} %get-tuple-element.62.refs_3_, ...), custom_call_target="tpu_custom_call" | custom-call | flops 80000000000 | bytes 62914560 | tf_op jit(solution)/shard_map/pallas_call | solution.py:1050
  631.2 5.2 multiply_reduce_fusion
  640.0 11.2 convolution_convert_fusion.6.refs_0_
  651.2 6.9 convolution_convert_fusion.1.refs_4_
  658.1 43.3 %convolution_convert_fusion.2.refs_2_ = bf16[2048,2048]{1,0:T(8,128)(2,1)} fusion(bf16[4096,2048]{1,0:T(8,128)(2,1)} %get-tuple-element.65, bf16[4096,2048]{1,0:T(8,128)(2,1)} %get-tuple-element.66), kind=kOutput, calls=%fused_computation.7 | convolution fusion | flops 34363932672 | bytes 41943040 | tf_op jit(solution)/shard_map/dot_general | solution.py:2142
  701.4 232.8 %shard_map.358 = (bf16[4096,512]{1,0:T(8,128)(2,1)}, bf16[4096,256]{1,0:T(8,128)(2,1)}, bf16[2,512,2048]{2,1,0:T(8,128)(2,1)}, bf16[2,512,1024]{2,1,0:T(8,128)(2...) custom-call(bf16[4096,256]{1,0:T(8,128)(2,1)} %get-tuple-element.50., ...), custom_call_target="tpu_custom_call" | custom-call | flops 152000004096 | bytes 20971520 | tf_op jit(solution)/shard_map/pallas_call | solution.py:2004
  937.6 19.7 %convolution_convert_fusion.4.clone.5 = bf16[2048,768]{1,0:T(8,128)(2,1)S(1)} fusion(bf16[4096,2048]{1,0:T(8,128)(2,1)} %get-tuple-element.70, bf16[4096,768]{1,0:T(8,128)(2,1)S(1)} %constant_dynamic-update-slice_fusion.refs_0_), kind=kOutput, calls=%fused_computation.52.clone.clone.clone.2 | convolution fusion | flops 12886474752 | bytes 26214400 | tf_op jit(solution)/shard_map/dot_general | solution.py:2173
  957.4 4.9 convolution_convert_fusion.5.refs_2_
  962.3 147.6 %shard_map.359 = (f32[512,2048]{1,0:T(8,128)}, bf16[2,512,768]{2,1,0:T(8,128)(2,1)}, bf16[2,512,768]{2,1,0:T(8,128)(2,1)}, bf16[512,2048]{1,0:T(8,128)(2,1)}) custom-call(bf16[4096,768]{1,0:T(8,128)(2,1)} %copy-done.34, bf16[2048,768]{1,0:T(8,128)(2,1)} %get-tuple-element.69.refs_1_, bf16[2048,768]{1,0:T(8,128)(2,1)} %convolution_convert_fusion.5.refs_2_, ...), custom_call_target="tpu_custom_call" | custom-call | flops 80000000000 | bytes 31457280 | tf_op jit(solution)/shard_map/pallas_call | solution.py:1080
  1109.9 3.6 fusion.11
  1113.6 3.7 fusion.7
  1122.5 3.6 fusion.60
  1131.9 3.3 fusion.59
  1145.0 3.8 collective-permute-start.10
  1149.8 18.9 %collective-permute-done.10 = f32[2,2048]{1,0:T(2,128)S(1)} collective-permute-done((f32[2,2048]{1,0:T(2,128)S(1)}, f32[2,2048]{1,0:T(2,128)S(1)}, u32[]{:S(2)}, u32[]{:S(2)}) %collective-permute-start.10) | collective-permute-done | bytes 16416 | tf_op jit(solution)/shard_map/ppermute | solution.py:354
  (197 shorter events, 63.5 us)
Async XLA Ops:
  0.7 39.6 %collective-permute-start = (bf16[512,2048]{1,0:T(8,128)(2,1)}, bf16[512,2048]{1,0:T(8,128)(2,1)S(1)}, u32[]{:S(2)}, u32[]{:S(2)}) collective-permute-start(bf16[512,2048]{1,0:T(8,128)(2,1)} %param.19), channel_id=1, source_target_pairs={{0,0},{1,1},{2,2},{3,3},{4,8},{5,9},{6,10},{7,11},{8,4},{9,5},{10,... | collective-permute-start | bytes 6291464 | tf_op jit(solution)/shard_map/ppermute | solution.py:354
  3.6 21.6 %collective-permute-start.1 = (bf16[2,512]{1,0:T(2,128)(2,1)S(1)}, bf16[2,512]{1,0:T(2,128)(2,1)S(1)}, u32[]{:S(2)}, u32[]{:S(2)}) collective-permute-start(bf16[2,512]{1,0:T(2,128)(2,1)S(1)} %convert_element_type.124), channel_id=1, source_target_pairs={{0,8},{1,9},{2,10},{3,11},{4,12},{5,13},{6,14},{7,15},{8,0},{9,1},... | collective-permute-start | bytes 6152 | tf_op jit(solution)/shard_map/ppermute | solution.py:354
  7.4 23.5 %collective-permute-start.3 = (s32[4096]{0:T(1024)}, s32[4096]{0:T(1024)S(1)}, u32[]{:S(2)}, u32[]{:S(2)}) collective-permute-start(s32[4096]{0:T(1024)} %param.22), channel_id=1, source_target_pairs={{0,8},{1,9},{2,10},{3,11},{4,12},{5,13},{6,14},{7,15},{8,0},{9,1},... | collective-permute-start | bytes 49160 | tf_op jit(solution)/shard_map/ppermute | solution.py:354
  8.1 12.2 %collective-permute-start.4 = (f32[1]{0:T(128)}, f32[1]{0:T(128)}, u32[]{:S(2)}, u32[]{:S(2)}) collective-permute-start(f32[1]{0:T(128)} %convert_element_type.132), channel_id=1, source_target_pairs={{0,8},{1,9},{2,10},{3,11},{4,12},{5,13},{6,14},{7,15},{8,0},{9,1},... | collective-permute-start | bytes 20 | tf_op jit(solution)/shard_map/ppermute | solution.py:354
  20.9 3.7 collective-permute-start.5
  25.3 5.0 collective-permute-start.2
  158.0 191.5 %copy-start.7 = (bf16[512,2048]{1,0:T(8,128)(2,1)S(1)}, bf16[512,2048]{1,0:T(8,128)(2,1)}, u32[]{:S(2)}) copy-start(bf16[512,2048]{1,0:T(8,128)(2,1)} %copy-done.6) | copy-start | bytes 6291460
  472.8 23.8 %copy-start.65 = (bf16[4096,1024]{1,0:T(8,128)(2,1)S(1)}, bf16[4096,1024]{1,0:T(8,128)(2,1)}, u32[]{:S(2)}) copy-start(bf16[4096,1024]{1,0:T(8,128)(2,1)} %get-tuple-element.64) | copy-start | bytes 25165828
  518.0 113.2 %copy-start.41 = (f32[1,2048]{1,0:T(1,128)S(1)}, f32[1,2048]{1,0:T(1,128)}, u32[]{:S(2)}) copy-start(f32[1,2048]{1,0:T(1,128)} %get-tuple-element.103) | copy-start | bytes 24580
  518.0 113.2 %copy-start.48 = (f32[512]{0:T(512)S(1)}, f32[512]{0:T(512)}, u32[]{:S(2)}) copy-start(f32[512]{0:T(512)} %copy-done.47) | copy-start | bytes 6148
  962.3 147.6 %copy-start.8 = (bf16[512,2048]{1,0:T(8,128)(2,1)S(1)}, bf16[512,2048]{1,0:T(8,128)(2,1)}, u32[]{:S(2)}) copy-start(bf16[512,2048]{1,0:T(8,128)(2,1)} %copy-done.6) | copy-start | bytes 6291460
  962.3 147.6 %copy-start.39 = (f32[1,2048]{1,0:T(1,128)S(1)}, f32[1,2048]{1,0:T(1,128)}, u32[]{:S(2)}) copy-start(f32[1,2048]{1,0:T(1,128)} %copy-done.38) | copy-start | bytes 24580
  962.3 147.6 %copy-start.46 = (f32[512]{0:T(512)S(1)}, f32[512]{0:T(512)}, u32[]{:S(2)}) copy-start(f32[512]{0:T(512)} %copy-done.45) | copy-start | bytes 6148
  1117.3 56.5 %collective-permute-start.6 = (bf16[512,2048]{1,0:T(8,128)(2,1)S(1)}, bf16[512,2048]{1,0:T(8,128)(2,1)S(1)}, u32[]{:S(2)}, u32[]{:S(2)}) collective-permute-start(bf16[512,2048]{1,0:T(8,128)(2,1)S(1)} %fusion.7), channel_id=1, source_target_pairs={{0,0},{1,1},{2,2},{3,3},{4,8},{5,9},{6,10},{7,11},{8,4},{9,5},{10,... | collective-permute-start | bytes 6291464 | tf_op jit(solution)/shard_map/ppermute | solution.py:354
  1119.3 17.9 %collective-permute-start.7 = (f32[2,2048]{1,0:T(2,128)S(1)}, f32[2,2048]{1,0:T(2,128)S(1)}, u32[]{:S(2)}, u32[]{:S(2)}) collective-permute-start(f32[2,2048]{1,0:T(2,128)S(1)} %pad_maximum_fusion.2), channel_id=1, source_target_pairs={{0,1},{1,0},{2,3},{3,2},{4,5},{5,4},{6,7},{7,6},{8,9},{9,8},{10,11... | collective-permute-start | bytes 49160 | tf_op jit(solution)/shard_map/ppermute | solution.py:354
  1137.2 3.8 collective-permute-start.8
  1141.1 3.9 collective-permute-start.9
  1145.0 25.2 %copy-start.35 = (f32[256,512]{1,0:T(8,128)S(1)}, f32[256,512]{1,0:T(8,128)}, u32[]{:S(2)}) copy-start(f32[256,512]{1,0:T(8,128)} %param.28) | copy-start | bytes 1572868
  1145.0 27.6 %copy-start.44 = (f32[2,512]{1,0:T(2,128)S(1)}, f32[2,512]{1,0:T(2,128)}, u32[]{:S(2)}) copy-start(f32[2,512]{1,0:T(2,128)} %param.35) | copy-start | bytes 12292
  1145.0 27.6 %copy-start.60 = (f32[2,512]{1,0:T(2,128)S(1)}, f32[2,512]{1,0:T(2,128)}, u32[]{:S(2)}) copy-start(f32[2,512]{1,0:T(2,128)} %param.36) | copy-start | bytes 12292
  1145.0 28.2 %copy-start.51 = (f32[2,512]{1,0:T(2,128)S(1)}, f32[2,512]{1,0:T(2,128)}, u32[]{:S(2)}) copy-start(f32[2,512]{1,0:T(2,128)} %param.37) | copy-start | bytes 12292
  1145.0 23.8 %collective-permute-start.10 = (f32[2,2048]{1,0:T(2,128)S(1)}, f32[2,2048]{1,0:T(2,128)S(1)}, u32[]{:S(2)}, u32[]{:S(2)}) collective-permute-start(f32[2,2048]{1,0:T(2,128)S(1)} %add.228), channel_id=1, source_target_pairs={{0,4},{1,5},{2,6},{3,7},{4,0},{5,1},{6,2},{7,3},{8,12},{9,13},{10,... | collective-permute-start | bytes 49160 | tf_op jit(solution)/shard_map/ppermute | solution.py:354
  1149.8 26.5 %copy-start.23 = (f32[256,512]{1,0:T(8,128)}, f32[256,512]{1,0:T(8,128)S(1)}, u32[]{:S(2)}) copy-start(f32[256,512]{1,0:T(8,128)S(1)} %get-tuple-element.145) | copy-start | bytes 1572868
  1168.8 3.8 collective-permute-start.11
  (54 other events, 375.1 us)

commit v7 on v6

--- a/solution.py
+++ b/solution.py
@@ -1464,7 +1464,9 @@
 class Sums:
     def __init__(self, stage, result, stage_sems):
         self.stage, self.result, self.stage_sems = stage, result, stage_sems
+        self.depth = result.shape[0]
         self.items = []
+        self.early = ()
 
     def item(self, due, rows, terms, sends, waits=(), extra=None, then=None):
         self.items.append((due, rows, terms, sends, waits, extra, then))
@@ -1493,9 +1495,9 @@
         turn = k % 2
         for copy in self.loads(k):
             copy.wait()
-        if k >= 2:
-            self.sent(k - 2)
-        target = self.result.at[turn]
+        if k >= self.depth and k - self.depth not in self.early:
+            self.sent(k - self.depth)
+        target = self.result.at[k % self.depth]
         size = rows // 8
 
         def chunk(index, carry):
@@ -1509,7 +1511,7 @@
             return carry
 
         lax.fori_loop(0, 8, chunk, 0)
-        for here, away, local in sends(self.result.at[turn, pl.ds(0, rows)]):
+        for here, away, local in sends(self.result.at[k % self.depth, pl.ds(0, rows)]):
             self.either(here, away, local, "start")
         if then is not None:
             then()
@@ -1532,7 +1534,7 @@
 
     def sent(self, k):
         _, rows, _, sends, _, _, _ = self.items[k]
-        for here, away, local in sends(self.result.at[k % 2, pl.ds(0, rows)]):
+        for here, away, local in sends(self.result.at[k % self.depth, pl.ds(0, rows)]):
             self.either(here, away, local, "wait_send")
 
     def poll(self, unit):
@@ -1547,8 +1549,9 @@
                 self.add(k)
 
     def last_sent(self):
-        for k in range(len(self.items) - 2, len(self.items)):
-            self.sent(k)
+        for k in range(max(len(self.items) - self.depth, 0), len(self.items)):
+            if k not in self.early:
+                self.sent(k)
 
 
 def half_columns(half):
@@ -1742,6 +1745,9 @@
         work.sort(key=lambda item: item[0])
         for item in work:
             self.sums.item(*item)
+        last = [item[0] for item in work].index(64)
+        depth = self.sums.depth
+        self.sums.early = [k for k, item in enumerate(work) if item[0] in (37, 26) and k + depth >= last]
 
     def arrived(self, name):
         def wait():
@@ -1753,6 +1759,8 @@
         return wait
 
     def out_landed(self):
+        for k in self.sums.early:
+            self.sums.sent(k)
         remote(
             self.out_own, self.out_y_land, self.out_sems.at[0], self.out_sems.at[2], {"y": 1 - self.y}
         ).wait_recv()
@@ -2024,7 +2032,7 @@
             pltpu.VMEM((length, 128), F32),
             pltpu.VMEM((length, 128), F32),
             pltpu.VMEM((2, 4, ROW, 1024), BF),
-            pltpu.VMEM((2, ROW, 1024), BF),
+            pltpu.VMEM((8, ROW, 1024), BF),
             pltpu.VMEM((ROW, 1024), F32),
             dma((8,)),
             dma((8,)),

time: 1190 us -> 1130 us (0.950)
  Pallas kernels: 912 us -> 857 us
    pallas_call x1, Pallas kernels: 233 us -> 198 us  [attend_back(): pl.pallas_call(attend_back_kernel, grid=(blocks, 2), in_specs=[key_spec(2...]
    pallas_call x1, Pallas kernels: 148 us -> 127 us  [product_scatter(): pl.pallas_call(lambda *refs: scatter_kernel(dims, cut, len(more), *refs),...]
where the time goes in v7:
time: 1130 us; the launch traced here: 1120 us
  Pallas kernels  857 us (76%)
  matrix products  145 us (13%)
  other arithmetic  59.2 us (5%)
  waiting for transfers between devices  24.1 us (2%)
  starting transfers between devices  19.6 us (2%)
  local copies, waits for them, and re-layouts  13.9 us (1%)
    pallas_call x2, Pallas kernels, gather_product(): pl.pallas_call(lambda *refs: gather_kernel(finish, beside, inputs, len(ex...  227 us
    pallas_call x1, Pallas kernels, attend_back(): pl.pallas_call(attend_back_kernel, grid=(blocks, 2), in_specs=[key_spec(2...  198 us
    pallas_call x1, Pallas kernels, attend(): pl.pallas_call(attend_kernel, grid=(blocks, 4), in_specs=[pl.BlockSpec((R...  191 us
    pallas_call x1, Pallas kernels, product_scatter(): pl.pallas_call(lambda *refs: scatter_kernel(dims, cut, len(more), *refs),...  127 us
    pallas_call x1, Pallas kernels, feed_forward_back(): pl.pallas_call(lambda *refs: scatter_kernel(NT, ROW // 2, 3, *refs), in_s...  113 us
    dot_general x1, matrix products, ring_shards(): lax.dot_general(normed_second, grad_gate_up, TN, preferred_element_type=F32)  43.3 us
    ppermute x12, waiting for transfers between devices, move(): return lax.ppermute(values, AXES, device_pairs(target))  24.1 us
    dot_general x1, matrix products, ring_shards(): jnp.dot(activation, down_weight, preferred_element_type=F32).astype(BF)  23.8 us
  transfers between devices with their start and end apart: 12, of which 4 were waited for; matrix products, arithmetic and copies ran while one was open for 4% of the time, Pallas kernels for 0%

profile of v7, /device:TPU:0, one launch (start us, length us, event | category | flops | bytes accessed | tf_op | source)
XLA Modules:
  0.0 1122.8 jit_solution(14122840740249225767)
XLA Ops:
  3.6 3.8 collective-permute-start.1
  26.9 3.4 multiply_convert_fusion.1.refs_4_
  30.9 9.3 multiply_sine_fusion
  42.6 115.4 %shard_map.354 = (bf16[4096,2048]{1,0:T(8,128)(2,1)}, bf16[4096,256]{1,0:T(8,128)(2,1)}, bf16[4096,256]{1,0:T(8,128)(2,1)}, bf16[4096,256]{1,0:T(8,128)(2,1)}, b...) custom-call(bf16[512,2048]{1,0:T(8,128)(2,1)} %fusion.2.refs_0_, f32[4096,128]{1,0:T(8,128)} %get-tuple-element.102.refs_1_.refs_6_, ...), custom_call_target="tpu_custom_call" | custom-call | flops 80000000000 | bytes 31457280 | tf_op jit(solution)/shard_map/pallas_call | solution.py:777
  158.0 191.4 %shard_map.355 = (bf16[4096,256]{1,0:T(8,128)(2,1)S(1)}, f32[8,4,512]{2,1,0:T(4,128)S(1)}, bf16[2048,2048]{1,0:T(8,128)(2,1)}, bf16[2048,2048]{1,0:T(8,128)(2,1)...) custom-call(bf16[4096,256]{1,0:T(8,128)(2,1)} %get-tuple-element.50.q_ref, ...), custom_call_target="tpu_custom_call" | custom-call | flops 112000000000 | bytes 10485760 | tf_op jit(solution)/shard_map/pallas_call | solution.py:1424
  349.5 8.6 multiply_reduce_fusion.2
  360.7 112.0 %shard_map.356 = (bf16[4096,2048]{1,0:T(8,128)(2,1)}, bf16[4096,1024]{1,0:T(8,128)(2,1)}, bf16[4096,1024]{1,0:T(8,128)(2,1)}, bf16[4096,1024]{1,0:T(8,128)(2,1)}, bf16[1024,2048]{1,0:T(8,128)(2,1)}) custom-call(bf16[512,2048]{1,0:T(8,128)(2,1)} %multiply_convert_fusion.refs_0_, bf16[2048,2048]{1,0:T(8,128)(2,1)} %get-tuple-element.59.refs_1_.refs_4_, ...), custom_call_target="tpu_custom_call" | custom-call | flops 80000000000 | bytes 31457280 | tf_op jit(solution)/shard_map/pallas_call | solution.py:777
  472.8 23.8 %convolution_convert_fusion.refs_1_ = bf16[4096,2048]{1,0:T(8,128)(2,1)} fusion(bf16[4096,1024]{1,0:T(8,128)(2,1)} %get-tuple-element.64, bf16[1024,2048]{1,0:T(8,128)(2,1)} %get-tuple-element.62.refs_3_), kind=kOutput, calls=%fused_computation | convolution fusion | flops 17188257792 | bytes 29360128 | tf_op jit(solution)/shard_map/dot_general | solution.py:2154
  496.6 21.4 %convolution_convert_fusion.3.refs_3_ = bf16[2048,1024]{1,0:T(8,128)(2,1)} fusion(bf16[4096,2048]{1,0:T(8,128)(2,1)} %get-tuple-element.58.refs_0_, bf16[4096,1024]{1,0:T(8,128)(2,1)S(1)} %copy-done.65), kind=kOutput, calls=%fused_computation.35 | convolution fusion | flops 17181966336 | bytes 29360128 | tf_op jit(solution)/shard_map/dot_general | solution.py:2153
  518.0 113.1 %shard_map.357 = (f32[512,2048]{1,0:T(8,128)}, bf16[4096,2048]{1,0:T(8,128)(2,1)}) custom-call(bf16[4096,2048]{1,0:T(8,128)(2,1)} %get-tuple-element.58.refs_0_, bf16[4096,1024]{1,0:T(8,128)(2,1)} %get-tuple-element.60.refs_1_, bf16[4096,1024]{1,0:T(8,128)(2,1)} %get-tuple-element.61.refs_2_, bf16[1024,2048]{1,0:T(8,128)(2,1)} %get-tuple-element.62.refs_3_, ...), custom_call_target="tpu_custom_call" | custom-call | flops 80000000000 | bytes 62914560 | tf_op jit(solution)/shard_map/pallas_call | solution.py:1050
  631.2 5.2 multiply_reduce_fusion
  640.0 11.2 %convolution_convert_fusion.6.refs_0_ = bf16[512,2048]{1,0:T(8,128)(2,1)} fusion(bf16[2048,2048]{1,0:T(8,128)(2,1)} %get-tuple-element.57, f32[512,2048]{1,0:T(8,128)S(1)} %convert_add_fusion.1), kind=kOutput, calls=%fused_computation.56 | convolution fusion | flops 4297064448 | bytes 14680064 | tf_op jit(solution)/shard_map/dot_general | solution.py:2168
  651.2 6.9 convolution_convert_fusion.1.refs_4_
  658.1 43.3 %convolution_convert_fusion.2.refs_2_ = bf16[2048,2048]{1,0:T(8,128)(2,1)} fusion(bf16[4096,2048]{1,0:T(8,128)(2,1)} %get-tuple-element.65, bf16[4096,2048]{1,0:T(8,128)(2,1)} %get-tuple-element.66), kind=kOutput, calls=%fused_computation.7 | convolution fusion | flops 34363932672 | bytes 41943040 | tf_op jit(solution)/shard_map/dot_general | solution.py:2150
  701.4 197.6 %shard_map.358 = (bf16[4096,512]{1,0:T(8,128)(2,1)}, bf16[4096,256]{1,0:T(8,128)(2,1)}, bf16[2,512,2048]{2,1,0:T(8,128)(2,1)}, bf16[2,512,1024]{2,1,0:T(8,128)(2...) custom-call(bf16[4096,256]{1,0:T(8,128)(2,1)} %get-tuple-element.50., ...), custom_call_target="tpu_custom_call" | custom-call | flops 152000004096 | bytes 20971520 | tf_op jit(solution)/shard_map/pallas_call | solution.py:2012
  902.4 19.7 %convolution_convert_fusion.4.clone.5 = bf16[2048,768]{1,0:T(8,128)(2,1)S(1)} fusion(bf16[4096,2048]{1,0:T(8,128)(2,1)} %get-tuple-element.70, bf16[4096,768]{1,0:T(8,128)(2,1)S(1)} %constant_dynamic-update-slice_fusion.refs_0_), kind=kOutput, calls=%fused_computation.52.clone.clone.clone.2 | convolution fusion | flops 12886474752 | bytes 26214400 | tf_op jit(solution)/shard_map/dot_general | solution.py:2181
  922.2 4.9 convolution_convert_fusion.5.refs_2_
  927.1 127.3 %shard_map.359 = (f32[512,2048]{1,0:T(8,128)}, bf16[2,512,768]{2,1,0:T(8,128)(2,1)}, bf16[2,512,768]{2,1,0:T(8,128)(2,1)}, bf16[512,2048]{1,0:T(8,128)(2,1)}) custom-call(bf16[4096,768]{1,0:T(8,128)(2,1)} %copy-done.34, bf16[2048,768]{1,0:T(8,128)(2,1)} %get-tuple-element.69.refs_1_, bf16[2048,768]{1,0:T(8,128)(2,1)} %convolution_convert_fusion.5.refs_2_, ...), custom_call_target="tpu_custom_call" | custom-call | flops 80000000000 | bytes 31457280 | tf_op jit(solution)/shard_map/pallas_call | solution.py:1080
  1054.5 3.6 fusion.11
  1058.1 3.7 fusion.7
  1066.9 3.6 fusion.60
  1076.3 3.3 fusion.59
  1089.1 3.8 collective-permute-start.10
  1093.9 19.5 %collective-permute-done.10 = f32[2,2048]{1,0:T(2,128)S(1)} collective-permute-done((f32[2,2048]{1,0:T(2,128)S(1)}, f32[2,2048]{1,0:T(2,128)S(1)}, u32[]{:S(2)}, u32[]{:S(2)}) %collective-permute-start.10) | collective-permute-done | bytes 16416 | tf_op jit(solution)/shard_map/ppermute | solution.py:354
  (197 shorter events, 63.1 us)
Async XLA Ops:
  0.7 39.6 %collective-permute-start = (bf16[512,2048]{1,0:T(8,128)(2,1)}, bf16[512,2048]{1,0:T(8,128)(2,1)S(1)}, u32[]{:S(2)}, u32[]{:S(2)}) collective-permute-start(bf16[512,2048]{1,0:T(8,128)(2,1)} %param.19), channel_id=1, source_target_pairs={{0,0},{1,1},{2,2},{3,3},{4,8},{5,9},{6,10},{7,11},{8,4},{9,5},{10,... | collective-permute-start | bytes 6291464 | tf_op jit(solution)/shard_map/ppermute | solution.py:354
  3.6 21.6 %collective-permute-start.1 = (bf16[2,512]{1,0:T(2,128)(2,1)S(1)}, bf16[2,512]{1,0:T(2,128)(2,1)S(1)}, u32[]{:S(2)}, u32[]{:S(2)}) collective-permute-start(bf16[2,512]{1,0:T(2,128)(2,1)S(1)} %convert_element_type.124), channel_id=1, source_target_pairs={{0,8},{1,9},{2,10},{3,11},{4,12},{5,13},{6,14},{7,15},{8,0},{9,1},... | collective-permute-start | bytes 6152 | tf_op jit(solution)/shard_map/ppermute | solution.py:354
  7.4 23.5 %collective-permute-start.3 = (s32[4096]{0:T(1024)}, s32[4096]{0:T(1024)S(1)}, u32[]{:S(2)}, u32[]{:S(2)}) collective-permute-start(s32[4096]{0:T(1024)} %param.22), channel_id=1, source_target_pairs={{0,8},{1,9},{2,10},{3,11},{4,12},{5,13},{6,14},{7,15},{8,0},{9,1},... | collective-permute-start | bytes 49160 | tf_op jit(solution)/shard_map/ppermute | solution.py:354
  8.1 12.2 %collective-permute-start.4 = (f32[1]{0:T(128)}, f32[1]{0:T(128)}, u32[]{:S(2)}, u32[]{:S(2)}) collective-permute-start(f32[1]{0:T(128)} %convert_element_type.132), channel_id=1, source_target_pairs={{0,8},{1,9},{2,10},{3,11},{4,12},{5,13},{6,14},{7,15},{8,0},{9,1},... | collective-permute-start | bytes 20 | tf_op jit(solution)/shard_map/ppermute | solution.py:354
  20.9 3.7 collective-permute-start.5
  25.3 5.0 collective-permute-start.2
  158.0 191.5 %copy-start.7 = (bf16[512,2048]{1,0:T(8,128)(2,1)S(1)}, bf16[512,2048]{1,0:T(8,128)(2,1)}, u32[]{:S(2)}) copy-start(bf16[512,2048]{1,0:T(8,128)(2,1)} %copy-done.6) | copy-start | bytes 6291460
  472.8 23.8 %copy-start.65 = (bf16[4096,1024]{1,0:T(8,128)(2,1)S(1)}, bf16[4096,1024]{1,0:T(8,128)(2,1)}, u32[]{:S(2)}) copy-start(bf16[4096,1024]{1,0:T(8,128)(2,1)} %get-tuple-element.64) | copy-start | bytes 25165828
  518.0 113.2 %copy-start.41 = (f32[1,2048]{1,0:T(1,128)S(1)}, f32[1,2048]{1,0:T(1,128)}, u32[]{:S(2)}) copy-start(f32[1,2048]{1,0:T(1,128)} %get-tuple-element.103) | copy-start | bytes 24580
  518.0 113.2 %copy-start.48 = (f32[512]{0:T(512)S(1)}, f32[512]{0:T(512)}, u32[]{:S(2)}) copy-start(f32[512]{0:T(512)} %copy-done.47) | copy-start | bytes 6148
  927.1 127.3 %copy-start.8 = (bf16[512,2048]{1,0:T(8,128)(2,1)S(1)}, bf16[512,2048]{1,0:T(8,128)(2,1)}, u32[]{:S(2)}) copy-start(bf16[512,2048]{1,0:T(8,128)(2,1)} %copy-done.6) | copy-start | bytes 6291460
  927.1 127.3 %copy-start.39 = (f32[1,2048]{1,0:T(1,128)S(1)}, f32[1,2048]{1,0:T(1,128)}, u32[]{:S(2)}) copy-start(f32[1,2048]{1,0:T(1,128)} %copy-done.38) | copy-start | bytes 24580
  927.1 127.3 %copy-start.46 = (f32[512]{0:T(512)S(1)}, f32[512]{0:T(512)}, u32[]{:S(2)}) copy-start(f32[512]{0:T(512)} %copy-done.45) | copy-start | bytes 6148
  1061.8 56.6 %collective-permute-start.6 = (bf16[512,2048]{1,0:T(8,128)(2,1)S(1)}, bf16[512,2048]{1,0:T(8,128)(2,1)S(1)}, u32[]{:S(2)}, u32[]{:S(2)}) collective-permute-start(bf16[512,2048]{1,0:T(8,128)(2,1)S(1)} %fusion.7), channel_id=1, source_target_pairs={{0,0},{1,1},{2,2},{3,3},{4,8},{5,9},{6,10},{7,11},{8,4},{9,5},{10,... | collective-permute-start | bytes 6291464 | tf_op jit(solution)/shard_map/ppermute | solution.py:354
  1063.8 17.8 %collective-permute-start.7 = (f32[2,2048]{1,0:T(2,128)S(1)}, f32[2,2048]{1,0:T(2,128)S(1)}, u32[]{:S(2)}, u32[]{:S(2)}) collective-permute-start(f32[2,2048]{1,0:T(2,128)S(1)} %pad_maximum_fusion.2), channel_id=1, source_target_pairs={{0,1},{1,0},{2,3},{3,2},{4,5},{5,4},{6,7},{7,6},{8,9},{9,8},{10,11... | collective-permute-start | bytes 49160 | tf_op jit(solution)/shard_map/ppermute | solution.py:354
  1081.6 3.8 collective-permute-start.8
  1085.5 3.6 collective-permute-start.9
  1089.0 24.5 %copy-start.35 = (f32[256,512]{1,0:T(8,128)S(1)}, f32[256,512]{1,0:T(8,128)}, u32[]{:S(2)}) copy-start(f32[256,512]{1,0:T(8,128)} %param.28) | copy-start | bytes 1572868
  1089.0 28.2 %copy-start.44 = (f32[2,512]{1,0:T(2,128)S(1)}, f32[2,512]{1,0:T(2,128)}, u32[]{:S(2)}) copy-start(f32[2,512]{1,0:T(2,128)} %param.35) | copy-start | bytes 12292
  1089.0 28.2 %copy-start.60 = (f32[2,512]{1,0:T(2,128)S(1)}, f32[2,512]{1,0:T(2,128)}, u32[]{:S(2)}) copy-start(f32[2,512]{1,0:T(2,128)} %param.36) | copy-start | bytes 12292
  1089.0 28.8 %copy-start.51 = (f32[2,512]{1,0:T(2,128)S(1)}, f32[2,512]{1,0:T(2,128)}, u32[]{:S(2)}) copy-start(f32[2,512]{1,0:T(2,128)} %param.37) | copy-start | bytes 12292
  1089.1 24.4 %collective-permute-start.10 = (f32[2,2048]{1,0:T(2,128)S(1)}, f32[2,2048]{1,0:T(2,128)S(1)}, u32[]{:S(2)}, u32[]{:S(2)}) collective-permute-start(f32[2,2048]{1,0:T(2,128)S(1)} %add.228), channel_id=1, source_target_pairs={{0,4},{1,5},{2,6},{3,7},{4,0},{5,1},{6,2},{7,3},{8,12},{9,13},{10,... | collective-permute-start | bytes 49160 | tf_op jit(solution)/shard_map/ppermute | solution.py:354
  1093.9 27.1 %copy-start.23 = (f32[256,512]{1,0:T(8,128)}, f32[256,512]{1,0:T(8,128)S(1)}, u32[]{:S(2)}) copy-start(f32[256,512]{1,0:T(8,128)S(1)} %get-tuple-element.145) | copy-start | bytes 1572868
  1113.4 3.8 collective-permute-start.11
  (54 other events, 372.9 us)

commit v8 on v7

--- a/solution.py
+++ b/solution.py
@@ -1076,7 +1076,7 @@
     vmem = pl.BlockSpec(memory_space=pltpu.VMEM)
     depth = a.shape[1]
     width = weight.shape[0] if dims == NT else weight.shape[1]
-    cut = 384 if more else 256
+    cut = 448 if more else 256
     return pl.pallas_call(
         lambda *refs: scatter_kernel(dims, cut, len(more), *refs),
         in_specs=[anywhere, vmem] + [anywhere] * len(more),
@@ -1273,13 +1273,12 @@
         when(0, self.begin)
         when(3, out_on)
         when(6, out_ring_on)
-        when(7, grad_one)
-        when(9, lambda: self.piece_over_y(0), self.pieces[2].start)
-        when(11, grad_two)
+        when(9, grad_one, lambda: self.piece_over_y(0), self.pieces[2].start)
+        when(12, grad_two)
         when(14, lambda: self.piece_over_y(1), self.pieces[3].start)
-        when(16, out_one)
+        when(17, out_one)
         when(19, lambda: self.piece_over_y(2))
-        when(22, out_two)
+        when(24, out_two)
         when(28, lambda: self.piece_over_y(3))
 
     def row_local(self, block, o_all):
@@ -1738,7 +1737,7 @@
         self.out_pieces = PieceSums(out_names, None, None, self.sums_at, out_y_sems, out_z_sems)
         work = self.layer_ring.work((22, 35, 48, 61, 36, 56, 62, 70), self.layer_sends, self.residual_half)
         work += self.out_ring.work((1, 2, 8, 14, 15, 25, 37, 26), self.out_sends, lambda half: None)
-        for name, due in zip(names, (3, 16, 29, 44, 57, 69)):
+        for name, due in zip(names, (3, 12, 24, 38, 47, 58)):
             terms = [self.piece(name, self.y), self.y_land.at[names.index(name)]]
             work.append((due, ROW, terms, self.pieces.sends(name), [self.arrived(name)], None))
         work.append((64, 256, [self.out_own, self.out_y_land], self.out_owners, [self.out_landed], None))
@@ -1752,7 +1751,7 @@
     def arrived(self, name):
         def wait():
             self.pieces.over_y(name).wait_recv()
-            place = self.names.index(name) + 1
+            place = self.names.index(name) + 2
             if place < 6:
                 self.pieces.over_y(self.names[place]).start()
 
@@ -1855,7 +1854,8 @@
         lax.fori_loop(0, 8, send, 0)
         self.layer_ring.begin()
         self.out_ring.begin()
-        self.pieces.over_y(self.names[0]).start()
+        for name in self.names[:2]:
+            self.pieces.over_y(name).start()
         for copy in self.tables():
             copy.wait()
 

time: 1130 us -> 1120 us (level)
  no operation moved by 1% of the time
where the time goes in v8:
time: 1120 us; the launch traced here: 1110 us
  Pallas kernels  848 us (76%)
  matrix products  145 us (13%)
  other arithmetic  59.2 us (5%)
  waiting for transfers between devices  23.1 us (2%)
  starting transfers between devices  20.3 us (2%)
  local copies, waits for them, and re-layouts  13 us (1%)
    pallas_call x2, Pallas kernels, gather_product(): pl.pallas_call(lambda *refs: gather_kernel(finish, beside, inputs, len(ex...  227 us
    pallas_call x1, Pallas kernels, attend_back(): pl.pallas_call(attend_back_kernel, grid=(blocks, 2), in_specs=[key_spec(2...  199 us
    pallas_call x1, Pallas kernels, attend(): pl.pallas_call(attend_kernel, grid=(blocks, 4), in_specs=[pl.BlockSpec((R...  187 us
    pallas_call x1, Pallas kernels, product_scatter(): pl.pallas_call(lambda *refs: scatter_kernel(dims, cut, len(more), *refs),...  122 us
    pallas_call x1, Pallas kernels, feed_forward_back(): pl.pallas_call(lambda *refs: scatter_kernel(NT, ROW // 2, 3, *refs), in_s...  113 us
    dot_general x1, matrix products, ring_shards(): lax.dot_general(normed_second, grad_gate_up, TN, preferred_element_type=F32)  43.3 us
    dot_general x1, matrix products, ring_shards(): jnp.dot(activation, down_weight, preferred_element_type=F32).astype(BF)  23.8 us
    ppermute x12, waiting for transfers between devices, move(): return lax.ppermute(values, AXES, device_pairs(target))  23.1 us
  transfers between devices with their start and end apart: 12, of which 4 were waited for; matrix products, arithmetic and copies ran while one was open for 4% of the time, Pallas kernels for 0%

profile of v8, /device:TPU:0, one launch (start us, length us, event | category | flops | bytes accessed | tf_op | source)
XLA Modules:
  0.0 1113.3 jit_solution(5934916205065451785)
XLA Ops:
  3.6 3.8 collective-permute-start.1
  26.9 3.4 multiply_convert_fusion.1.refs_4_
  30.9 9.3 multiply_sine_fusion
  42.6 115.4 %shard_map.354 = (bf16[4096,2048]{1,0:T(8,128)(2,1)}, bf16[4096,256]{1,0:T(8,128)(2,1)}, bf16[4096,256]{1,0:T(8,128)(2,1)}, bf16[4096,256]{1,0:T(8,128)(2,1)}, b...) custom-call(bf16[512,2048]{1,0:T(8,128)(2,1)} %fusion.2.refs_0_, f32[4096,128]{1,0:T(8,128)} %get-tuple-element.102.refs_1_.refs_6_, ...), custom_call_target="tpu_custom_call" | custom-call | flops 80000000000 | bytes 31457280 | tf_op jit(solution)/shard_map/pallas_call | solution.py:777
  158.0 186.6 %shard_map.355 = (bf16[4096,256]{1,0:T(8,128)(2,1)S(1)}, f32[8,4,512]{2,1,0:T(4,128)S(1)}, bf16[2048,2048]{1,0:T(8,128)(2,1)}, bf16[2048,2048]{1,0:T(8,128)(2,1)...) custom-call(bf16[4096,256]{1,0:T(8,128)(2,1)} %get-tuple-element.50.q_ref, ...), custom_call_target="tpu_custom_call" | custom-call | flops 112000000000 | bytes 10485760 | tf_op jit(solution)/shard_map/pallas_call | solution.py:1423
  344.7 8.6 multiply_reduce_fusion.2
  356.0 112.0 %shard_map.356 = (bf16[4096,2048]{1,0:T(8,128)(2,1)}, bf16[4096,1024]{1,0:T(8,128)(2,1)}, bf16[4096,1024]{1,0:T(8,128)(2,1)}, bf16[4096,1024]{1,0:T(8,128)(2,1)}, bf16[1024,2048]{1,0:T(8,128)(2,1)}) custom-call(bf16[512,2048]{1,0:T(8,128)(2,1)} %multiply_convert_fusion.refs_0_, bf16[2048,2048]{1,0:T(8,128)(2,1)} %get-tuple-element.59.refs_1_.refs_4_, ...), custom_call_target="tpu_custom_call" | custom-call | flops 80000000000 | bytes 31457280 | tf_op jit(solution)/shard_map/pallas_call | solution.py:777
  468.0 23.8 %convolution_convert_fusion.refs_1_ = bf16[4096,2048]{1,0:T(8,128)(2,1)} fusion(bf16[4096,1024]{1,0:T(8,128)(2,1)} %get-tuple-element.64, bf16[1024,2048]{1,0:T(8,128)(2,1)} %get-tuple-element.62.refs_3_), kind=kOutput, calls=%fused_computation | convolution fusion | flops 17188257792 | bytes 29360128 | tf_op jit(solution)/shard_map/dot_general | solution.py:2154
  491.8 21.4 %convolution_convert_fusion.3.refs_3_ = bf16[2048,1024]{1,0:T(8,128)(2,1)} fusion(bf16[4096,2048]{1,0:T(8,128)(2,1)} %get-tuple-element.58.refs_0_, bf16[4096,1024]{1,0:T(8,128)(2,1)S(1)} %copy-done.65), kind=kOutput, calls=%fused_computation.35 | convolution fusion | flops 17181966336 | bytes 29360128 | tf_op jit(solution)/shard_map/dot_general | solution.py:2153
  513.2 113.1 %shard_map.357 = (f32[512,2048]{1,0:T(8,128)}, bf16[4096,2048]{1,0:T(8,128)(2,1)}) custom-call(bf16[4096,2048]{1,0:T(8,128)(2,1)} %get-tuple-element.58.refs_0_, bf16[4096,1024]{1,0:T(8,128)(2,1)} %get-tuple-element.60.refs_1_, bf16[4096,1024]{1,0:T(8,128)(2,1)} %get-tuple-element.61.refs_2_, bf16[1024,2048]{1,0:T(8,128)(2,1)} %get-tuple-element.62.refs_3_, ...), custom_call_target="tpu_custom_call" | custom-call | flops 80000000000 | bytes 62914560 | tf_op jit(solution)/shard_map/pallas_call | solution.py:1050
  626.4 5.2 multiply_reduce_fusion
  635.2 11.2 %convolution_convert_fusion.6.refs_0_ = bf16[512,2048]{1,0:T(8,128)(2,1)} fusion(bf16[2048,2048]{1,0:T(8,128)(2,1)} %get-tuple-element.57, f32[512,2048]{1,0:T(8,128)S(1)} %convert_add_fusion.1), kind=kOutput, calls=%fused_computation.56 | convolution fusion | flops 4297064448 | bytes 14680064 | tf_op jit(solution)/shard_map/dot_general | solution.py:2168
  646.4 6.9 convolution_convert_fusion.1.refs_4_
  653.3 43.3 %convolution_convert_fusion.2.refs_2_ = bf16[2048,2048]{1,0:T(8,128)(2,1)} fusion(bf16[4096,2048]{1,0:T(8,128)(2,1)} %get-tuple-element.65, bf16[4096,2048]{1,0:T(8,128)(2,1)} %get-tuple-element.66), kind=kOutput, calls=%fused_computation.7 | convolution fusion | flops 34363932672 | bytes 41943040 | tf_op jit(solution)/shard_map/dot_general | solution.py:2150
  696.6 198.9 %shard_map.358 = (bf16[4096,512]{1,0:T(8,128)(2,1)}, bf16[4096,256]{1,0:T(8,128)(2,1)}, bf16[2,512,2048]{2,1,0:T(8,128)(2,1)}, bf16[2,512,1024]{2,1,0:T(8,128)(2...) custom-call(bf16[4096,256]{1,0:T(8,128)(2,1)} %get-tuple-element.50., ...), custom_call_target="tpu_custom_call" | custom-call | flops 152000004096 | bytes 20971520 | tf_op jit(solution)/shard_map/pallas_call | solution.py:2012
  899.0 19.7 %convolution_convert_fusion.4.clone.5 = bf16[2048,768]{1,0:T(8,128)(2,1)S(1)} fusion(bf16[4096,2048]{1,0:T(8,128)(2,1)} %get-tuple-element.70, bf16[4096,768]{1,0:T(8,128)(2,1)S(1)} %constant_dynamic-update-slice_fusion.refs_0_), kind=kOutput, calls=%fused_computation.52.clone.clone.clone.2 | convolution fusion | flops 12886474752 | bytes 26214400 | tf_op jit(solution)/shard_map/dot_general | solution.py:2181
  918.7 4.9 convolution_convert_fusion.5.refs_2_
  923.7 122.4 %shard_map.359 = (f32[512,2048]{1,0:T(8,128)}, bf16[2,512,768]{2,1,0:T(8,128)(2,1)}, bf16[2,512,768]{2,1,0:T(8,128)(2,1)}, bf16[512,2048]{1,0:T(8,128)(2,1)}) custom-call(bf16[4096,768]{1,0:T(8,128)(2,1)} %copy-done.34, bf16[2048,768]{1,0:T(8,128)(2,1)} %get-tuple-element.69.refs_1_, bf16[2048,768]{1,0:T(8,128)(2,1)} %convolution_convert_fusion.5.refs_2_, ...), custom_call_target="tpu_custom_call" | custom-call | flops 80000000000 | bytes 31457280 | tf_op jit(solution)/shard_map/pallas_call | solution.py:1080
  1046.1 3.6 fusion.11
  1049.8 3.7 fusion.7
  1058.6 3.6 fusion.60
  1068.0 3.3 fusion.59
  1080.6 3.8 collective-permute-start.10
  1085.4 18.6 %collective-permute-done.10 = f32[2,2048]{1,0:T(2,128)S(1)} collective-permute-done((f32[2,2048]{1,0:T(2,128)S(1)}, f32[2,2048]{1,0:T(2,128)S(1)}, u32[]{:S(2)}, u32[]{:S(2)}) %collective-permute-start.10) | collective-permute-done | bytes 16416 | tf_op jit(solution)/shard_map/ppermute | solution.py:354
  (197 shorter events, 62.9 us)
Async XLA Ops:
  0.7 39.6 %collective-permute-start = (bf16[512,2048]{1,0:T(8,128)(2,1)}, bf16[512,2048]{1,0:T(8,128)(2,1)S(1)}, u32[]{:S(2)}, u32[]{:S(2)}) collective-permute-start(bf16[512,2048]{1,0:T(8,128)(2,1)} %param.19), channel_id=1, source_target_pairs={{0,0},{1,1},{2,2},{3,3},{4,8},{5,9},{6,10},{7,11},{8,4},{9,5},{10,... | collective-permute-start | bytes 6291464 | tf_op jit(solution)/shard_map/ppermute | solution.py:354
  3.6 21.6 %collective-permute-start.1 = (bf16[2,512]{1,0:T(2,128)(2,1)S(1)}, bf16[2,512]{1,0:T(2,128)(2,1)S(1)}, u32[]{:S(2)}, u32[]{:S(2)}) collective-permute-start(bf16[2,512]{1,0:T(2,128)(2,1)S(1)} %convert_element_type.124), channel_id=1, source_target_pairs={{0,8},{1,9},{2,10},{3,11},{4,12},{5,13},{6,14},{7,15},{8,0},{9,1},... | collective-permute-start | bytes 6152 | tf_op jit(solution)/shard_map/ppermute | solution.py:354
  7.4 23.5 %collective-permute-start.3 = (s32[4096]{0:T(1024)}, s32[4096]{0:T(1024)S(1)}, u32[]{:S(2)}, u32[]{:S(2)}) collective-permute-start(s32[4096]{0:T(1024)} %param.22), channel_id=1, source_target_pairs={{0,8},{1,9},{2,10},{3,11},{4,12},{5,13},{6,14},{7,15},{8,0},{9,1},... | collective-permute-start | bytes 49160 | tf_op jit(solution)/shard_map/ppermute | solution.py:354
  8.1 12.2 %collective-permute-start.4 = (f32[1]{0:T(128)}, f32[1]{0:T(128)}, u32[]{:S(2)}, u32[]{:S(2)}) collective-permute-start(f32[1]{0:T(128)} %convert_element_type.132), channel_id=1, source_target_pairs={{0,8},{1,9},{2,10},{3,11},{4,12},{5,13},{6,14},{7,15},{8,0},{9,1},... | collective-permute-start | bytes 20 | tf_op jit(solution)/shard_map/ppermute | solution.py:354
  20.9 3.7 collective-permute-start.5
  25.3 5.0 collective-permute-start.2
  158.0 186.7 %copy-start.7 = (bf16[512,2048]{1,0:T(8,128)(2,1)S(1)}, bf16[512,2048]{1,0:T(8,128)(2,1)}, u32[]{:S(2)}) copy-start(bf16[512,2048]{1,0:T(8,128)(2,1)} %copy-done.6) | copy-start | bytes 6291460
  468.0 23.8 %copy-start.65 = (bf16[4096,1024]{1,0:T(8,128)(2,1)S(1)}, bf16[4096,1024]{1,0:T(8,128)(2,1)}, u32[]{:S(2)}) copy-start(bf16[4096,1024]{1,0:T(8,128)(2,1)} %get-tuple-element.64) | copy-start | bytes 25165828
  513.2 113.2 %copy-start.41 = (f32[1,2048]{1,0:T(1,128)S(1)}, f32[1,2048]{1,0:T(1,128)}, u32[]{:S(2)}) copy-start(f32[1,2048]{1,0:T(1,128)} %get-tuple-element.103) | copy-start | bytes 24580
  513.2 113.2 %copy-start.48 = (f32[512]{0:T(512)S(1)}, f32[512]{0:T(512)}, u32[]{:S(2)}) copy-start(f32[512]{0:T(512)} %copy-done.47) | copy-start | bytes 6148
  923.7 122.4 %copy-start.8 = (bf16[512,2048]{1,0:T(8,128)(2,1)S(1)}, bf16[512,2048]{1,0:T(8,128)(2,1)}, u32[]{:S(2)}) copy-start(bf16[512,2048]{1,0:T(8,128)(2,1)} %copy-done.6) | copy-start | bytes 6291460
  923.7 122.4 %copy-start.39 = (f32[1,2048]{1,0:T(1,128)S(1)}, f32[1,2048]{1,0:T(1,128)}, u32[]{:S(2)}) copy-start(f32[1,2048]{1,0:T(1,128)} %copy-done.38) | copy-start | bytes 24580
  923.7 122.4 %copy-start.46 = (f32[512]{0:T(512)S(1)}, f32[512]{0:T(512)}, u32[]{:S(2)}) copy-start(f32[512]{0:T(512)} %copy-done.45) | copy-start | bytes 6148
  1053.5 55.5 %collective-permute-start.6 = (bf16[512,2048]{1,0:T(8,128)(2,1)S(1)}, bf16[512,2048]{1,0:T(8,128)(2,1)S(1)}, u32[]{:S(2)}, u32[]{:S(2)}) collective-permute-start(bf16[512,2048]{1,0:T(8,128)(2,1)S(1)} %fusion.7), channel_id=1, source_target_pairs={{0,0},{1,1},{2,2},{3,3},{4,8},{5,9},{6,10},{7,11},{8,4},{9,5},{10,... | collective-permute-start | bytes 6291464 | tf_op jit(solution)/shard_map/ppermute | solution.py:354
  1055.5 17.8 %collective-permute-start.7 = (f32[2,2048]{1,0:T(2,128)S(1)}, f32[2,2048]{1,0:T(2,128)S(1)}, u32[]{:S(2)}, u32[]{:S(2)}) collective-permute-start(f32[2,2048]{1,0:T(2,128)S(1)} %pad_maximum_fusion.2), channel_id=1, source_target_pairs={{0,1},{1,0},{2,3},{3,2},{4,5},{5,4},{6,7},{7,6},{8,9},{9,8},{10,11... | collective-permute-start | bytes 49160 | tf_op jit(solution)/shard_map/ppermute | solution.py:354
  1073.3 3.8 collective-permute-start.8
  1077.2 3.4 collective-permute-start.9
  1080.5 23.5 %copy-start.35 = (f32[256,512]{1,0:T(8,128)S(1)}, f32[256,512]{1,0:T(8,128)}, u32[]{:S(2)}) copy-start(f32[256,512]{1,0:T(8,128)} %param.28) | copy-start | bytes 1572868
  1080.5 27.3 %copy-start.44 = (f32[2,512]{1,0:T(2,128)S(1)}, f32[2,512]{1,0:T(2,128)}, u32[]{:S(2)}) copy-start(f32[2,512]{1,0:T(2,128)} %param.35) | copy-start | bytes 12292
  1080.5 27.3 %copy-start.60 = (f32[2,512]{1,0:T(2,128)S(1)}, f32[2,512]{1,0:T(2,128)}, u32[]{:S(2)}) copy-start(f32[2,512]{1,0:T(2,128)} %param.36) | copy-start | bytes 12292
  1080.5 27.9 %copy-start.51 = (f32[2,512]{1,0:T(2,128)S(1)}, f32[2,512]{1,0:T(2,128)}, u32[]{:S(2)}) copy-start(f32[2,512]{1,0:T(2,128)} %param.37) | copy-start | bytes 12292
  1080.6 23.4 %collective-permute-start.10 = (f32[2,2048]{1,0:T(2,128)S(1)}, f32[2,2048]{1,0:T(2,128)S(1)}, u32[]{:S(2)}, u32[]{:S(2)}) collective-permute-start(f32[2,2048]{1,0:T(2,128)S(1)} %add.228), channel_id=1, source_target_pairs={{0,4},{1,5},{2,6},{3,7},{4,0},{5,1},{6,2},{7,3},{8,12},{9,13},{10,... | collective-permute-start | bytes 49160 | tf_op jit(solution)/shard_map/ppermute | solution.py:354
  1085.4 26.1 %copy-start.23 = (f32[256,512]{1,0:T(8,128)}, f32[256,512]{1,0:T(8,128)S(1)}, u32[]{:S(2)}) copy-start(f32[256,512]{1,0:T(8,128)S(1)} %get-tuple-element.145) | copy-start | bytes 1572868
  1104.0 3.8 collective-permute-start.11
  (54 other events, 372.6 us)
